TPU v7x, 32 devices: a whole 2x2x4 slice. The times are simulated.
32 devices in a mesh: inl: 8 (over y, x, core), xl: 4 (over z).
Axes of the slice: x: 2, y: 2, z: 4, core: 2. Of those that a mesh axis runs over, the one named last changes fastest.
Arguments:
- traces: bfloat16 [8192, 512], P(('inl', 'xl')), may hold values from -6 to 6
- trace_owner: int32 [8192, 1], P(('inl', 'xl')), may hold values from 0 to 31, as said below
- trace_cell: int32 [8192], P(('inl', 'xl')), may hold values from 0 to 1023, as said below
- acquired: int32 [8192], P(('inl', 'xl')), may hold values 0 or 1
- inline_dip: float32 [64, 512, 512], P('inl', 'xl'), may hold values from -1 to 1
- cross_dip: float32 [64, 512, 512], P('inl', 'xl'), may hold values from -1 to 1
Outputs:
- model: float32 [64, 512, 512], P('inl', 'xl')
- residual: float32 [64, 512, 512], P('inl', 'xl')
Inputs may be any that keep to these rules, and one draw needn't show every extreme that they name: `trace_owner`: owners are numbered inline tile times n_xl plus crossline tile. Among the 256 traces of one device at most 16 name one owner, and some owner is named exactly 16 times by some device. `trace_cell`: bin within the owner's tile, crossline fastest; several traces may share a bin.
All inputs are finite; a program needn't handle non-finite values. No bound on the sum of `acquired` on one device may be relied on, other than what follows from the above.
Results may differ from a plain program's by a relative error of at most 0.0003.
Values may be sent and summed in bfloat16 or wider, within the bound.
No kernel may reach another device: no remote copies, remote signals or barrier semaphores. Data moves between devices by JAX's collectives and lax.ppermute only.
A program may use at most 128 MiB of HBM per device.

v0:
```python
import jax
import jax.numpy as jnp
from jax import lax
from jax.sharding import PartitionSpec as P

ITERS = 3


reg_weight = 0.5


def shifted(value, axis, steps):
    count = lax.axis_size(axis)
    initial, last = (max(0, -steps), min(count, count - steps))
    return lax.ppermute(value, axis, [(source, source + steps) for source in range(initial, last)])


def time_earlier(field):
    return jnp.pad(field[:, :, :-1], ((0, 0), (0, 0), (1, 0)))


def time_later(field):
    return jnp.pad(field[:, :, 1:], ((0, 0), (0, 0), (0, 1)))


def lagrange(slope):
    return (0.5 * (slope * slope + slope), 1.0 - slope * slope, 0.5 * (slope * slope - slope))


def delay(field, slope):
    lower, centre, upper = lagrange(slope)
    return lower * time_earlier(field) + centre * field + upper * time_later(field)


def delay_adjoint(field, slope):
    lower, centre, upper = lagrange(slope)
    return time_earlier(upper * field) + centre * field + time_later(lower * field)


def bin_traces(traces, trace_owner, trace_cell, acquired, tile_rows, tile_cols):
    devices = lax.axis_size("inl") * lax.axis_size("xl")
    held = traces.shape[0]
    capacity = max(2, 2 * held // devices)
    owner = trace_owner[:, 0]
    owner_hot = (owner[:, None] == jnp.arange(devices, dtype=jnp.int32)[None, :]).astype(jnp.int32)
    ranks = jnp.cumsum(owner_hot, axis=0) - 1
    rank = jnp.sum(ranks * owner_hot, axis=1)
    slot = owner * capacity + rank
    upper_code = jnp.where(acquired > 0, trace_cell // 64, -1)
    codes = jnp.stack([upper_code, trace_cell % 64], axis=1).astype(jnp.bfloat16)
    send_rows = jnp.zeros((devices * capacity, traces.shape[1]), jnp.bfloat16).at[slot].set(traces)
    send_codes = jnp.full((devices * capacity, 2), -1.0, jnp.bfloat16).at[slot].set(codes)
    got_rows, got_codes = (
        lax.all_to_all(send_rows, ("inl", "xl"), split_axis=0, concat_axis=0, tiled=True),
        lax.all_to_all(send_codes, ("inl", "xl"), split_axis=0, concat_axis=0, tiled=True),
    )
    cell_value = got_codes[:, 0].astype(jnp.float32) * 64.0 + got_codes[:, 1].astype(jnp.float32)
    cells = jnp.arange(tile_rows * tile_cols, dtype=jnp.float32)
    placed = (cells[:, None] == cell_value[None, :]).astype(jnp.bfloat16)
    data_sum = jnp.dot(placed, got_rows, preferred_element_type=jnp.float32)
    hits = jnp.sum(placed.astype(jnp.float32), axis=1)
    return (data_sum.reshape(tile_rows, tile_cols, -1), hits.reshape(tile_rows, tile_cols, 1))


def per_device(traces, trace_owner, trace_cell, acquired, inline_dip, cross_dip):
    tile_rows, tile_cols = (inline_dip.shape[0], inline_dip.shape[1])
    data_sum, hits = bin_traces(traces, trace_owner, trace_cell, acquired, tile_rows, tile_cols)
    model = jnp.zeros_like(data_sum)
    residual = data_sum
    direction = data_sum

    def squares(field):
        return lax.psum(jnp.sum(field * field), ("inl", "xl"))

    norm_now = squares(residual)
    for sweep in range(ITERS):
        next_row = shifted(direction[:1], "inl", -1)
        next_col = shifted(direction[:, :1], "xl", -1)
        first = jnp.concatenate([direction[1:], next_row], 0) - delay(direction, inline_dip)
        second = jnp.concatenate([direction[:, 1:], next_col], 1) - delay(direction, cross_dip)
        prev_row = shifted(first[-1:], "inl", 1)
        prev_col = shifted(second[:, -1:], "xl", 1)
        before_first = jnp.concatenate([prev_row, first[:-1]], 0)
        before_second = jnp.concatenate([prev_col, second[:, :-1]], 1)
        smooth = (
            before_first
            - delay_adjoint(first, inline_dip)
            + before_second
            - delay_adjoint(second, cross_dip)
        )
        image = hits * direction + reg_weight * smooth
        alpha = norm_now / lax.psum(jnp.sum(direction * image), ("inl", "xl"))
        model = model + alpha * direction
        residual = residual - alpha * image
        norm_next = squares(residual)
        direction = residual + norm_next / norm_now * direction
        norm_now = norm_next
    return (model, residual)


def solution(mesh):
    placed = (
        P(("inl", "xl"), None),
        P(("inl", "xl"), None),
        P(("inl", "xl")),
        P(("inl", "xl")),
        P("inl", "xl", None),
        P("inl", "xl", None),
    )
    return jax.shard_map(
        per_device,
        mesh=mesh,
        in_specs=placed,
        out_specs=(P("inl", "xl", None), P("inl", "xl", None)),
        check_vma=False,
    )
```

profile of v0, /device:TPU:0, one launch (start us, length us, event | category | flops | bytes accessed | tf_op | source)
XLA Modules:
  0.0 367.1 jit_solution(4419071604751002571)
XLA Ops:
  0.6 0.7 fusion.28
  1.4 0.7 fusion.25
  2.1 0.6 reduce-window.6
  2.9 0.8 fusion.24
  3.6 0.7 compare_select_fusion
  4.5 1.2 scatter_custom_fusion
  5.7 0.9 copy.20
  6.6 7.3 %all-to-all-start = ((bf16[32,16,2]{1,2,0:T(2,128)(2,1)}), bf16[32,16,2]{1,2,0:T(2,128)(2,1)S(1)}, u32[]{:S(2)}, u32[]{:S(2)}) async-start(bf16[32,16,2]{1,2,0:T(2,128)(2,1)} %copy.20), calls=%async_computation | async-start | bytes 32768 | tf_op jit(solution)/shard_map/all_to_all | solution.py:55
  13.9 2.7 scatter_custom_fusion.1
  16.6 4.4 %all-to-all-done = bf16[32,16,2]{1,2,0:T(2,128)(2,1)S(1)} async-done(((bf16[32,16,2]{1,2,0:T(2,128)(2,1)}), bf16[32,16,2]{1,2,0:T(2,128)(2,1)S(1)}, u32[]{:S(2)}, u32[]{:S(2)}) %all-to-all-start) | async-done | bytes 2080 | tf_op jit(solution)/shard_map/all_to_all | solution.py:55
  21.0 2.6 all-to-all-start.1
  23.7 0.4 convert_reduce_fusion
  24.1 13.8 %all-to-all-done.1 = bf16[32,16,512]{2,1,0:T(8,128)(2,1)S(1)} async-done(((bf16[32,16,512]{2,1,0:T(8,128)(2,1)}), bf16[32,16,512]{2,1,0:T(8,128)(2,1)S(1)}, u32[]{:S(2)}, u32[]{:S(2)}) %all-to-all-start.1) | async-done | bytes 524320 | tf_op jit(solution)/shard_map/all_to_all | solution.py:54
  38.0 1.6 multiply_reduce_fusion.5
  39.6 1.3 collective-permute-start.2
  40.9 1.3 collective-permute-start
  42.2 0.7 fusion.34
  43.1 0.3 slice.211
  43.4 2.4 collective-permute-done.2
  45.8 3.0 maximum_subtract_fusion.2
  48.9 4.6 %collective-permute-start.3 = (f32[8,1,512]{2,1,0:T(1,128)S(1)}, f32[8,1,512]{2,1,0:T(1,128)S(1)}, u32[]{:S(2)}, u32[]{:S(2)}) collective-permute-start(f32[8,1,512]{2,1,0:T(1,128)S(1)} %slice.213), channel_id=1, source_target_pairs={{0,1},{1,2},{2,3},{4,5},{5,6},{6,7},{8,9},{9,10},{10,11},{12,13},{... | collective-permute-start | bytes 49160 | tf_op jit(solution)/shard_map/ppermute | solution.py:15
  53.5 5.5 %collective-permute-start.1 = (f32[1,128,512]{2,1,0:T(8,128)S(1)}, f32[1,128,512]{2,1,0:T(8,128)S(1)}, u32[]{:S(2)}, u32[]{:S(2)}) collective-permute-start(f32[1,128,512]{2,1,0:T(8,128)S(1)} %slice.205), channel_id=1, source_target_pairs={{0,4},{4,8},{8,12},{12,16},{16,20},{20,24},{24,28},{1,5},{5,9},{9,... | collective-permute-start | bytes 786440 | tf_op jit(solution)/shard_map/ppermute | solution.py:15
  59.0 1.5 slice_multiply_fusion.11
  60.5 1.5 slice_multiply_fusion.9
  62.3 3.3 fusion.7
  65.6 1.3 multiply_reduce_fusion.4
  67.0 40.2 %all-reduce.18 = (f32[]{:T(128)}, f32[]{:T(128)}) all-reduce(f32[]{:T(128)} %get-tuple-element.38, f32[]{:T(128)} %multiply_reduce_fusion.4), channel_id=1, replica_groups=mesh['inl'=8,'xl'=4] {'inl','xl'}, use_global_device_ids=true, to_apply=%region_6.7 | all-reduce | flops 2 | bytes 16 | tf_op jit(solution)/shard_map/psum | solution.py:73
  108.5 2.8 multiply_reduce_fusion.3
  111.3 42.2 %psum.44 = f32[]{:T(128)} all-reduce(f32[]{:T(128)} %multiply_reduce_fusion.3), channel_id=1, replica_groups=mesh['inl'=8,'xl'=4] {'inl','xl'}, use_global_device_ids=true, to_apply=%region_11.12 | all-reduce | flops 1 | bytes 8 | tf_op jit(solution)/shard_map/psum | solution.py:73
  154.9 2.1 multiply_add_fusion.4
  157.0 1.3 collective-permute-start.6
  158.3 1.5 collective-permute-start.4
  159.9 0.8 fusion.33
  160.9 0.3 slice.229
  161.2 1.5 collective-permute-done.6
  162.9 0.6 copy-done.4
  163.6 2.7 maximum_subtract_fusion.3
  166.4 1.5 slice_multiply_fusion.7
  167.9 4.5 %collective-permute-start.7 = (f32[8,1,512]{2,1,0:T(1,128)S(1)}, f32[8,1,512]{2,1,0:T(1,128)S(1)}, u32[]{:S(2)}, u32[]{:S(2)}) collective-permute-start(f32[8,1,512]{2,1,0:T(1,128)S(1)} %slice.231), channel_id=1, source_target_pairs={{0,1},{1,2},{2,3},{4,5},{5,6},{6,7},{8,9},{9,10},{10,11},{12,13},{... | collective-permute-start | bytes 49160 | tf_op jit(solution)/shard_map/ppermute | solution.py:15
  172.5 4.8 %collective-permute-start.5 = (f32[1,128,512]{2,1,0:T(8,128)S(1)}, f32[1,128,512]{2,1,0:T(8,128)S(1)}, u32[]{:S(2)}, u32[]{:S(2)}) collective-permute-start(f32[1,128,512]{2,1,0:T(8,128)S(1)} %slice.223), channel_id=1, source_target_pairs={{0,4},{4,8},{8,12},{12,16},{16,20},{20,24},{24,28},{1,5},{5,9},{9,... | collective-permute-start | bytes 786440 | tf_op jit(solution)/shard_map/ppermute | solution.py:15
  177.3 1.5 slice_multiply_fusion.5
  179.1 5.0 %multiply_reduce_fusion.2 = (f32[]{:T(128)}, f32[8,128,512]{2,1,0:T(8,128)}) fusion(f32[8,128,512]{2,1,0:T(8,128)S(1)} %multiply_add_fusion.4, f32[8,128,511]{2,1,0:T(8,128)S(1)} %get-tuple-element.25, f32[8,128,512]{2,1,0:T(8,128)S(1)} %get-tuple-element.11, f32[8,128,512]{2,1,0:T(8,128)S(1)} %copy-done.4, f32[8,128,511]{2,1,0:T(8,128)S(1)} %get-tuple-element.24, ...), kind=kLoop, calls=%fused_computation.51 | loop fusion | flops 10485759 | bytes 25153540 | tf_op jit(solution)/shard_map/reduce_sum | solution.py:92
  184.1 41.1 %psum.45 = f32[]{:T(128)} all-reduce(f32[]{:T(128)} %get-tuple-element.6), channel_id=1, replica_groups=mesh['inl'=8,'xl'=4] {'inl','xl'}, use_global_device_ids=true, to_apply=%region_13.14 | all-reduce | flops 1 | bytes 8 | tf_op jit(solution)/shard_map/psum | solution.py:92
  226.5 3.1 multiply_subtract_fusion.5
  229.7 1.3 copy-done.12
  231.0 1.2 multiply_reduce_fusion.1
  232.2 42.2 %psum.46 = f32[]{:T(128)} all-reduce(f32[]{:T(128)} %multiply_reduce_fusion.1), channel_id=1, replica_groups=mesh['inl'=8,'xl'=4] {'inl','xl'}, use_global_device_ids=true, to_apply=%region_15.16 | all-reduce | flops 1 | bytes 8 | tf_op jit(solution)/shard_map/psum | solution.py:73
  275.8 3.0 multiply_add_fusion.3
  278.8 1.3 collective-permute-start.10
  280.1 1.6 collective-permute-start.8
  281.7 0.7 fusion.32
  282.9 1.5 collective-permute-done.10
  284.4 0.4 copy-done.8
  284.8 2.5 maximum_subtract_fusion.6
  287.3 1.3 copy-done.10
  288.6 4.5 %collective-permute-start.11 = (f32[8,1,512]{2,1,0:T(1,128)S(1)}, f32[8,1,512]{2,1,0:T(1,128)S(1)}, u32[]{:S(2)}, u32[]{:S(2)}) collective-permute-start(f32[8,1,512]{2,1,0:T(1,128)S(1)} %slice.249), channel_id=1, source_target_pairs={{0,1},{1,2},{2,3},{4,5},{5,6},{6,7},{8,9},{9,10},{10,11},{12,13},{... | collective-permute-start | bytes 49160 | tf_op jit(solution)/shard_map/ppermute | solution.py:15
  293.2 0.7 slice.241
  293.9 5.3 %collective-permute-start.9 = (f32[1,128,512]{2,1,0:T(8,128)}, f32[1,128,512]{2,1,0:T(8,128)S(1)}, u32[]{:S(2)}, u32[]{:S(2)}) collective-permute-start(f32[1,128,512]{2,1,0:T(8,128)} %slice.241), channel_id=1, source_target_pairs={{0,4},{4,8},{8,12},{12,16},{16,20},{20,24},{24,28},{1,5},{5,9},{9,... | collective-permute-start | bytes 786440 | tf_op jit(solution)/shard_map/ppermute | solution.py:15
  299.2 11.5 %slice_multiply_fusion.1 = (f32[8,128,511]{2,1,0:T(8,128)}, f32[8,128,511]{2,1,0:T(8,128)}, f32[8,128,511]{2,1,0:T(8,128)}, f32[8,128,511]{2,1,0:T(8,128)}) fusion(f32[8,128,512]{2,1,0:T(8,128)} %copy-done.10, f32[8,128,512]{2,1,0:T(8,128)} %copy-done.18, f32[8,128,512]{2,1,0:T(8,128)} %copy-done.20, f32[8,128,512]{2,1,0:T(8,128)} %copy-done.11, ...), kind=kLoop, calls=%fused_computation.13 | loop fusion | flops 2093056 | bytes 25116672 | tf_op jit(solution)/shard_map/mul | solution.py:37
  310.7 1.8 slice.242
  312.8 8.3 %multiply_reduce_fusion = (f32[]{:T(128)}, f32[8,128,512]{2,1,0:T(8,128)}) fusion(f32[8,128,512]{2,1,0:T(8,128)S(1)} %multiply_add_fusion.3, f32[8,128,511]{2,1,0:T(8,128)} %get-tuple-element.19, f32[8,128,512]{2,1,0:T(8,128)} %copy-done.10, f32[8,128,512]{2,1,0:T(8,128)S(1)} %copy-done.5, f32[8,128,511]{2,1,0:T(8,128)} %get-tuple-element.18, ...), kind=kLoop, calls=%fused_computation.47 | loop fusion | flops 10485759 | bytes 25153540 | tf_op jit(solution)/shard_map/reduce_sum | solution.py:92
  321.1 38.2 %psum.47 = f32[]{:T(128)} all-reduce(f32[]{:T(128)} %get-tuple-element.4), channel_id=1, replica_groups=mesh['inl'=8,'xl'=4] {'inl','xl'}, use_global_device_ids=true, to_apply=%region_17.18 | all-reduce | flops 1 | bytes 8 | tf_op jit(solution)/shard_map/psum | solution.py:92
  360.7 4.5 %multiply_add_fusion.2 = f32[8,128,512]{2,1,0:T(8,128)} fusion(f32[8,128,512]{2,1,0:T(8,128)} %copy-done, f32[]{:T(128)S(6)} %div.35, f32[]{:T(128)S(6)} %div.33, f32[]{:T(128)S(6)} %div.31, f32[1024,512]{1,0:T(8,128)S(1)} %get-tuple-element.39, f32[]{:T(128)S(6)} %div.32, f32[8,128,512]{2,1,0:T(8,128)} %copy-done.1), kind=kLoop, calls=%fused_computation.46 | loop fusion | flops 4718592 | bytes 8388624 | tf_op jit(solution)/shard_map/add | solution.py:93
  365.2 1.9 multiply_subtract_fusion.4
  (78 shorter events, 2.6 us)
Async XLA Ops:
  6.6 14.4 %all-to-all-start = ((bf16[32,16,2]{1,2,0:T(2,128)(2,1)}), bf16[32,16,2]{1,2,0:T(2,128)(2,1)S(1)}, u32[]{:S(2)}, u32[]{:S(2)}) async-start(bf16[32,16,2]{1,2,0:T(2,128)(2,1)} %copy.20), calls=%async_computation | async-start | bytes 32768 | tf_op jit(solution)/shard_map/all_to_all | solution.py:55
  21.0 17.0 %all-to-all-start.1 = ((bf16[32,16,512]{2,1,0:T(8,128)(2,1)}), bf16[32,16,512]{2,1,0:T(8,128)(2,1)S(1)}, u32[]{:S(2)}, u32[]{:S(2)}) async-start(bf16[32,16,512]{2,1,0:T(8,128)(2,1)} %bitcast.7), calls=%async_computation.1 | async-start | bytes 1048576 | tf_op jit(solution)/shard_map/all_to_all | solution.py:54
  39.6 6.2 %collective-permute-start.2 = (f32[8,1,512]{2,1,0:T(1,128)S(1)}, f32[8,1,512]{2,1,0:T(1,128)S(1)}, u32[]{:S(2)}, u32[]{:S(2)}) collective-permute-start(f32[8,1,512]{2,1,0:T(1,128)S(1)} %slice.212), channel_id=1, source_target_pairs={{1,0},{2,1},{3,2},{5,4},{6,5},{7,6},{9,8},{10,9},{11,10},{13,12},{... | collective-permute-start | bytes 49160 | tf_op jit(solution)/shard_map/ppermute | solution.py:15
  40.9 4.9 %collective-permute-start = (f32[1,128,512]{2,1,0:T(8,128)S(1)}, f32[1,128,512]{2,1,0:T(8,128)S(1)}, u32[]{:S(2)}, u32[]{:S(2)}) collective-permute-start(f32[1,128,512]{2,1,0:T(8,128)S(1)} %slice_bitcast_fusion), channel_id=1, source_target_pairs={{4,0},{8,4},{12,8},{16,12},{20,16},{24,20},{28,24},{5,1},{9,5},{13... | collective-permute-start | bytes 786440 | tf_op jit(solution)/shard_map/ppermute | solution.py:15
  43.1 2.7 copy-start.3
  43.1 2.7 copy-start.6
  48.8 11.7 %copy-start.14 = (f32[8,128,512]{2,1,0:T(8,128)}, f32[8,128,512]{2,1,0:T(8,128)S(1)}, u32[]{:S(2)}) copy-start(f32[8,128,512]{2,1,0:T(8,128)S(1)} %get-tuple-element.14) | copy-start | bytes 6291460
  48.8 11.7 %copy-start.16 = (f32[8,128,512]{2,1,0:T(8,128)}, f32[8,128,512]{2,1,0:T(8,128)S(1)}, u32[]{:S(2)}) copy-start(f32[8,128,512]{2,1,0:T(8,128)S(1)} %get-tuple-element.15) | copy-start | bytes 6291460
  48.8 11.7 %copy-start.18 = (f32[8,128,512]{2,1,0:T(8,128)}, f32[8,128,512]{2,1,0:T(8,128)S(1)}, u32[]{:S(2)}) copy-start(f32[8,128,512]{2,1,0:T(8,128)S(1)} %get-tuple-element.32) | copy-start | bytes 6291460
  48.8 11.7 %copy-start.20 = (f32[8,128,512]{2,1,0:T(8,128)}, f32[8,128,512]{2,1,0:T(8,128)S(1)}, u32[]{:S(2)}) copy-start(f32[8,128,512]{2,1,0:T(8,128)S(1)} %get-tuple-element.33) | copy-start | bytes 6291460
  48.9 13.4 %collective-permute-start.3 = (f32[8,1,512]{2,1,0:T(1,128)S(1)}, f32[8,1,512]{2,1,0:T(1,128)S(1)}, u32[]{:S(2)}, u32[]{:S(2)}) collective-permute-start(f32[8,1,512]{2,1,0:T(1,128)S(1)} %slice.213), channel_id=1, source_target_pairs={{0,1},{1,2},{2,3},{4,5},{5,6},{6,7},{8,9},{9,10},{10,11},{12,13},{... | collective-permute-start | bytes 49160 | tf_op jit(solution)/shard_map/ppermute | solution.py:15
  53.5 8.8 %collective-permute-start.1 = (f32[1,128,512]{2,1,0:T(8,128)S(1)}, f32[1,128,512]{2,1,0:T(8,128)S(1)}, u32[]{:S(2)}, u32[]{:S(2)}) collective-permute-start(f32[1,128,512]{2,1,0:T(8,128)S(1)} %slice.205), channel_id=1, source_target_pairs={{0,4},{4,8},{8,12},{12,16},{16,20},{20,24},{24,28},{1,5},{5,9},{9,... | collective-permute-start | bytes 786440 | tf_op jit(solution)/shard_map/ppermute | solution.py:15
  65.6 1.3 copy-start.1
  157.0 5.6 %collective-permute-start.6 = (f32[8,1,512]{2,1,0:T(1,128)S(1)}, f32[8,1,512]{2,1,0:T(1,128)S(1)}, u32[]{:S(2)}, u32[]{:S(2)}) collective-permute-start(f32[8,1,512]{2,1,0:T(1,128)S(1)} %slice.230), channel_id=1, source_target_pairs={{1,0},{2,1},{3,2},{5,4},{6,5},{7,6},{9,8},{10,9},{11,10},{13,12},{... | collective-permute-start | bytes 49160 | tf_op jit(solution)/shard_map/ppermute | solution.py:15
  158.3 4.3 %collective-permute-start.4 = (f32[1,128,512]{2,1,0:T(8,128)S(1)}, f32[1,128,512]{2,1,0:T(8,128)S(1)}, u32[]{:S(2)}, u32[]{:S(2)}) collective-permute-start(f32[1,128,512]{2,1,0:T(8,128)S(1)} %slice.220), channel_id=1, source_target_pairs={{4,0},{8,4},{12,8},{16,12},{20,16},{24,20},{28,24},{5,1},{9,5},{13... | collective-permute-start | bytes 786440 | tf_op jit(solution)/shard_map/ppermute | solution.py:15
  160.6 2.0 copy-start.7
  160.9 2.1 copy-start.2
  160.9 2.7 copy-start.4
  163.6 2.8 copy-start.15
  163.6 2.8 copy-start.17
  166.3 11.0 %copy-start.19 = (f32[8,128,512]{2,1,0:T(8,128)S(1)}, f32[8,128,512]{2,1,0:T(8,128)}, u32[]{:S(2)}) copy-start(f32[8,128,512]{2,1,0:T(8,128)} %copy-done.18) | copy-start | bytes 6291460
  166.4 11.0 %copy-start.21 = (f32[8,128,512]{2,1,0:T(8,128)S(1)}, f32[8,128,512]{2,1,0:T(8,128)}, u32[]{:S(2)}) copy-start(f32[8,128,512]{2,1,0:T(8,128)} %copy-done.20) | copy-start | bytes 6291460
  167.9 11.1 %collective-permute-start.7 = (f32[8,1,512]{2,1,0:T(1,128)S(1)}, f32[8,1,512]{2,1,0:T(1,128)S(1)}, u32[]{:S(2)}, u32[]{:S(2)}) collective-permute-start(f32[8,1,512]{2,1,0:T(1,128)S(1)} %slice.231), channel_id=1, source_target_pairs={{0,1},{1,2},{2,3},{4,5},{5,6},{6,7},{8,9},{9,10},{10,11},{12,13},{... | collective-permute-start | bytes 49160 | tf_op jit(solution)/shard_map/ppermute | solution.py:15
  172.5 6.6 %collective-permute-start.5 = (f32[1,128,512]{2,1,0:T(8,128)S(1)}, f32[1,128,512]{2,1,0:T(8,128)S(1)}, u32[]{:S(2)}, u32[]{:S(2)}) collective-permute-start(f32[1,128,512]{2,1,0:T(8,128)S(1)} %slice.223), channel_id=1, source_target_pairs={{0,4},{4,8},{8,12},{12,16},{16,20},{20,24},{24,28},{1,5},{5,9},{9,... | collective-permute-start | bytes 786440 | tf_op jit(solution)/shard_map/ppermute | solution.py:15
  229.7 1.3 copy-start.12
  278.8 33.8 %copy-start = (f32[8,128,512]{2,1,0:T(8,128)}, f32[8,128,512]{2,1,0:T(8,128)S(1)}, u32[]{:S(2)}) copy-start(f32[8,128,512]{2,1,0:T(8,128)S(1)} %multiply_add_fusion.3) | copy-start | bytes 6291460
  278.8 5.6 %collective-permute-start.10 = (f32[8,1,512]{2,1,0:T(1,128)S(1)}, f32[8,1,512]{2,1,0:T(1,128)S(1)}, u32[]{:S(2)}, u32[]{:S(2)}) collective-permute-start(f32[8,1,512]{2,1,0:T(1,128)S(1)} %slice.248), channel_id=1, source_target_pairs={{1,0},{2,1},{3,2},{5,4},{6,5},{7,6},{9,8},{10,9},{11,10},{13,12},{... | collective-permute-start | bytes 49160 | tf_op jit(solution)/shard_map/ppermute | solution.py:15
  280.1 4.3 %collective-permute-start.8 = (f32[1,128,512]{2,1,0:T(8,128)S(1)}, f32[1,128,512]{2,1,0:T(8,128)S(1)}, u32[]{:S(2)}, u32[]{:S(2)}) collective-permute-start(f32[1,128,512]{2,1,0:T(8,128)S(1)} %slice.238), channel_id=1, source_target_pairs={{4,0},{8,4},{12,8},{16,12},{20,16},{24,20},{28,24},{5,1},{9,5},{13... | collective-permute-start | bytes 786440 | tf_op jit(solution)/shard_map/ppermute | solution.py:15
  282.6 1.8 copy-start.5
  282.6 2.2 copy-start.8
  287.3 1.3 copy-start.10
  287.3 5.9 %copy-start.11 = (f32[8,128,512]{2,1,0:T(8,128)}, f32[8,128,512]{2,1,0:T(8,128)S(1)}, u32[]{:S(2)}) copy-start(f32[8,128,512]{2,1,0:T(8,128)S(1)} %get-tuple-element.8) | copy-start | bytes 6291460
  288.6 23.9 %collective-permute-start.11 = (f32[8,1,512]{2,1,0:T(1,128)S(1)}, f32[8,1,512]{2,1,0:T(1,128)S(1)}, u32[]{:S(2)}, u32[]{:S(2)}) collective-permute-start(f32[8,1,512]{2,1,0:T(1,128)S(1)} %slice.249), channel_id=1, source_target_pairs={{0,1},{1,2},{2,3},{4,5},{5,6},{6,7},{8,9},{9,10},{10,11},{12,13},{... | collective-permute-start | bytes 49160 | tf_op jit(solution)/shard_map/ppermute | solution.py:15
  293.9 18.6 %collective-permute-start.9 = (f32[1,128,512]{2,1,0:T(8,128)}, f32[1,128,512]{2,1,0:T(8,128)S(1)}, u32[]{:S(2)}, u32[]{:S(2)}) collective-permute-start(f32[1,128,512]{2,1,0:T(8,128)} %slice.241), channel_id=1, source_target_pairs={{0,4},{4,8},{8,12},{12,16},{16,20},{20,24},{24,28},{1,5},{5,9},{9,... | collective-permute-start | bytes 786440 | tf_op jit(solution)/shard_map/ppermute | solution.py:15
  310.7 2.1 copy-start.9
  360.6 4.5 %copy-start.13 = (f32[8,128,512]{2,1,0:T(8,128)S(1)}, f32[8,128,512]{2,1,0:T(8,128)}, u32[]{:S(2)}) copy-start(f32[8,128,512]{2,1,0:T(8,128)} %copy-done.12) | copy-start | bytes 6291460
  360.6 4.5 %copy-start.22 = (f32[8,128,512]{2,1,0:T(8,128)S(1)}, f32[8,128,512]{2,1,0:T(8,128)}, u32[]{:S(2)}) copy-start(f32[8,128,512]{2,1,0:T(8,128)} %get-tuple-element.5) | copy-start | bytes 6291460
where the time goes:
time: 369 us; the launch traced here: 367 us
  blocking collectives  204 us (55%)
  other arithmetic  66.3 us (18%)
  starting transfers between devices  47.4 us (13%)
  waiting for transfers between devices  23.6 us (6%)
  local copies, waits for them, and re-layouts  16.3 us (4%)
  between operations  8 us (2%)
    psum x3, blocking collectives, squares(): return lax.psum(jnp.sum(field * field), ('inl', 'xl'))  125 us
    psum x2, blocking collectives, per_device(): alpha = norm_now / lax.psum(jnp.sum(direction * image), ('inl', 'xl'))  79.3 us
    ppermute x12, starting transfers between devices, shifted(): lax.ppermute(value, axis, [(source, source + steps) for source in range(i...  37.4 us
    mul x5, other arithmetic, delay_adjoint(): upper * field  17.7 us
    reduce_sum x3, other arithmetic, per_device(): alpha = norm_now / lax.psum(jnp.sum(direction * image), ('inl', 'xl'))  14.6 us
    all_to_all x1, waiting for transfers between devices, bin_traces(): lax.all_to_all(send_rows, ('inl', 'xl'), split_axis=0, concat_axis=0, til...  13.8 us
  transfers between devices with their start and end apart: 14, of which 5 were waited for; matrix products, arithmetic and copies ran while one was open for 7% of the time, Pallas kernels for 0%

commit v1 on v0

v1 whole, which is shorter than its diff:
```python
import functools

import jax
import jax.numpy as jnp
from jax import lax
from jax.experimental import pallas as pl
from jax.experimental.pallas import tpu as pltpu
from jax.sharding import PartitionSpec as P

ITERS = 3
LANES = 128
SUBLANES = 8

IN_VMEM = pl.BlockSpec(memory_space=pltpu.VMEM)
PARAMS = pltpu.CompilerParams(vmem_limit_bytes=16 << 20)


def shifted(value, axis, steps):
    count = lax.axis_size(axis)
    initial, last = (max(0, -steps), min(count, count - steps))
    return lax.ppermute(value, axis, [(source, source + steps) for source in range(initial, last)])


def iota(shape, dim):
    return lax.broadcasted_iota(jnp.int32, shape, dim)


def earlier(tiles):
    lane = iota(tiles[0].shape, 1)
    rolled = [pltpu.roll(tile, 1, 1) for tile in tiles]
    before = [jnp.zeros_like(tiles[0])] + rolled[:-1]
    return [jnp.where(lane == 0, edge, inner) for edge, inner in zip(before, rolled)]


def later(tiles):
    lane = iota(tiles[0].shape, 1)
    rolled = [pltpu.roll(tile, LANES - 1, 1) for tile in tiles]
    after = rolled[1:] + [jnp.zeros_like(tiles[0])]
    return [jnp.where(lane == LANES - 1, edge, inner) for edge, inner in zip(after, rolled)]


def stencil(v):
    em, ep = earlier(v), later(v)
    odd = [m - p for m, p in zip(em, ep)]
    even = [(m + p) - (c + c) for m, p, c in zip(em, ep, v)]
    return odd, even


def dip_part(p, odd, even):
    return [(0.5 * d) * (o + d * e) for d, o, e in zip(p, odd, even)]


def adjoint_terms(p, r):
    a = [(0.5 * d) * x for d, x in zip(p, r)]
    b = [d * x for d, x in zip(p, a)]
    return a, b


def adjoint_finish(r, a, b):
    up = later([x + y for x, y in zip(a, b)])
    down = earlier([y - x for x, y in zip(a, b)])
    return [(x + u) + (d - (y + y)) for x, u, d, y in zip(r, up, down, b)]


def load(ref, *index):
    count = ref.shape[-1] // LANES
    return [ref[(*index, slice(c * LANES, (c + 1) * LANES))] for c in range(count)]


def store(ref, tiles, *index):
    for c, tile in enumerate(tiles):
        ref[(*index, slice(c * LANES, (c + 1) * LANES))] = tile


def add(x, y):
    return [a + b for a, b in zip(x, y)]


def sub(x, y):
    return [a - b for a, b in zip(x, y)]


def dot(x, y):
    return functools.reduce(lambda s, t: s + t, [a * b for a, b in zip(x, y)])


def pack_kernel(capacity, owner_ref, cell_ref, live_ref, traces_ref, out_ref):
    held, samples = traces_ref.shape
    slots = out_ref.shape[0]
    spread = jnp.broadcast_to(owner_ref[...], (held, held))
    row, col = iota((held, held), 0), iota((held, held), 1)
    owner = jnp.sum(jnp.where(row == col, spread, 0), axis=0, keepdims=True)
    rank = jnp.sum(jnp.where((spread == owner) & (row < col), 1, 0), axis=0, keepdims=True)
    slot = jnp.where(live_ref[...] > 0, owner * capacity + rank, -1)
    chosen = (iota((slots, held), 0) == slot).astype(jnp.float32).astype(jnp.bfloat16)
    cell = cell_ref[...]
    kind = iota((LANES, held), 0)
    upper = (lax.shift_right_logical(cell, 6) + 1).astype(jnp.float32)
    lower = (cell & 63).astype(jnp.float32)
    codes = jnp.where(kind == 0, upper, jnp.where(kind == 1, lower, 0.0)).astype(jnp.bfloat16)
    rows = jnp.dot(chosen, traces_ref[...], preferred_element_type=jnp.float32)
    out_ref[:, :samples] = rows.astype(jnp.bfloat16)
    sent = lax.dot_general(chosen, codes, (((1,), (1,)), ((), ())), preferred_element_type=jnp.float32)
    out_ref[:, samples:] = sent.astype(jnp.bfloat16)


def bin_kernel(got_ref, p1_ref, p2_ref, b_ref, diag_ref, row0_ref, row7_ref, col0_ref, col7_ref):
    rows, cols, samples = b_ref.shape
    slots = got_ref.shape[0]
    kind = iota((SUBLANES, LANES), 1)
    weight = jnp.where(kind == 0, 64.0, jnp.where(kind == 1, 1.0, 0.0)).astype(jnp.bfloat16)
    value = lax.dot_general(
        weight, got_ref[:, samples:], (((1,), (1,)), ((), ())), preferred_element_type=jnp.float32
    )
    bin_of = value[:1].astype(jnp.int32) - 64
    not_first_row = (lax.axis_index("inl") > 0).astype(jnp.float32)
    not_first_col = (lax.axis_index("xl") > 0).astype(jnp.float32)
    ones = jnp.ones((slots, LANES), jnp.bfloat16)
    first_col = jnp.where(iota((cols, LANES), 0) == 0, not_first_col, 0.0)
    got = got_ref[:, :samples]
    for i in range(rows):
        place = (iota((cols, slots), 0) + i * cols == bin_of).astype(jnp.float32).astype(jnp.bfloat16)
        b_ref[i] = jnp.dot(place, got, preferred_element_type=jnp.float32)
        hits = jnp.dot(place, ones, preferred_element_type=jnp.float32)
        diag = 2.0 * hits + first_col
        diag_ref[i] = diag + not_first_row if i == 0 else diag
    write_edges(b_ref, p1_ref, p2_ref, row0_ref, row7_ref, col0_ref, col7_ref)


def write_edges(v_ref, p1_ref, p2_ref, row0_ref, row7_ref, col0_ref, col7_ref):
    rows, cols, _ = v_ref.shape
    last = rows - 1
    for x in range(0, cols, SUBLANES):
        at = slice(x, x + SUBLANES)
        store(row0_ref, load(v_ref, 0, at), at)
        v = load(v_ref, last, at)
        store(row7_ref, add(v, dip_part(load(p1_ref, last, at), *stencil(v))), at)
    for i in range(rows):
        store(col0_ref, load(v_ref, i, slice(0, 1)), slice(i, i + 1))
        at = slice(cols - SUBLANES, cols)
        v = load(v_ref, i, at)
        moved = add(v, dip_part(load(p2_ref, i, at), *stencil(v)))
        store(col7_ref, [t[SUBLANES - 1 :] for t in moved], slice(i, i + 1))


def apply_kernel(v_ref, p1_ref, p2_ref, diag_ref, out_ref, sums_ref, first_ref):
    rows, cols, samples = v_ref.shape
    tiles = samples // LANES
    sub_index = iota((SUBLANES, LANES), 0)
    zero = [jnp.zeros((SUBLANES, LANES), jnp.float32)] * tiles
    first_ref[...] = jnp.zeros_like(first_ref)

    def body(i, carry):
        vout, vv = carry
        after = jnp.where(i + 1 < rows, 1.0, 0.0)
        nxt = jnp.minimum(i + 1, rows - 1)
        v = load(v_ref, i, slice(0, SUBLANES))
        up = [pltpu.roll(t, SUBLANES - 1, 0) for t in v]
        down_before = zero
        for x in range(0, cols, SUBLANES):
            at = slice(x, x + SUBLANES)
            if x + SUBLANES < cols:
                v_ahead = load(v_ref, i, slice(x + SUBLANES, x + 2 * SUBLANES))
                up_ahead = [pltpu.roll(t, SUBLANES - 1, 0) for t in v_ahead]
            else:
                v_ahead, up_ahead = zero, zero
            right = [jnp.where(sub_index == SUBLANES - 1, b, a) for a, b in zip(up, up_ahead)]
            below = [after * t for t in load(v_ref, nxt, at)]
            p1, p2 = load(p1_ref, i, at), load(p2_ref, i, at)
            odd, even = stencil(v)
            first = sub(sub(below, v), dip_part(p1, odd, even))
            second = sub(sub(right, v), dip_part(p2, odd, even))
            a1, b1 = adjoint_terms(p1, first)
            a2, b2 = adjoint_terms(p2, second)
            moved = adjoint_finish(add(first, second), add(a1, a2), add(b1, b2))
            down = [pltpu.roll(t, 1, 0) for t in second]
            left = [jnp.where(sub_index == 0, b, a) for a, b in zip(down, down_before)]
            above = load(first_ref, at)
            store(first_ref, first, at)
            diag = diag_ref[i, at, :]
            out = [diag * c + ((f + s) - m) for c, f, s, m in zip(v, above, left, moved)]
            store(out_ref, out, i, at)
            vout = vout + dot(v, out)
            vv = vv + dot(v, v)
            v, up, down_before = v_ahead, up_ahead, down
        return vout, vv

    vout, vv = lax.fori_loop(0, rows, body, (zero[0], zero[0]))
    sums_ref[0] = vout
    sums_ref[1] = vv


def halo_corrections(out_ref, p1_ref, p2_ref, below_ref, above_ref, right_ref, left_ref):
    rows, cols, _ = out_ref.shape
    last = rows - 1
    sub_index = iota((SUBLANES, LANES), 0)
    for x in range(0, cols, SUBLANES):
        at = slice(x, x + SUBLANES)
        store(out_ref, sub(load(out_ref, 0, at), load(above_ref, at)), 0, at)
        r = load(below_ref, at)
        moved = adjoint_finish(r, *adjoint_terms(load(p1_ref, last, at), r))
        store(out_ref, sub(load(out_ref, last, at), moved), last, at)
    for i in range(rows):
        at = slice(0, SUBLANES)
        r = [jnp.where(sub_index == 0, t, 0.0) for t in load(left_ref, slice(i, i + 1))]
        store(out_ref, sub(load(out_ref, i, at), r), i, at)
        at = slice(cols - SUBLANES, cols)
        r = [jnp.where(sub_index == SUBLANES - 1, t, 0.0) for t in load(right_ref, slice(i, i + 1))]
        moved = adjoint_finish(r, *adjoint_terms(load(p2_ref, i, at), r))
        store(out_ref, sub(load(out_ref, i, at), moved), i, at)


def correct_kernel(
    image_ref, p1_ref, p2_ref, below_ref, above_ref, right_ref, left_ref, out_ref, *edge_refs
):
    halo_corrections(out_ref, p1_ref, p2_ref, below_ref, above_ref, right_ref, left_ref)
    if edge_refs:
        write_edges(out_ref, p1_ref, p2_ref, *edge_refs)


def moments_kernel(*refs):
    out_ref = refs[-1]
    m = []
    for step in range(ITERS):
        sums_ref, row7, below, col7, right = refs[5 * step : 5 * step + 5]
        across = jnp.zeros((SUBLANES, LANES), jnp.float32)
        for mine, theirs in ((row7, below), (col7, right)):
            for x in range(0, mine.shape[0], SUBLANES):
                at = slice(x, x + SUBLANES)
                across = across + dot(load(mine, at), load(theirs, at))
        m.append(sums_ref[1])
        m.append(sums_ref[0] - 2.0 * across)
    sub_index, lane = iota((SUBLANES, LANES), 0), iota((SUBLANES, LANES), 1)
    block = jnp.zeros((SUBLANES, LANES), jnp.float32)
    for k, part in enumerate(m):
        block = jnp.where(sub_index == k, jnp.sum(part, axis=0, keepdims=True), block)
    total = jnp.sum(block, axis=1, keepdims=True)
    line = jnp.sum(jnp.where(sub_index == lane, total, 0.0), axis=0, keepdims=True)
    out_ref[...] = jnp.broadcast_to(line[None], out_ref.shape)


def coefficients(m):
    zero = jnp.zeros_like(m[0])
    model = [zero] * ITERS
    residual = [zero + 1.0] + [zero] * ITERS
    direction = [zero + 1.0] + [zero] * (ITERS - 1)
    norm_now = m[0]

    def inner(x, y, power, count):
        total = zero
        for i in range(count):
            for j in range(count):
                total = total + x[i] * y[j] * m[i + j + power]
        return total

    for sweep in range(ITERS):
        alpha = norm_now / inner(direction, direction, 1, sweep + 1)
        model = [s + alpha * d for s, d in zip(model, direction)]
        residual = [residual[0]] + [r - alpha * d for r, d in zip(residual[1:], direction)]
        if sweep + 1 < ITERS:
            norm_next = inner(residual, residual, 0, sweep + 2)
            beta = norm_next / norm_now
            direction = [r + beta * d for r, d in zip(residual, direction)]
            norm_now = norm_next
    return model, residual


def finish_kernel(parts_ref, b_ref, v1_ref, v2_ref, v3_ref, model_ref, residual_ref):
    rows, cols, samples = b_ref.shape
    line = jnp.sum(parts_ref[...], axis=0)
    sub_index, lane = iota((SUBLANES, LANES), 0), iota((SUBLANES, LANES), 1)
    total = jnp.sum(jnp.where(sub_index == lane, line, 0.0), axis=1, keepdims=True)
    total = jnp.broadcast_to(total, (SUBLANES, LANES))
    m = [jnp.broadcast_to(total[k : k + 1], (SUBLANES, LANES)) for k in range(2 * ITERS)]
    model, residual = coefficients(m)

    def body(i, carry):
        for x in range(0, cols, SUBLANES):
            at = slice(x, x + SUBLANES)
            b, v1, v2, v3 = (load(ref, i, at) for ref in (b_ref, v1_ref, v2_ref, v3_ref))
            store(model_ref, [(2.0 * model[0]) * s + (2.0 * model[1]) * t + (2.0 * model[2]) * u for s, t, u in zip(b, v1, v2)], i, at)
            store(
                residual_ref,
                [residual[0] * s + residual[1] * t + residual[2] * u + residual[3] * w for s, t, u, w in zip(b, v1, v2, v3)],
                i, at,
            )
        return carry

    lax.fori_loop(0, rows, body, 0)


def f32(*shape):
    return pltpu.VMEM(shape, jnp.float32)


def call(kernel, outs, *args, name, scratch=(), aliases=None, cost=None, params=PARAMS):
    return pl.pallas_call(
        kernel,
        out_shape=outs,
        in_specs=[IN_VMEM] * len(args),
        out_specs=[IN_VMEM] * len(outs),
        scratch_shapes=list(scratch),
        input_output_aliases=aliases or {},
        compiler_params=params,
        cost_estimate=cost,
        name=name,
    )(*args)


def exchange(row0, row7, col0, col7):
    below = shifted(row0, "inl", -1)
    above = shifted(row7, "inl", 1)
    right = shifted(col0, "xl", -1)
    left = shifted(col7, "xl", 1)
    return below, above, right, left


def per_device(traces, trace_owner, trace_cell, acquired, inline_dip, cross_dip):
    rows, cols, samples = inline_dip.shape
    devices = lax.axis_size("inl") * lax.axis_size("xl")
    held = traces.shape[0]
    capacity = max(2, 2 * held // devices)
    slots = devices * capacity
    (sent,) = call(
        functools.partial(pack_kernel, capacity),
        [jax.ShapeDtypeStruct((slots, samples + LANES), jnp.bfloat16)],
        trace_owner, trace_cell[None], acquired[None], traces,
        name="pack",
    )
    got = lax.all_to_all(sent, ("inl", "xl"), split_axis=0, concat_axis=0, tiled=True)
    edge_shapes = [f32(cols, samples), f32(cols, samples), f32(rows, samples), f32(rows, samples)]
    tile = f32(rows, cols, samples)
    b, diag, *edges = call(
        bin_kernel, [tile, f32(rows, cols, LANES)] + edge_shapes, got, inline_dip, cross_dip, name="bin"
    )
    fields, products = [b], []
    cost = pl.CostEstimate(
        flops=60 * rows * cols * samples, bytes_accessed=16 * rows * cols * samples, transcendentals=0
    )
    for step in range(ITERS):
        halo = exchange(*edges)
        image, sums = call(
            apply_kernel,
            [tile, f32(2, SUBLANES, LANES)],
            fields[-1], inline_dip, cross_dip, diag,
            name="apply", scratch=[pltpu.VMEM((cols, samples), jnp.float32)], cost=cost,
        )
        products += [sums, edges[1], halo[0], edges[3], halo[2]]
        image, *edges = call(
            correct_kernel,
            [tile] + (edge_shapes if step + 1 < ITERS else []),
            image, inline_dip, cross_dip, *halo,
            name="correct", aliases={0: 0},
        )
        fields.append(image)
    (parts,) = call(moments_kernel, [jax.ShapeDtypeStruct((devices, 1, LANES), jnp.float32)], *products, name="moments")
    parts = lax.all_to_all(parts, ("inl", "xl"), split_axis=0, concat_axis=0, tiled=True)
    out = jax.ShapeDtypeStruct((rows, cols, samples), jnp.float32)
    return tuple(call(finish_kernel, [out, out], parts, *fields, name="finish"))


def solution(mesh):
    placed = (
        P(("inl", "xl"), None),
        P(("inl", "xl"), None),
        P(("inl", "xl")),
        P(("inl", "xl")),
        P("inl", "xl", None),
        P("inl", "xl", None),
    )
    return jax.shard_map(
        per_device,
        mesh=mesh,
        in_specs=placed,
        out_specs=(P("inl", "xl", None), P("inl", "xl", None)),
        check_vma=False,
    )
```

time: 369 us -> 112 us (0.30)
  blocking collectives: 204 us -> 24 us
  other arithmetic: 66.3 us -> 0 us
  Pallas kernels: 0 us -> 28.2 us
  waiting for transfers between devices: 23.6 us -> 1.46 us
  starting transfers between devices: 47.4 us -> 39.7 us
  between operations: 8 us -> 0.95 us
    psum x5 -> x0, blocking collectives: 204 us -> none  [the longest x3 125 us: squares(): return lax.psum(jnp.sum(field * field), ('inl', 'xl'))]
    pallas_call x0 -> x10, Pallas kernels: none -> 28.2 us  [call(): pl.pallas_call(kernel, out_shape=outs, in_specs=[IN_VMEM] * len(args), ou...]
    all_to_all x0 -> x1, blocking collectives: none -> 24 us  [per_device(): lax.all_to_all(sent, ('inl', 'xl'), split_axis=0, concat_axis=0, tiled=True)]
    reduce_sum x7 -> x0, other arithmetic: 19.7 us -> none  [the longest x3 14.6 us: per_device(): alpha = norm_now / lax.psum(jnp.sum(direction * image), ('inl', 'xl'))]
    all_to_all x2 -> x1, waiting for transfers between devices: 18.2 us -> 0.01 us  [per_device(): lax.all_to_all(parts, ('inl', 'xl'), split_axis=0, concat_axis=0, tiled=T...]
    mul x5 -> x0, other arithmetic: 17.7 us -> none  [delay_adjoint(): upper * field]
    sub x5 -> x0, other arithmetic: 13.3 us -> none  [the longest x2 5.19 us: per_device(): jnp.concatenate([direction[1:], next_row], 0) - delay(direction, inline_dip)]
    add x5 -> x0, other arithmetic: 12.9 us -> none  [the longest x2 5.11 us: per_device(): direction = residual + norm_next / norm_now * direction]
  transfers between devices with their start and end apart: 14 -> 13, of which waited for: 5 -> 1; matrix products, arithmetic and copies ran while one was open for 7% -> 0% of each run, Pallas kernels for 0% -> 20%
where the time goes in v1:
time: 112 us; the launch traced here: 111 us
  starting transfers between devices  39.7 us (35%)
  Pallas kernels  28.2 us (25%)
  blocking collectives  24 us (21%)
  local copies, waits for them, and re-layouts  17.1 us (15%)
  waiting for transfers between devices  1.46 us (1%)
    ppermute x12, starting transfers between devices, shifted(): lax.ppermute(value, axis, [(source, source + steps) for source in range(i...  31.9 us
    pallas_call x10, Pallas kernels, call(): pl.pallas_call(kernel, out_shape=outs, in_specs=[IN_VMEM] * len(args), ou...  28.2 us
    all_to_all x1, blocking collectives, per_device(): lax.all_to_all(sent, ('inl', 'xl'), split_axis=0, concat_axis=0, tiled=True)  24 us
    unnamed x33, local copies, waits for them, and re-layouts  17.1 us
    all_to_all x1, starting transfers between devices, per_device(): lax.all_to_all(parts, ('inl', 'xl'), split_axis=0, concat_axis=0, tiled=T...  7.86 us
  transfers between devices with their start and end apart: 13, of which 1 were waited for; matrix products, arithmetic and copies ran while one was open for 0% of the time, Pallas kernels for 20%

profile of v1, /device:TPU:0, one launch (start us, length us, event | category | flops | bytes accessed | tf_op | source)
XLA Modules:
  0.0 111.4 jit_solution(12221906815376799305)
XLA Ops:
  0.6 0.0 copy-start
  0.6 1.0 copy.11.owner_ref
  1.6 0.0 copy-start.13
  1.6 0.9 copy-done.13
  2.6 0.0 copy-start.14
  2.6 0.7 copy-done.14
  3.2 0.0 copy-start.15
  3.2 0.7 copy-done.15
  3.9 0.5 pack.1
  4.4 24.0 %all_to_all.16 = bf16[32,16,640]{2,1,0:T(8,128)(2,1)S(1)} all-to-all(bf16[32,16,640]{2,1,0:T(8,128)(2,1)S(1)} %bitcast.5), channel_id=1, replica_groups=mesh['inl'=8,'xl'=4] {'inl','xl'}, dimensions={0} | all-to-all | bytes 1310720 | tf_op jit(solution)/shard_map/all_to_all | solution.py:330
  28.4 0.0 copy-done
  28.4 0.0 copy-start.1
  28.4 1.6 %copy-done.1 = f32[8,128,512]{2,1,0:T(8,128)S(1)} copy-done((f32[8,128,512]{2,1,0:T(8,128)S(1)}, f32[8,128,512]{2,1,0:T(8,128)}, u32[]{:S(2)}) %copy-start.1) | copy-done | bytes 2097176
  30.0 1.3 %bin.1 = (f32[8,128,512]{2,1,0:T(8,128)S(1)}, f32[8,128,128]{2,1,0:T(8,128)S(1)}, f32[128,512]{1,0:T(8,128)S(1)}, f32[128,512]{1,0:T(8,128)S(1)}, f32[8,512]{1,0:T(8,128)S(1)}, /*index=5*/f32[8,512]{1,0:T(8,128)S(1)}) custom-call(bf16[512,640]{1,0:T(8,128)(2,1)S(1)} %bitcast.4, f32[8,128,512]{2,1,0:T(8,128)S(1)} %copy-done, f32[8,128,512]{2,1,0:T(8,128)S(1)} %copy-done.1), custom_call_target="tpu_custom_call" | custom-call | tf_op jit(solution)/shard_map/bin/pallas_call | solution.py:297
  31.3 0.0 copy-start.11
  31.3 1.3 %collective-permute-start = (f32[128,512]{1,0:T(8,128)S(1)}, f32[128,512]{1,0:T(8,128)S(1)}, u32[]{:S(2)}, u32[]{:S(2)}) collective-permute-start(f32[128,512]{1,0:T(8,128)S(1)} %get-tuple-element.28), channel_id=1, source_target_pairs={{4,0},{8,4},{12,8},{16,12},{20,16},{24,20},{28,24},{5,1},{9,5},{13... | collective-permute-start | bytes 786440 | tf_op jit(solution)/shard_map/ppermute | solution.py:21
  32.6 3.9 %collective-permute-start.2 = (f32[128,512]{1,0:T(8,128)S(1)}, f32[128,512]{1,0:T(8,128)S(1)}, u32[]{:S(2)}, u32[]{:S(2)}) collective-permute-start(f32[128,512]{1,0:T(8,128)S(1)} %get-tuple-element.27.refs_1_), channel_id=1, source_target_pairs={{0,4},{4,8},{8,12},{12,16},{16,20},{20,24},{24,28},{1,5},{5,9},{9,... | collective-permute-start | bytes 786440 | tf_op jit(solution)/shard_map/ppermute | solution.py:21
  36.6 1.3 %collective-permute-start.1 = (f32[8,512]{1,0:T(8,128)S(1)}, f32[8,512]{1,0:T(8,128)S(1)}, u32[]{:S(2)}, u32[]{:S(2)}) collective-permute-start(f32[8,512]{1,0:T(8,128)S(1)} %get-tuple-element.30), channel_id=1, source_target_pairs={{1,0},{2,1},{3,2},{5,4},{6,5},{7,6},{9,8},{10,9},{11,10},{13,12},{... | collective-permute-start | bytes 49160 | tf_op jit(solution)/shard_map/ppermute | solution.py:21
  37.9 4.5 %collective-permute-start.3 = (f32[8,512]{1,0:T(8,128)S(1)}, f32[8,512]{1,0:T(8,128)S(1)}, u32[]{:S(2)}, u32[]{:S(2)}) collective-permute-start(f32[8,512]{1,0:T(8,128)S(1)} %get-tuple-element.29.refs_3_), channel_id=1, source_target_pairs={{0,1},{1,2},{2,3},{4,5},{5,6},{6,7},{8,9},{9,10},{10,11},{12,13},{... | collective-permute-start | bytes 49160 | tf_op jit(solution)/shard_map/ppermute | solution.py:21
  42.4 7.0 %apply.3 = (f32[8,128,512]{2,1,0:T(8,128)S(1)}, f32[2,8,128]{2,1,0:T(8,128)S(1)}) custom-call(f32[8,128,512]{2,1,0:T(8,128)S(1)} %get-tuple-element.24.v_ref.b_ref, f32[8,128,512]{2,1,0:T(8,128)S(1)} %copy-done, f32[8,128,512]{2,1,0:T(8,128)S(1)} %copy-done.1, f32[8,128,128]{2,1,0:T(8,128)S(1)} %get-tuple-element.25.diag_ref), custom_call_target="tpu_custom_call" | custom-call | flops 31457280 | bytes 8388608 | tf_op jit(solution)/shard_map/apply/pallas_call | solution.py:297
  49.5 0.0 copy-done.11
  49.5 0.0 collective-permute-done.1.right_ref.refs_4_
  49.5 0.0 collective-permute-done.3.left_ref
  49.5 0.0 collective-permute-done.below_ref.refs_2_
  49.5 0.0 collective-permute-done.2.above_ref
  49.5 0.5 correct.3
  50.1 0.0 copy-start.3
  50.1 1.3 %collective-permute-start.4 = (f32[128,512]{1,0:T(8,128)S(1)}, f32[128,512]{1,0:T(8,128)S(1)}, u32[]{:S(2)}, u32[]{:S(2)}) collective-permute-start(f32[128,512]{1,0:T(8,128)S(1)} %get-tuple-element.35), channel_id=1, source_target_pairs={{4,0},{8,4},{12,8},{16,12},{20,16},{24,20},{28,24},{5,1},{9,5},{13... | collective-permute-start | bytes 786440 | tf_op jit(solution)/shard_map/ppermute | solution.py:21
  51.4 3.7 %collective-permute-start.6 = (f32[128,512]{1,0:T(8,128)S(1)}, f32[128,512]{1,0:T(8,128)S(1)}, u32[]{:S(2)}, u32[]{:S(2)}) collective-permute-start(f32[128,512]{1,0:T(8,128)S(1)} %get-tuple-element.34.refs_6_), channel_id=1, source_target_pairs={{0,4},{4,8},{8,12},{12,16},{16,20},{20,24},{24,28},{1,5},{5,9},{9,... | collective-permute-start | bytes 786440 | tf_op jit(solution)/shard_map/ppermute | solution.py:21
  55.1 1.3 %collective-permute-start.5 = (f32[8,512]{1,0:T(8,128)S(1)}, f32[8,512]{1,0:T(8,128)S(1)}, u32[]{:S(2)}, u32[]{:S(2)}) collective-permute-start(f32[8,512]{1,0:T(8,128)S(1)} %get-tuple-element.37), channel_id=1, source_target_pairs={{1,0},{2,1},{3,2},{5,4},{6,5},{7,6},{9,8},{10,9},{11,10},{13,12},{... | collective-permute-start | bytes 49160 | tf_op jit(solution)/shard_map/ppermute | solution.py:21
  56.4 4.5 %collective-permute-start.7 = (f32[8,512]{1,0:T(8,128)S(1)}, f32[8,512]{1,0:T(8,128)S(1)}, u32[]{:S(2)}, u32[]{:S(2)}) collective-permute-start(f32[8,512]{1,0:T(8,128)S(1)} %get-tuple-element.36.refs_8_), channel_id=1, source_target_pairs={{0,1},{1,2},{2,3},{4,5},{5,6},{6,7},{8,9},{9,10},{10,11},{12,13},{... | collective-permute-start | bytes 49160 | tf_op jit(solution)/shard_map/ppermute | solution.py:21
  60.9 7.1 %apply.4 = (f32[8,128,512]{2,1,0:T(8,128)S(1)}, f32[2,8,128]{2,1,0:T(8,128)S(1)}) custom-call(f32[8,128,512]{2,1,0:T(8,128)S(1)} %get-tuple-element.32.v_ref.v1_ref, f32[8,128,512]{2,1,0:T(8,128)S(1)} %copy-done, f32[8,128,512]{2,1,0:T(8,128)S(1)} %copy-done.1, f32[8,128,128]{2,1,0:T(8,128)S(1)} %get-tuple-element.25.diag_ref), custom_call_target="tpu_custom_call" | custom-call | flops 31457280 | bytes 8388608 | tf_op jit(solution)/shard_map/apply/pallas_call | solution.py:297
  68.1 0.0 copy-done.3
  68.1 0.0 collective-permute-done.5.right_ref.refs_9_
  68.1 0.0 collective-permute-done.7.left_ref
  68.1 0.0 collective-permute-done.4.below_ref.refs_7_
  68.1 0.0 collective-permute-done.6.above_ref
  68.1 0.5 correct.4
  68.7 0.0 copy-start.5
  68.7 1.3 %collective-permute-start.8 = (f32[128,512]{1,0:T(8,128)S(1)}, f32[128,512]{1,0:T(8,128)S(1)}, u32[]{:S(2)}, u32[]{:S(2)}) collective-permute-start(f32[128,512]{1,0:T(8,128)S(1)} %get-tuple-element.42), channel_id=1, source_target_pairs={{4,0},{8,4},{12,8},{16,12},{20,16},{24,20},{28,24},{5,1},{9,5},{13... | collective-permute-start | bytes 786440 | tf_op jit(solution)/shard_map/ppermute | solution.py:21
  70.0 3.7 %collective-permute-start.10 = (f32[128,512]{1,0:T(8,128)S(1)}, f32[128,512]{1,0:T(8,128)S(1)}, u32[]{:S(2)}, u32[]{:S(2)}) collective-permute-start(f32[128,512]{1,0:T(8,128)S(1)} %get-tuple-element.41.refs_11_), channel_id=1, source_target_pairs={{0,4},{4,8},{8,12},{12,16},{16,20},{20,24},{24,28},{1,5},{5,9},{9,... | collective-permute-start | bytes 786440 | tf_op jit(solution)/shard_map/ppermute | solution.py:21
  73.7 1.3 %collective-permute-start.9 = (f32[8,512]{1,0:T(8,128)S(1)}, f32[8,512]{1,0:T(8,128)S(1)}, u32[]{:S(2)}, u32[]{:S(2)}) collective-permute-start(f32[8,512]{1,0:T(8,128)S(1)} %get-tuple-element.44), channel_id=1, source_target_pairs={{1,0},{2,1},{3,2},{5,4},{6,5},{7,6},{9,8},{10,9},{11,10},{13,12},{... | collective-permute-start | bytes 49160 | tf_op jit(solution)/shard_map/ppermute | solution.py:21
  75.0 7.1 %apply.5 = (f32[8,128,512]{2,1,0:T(8,128)S(1)}, f32[2,8,128]{2,1,0:T(8,128)S(1)}) custom-call(f32[8,128,512]{2,1,0:T(8,128)S(1)} %get-tuple-element.39.v_ref.v2_ref, f32[8,128,512]{2,1,0:T(8,128)S(1)} %copy-done, f32[8,128,512]{2,1,0:T(8,128)S(1)} %copy-done.1, f32[8,128,128]{2,1,0:T(8,128)S(1)} %get-tuple-element.25.diag_ref), custom_call_target="tpu_custom_call" | custom-call | flops 31457280 | bytes 8388608 | tf_op jit(solution)/shard_map/apply/pallas_call | solution.py:297
  82.1 0.0 copy-done.5
  82.2 0.0 copy-start.7
  82.2 1.3 %copy-done.7 = f32[8,128,512]{2,1,0:T(8,128)} copy-done((f32[8,128,512]{2,1,0:T(8,128)}, f32[8,128,512]{2,1,0:T(8,128)S(1)}, u32[]{:S(2)}) %copy-start.7) | copy-done | bytes 2097176
  83.5 0.0 collective-permute-done.9.refs_14_.right_ref
  83.5 0.0 collective-permute-done.8.refs_12_.below_ref
  83.5 0.8 moments.1
  84.3 7.9 %all-to-all-start.1 = ((f32[32,1,128]{2,1,0:T(1,128)}), f32[32,1,128]{2,1,0:T(1,128)S(1)}, u32[]{:S(2)}, u32[]{:S(2)}) async-start(f32[32,1,128]{2,1,0:T(1,128)} %moments.1), calls=%async_computation.1 | async-start | bytes 32768 | tf_op jit(solution)/shard_map/all_to_all | solution.py:357
  92.1 3.7 %collective-permute-start.11 = (f32[8,512]{1,0:T(8,128)S(1)}, f32[8,512]{1,0:T(8,128)S(1)}, u32[]{:S(2)}, u32[]{:S(2)}) collective-permute-start(f32[8,512]{1,0:T(8,128)S(1)} %get-tuple-element.43.refs_13_), channel_id=1, source_target_pairs={{0,1},{1,2},{2,3},{4,5},{5,6},{6,7},{8,9},{9,10},{10,11},{12,13},{... | collective-permute-start | bytes 49160 | tf_op jit(solution)/shard_map/ppermute | solution.py:21
  95.8 1.4 %collective-permute-done.11.left_ref = f32[8,512]{1,0:T(8,128)S(1)} collective-permute-done((f32[8,512]{1,0:T(8,128)S(1)}, f32[8,512]{1,0:T(8,128)S(1)}, u32[]{:S(2)}, u32[]{:S(2)}) %collective-permute-start.11) | collective-permute-done | bytes 16416 | tf_op jit(solution)/shard_map/ppermute | solution.py:21
  97.3 0.0 collective-permute-done.10.above_ref
  97.3 1.6 %copy-done.2 = f32[8,128,512]{2,1,0:T(8,128)S(1)} copy-done((f32[8,128,512]{2,1,0:T(8,128)S(1)}, f32[8,128,512]{2,1,0:T(8,128)}, u32[]{:S(2)}) %copy-start.2) | copy-done | bytes 2097176
  98.9 1.6 %copy-done.8 = f32[8,128,512]{2,1,0:T(8,128)S(1)} copy-done((f32[8,128,512]{2,1,0:T(8,128)S(1)}, f32[8,128,512]{2,1,0:T(8,128)}, u32[]{:S(2)}) %copy-start.8) | copy-done | bytes 2097176
  100.4 0.3 correct.5.v3_ref
  100.7 0.0 copy-start.9
  100.7 1.3 %copy-done.9 = f32[8,128,512]{2,1,0:T(8,128)} copy-done((f32[8,128,512]{2,1,0:T(8,128)}, f32[8,128,512]{2,1,0:T(8,128)S(1)}, u32[]{:S(2)}) %copy-start.9) | copy-done | bytes 2097176
  102.1 0.0 all-to-all-done.1.parts_ref
  102.1 1.6 %copy-done.4 = f32[8,128,512]{2,1,0:T(8,128)S(1)} copy-done((f32[8,128,512]{2,1,0:T(8,128)S(1)}, f32[8,128,512]{2,1,0:T(8,128)}, u32[]{:S(2)}) %copy-start.4) | copy-done | bytes 2097176
  103.7 1.6 %copy-done.6 = f32[8,128,512]{2,1,0:T(8,128)S(1)} copy-done((f32[8,128,512]{2,1,0:T(8,128)S(1)}, f32[8,128,512]{2,1,0:T(8,128)}, u32[]{:S(2)}) %copy-start.6) | copy-done | bytes 2097176
  105.2 1.6 %copy-done.10 = f32[8,128,512]{2,1,0:T(8,128)S(1)} copy-done((f32[8,128,512]{2,1,0:T(8,128)S(1)}, f32[8,128,512]{2,1,0:T(8,128)}, u32[]{:S(2)}) %copy-start.10) | copy-done | bytes 2097176
  106.8 1.6 %copy-done.12 = f32[8,128,512]{2,1,0:T(8,128)S(1)} copy-done((f32[8,128,512]{2,1,0:T(8,128)S(1)}, f32[8,128,512]{2,1,0:T(8,128)}, u32[]{:S(2)}) %copy-start.12) | copy-done | bytes 2097176
  108.4 3.0 %finish.1 = (f32[8,128,512]{2,1,0:T(8,128)}, f32[8,128,512]{2,1,0:T(8,128)}) custom-call(f32[32,1,128]{2,1,0:T(1,128)S(1)} %all-to-all-done.1.parts_ref, f32[8,128,512]{2,1,0:T(8,128)S(1)} %copy-done.12, f32[8,128,512]{2,1,0:T(8,128)S(1)} %copy-done.4, f32[8,128,512]{2,1,0:T(8,128)S(1)} %copy-done.6, f32[8,128,512]{2,1,0:T(8,128)S(1)} %copy-done.10), custom_call_target="tpu_custom_call" | custom-call | tf_op jit(solution)/shard_map/finish/pallas_call | solution.py:297
  (6 shorter events, 0.0 us)
Async XLA Ops:
  0.6 27.8 %copy-start = (f32[8,128,512]{2,1,0:T(8,128)S(1)}, f32[8,128,512]{2,1,0:T(8,128)}, u32[]{:S(2)}) copy-start(f32[8,128,512]{2,1,0:T(8,128)} %p1_ref.13) | copy-start | bytes 6291460
  1.6 1.0 copy-start.13
  2.6 0.7 copy-start.14
  3.2 0.7 copy-start.15
  28.4 1.6 %copy-start.1 = (f32[8,128,512]{2,1,0:T(8,128)S(1)}, f32[8,128,512]{2,1,0:T(8,128)}, u32[]{:S(2)}) copy-start(f32[8,128,512]{2,1,0:T(8,128)} %p2_ref.13) | copy-start | bytes 6291460
  31.3 18.2 %copy-start.11 = (f32[8,128,512]{2,1,0:T(8,128)}, f32[8,128,512]{2,1,0:T(8,128)S(1)}, u32[]{:S(2)}) copy-start(f32[8,128,512]{2,1,0:T(8,128)S(1)} %get-tuple-element.24.v_ref.b_ref) | copy-start | bytes 6291460
  31.3 18.2 %collective-permute-start = (f32[128,512]{1,0:T(8,128)S(1)}, f32[128,512]{1,0:T(8,128)S(1)}, u32[]{:S(2)}, u32[]{:S(2)}) collective-permute-start(f32[128,512]{1,0:T(8,128)S(1)} %get-tuple-element.28), channel_id=1, source_target_pairs={{4,0},{8,4},{12,8},{16,12},{20,16},{24,20},{28,24},{5,1},{9,5},{13... | collective-permute-start | bytes 786440 | tf_op jit(solution)/shard_map/ppermute | solution.py:21
  32.6 16.9 %collective-permute-start.2 = (f32[128,512]{1,0:T(8,128)S(1)}, f32[128,512]{1,0:T(8,128)S(1)}, u32[]{:S(2)}, u32[]{:S(2)}) collective-permute-start(f32[128,512]{1,0:T(8,128)S(1)} %get-tuple-element.27.refs_1_), channel_id=1, source_target_pairs={{0,4},{4,8},{8,12},{12,16},{16,20},{20,24},{24,28},{1,5},{5,9},{9,... | collective-permute-start | bytes 786440 | tf_op jit(solution)/shard_map/ppermute | solution.py:21
  36.6 12.9 %collective-permute-start.1 = (f32[8,512]{1,0:T(8,128)S(1)}, f32[8,512]{1,0:T(8,128)S(1)}, u32[]{:S(2)}, u32[]{:S(2)}) collective-permute-start(f32[8,512]{1,0:T(8,128)S(1)} %get-tuple-element.30), channel_id=1, source_target_pairs={{1,0},{2,1},{3,2},{5,4},{6,5},{7,6},{9,8},{10,9},{11,10},{13,12},{... | collective-permute-start | bytes 49160 | tf_op jit(solution)/shard_map/ppermute | solution.py:21
  37.9 11.6 %collective-permute-start.3 = (f32[8,512]{1,0:T(8,128)S(1)}, f32[8,512]{1,0:T(8,128)S(1)}, u32[]{:S(2)}, u32[]{:S(2)}) collective-permute-start(f32[8,512]{1,0:T(8,128)S(1)} %get-tuple-element.29.refs_3_), channel_id=1, source_target_pairs={{0,1},{1,2},{2,3},{4,5},{5,6},{6,7},{8,9},{9,10},{10,11},{12,13},{... | collective-permute-start | bytes 49160 | tf_op jit(solution)/shard_map/ppermute | solution.py:21
  50.1 18.0 %copy-start.3 = (f32[8,128,512]{2,1,0:T(8,128)}, f32[8,128,512]{2,1,0:T(8,128)S(1)}, u32[]{:S(2)}) copy-start(f32[8,128,512]{2,1,0:T(8,128)S(1)} %get-tuple-element.32.v_ref.v1_ref) | copy-start | bytes 6291460
  50.1 18.0 %collective-permute-start.4 = (f32[128,512]{1,0:T(8,128)S(1)}, f32[128,512]{1,0:T(8,128)S(1)}, u32[]{:S(2)}, u32[]{:S(2)}) collective-permute-start(f32[128,512]{1,0:T(8,128)S(1)} %get-tuple-element.35), channel_id=1, source_target_pairs={{4,0},{8,4},{12,8},{16,12},{20,16},{24,20},{28,24},{5,1},{9,5},{13... | collective-permute-start | bytes 786440 | tf_op jit(solution)/shard_map/ppermute | solution.py:21
  51.4 16.8 %collective-permute-start.6 = (f32[128,512]{1,0:T(8,128)S(1)}, f32[128,512]{1,0:T(8,128)S(1)}, u32[]{:S(2)}, u32[]{:S(2)}) collective-permute-start(f32[128,512]{1,0:T(8,128)S(1)} %get-tuple-element.34.refs_6_), channel_id=1, source_target_pairs={{0,4},{4,8},{8,12},{12,16},{16,20},{20,24},{24,28},{1,5},{5,9},{9,... | collective-permute-start | bytes 786440 | tf_op jit(solution)/shard_map/ppermute | solution.py:21
  55.1 13.0 %collective-permute-start.5 = (f32[8,512]{1,0:T(8,128)S(1)}, f32[8,512]{1,0:T(8,128)S(1)}, u32[]{:S(2)}, u32[]{:S(2)}) collective-permute-start(f32[8,512]{1,0:T(8,128)S(1)} %get-tuple-element.37), channel_id=1, source_target_pairs={{1,0},{2,1},{3,2},{5,4},{6,5},{7,6},{9,8},{10,9},{11,10},{13,12},{... | collective-permute-start | bytes 49160 | tf_op jit(solution)/shard_map/ppermute | solution.py:21
  56.4 11.7 %collective-permute-start.7 = (f32[8,512]{1,0:T(8,128)S(1)}, f32[8,512]{1,0:T(8,128)S(1)}, u32[]{:S(2)}, u32[]{:S(2)}) collective-permute-start(f32[8,512]{1,0:T(8,128)S(1)} %get-tuple-element.36.refs_8_), channel_id=1, source_target_pairs={{0,1},{1,2},{2,3},{4,5},{5,6},{6,7},{8,9},{9,10},{10,11},{12,13},{... | collective-permute-start | bytes 49160 | tf_op jit(solution)/shard_map/ppermute | solution.py:21
  68.7 13.5 %copy-start.5 = (f32[8,128,512]{2,1,0:T(8,128)}, f32[8,128,512]{2,1,0:T(8,128)S(1)}, u32[]{:S(2)}) copy-start(f32[8,128,512]{2,1,0:T(8,128)S(1)} %get-tuple-element.39.v_ref.v2_ref) | copy-start | bytes 6291460
  68.7 14.8 %collective-permute-start.8 = (f32[128,512]{1,0:T(8,128)S(1)}, f32[128,512]{1,0:T(8,128)S(1)}, u32[]{:S(2)}, u32[]{:S(2)}) collective-permute-start(f32[128,512]{1,0:T(8,128)S(1)} %get-tuple-element.42), channel_id=1, source_target_pairs={{4,0},{8,4},{12,8},{16,12},{20,16},{24,20},{28,24},{5,1},{9,5},{13... | collective-permute-start | bytes 786440 | tf_op jit(solution)/shard_map/ppermute | solution.py:21
  70.0 27.3 %collective-permute-start.10 = (f32[128,512]{1,0:T(8,128)S(1)}, f32[128,512]{1,0:T(8,128)S(1)}, u32[]{:S(2)}, u32[]{:S(2)}) collective-permute-start(f32[128,512]{1,0:T(8,128)S(1)} %get-tuple-element.41.refs_11_), channel_id=1, source_target_pairs={{0,4},{4,8},{8,12},{12,16},{16,20},{20,24},{24,28},{1,5},{5,9},{9,... | collective-permute-start | bytes 786440 | tf_op jit(solution)/shard_map/ppermute | solution.py:21
  73.7 9.8 %collective-permute-start.9 = (f32[8,512]{1,0:T(8,128)S(1)}, f32[8,512]{1,0:T(8,128)S(1)}, u32[]{:S(2)}, u32[]{:S(2)}) collective-permute-start(f32[8,512]{1,0:T(8,128)S(1)} %get-tuple-element.44), channel_id=1, source_target_pairs={{1,0},{2,1},{3,2},{5,4},{6,5},{7,6},{9,8},{10,9},{11,10},{13,12},{... | collective-permute-start | bytes 49160 | tf_op jit(solution)/shard_map/ppermute | solution.py:21
  82.2 1.3 %copy-start.7 = (f32[8,128,512]{2,1,0:T(8,128)}, f32[8,128,512]{2,1,0:T(8,128)S(1)}, u32[]{:S(2)}) copy-start(f32[8,128,512]{2,1,0:T(8,128)S(1)} %get-tuple-element.45.image_ref) | copy-start | bytes 6291460
  84.3 17.8 %all-to-all-start.1 = ((f32[32,1,128]{2,1,0:T(1,128)}), f32[32,1,128]{2,1,0:T(1,128)S(1)}, u32[]{:S(2)}, u32[]{:S(2)}) async-start(f32[32,1,128]{2,1,0:T(1,128)} %moments.1), calls=%async_computation.1 | async-start | bytes 32768 | tf_op jit(solution)/shard_map/all_to_all | solution.py:357
  92.1 5.1 %collective-permute-start.11 = (f32[8,512]{1,0:T(8,128)S(1)}, f32[8,512]{1,0:T(8,128)S(1)}, u32[]{:S(2)}, u32[]{:S(2)}) collective-permute-start(f32[8,512]{1,0:T(8,128)S(1)} %get-tuple-element.43.refs_13_), channel_id=1, source_target_pairs={{0,1},{1,2},{2,3},{4,5},{5,6},{6,7},{8,9},{9,10},{10,11},{12,13},{... | collective-permute-start | bytes 49160 | tf_op jit(solution)/shard_map/ppermute | solution.py:21
  97.3 1.6 %copy-start.2 = (f32[8,128,512]{2,1,0:T(8,128)S(1)}, f32[8,128,512]{2,1,0:T(8,128)}, u32[]{:S(2)}) copy-start(f32[8,128,512]{2,1,0:T(8,128)} %p2_ref.13) | copy-start | bytes 6291460
  98.9 1.6 %copy-start.8 = (f32[8,128,512]{2,1,0:T(8,128)S(1)}, f32[8,128,512]{2,1,0:T(8,128)}, u32[]{:S(2)}) copy-start(f32[8,128,512]{2,1,0:T(8,128)} %copy-done.7) | copy-start | bytes 6291460
  100.7 1.3 %copy-start.9 = (f32[8,128,512]{2,1,0:T(8,128)}, f32[8,128,512]{2,1,0:T(8,128)S(1)}, u32[]{:S(2)}) copy-start(f32[8,128,512]{2,1,0:T(8,128)S(1)} %correct.5.v3_ref) | copy-start | bytes 6291460
  102.1 1.6 %copy-start.4 = (f32[8,128,512]{2,1,0:T(8,128)S(1)}, f32[8,128,512]{2,1,0:T(8,128)}, u32[]{:S(2)}) copy-start(f32[8,128,512]{2,1,0:T(8,128)} %copy-done.3) | copy-start | bytes 6291460
  103.7 1.6 %copy-start.6 = (f32[8,128,512]{2,1,0:T(8,128)S(1)}, f32[8,128,512]{2,1,0:T(8,128)}, u32[]{:S(2)}) copy-start(f32[8,128,512]{2,1,0:T(8,128)} %copy-done.5) | copy-start | bytes 6291460
  105.2 1.6 %copy-start.10 = (f32[8,128,512]{2,1,0:T(8,128)S(1)}, f32[8,128,512]{2,1,0:T(8,128)}, u32[]{:S(2)}) copy-start(f32[8,128,512]{2,1,0:T(8,128)} %copy-done.9) | copy-start | bytes 6291460
  106.8 1.6 %copy-start.12 = (f32[8,128,512]{2,1,0:T(8,128)S(1)}, f32[8,128,512]{2,1,0:T(8,128)}, u32[]{:S(2)}) copy-start(f32[8,128,512]{2,1,0:T(8,128)} %copy-done.11) | copy-start | bytes 6291460

commit v2 on v1

--- a/solution.py
+++ b/solution.py
@@ -11,7 +11,9 @@
 LANES = 128
 SUBLANES = 8
 
+SHIFT = 6.0
 IN_VMEM = pl.BlockSpec(memory_space=pltpu.VMEM)
+IN_HBM = pl.BlockSpec(memory_space=pltpu.HBM)
 PARAMS = pltpu.CompilerParams(vmem_limit_bytes=16 << 20)
 
 
@@ -84,29 +86,43 @@
     return functools.reduce(lambda s, t: s + t, [a * b for a, b in zip(x, y)])
 
 
-def pack_kernel(capacity, owner_ref, cell_ref, live_ref, traces_ref, out_ref):
+def pack_kernel(capacity, owner_hbm, cell_hbm, live_hbm, traces_hbm, out_ref, owner_ref, cell_ref, live_ref, traces_ref, sems):
     held, samples = traces_ref.shape
     slots = out_ref.shape[0]
-    spread = jnp.broadcast_to(owner_ref[...], (held, held))
+    pairs = ((owner_hbm, owner_ref), (cell_hbm, cell_ref), (live_hbm, live_ref), (traces_hbm, traces_ref))
+    copies = [pltpu.make_async_copy(src, dst, sems.at[k]) for k, (src, dst) in enumerate(pairs)]
+    for copy in copies:
+        copy.start()
+    for copy in copies[:3]:
+        copy.wait()
+    owner = owner_ref[...].astype(jnp.float32)
     row, col = iota((held, held), 0), iota((held, held), 1)
-    owner = jnp.sum(jnp.where(row == col, spread, 0), axis=0, keepdims=True)
-    rank = jnp.sum(jnp.where((spread == owner) & (row < col), 1, 0), axis=0, keepdims=True)
-    slot = jnp.where(live_ref[...] > 0, owner * capacity + rank, -1)
+    owner_down = jnp.sum(jnp.where(row == col, owner, 0.0), axis=1, keepdims=True)
+    earlier_same = (owner_down == owner) & (row < col)
+    rank = jnp.sum(jnp.where(earlier_same, 1.0, 0.0), axis=0, keepdims=True)
+    slot = jnp.where(live_ref[...] > 0, owner * capacity + rank, -1.0).astype(jnp.int32)
     chosen = (iota((slots, held), 0) == slot).astype(jnp.float32).astype(jnp.bfloat16)
     cell = cell_ref[...]
     kind = iota((LANES, held), 0)
     upper = (lax.shift_right_logical(cell, 6) + 1).astype(jnp.float32)
     lower = (cell & 63).astype(jnp.float32)
     codes = jnp.where(kind == 0, upper, jnp.where(kind == 1, lower, 0.0)).astype(jnp.bfloat16)
+    sent = lax.dot_general(chosen, codes, (((1,), (1,)), ((), ())), preferred_element_type=jnp.float32)
+    out_ref[:, samples:] = sent.astype(jnp.bfloat16)
+    copies[3].wait()
     rows = jnp.dot(chosen, traces_ref[...], preferred_element_type=jnp.float32)
     out_ref[:, :samples] = rows.astype(jnp.bfloat16)
-    sent = lax.dot_general(chosen, codes, (((1,), (1,)), ((), ())), preferred_element_type=jnp.float32)
-    out_ref[:, samples:] = sent.astype(jnp.bfloat16)
-
-
-def bin_kernel(got_ref, p1_ref, p2_ref, b_ref, diag_ref, row0_ref, row7_ref, col0_ref, col7_ref):
+
+
+def bin_kernel(got_ref, p1_hbm, p2_hbm, b_ref, diag_ref, row0_ref, row7_ref, col0_ref, col7_ref, p1_ref, p2_ref, sems):
     rows, cols, samples = b_ref.shape
     slots = got_ref.shape[0]
+    copies = (
+        pltpu.make_async_copy(p1_hbm.at[rows - 1], p1_ref, sems.at[0]),
+        pltpu.make_async_copy(p2_hbm.at[:, pl.ds(cols - SUBLANES, SUBLANES)], p2_ref, sems.at[1]),
+    )
+    for copy in copies:
+        copy.start()
     kind = iota((SUBLANES, LANES), 1)
     weight = jnp.where(kind == 0, 64.0, jnp.where(kind == 1, 1.0, 0.0)).astype(jnp.bfloat16)
     value = lax.dot_general(
@@ -116,7 +132,7 @@
     not_first_row = (lax.axis_index("inl") > 0).astype(jnp.float32)
     not_first_col = (lax.axis_index("xl") > 0).astype(jnp.float32)
     ones = jnp.ones((slots, LANES), jnp.bfloat16)
-    first_col = jnp.where(iota((cols, LANES), 0) == 0, not_first_col, 0.0)
+    first_col = jnp.where(iota((cols, LANES), 0) == 0, not_first_col, 0.0) - SHIFT
     got = got_ref[:, :samples]
     for i in range(rows):
         place = (iota((cols, slots), 0) + i * cols == bin_of).astype(jnp.float32).astype(jnp.bfloat16)
@@ -124,22 +140,25 @@
         hits = jnp.dot(place, ones, preferred_element_type=jnp.float32)
         diag = 2.0 * hits + first_col
         diag_ref[i] = diag + not_first_row if i == 0 else diag
-    write_edges(b_ref, p1_ref, p2_ref, row0_ref, row7_ref, col0_ref, col7_ref)
-
-
-def write_edges(v_ref, p1_ref, p2_ref, row0_ref, row7_ref, col0_ref, col7_ref):
+    for copy in copies:
+        copy.wait()
+    write_edges(
+        b_ref, lambda at: load(p1_ref, at), lambda i: load(p2_ref, i, slice(None)),
+        row0_ref, row7_ref, col0_ref, col7_ref,
+    )
+
+
+def write_edges(v_ref, p1_last_row, p2_last_cols, row0_ref, row7_ref, col0_ref, col7_ref):
     rows, cols, _ = v_ref.shape
-    last = rows - 1
     for x in range(0, cols, SUBLANES):
         at = slice(x, x + SUBLANES)
         store(row0_ref, load(v_ref, 0, at), at)
-        v = load(v_ref, last, at)
-        store(row7_ref, add(v, dip_part(load(p1_ref, last, at), *stencil(v))), at)
+        v = load(v_ref, rows - 1, at)
+        store(row7_ref, add(v, dip_part(p1_last_row(at), *stencil(v))), at)
     for i in range(rows):
         store(col0_ref, load(v_ref, i, slice(0, 1)), slice(i, i + 1))
-        at = slice(cols - SUBLANES, cols)
-        v = load(v_ref, i, at)
-        moved = add(v, dip_part(load(p2_ref, i, at), *stencil(v)))
+        v = load(v_ref, i, slice(cols - SUBLANES, cols))
+        moved = add(v, dip_part(p2_last_cols(i), *stencil(v)))
         store(col7_ref, [t[SUBLANES - 1 :] for t in moved], slice(i, i + 1))
 
 
@@ -150,23 +169,22 @@
     zero = [jnp.zeros((SUBLANES, LANES), jnp.float32)] * tiles
     first_ref[...] = jnp.zeros_like(first_ref)
 
-    def body(i, carry):
-        vout, vv = carry
-        after = jnp.where(i + 1 < rows, 1.0, 0.0)
-        nxt = jnp.minimum(i + 1, rows - 1)
-        v = load(v_ref, i, slice(0, SUBLANES))
-        up = [pltpu.roll(t, SUBLANES - 1, 0) for t in v]
-        down_before = zero
+    def row(i, sums, last):
+        def fetch(x):
+            at = slice(x, x + SUBLANES)
+            v = load(v_ref, i, at)
+            below = zero if last else load(v_ref, i + 1, at)
+            lead = [pltpu.roll(t, SUBLANES - 1, 0) for t in v]
+            return v, lead, below, load(p1_ref, i, at), load(p2_ref, i, at), load(first_ref, at), diag_ref[i, at, :]
+
+        vout, vv = zero[0], zero[0]
+        left_from = zero
+        ahead = fetch(0)
         for x in range(0, cols, SUBLANES):
             at = slice(x, x + SUBLANES)
-            if x + SUBLANES < cols:
-                v_ahead = load(v_ref, i, slice(x + SUBLANES, x + 2 * SUBLANES))
-                up_ahead = [pltpu.roll(t, SUBLANES - 1, 0) for t in v_ahead]
-            else:
-                v_ahead, up_ahead = zero, zero
-            right = [jnp.where(sub_index == SUBLANES - 1, b, a) for a, b in zip(up, up_ahead)]
-            below = [after * t for t in load(v_ref, nxt, at)]
-            p1, p2 = load(p1_ref, i, at), load(p2_ref, i, at)
+            v, lead, below, p1, p2, above, diag = ahead
+            ahead = fetch(x + SUBLANES) if x + SUBLANES < cols else (zero, zero)
+            right = [jnp.where(sub_index == SUBLANES - 1, b, a) for a, b in zip(lead, ahead[1])]
             odd, even = stencil(v)
             first = sub(sub(below, v), dip_part(p1, odd, even))
             second = sub(sub(right, v), dip_part(p2, odd, even))
@@ -174,20 +192,17 @@
             a2, b2 = adjoint_terms(p2, second)
             moved = adjoint_finish(add(first, second), add(a1, a2), add(b1, b2))
             down = [pltpu.roll(t, 1, 0) for t in second]
-            left = [jnp.where(sub_index == 0, b, a) for a, b in zip(down, down_before)]
-            above = load(first_ref, at)
-            store(first_ref, first, at)
-            diag = diag_ref[i, at, :]
+            left = [jnp.where(sub_index == 0, b, a) for a, b in zip(down, left_from)]
+            left_from = down
             out = [diag * c + ((f + s) - m) for c, f, s, m in zip(v, above, left, moved)]
-            store(out_ref, out, i, at)
             vout = vout + dot(v, out)
             vv = vv + dot(v, v)
-            v, up, down_before = v_ahead, up_ahead, down
-        return vout, vv
-
-    vout, vv = lax.fori_loop(0, rows, body, (zero[0], zero[0]))
-    sums_ref[0] = vout
-    sums_ref[1] = vv
+            store(first_ref, first, at)
+            store(out_ref, out, i, at)
+        return sums[0] + vout, sums[1] + vv
+
+    sums = lax.fori_loop(0, rows - 1, lambda i, sums: row(i, sums, False), (zero[0], zero[0]))
+    sums_ref[0], sums_ref[1] = row(rows - 1, sums, True)
 
 
 def halo_corrections(out_ref, p1_ref, p2_ref, below_ref, above_ref, right_ref, left_ref):
@@ -215,7 +230,13 @@
 ):
     halo_corrections(out_ref, p1_ref, p2_ref, below_ref, above_ref, right_ref, left_ref)
     if edge_refs:
-        write_edges(out_ref, p1_ref, p2_ref, *edge_refs)
+        rows, cols, _ = out_ref.shape
+        write_edges(
+            out_ref,
+            lambda at: load(p1_ref, rows - 1, at),
+            lambda i: load(p2_ref, i, slice(cols - SUBLANES, cols)),
+            *edge_refs,
+        )
 
 
 def moments_kernel(*refs):
@@ -246,62 +267,68 @@
     direction = [zero + 1.0] + [zero] * (ITERS - 1)
     norm_now = m[0]
 
-    def inner(x, y, power, count):
+    def inner(x, y, count):
         total = zero
         for i in range(count):
-            for j in range(count):
-                total = total + x[i] * y[j] * m[i + j + power]
+            for j in range(len(y)):
+                if i + j < len(m):
+                    total = total + x[i] * y[j] * m[i + j]
         return total
 
     for sweep in range(ITERS):
-        alpha = norm_now / inner(direction, direction, 1, sweep + 1)
+        image = [SHIFT * d for d in direction] + [zero]
+        image = [image[0]] + [s + d for s, d in zip(image[1:], direction)]
+        alpha = norm_now / inner(direction, image[: sweep + 2], sweep + 1)
         model = [s + alpha * d for s, d in zip(model, direction)]
-        residual = [residual[0]] + [r - alpha * d for r, d in zip(residual[1:], direction)]
+        residual = [r - alpha * d for r, d in zip(residual, image)]
         if sweep + 1 < ITERS:
-            norm_next = inner(residual, residual, 0, sweep + 2)
+            norm_next = inner(residual, residual[: sweep + 2], sweep + 2)
             beta = norm_next / norm_now
             direction = [r + beta * d for r, d in zip(residual, direction)]
             norm_now = norm_next
-    return model, residual
-
-
-def finish_kernel(parts_ref, b_ref, v1_ref, v2_ref, v3_ref, model_ref, residual_ref):
-    rows, cols, samples = b_ref.shape
-    line = jnp.sum(parts_ref[...], axis=0)
-    sub_index, lane = iota((SUBLANES, LANES), 0), iota((SUBLANES, LANES), 1)
-    total = jnp.sum(jnp.where(sub_index == lane, line, 0.0), axis=1, keepdims=True)
-    total = jnp.broadcast_to(total, (SUBLANES, LANES))
-    m = [jnp.broadcast_to(total[k : k + 1], (SUBLANES, LANES)) for k in range(2 * ITERS)]
-    model, residual = coefficients(m)
-
-    def body(i, carry):
-        for x in range(0, cols, SUBLANES):
-            at = slice(x, x + SUBLANES)
-            b, v1, v2, v3 = (load(ref, i, at) for ref in (b_ref, v1_ref, v2_ref, v3_ref))
-            store(model_ref, [(2.0 * model[0]) * s + (2.0 * model[1]) * t + (2.0 * model[2]) * u for s, t, u in zip(b, v1, v2)], i, at)
-            store(
-                residual_ref,
-                [residual[0] * s + residual[1] * t + residual[2] * u + residual[3] * w for s, t, u, w in zip(b, v1, v2, v3)],
-                i, at,
-            )
-        return carry
-
-    lax.fori_loop(0, rows, body, 0)
+    return [2.0 * s for s in model] + residual
+
+
+def finish_kernel(parts_ref, b_ref, v1_ref, v2_ref, v3_ref, model_ref, residual_ref, weight_ref):
+    cols = b_ref.shape[1]
+    i = pl.program_id(0)
+
+    @pl.when(i == 0)
+    def _():
+        line = jnp.sum(parts_ref[...], axis=0)
+        sub_index, lane = iota((SUBLANES, LANES), 0), iota((SUBLANES, LANES), 1)
+        total = jnp.sum(jnp.where(sub_index == lane, line, 0.0), axis=1, keepdims=True)
+        total = jnp.broadcast_to(total, (SUBLANES, LANES))
+        m = [jnp.broadcast_to(total[k : k + 1], (SUBLANES, LANES)) for k in range(2 * ITERS)]
+        for k, weight in enumerate(coefficients(m)):
+            weight_ref[k] = weight
+
+    weights = [weight_ref[k] for k in range(2 * ITERS + 1)]
+    model, residual = weights[:ITERS], weights[ITERS:]
+    for x in range(0, cols, SUBLANES):
+        at = slice(x, x + SUBLANES)
+        b, v1, v2, v3 = (load(ref, i, at) for ref in (b_ref, v1_ref, v2_ref, v3_ref))
+        store(model_ref, [model[0] * s + model[1] * t + model[2] * u for s, t, u in zip(b, v1, v2)], 0, at)
+        store(
+            residual_ref,
+            [(residual[0] * s + residual[1] * t) + (residual[2] * u + residual[3] * w) for s, t, u, w in zip(b, v1, v2, v3)],
+            0, at,
+        )
 
 
 def f32(*shape):
     return pltpu.VMEM(shape, jnp.float32)
 
 
-def call(kernel, outs, *args, name, scratch=(), aliases=None, cost=None, params=PARAMS):
+def call(kernel, outs, *args, name, scratch=(), aliases=None, cost=None, ins=None):
     return pl.pallas_call(
         kernel,
         out_shape=outs,
-        in_specs=[IN_VMEM] * len(args),
+        in_specs=ins or [IN_VMEM] * len(args),
         out_specs=[IN_VMEM] * len(outs),
         scratch_shapes=list(scratch),
         input_output_aliases=aliases or {},
-        compiler_params=params,
+        compiler_params=PARAMS,
         cost_estimate=cost,
         name=name,
     )(*args)
@@ -321,17 +348,25 @@
     held = traces.shape[0]
     capacity = max(2, 2 * held // devices)
     slots = devices * capacity
+    small = pltpu.VMEM((1, held), jnp.int32)
     (sent,) = call(
         functools.partial(pack_kernel, capacity),
         [jax.ShapeDtypeStruct((slots, samples + LANES), jnp.bfloat16)],
-        trace_owner, trace_cell[None], acquired[None], traces,
-        name="pack",
+        trace_owner.reshape(1, held), trace_cell[None], acquired[None], traces,
+        name="pack", ins=[IN_HBM] * 4,
+        scratch=[small, small, small, pltpu.VMEM((held, samples), jnp.bfloat16), pltpu.SemaphoreType.DMA((4,))],
     )
     got = lax.all_to_all(sent, ("inl", "xl"), split_axis=0, concat_axis=0, tiled=True)
     edge_shapes = [f32(cols, samples), f32(cols, samples), f32(rows, samples), f32(rows, samples)]
     tile = f32(rows, cols, samples)
     b, diag, *edges = call(
-        bin_kernel, [tile, f32(rows, cols, LANES)] + edge_shapes, got, inline_dip, cross_dip, name="bin"
+        bin_kernel, [tile, f32(rows, cols, LANES)] + edge_shapes, got, inline_dip, cross_dip,
+        name="bin", ins=[IN_VMEM, IN_HBM, IN_HBM],
+        scratch=[
+            pltpu.VMEM((cols, samples), jnp.float32),
+            pltpu.VMEM((rows, SUBLANES, samples), jnp.float32),
+            pltpu.SemaphoreType.DMA((2,)),
+        ],
     )
     fields, products = [b], []
     cost = pl.CostEstimate(
@@ -353,10 +388,22 @@
             name="correct", aliases={0: 0},
         )
         fields.append(image)
-    (parts,) = call(moments_kernel, [jax.ShapeDtypeStruct((devices, 1, LANES), jnp.float32)], *products, name="moments")
+    (parts,) = call(moments_kernel, [f32(devices, 1, LANES)], *products, name="moments")
     parts = lax.all_to_all(parts, ("inl", "xl"), split_axis=0, concat_axis=0, tiled=True)
     out = jax.ShapeDtypeStruct((rows, cols, samples), jnp.float32)
-    return tuple(call(finish_kernel, [out, out], parts, *fields, name="finish"))
+    by_row = pl.BlockSpec((1, cols, samples), lambda i: (i, 0, 0))
+    return tuple(
+        pl.pallas_call(
+            finish_kernel,
+            grid=(rows,),
+            out_shape=[out, out],
+            in_specs=[IN_VMEM] * (ITERS + 2),
+            out_specs=[by_row, by_row],
+            scratch_shapes=[pltpu.VMEM((2 * ITERS + 1, SUBLANES, LANES), jnp.float32)],
+            compiler_params=PARAMS,
+            name="finish",
+        )(parts, *fields)
+    )
 
 
 def solution(mesh):

time: 112 us -> 113 us (level)
  Pallas kernels: 28.2 us -> 29.4 us
    pallas_call x10, Pallas kernels: 28.2 us -> 29.4 us  [the longest x9 25.5 us: call(): pl.pallas_call(kernel, out_shape=outs, in_specs=ins or [IN_VMEM] * len(ar...]
    unnamed x33 -> x34, local copies, waits for them, and re-layouts: 17.1 us -> 16.9 us
where the time goes in v2:
time: 113 us
  starting transfers between devices  39.8 us (35%)
  Pallas kernels  29.4 us (26%)
  blocking collectives  24 us (21%)
  local copies, waits for them, and re-layouts  16.9 us (15%)
  waiting for transfers between devices  1.46 us (1%)
    ppermute x12, starting transfers between devices, shifted(): lax.ppermute(value, axis, [(source, source + steps) for source in range(i...  31.9 us
    pallas_call x9, Pallas kernels, call(): pl.pallas_call(kernel, out_shape=outs, in_specs=ins or [IN_VMEM] * len(ar...  25.5 us
    all_to_all x1, blocking collectives, per_device(): lax.all_to_all(sent, ('inl', 'xl'), split_axis=0, concat_axis=0, tiled=True)  24 us
    unnamed x34, local copies, waits for them, and re-layouts  16.9 us
    all_to_all x1, starting transfers between devices, per_device(): lax.all_to_all(parts, ('inl', 'xl'), split_axis=0, concat_axis=0, tiled=T...  7.87 us
    pallas_call x1, Pallas kernels, per_device(): pl.pallas_call(finish_kernel, grid=(rows,), out_shape=[out, out], in_spec...  3.92 us
  transfers between devices with their start and end apart: 13, of which 1 were waited for; matrix products, arithmetic and copies ran while one was open for 0% of the time, Pallas kernels for 20%

profile of v2, /device:TPU:0, one launch (start us, length us, event | category | flops | bytes accessed | tf_op | source)
XLA Modules:
  0.0 112.5 jit_solution(10218872627891182130)
XLA Ops:
  0.6 0.0 copy-start
  0.6 0.0 copy-start.13
  0.7 1.1 copy-done.13
  1.7 0.0 copy-start.14
  1.7 0.7 copy-done.14
  2.4 0.0 copy-start.15
  2.4 0.7 copy-done.15
  3.1 0.7 copy-done.16
  3.8 0.7 pack.1
  4.5 24.0 %all_to_all.16 = bf16[32,16,640]{2,1,0:T(8,128)(2,1)S(1)} all-to-all(bf16[32,16,640]{2,1,0:T(8,128)(2,1)S(1)} %bitcast.6), channel_id=1, replica_groups=mesh['inl'=8,'xl'=4] {'inl','xl'}, dimensions={0} | all-to-all | bytes 1310720 | tf_op jit(solution)/shard_map/all_to_all | solution.py:359
  28.5 0.0 copy-done
  28.5 0.0 copy-start.1
  28.5 1.6 %copy-done.1 = f32[8,128,512]{2,1,0:T(8,128)S(1)} copy-done((f32[8,128,512]{2,1,0:T(8,128)S(1)}, f32[8,128,512]{2,1,0:T(8,128)}, u32[]{:S(2)}) %copy-start.1) | copy-done | bytes 2097176
  30.1 1.5 %bin.1 = (f32[8,128,512]{2,1,0:T(8,128)S(1)}, f32[8,128,128]{2,1,0:T(8,128)S(1)}, f32[128,512]{1,0:T(8,128)S(1)}, f32[128,512]{1,0:T(8,128)S(1)}, f32[8,512]{1,0:T(8,128)S(1)}, /*index=5*/f32[8,512]{1,0:T(8,128)S(1)}) custom-call(bf16[512,640]{1,0:T(8,128)(2,1)S(1)} %bitcast.5, f32[8,128,512]{2,1,0:T(8,128)S(1)} %copy-done, f32[8,128,512]{2,1,0:T(8,128)S(1)} %copy-done.1), custom_call_target="tpu_custom_call" | custom-call | tf_op jit(solution)/shard_map/bin/pallas_call | solution.py:324
  31.6 0.0 copy-start.11
  31.6 1.3 %collective-permute-start = (f32[128,512]{1,0:T(8,128)S(1)}, f32[128,512]{1,0:T(8,128)S(1)}, u32[]{:S(2)}, u32[]{:S(2)}) collective-permute-start(f32[128,512]{1,0:T(8,128)S(1)} %get-tuple-element.28), channel_id=1, source_target_pairs={{4,0},{8,4},{12,8},{16,12},{20,16},{24,20},{28,24},{5,1},{9,5},{13... | collective-permute-start | bytes 786440 | tf_op jit(solution)/shard_map/ppermute | solution.py:23
  32.9 3.9 %collective-permute-start.2 = (f32[128,512]{1,0:T(8,128)S(1)}, f32[128,512]{1,0:T(8,128)S(1)}, u32[]{:S(2)}, u32[]{:S(2)}) collective-permute-start(f32[128,512]{1,0:T(8,128)S(1)} %get-tuple-element.27.refs_1_), channel_id=1, source_target_pairs={{0,4},{4,8},{8,12},{12,16},{16,20},{20,24},{24,28},{1,5},{5,9},{9,... | collective-permute-start | bytes 786440 | tf_op jit(solution)/shard_map/ppermute | solution.py:23
  36.9 1.3 %collective-permute-start.1 = (f32[8,512]{1,0:T(8,128)S(1)}, f32[8,512]{1,0:T(8,128)S(1)}, u32[]{:S(2)}, u32[]{:S(2)}) collective-permute-start(f32[8,512]{1,0:T(8,128)S(1)} %get-tuple-element.30), channel_id=1, source_target_pairs={{1,0},{2,1},{3,2},{5,4},{6,5},{7,6},{9,8},{10,9},{11,10},{13,12},{... | collective-permute-start | bytes 49160 | tf_op jit(solution)/shard_map/ppermute | solution.py:23
  38.2 4.5 %collective-permute-start.3 = (f32[8,512]{1,0:T(8,128)S(1)}, f32[8,512]{1,0:T(8,128)S(1)}, u32[]{:S(2)}, u32[]{:S(2)}) collective-permute-start(f32[8,512]{1,0:T(8,128)S(1)} %get-tuple-element.29.refs_3_), channel_id=1, source_target_pairs={{0,1},{1,2},{2,3},{4,5},{5,6},{6,7},{8,9},{9,10},{10,11},{12,13},{... | collective-permute-start | bytes 49160 | tf_op jit(solution)/shard_map/ppermute | solution.py:23
  42.7 7.0 %apply.3 = (f32[8,128,512]{2,1,0:T(8,128)S(1)}, f32[2,8,128]{2,1,0:T(8,128)S(1)}) custom-call(f32[8,128,512]{2,1,0:T(8,128)S(1)} %get-tuple-element.24.v_ref.b_ref, f32[8,128,512]{2,1,0:T(8,128)S(1)} %copy-done, f32[8,128,512]{2,1,0:T(8,128)S(1)} %copy-done.1, f32[8,128,128]{2,1,0:T(8,128)S(1)} %get-tuple-element.25.diag_ref), custom_call_target="tpu_custom_call" | custom-call | flops 31457280 | bytes 8388608 | tf_op jit(solution)/shard_map/apply/pallas_call | solution.py:324
  49.7 0.0 copy-done.11
  49.8 0.0 collective-permute-done.1.right_ref.refs_4_
  49.8 0.0 collective-permute-done.3.left_ref
  49.8 0.0 collective-permute-done.below_ref.refs_2_
  49.8 0.0 collective-permute-done.2.above_ref
  49.8 0.5 correct.3
  50.3 0.0 copy-start.3
  50.3 1.3 %collective-permute-start.4 = (f32[128,512]{1,0:T(8,128)S(1)}, f32[128,512]{1,0:T(8,128)S(1)}, u32[]{:S(2)}, u32[]{:S(2)}) collective-permute-start(f32[128,512]{1,0:T(8,128)S(1)} %get-tuple-element.35), channel_id=1, source_target_pairs={{4,0},{8,4},{12,8},{16,12},{20,16},{24,20},{28,24},{5,1},{9,5},{13... | collective-permute-start | bytes 786440 | tf_op jit(solution)/shard_map/ppermute | solution.py:23
  51.6 3.7 %collective-permute-start.6 = (f32[128,512]{1,0:T(8,128)S(1)}, f32[128,512]{1,0:T(8,128)S(1)}, u32[]{:S(2)}, u32[]{:S(2)}) collective-permute-start(f32[128,512]{1,0:T(8,128)S(1)} %get-tuple-element.34.refs_6_), channel_id=1, source_target_pairs={{0,4},{4,8},{8,12},{12,16},{16,20},{20,24},{24,28},{1,5},{5,9},{9,... | collective-permute-start | bytes 786440 | tf_op jit(solution)/shard_map/ppermute | solution.py:23
  55.4 1.3 %collective-permute-start.5 = (f32[8,512]{1,0:T(8,128)S(1)}, f32[8,512]{1,0:T(8,128)S(1)}, u32[]{:S(2)}, u32[]{:S(2)}) collective-permute-start(f32[8,512]{1,0:T(8,128)S(1)} %get-tuple-element.37), channel_id=1, source_target_pairs={{1,0},{2,1},{3,2},{5,4},{6,5},{7,6},{9,8},{10,9},{11,10},{13,12},{... | collective-permute-start | bytes 49160 | tf_op jit(solution)/shard_map/ppermute | solution.py:23
  56.7 4.5 %collective-permute-start.7 = (f32[8,512]{1,0:T(8,128)S(1)}, f32[8,512]{1,0:T(8,128)S(1)}, u32[]{:S(2)}, u32[]{:S(2)}) collective-permute-start(f32[8,512]{1,0:T(8,128)S(1)} %get-tuple-element.36.refs_8_), channel_id=1, source_target_pairs={{0,1},{1,2},{2,3},{4,5},{5,6},{6,7},{8,9},{9,10},{10,11},{12,13},{... | collective-permute-start | bytes 49160 | tf_op jit(solution)/shard_map/ppermute | solution.py:23
  61.2 7.1 %apply.4 = (f32[8,128,512]{2,1,0:T(8,128)S(1)}, f32[2,8,128]{2,1,0:T(8,128)S(1)}) custom-call(f32[8,128,512]{2,1,0:T(8,128)S(1)} %get-tuple-element.32.v_ref.v1_ref, f32[8,128,512]{2,1,0:T(8,128)S(1)} %copy-done, f32[8,128,512]{2,1,0:T(8,128)S(1)} %copy-done.1, f32[8,128,128]{2,1,0:T(8,128)S(1)} %get-tuple-element.25.diag_ref), custom_call_target="tpu_custom_call" | custom-call | flops 31457280 | bytes 8388608 | tf_op jit(solution)/shard_map/apply/pallas_call | solution.py:324
  68.3 0.0 copy-done.3
  68.3 0.0 collective-permute-done.5.right_ref.refs_9_
  68.3 0.0 collective-permute-done.7.left_ref
  68.3 0.0 collective-permute-done.4.below_ref.refs_7_
  68.3 0.0 collective-permute-done.6.above_ref
  68.4 0.5 correct.4
  68.9 0.0 copy-start.5
  68.9 1.3 %collective-permute-start.8 = (f32[128,512]{1,0:T(8,128)S(1)}, f32[128,512]{1,0:T(8,128)S(1)}, u32[]{:S(2)}, u32[]{:S(2)}) collective-permute-start(f32[128,512]{1,0:T(8,128)S(1)} %get-tuple-element.42), channel_id=1, source_target_pairs={{4,0},{8,4},{12,8},{16,12},{20,16},{24,20},{28,24},{5,1},{9,5},{13... | collective-permute-start | bytes 786440 | tf_op jit(solution)/shard_map/ppermute | solution.py:23
  70.2 3.7 %collective-permute-start.10 = (f32[128,512]{1,0:T(8,128)S(1)}, f32[128,512]{1,0:T(8,128)S(1)}, u32[]{:S(2)}, u32[]{:S(2)}) collective-permute-start(f32[128,512]{1,0:T(8,128)S(1)} %get-tuple-element.41.refs_11_), channel_id=1, source_target_pairs={{0,4},{4,8},{8,12},{12,16},{16,20},{20,24},{24,28},{1,5},{5,9},{9,... | collective-permute-start | bytes 786440 | tf_op jit(solution)/shard_map/ppermute | solution.py:23
  73.9 1.3 %collective-permute-start.9 = (f32[8,512]{1,0:T(8,128)S(1)}, f32[8,512]{1,0:T(8,128)S(1)}, u32[]{:S(2)}, u32[]{:S(2)}) collective-permute-start(f32[8,512]{1,0:T(8,128)S(1)} %get-tuple-element.44), channel_id=1, source_target_pairs={{1,0},{2,1},{3,2},{5,4},{6,5},{7,6},{9,8},{10,9},{11,10},{13,12},{... | collective-permute-start | bytes 49160 | tf_op jit(solution)/shard_map/ppermute | solution.py:23
  75.2 7.1 %apply.5 = (f32[8,128,512]{2,1,0:T(8,128)S(1)}, f32[2,8,128]{2,1,0:T(8,128)S(1)}) custom-call(f32[8,128,512]{2,1,0:T(8,128)S(1)} %get-tuple-element.39.v_ref.v2_ref, f32[8,128,512]{2,1,0:T(8,128)S(1)} %copy-done, f32[8,128,512]{2,1,0:T(8,128)S(1)} %copy-done.1, f32[8,128,128]{2,1,0:T(8,128)S(1)} %get-tuple-element.25.diag_ref), custom_call_target="tpu_custom_call" | custom-call | flops 31457280 | bytes 8388608 | tf_op jit(solution)/shard_map/apply/pallas_call | solution.py:324
  82.3 0.0 copy-done.5
  82.3 0.0 copy-start.7
  82.3 1.3 %copy-done.7 = f32[8,128,512]{2,1,0:T(8,128)} copy-done((f32[8,128,512]{2,1,0:T(8,128)}, f32[8,128,512]{2,1,0:T(8,128)S(1)}, u32[]{:S(2)}) %copy-start.7) | copy-done | bytes 2097176
  83.7 0.0 collective-permute-done.9.refs_14_.right_ref
  83.7 0.0 collective-permute-done.8.refs_12_.below_ref
  83.7 0.8 moments.1
  84.5 7.9 %all-to-all-start.1 = ((f32[32,1,128]{2,1,0:T(1,128)}), f32[32,1,128]{2,1,0:T(1,128)S(1)}, u32[]{:S(2)}, u32[]{:S(2)}) async-start(f32[32,1,128]{2,1,0:T(1,128)} %moments.1), calls=%async_computation.1 | async-start | bytes 32768 | tf_op jit(solution)/shard_map/all_to_all | solution.py:392
  92.3 3.7 %collective-permute-start.11 = (f32[8,512]{1,0:T(8,128)S(1)}, f32[8,512]{1,0:T(8,128)S(1)}, u32[]{:S(2)}, u32[]{:S(2)}) collective-permute-start(f32[8,512]{1,0:T(8,128)S(1)} %get-tuple-element.43.refs_13_), channel_id=1, source_target_pairs={{0,1},{1,2},{2,3},{4,5},{5,6},{6,7},{8,9},{9,10},{10,11},{12,13},{... | collective-permute-start | bytes 49160 | tf_op jit(solution)/shard_map/ppermute | solution.py:23
  96.0 1.4 %collective-permute-done.11.left_ref = f32[8,512]{1,0:T(8,128)S(1)} collective-permute-done((f32[8,512]{1,0:T(8,128)S(1)}, f32[8,512]{1,0:T(8,128)S(1)}, u32[]{:S(2)}, u32[]{:S(2)}) %collective-permute-start.11) | collective-permute-done | bytes 16416 | tf_op jit(solution)/shard_map/ppermute | solution.py:23
  97.4 0.0 collective-permute-done.10.above_ref
  97.4 1.6 %copy-done.2 = f32[8,128,512]{2,1,0:T(8,128)S(1)} copy-done((f32[8,128,512]{2,1,0:T(8,128)S(1)}, f32[8,128,512]{2,1,0:T(8,128)}, u32[]{:S(2)}) %copy-start.2) | copy-done | bytes 2097176
  99.0 1.6 %copy-done.8 = f32[8,128,512]{2,1,0:T(8,128)S(1)} copy-done((f32[8,128,512]{2,1,0:T(8,128)S(1)}, f32[8,128,512]{2,1,0:T(8,128)}, u32[]{:S(2)}) %copy-start.8) | copy-done | bytes 2097176
  100.6 0.3 correct.5.v3_ref
  100.9 0.0 copy-start.9
  100.9 1.3 %copy-done.9 = f32[8,128,512]{2,1,0:T(8,128)} copy-done((f32[8,128,512]{2,1,0:T(8,128)}, f32[8,128,512]{2,1,0:T(8,128)S(1)}, u32[]{:S(2)}) %copy-start.9) | copy-done | bytes 2097176
  102.2 0.0 all-to-all-done.1.parts_ref
  102.2 1.6 %copy-done.4 = f32[8,128,512]{2,1,0:T(8,128)S(1)} copy-done((f32[8,128,512]{2,1,0:T(8,128)S(1)}, f32[8,128,512]{2,1,0:T(8,128)}, u32[]{:S(2)}) %copy-start.4) | copy-done | bytes 2097176
  103.8 1.6 %copy-done.6 = f32[8,128,512]{2,1,0:T(8,128)S(1)} copy-done((f32[8,128,512]{2,1,0:T(8,128)S(1)}, f32[8,128,512]{2,1,0:T(8,128)}, u32[]{:S(2)}) %copy-start.6) | copy-done | bytes 2097176
  105.4 1.6 %copy-done.10 = f32[8,128,512]{2,1,0:T(8,128)S(1)} copy-done((f32[8,128,512]{2,1,0:T(8,128)S(1)}, f32[8,128,512]{2,1,0:T(8,128)}, u32[]{:S(2)}) %copy-start.10) | copy-done | bytes 2097176
  107.0 1.6 %copy-done.12 = f32[8,128,512]{2,1,0:T(8,128)S(1)} copy-done((f32[8,128,512]{2,1,0:T(8,128)S(1)}, f32[8,128,512]{2,1,0:T(8,128)}, u32[]{:S(2)}) %copy-start.12) | copy-done | bytes 2097176
  108.6 3.9 %finish.1 = (f32[8,128,512]{2,1,0:T(8,128)}, f32[8,128,512]{2,1,0:T(8,128)}) custom-call(f32[32,1,128]{2,1,0:T(1,128)S(1)} %all-to-all-done.1.parts_ref, f32[8,128,512]{2,1,0:T(8,128)S(1)} %copy-done.12, f32[8,128,512]{2,1,0:T(8,128)S(1)} %copy-done.4, f32[8,128,512]{2,1,0:T(8,128)S(1)} %copy-done.6, f32[8,128,512]{2,1,0:T(8,128)S(1)} %copy-done.10), custom_call_target="tpu_custom_call" | custom-call | tf_op jit(solution)/shard_map/finish/pallas_call | solution.py:396
  (7 shorter events, 0.0 us)
Async XLA Ops:
  0.6 27.9 %copy-start = (f32[8,128,512]{2,1,0:T(8,128)S(1)}, f32[8,128,512]{2,1,0:T(8,128)}, u32[]{:S(2)}) copy-start(f32[8,128,512]{2,1,0:T(8,128)} %p1_ref.11) | copy-start | bytes 6291460
  0.6 1.1 copy-start.13
  1.7 0.7 copy-start.14
  2.4 0.7 copy-start.15
  3.1 0.7 copy-start.16
  28.5 1.6 %copy-start.1 = (f32[8,128,512]{2,1,0:T(8,128)S(1)}, f32[8,128,512]{2,1,0:T(8,128)}, u32[]{:S(2)}) copy-start(f32[8,128,512]{2,1,0:T(8,128)} %p2_ref.11) | copy-start | bytes 6291460
  31.6 18.2 %copy-start.11 = (f32[8,128,512]{2,1,0:T(8,128)}, f32[8,128,512]{2,1,0:T(8,128)S(1)}, u32[]{:S(2)}) copy-start(f32[8,128,512]{2,1,0:T(8,128)S(1)} %get-tuple-element.24.v_ref.b_ref) | copy-start | bytes 6291460
  31.6 18.2 %collective-permute-start = (f32[128,512]{1,0:T(8,128)S(1)}, f32[128,512]{1,0:T(8,128)S(1)}, u32[]{:S(2)}, u32[]{:S(2)}) collective-permute-start(f32[128,512]{1,0:T(8,128)S(1)} %get-tuple-element.28), channel_id=1, source_target_pairs={{4,0},{8,4},{12,8},{16,12},{20,16},{24,20},{28,24},{5,1},{9,5},{13... | collective-permute-start | bytes 786440 | tf_op jit(solution)/shard_map/ppermute | solution.py:23
  32.9 16.9 %collective-permute-start.2 = (f32[128,512]{1,0:T(8,128)S(1)}, f32[128,512]{1,0:T(8,128)S(1)}, u32[]{:S(2)}, u32[]{:S(2)}) collective-permute-start(f32[128,512]{1,0:T(8,128)S(1)} %get-tuple-element.27.refs_1_), channel_id=1, source_target_pairs={{0,4},{4,8},{8,12},{12,16},{16,20},{20,24},{24,28},{1,5},{5,9},{9,... | collective-permute-start | bytes 786440 | tf_op jit(solution)/shard_map/ppermute | solution.py:23
  36.9 12.9 %collective-permute-start.1 = (f32[8,512]{1,0:T(8,128)S(1)}, f32[8,512]{1,0:T(8,128)S(1)}, u32[]{:S(2)}, u32[]{:S(2)}) collective-permute-start(f32[8,512]{1,0:T(8,128)S(1)} %get-tuple-element.30), channel_id=1, source_target_pairs={{1,0},{2,1},{3,2},{5,4},{6,5},{7,6},{9,8},{10,9},{11,10},{13,12},{... | collective-permute-start | bytes 49160 | tf_op jit(solution)/shard_map/ppermute | solution.py:23
  38.2 11.6 %collective-permute-start.3 = (f32[8,512]{1,0:T(8,128)S(1)}, f32[8,512]{1,0:T(8,128)S(1)}, u32[]{:S(2)}, u32[]{:S(2)}) collective-permute-start(f32[8,512]{1,0:T(8,128)S(1)} %get-tuple-element.29.refs_3_), channel_id=1, source_target_pairs={{0,1},{1,2},{2,3},{4,5},{5,6},{6,7},{8,9},{9,10},{10,11},{12,13},{... | collective-permute-start | bytes 49160 | tf_op jit(solution)/shard_map/ppermute | solution.py:23
  50.3 18.0 %copy-start.3 = (f32[8,128,512]{2,1,0:T(8,128)}, f32[8,128,512]{2,1,0:T(8,128)S(1)}, u32[]{:S(2)}) copy-start(f32[8,128,512]{2,1,0:T(8,128)S(1)} %get-tuple-element.32.v_ref.v1_ref) | copy-start | bytes 6291460
  50.3 18.0 %collective-permute-start.4 = (f32[128,512]{1,0:T(8,128)S(1)}, f32[128,512]{1,0:T(8,128)S(1)}, u32[]{:S(2)}, u32[]{:S(2)}) collective-permute-start(f32[128,512]{1,0:T(8,128)S(1)} %get-tuple-element.35), channel_id=1, source_target_pairs={{4,0},{8,4},{12,8},{16,12},{20,16},{24,20},{28,24},{5,1},{9,5},{13... | collective-permute-start | bytes 786440 | tf_op jit(solution)/shard_map/ppermute | solution.py:23
  51.6 16.7 %collective-permute-start.6 = (f32[128,512]{1,0:T(8,128)S(1)}, f32[128,512]{1,0:T(8,128)S(1)}, u32[]{:S(2)}, u32[]{:S(2)}) collective-permute-start(f32[128,512]{1,0:T(8,128)S(1)} %get-tuple-element.34.refs_6_), channel_id=1, source_target_pairs={{0,4},{4,8},{8,12},{12,16},{16,20},{20,24},{24,28},{1,5},{5,9},{9,... | collective-permute-start | bytes 786440 | tf_op jit(solution)/shard_map/ppermute | solution.py:23
  55.4 13.0 %collective-permute-start.5 = (f32[8,512]{1,0:T(8,128)S(1)}, f32[8,512]{1,0:T(8,128)S(1)}, u32[]{:S(2)}, u32[]{:S(2)}) collective-permute-start(f32[8,512]{1,0:T(8,128)S(1)} %get-tuple-element.37), channel_id=1, source_target_pairs={{1,0},{2,1},{3,2},{5,4},{6,5},{7,6},{9,8},{10,9},{11,10},{13,12},{... | collective-permute-start | bytes 49160 | tf_op jit(solution)/shard_map/ppermute | solution.py:23
  56.7 11.7 %collective-permute-start.7 = (f32[8,512]{1,0:T(8,128)S(1)}, f32[8,512]{1,0:T(8,128)S(1)}, u32[]{:S(2)}, u32[]{:S(2)}) collective-permute-start(f32[8,512]{1,0:T(8,128)S(1)} %get-tuple-element.36.refs_8_), channel_id=1, source_target_pairs={{0,1},{1,2},{2,3},{4,5},{5,6},{6,7},{8,9},{9,10},{10,11},{12,13},{... | collective-permute-start | bytes 49160 | tf_op jit(solution)/shard_map/ppermute | solution.py:23
  68.9 13.4 %copy-start.5 = (f32[8,128,512]{2,1,0:T(8,128)}, f32[8,128,512]{2,1,0:T(8,128)S(1)}, u32[]{:S(2)}) copy-start(f32[8,128,512]{2,1,0:T(8,128)S(1)} %get-tuple-element.39.v_ref.v2_ref) | copy-start | bytes 6291460
  68.9 14.7 %collective-permute-start.8 = (f32[128,512]{1,0:T(8,128)S(1)}, f32[128,512]{1,0:T(8,128)S(1)}, u32[]{:S(2)}, u32[]{:S(2)}) collective-permute-start(f32[128,512]{1,0:T(8,128)S(1)} %get-tuple-element.42), channel_id=1, source_target_pairs={{4,0},{8,4},{12,8},{16,12},{20,16},{24,20},{28,24},{5,1},{9,5},{13... | collective-permute-start | bytes 786440 | tf_op jit(solution)/shard_map/ppermute | solution.py:23
  70.2 27.2 %collective-permute-start.10 = (f32[128,512]{1,0:T(8,128)S(1)}, f32[128,512]{1,0:T(8,128)S(1)}, u32[]{:S(2)}, u32[]{:S(2)}) collective-permute-start(f32[128,512]{1,0:T(8,128)S(1)} %get-tuple-element.41.refs_11_), channel_id=1, source_target_pairs={{0,4},{4,8},{8,12},{12,16},{16,20},{20,24},{24,28},{1,5},{5,9},{9,... | collective-permute-start | bytes 786440 | tf_op jit(solution)/shard_map/ppermute | solution.py:23
  73.9 9.7 %collective-permute-start.9 = (f32[8,512]{1,0:T(8,128)S(1)}, f32[8,512]{1,0:T(8,128)S(1)}, u32[]{:S(2)}, u32[]{:S(2)}) collective-permute-start(f32[8,512]{1,0:T(8,128)S(1)} %get-tuple-element.44), channel_id=1, source_target_pairs={{1,0},{2,1},{3,2},{5,4},{6,5},{7,6},{9,8},{10,9},{11,10},{13,12},{... | collective-permute-start | bytes 49160 | tf_op jit(solution)/shard_map/ppermute | solution.py:23
  82.3 1.3 %copy-start.7 = (f32[8,128,512]{2,1,0:T(8,128)}, f32[8,128,512]{2,1,0:T(8,128)S(1)}, u32[]{:S(2)}) copy-start(f32[8,128,512]{2,1,0:T(8,128)S(1)} %get-tuple-element.45.image_ref) | copy-start | bytes 6291460
  84.5 17.8 %all-to-all-start.1 = ((f32[32,1,128]{2,1,0:T(1,128)}), f32[32,1,128]{2,1,0:T(1,128)S(1)}, u32[]{:S(2)}, u32[]{:S(2)}) async-start(f32[32,1,128]{2,1,0:T(1,128)} %moments.1), calls=%async_computation.1 | async-start | bytes 32768 | tf_op jit(solution)/shard_map/all_to_all | solution.py:392
  92.3 5.1 %collective-permute-start.11 = (f32[8,512]{1,0:T(8,128)S(1)}, f32[8,512]{1,0:T(8,128)S(1)}, u32[]{:S(2)}, u32[]{:S(2)}) collective-permute-start(f32[8,512]{1,0:T(8,128)S(1)} %get-tuple-element.43.refs_13_), channel_id=1, source_target_pairs={{0,1},{1,2},{2,3},{4,5},{5,6},{6,7},{8,9},{9,10},{10,11},{12,13},{... | collective-permute-start | bytes 49160 | tf_op jit(solution)/shard_map/ppermute | solution.py:23
  97.4 1.6 %copy-start.2 = (f32[8,128,512]{2,1,0:T(8,128)S(1)}, f32[8,128,512]{2,1,0:T(8,128)}, u32[]{:S(2)}) copy-start(f32[8,128,512]{2,1,0:T(8,128)} %p2_ref.11) | copy-start | bytes 6291460
  99.0 1.6 %copy-start.8 = (f32[8,128,512]{2,1,0:T(8,128)S(1)}, f32[8,128,512]{2,1,0:T(8,128)}, u32[]{:S(2)}) copy-start(f32[8,128,512]{2,1,0:T(8,128)} %copy-done.7) | copy-start | bytes 6291460
  100.9 1.3 %copy-start.9 = (f32[8,128,512]{2,1,0:T(8,128)}, f32[8,128,512]{2,1,0:T(8,128)S(1)}, u32[]{:S(2)}) copy-start(f32[8,128,512]{2,1,0:T(8,128)S(1)} %correct.5.v3_ref) | copy-start | bytes 6291460
  102.2 1.6 %copy-start.4 = (f32[8,128,512]{2,1,0:T(8,128)S(1)}, f32[8,128,512]{2,1,0:T(8,128)}, u32[]{:S(2)}) copy-start(f32[8,128,512]{2,1,0:T(8,128)} %copy-done.3) | copy-start | bytes 6291460
  103.8 1.6 %copy-start.6 = (f32[8,128,512]{2,1,0:T(8,128)S(1)}, f32[8,128,512]{2,1,0:T(8,128)}, u32[]{:S(2)}) copy-start(f32[8,128,512]{2,1,0:T(8,128)} %copy-done.5) | copy-start | bytes 6291460
  105.4 1.6 %copy-start.10 = (f32[8,128,512]{2,1,0:T(8,128)S(1)}, f32[8,128,512]{2,1,0:T(8,128)}, u32[]{:S(2)}) copy-start(f32[8,128,512]{2,1,0:T(8,128)} %copy-done.9) | copy-start | bytes 6291460
  107.0 1.6 %copy-start.12 = (f32[8,128,512]{2,1,0:T(8,128)S(1)}, f32[8,128,512]{2,1,0:T(8,128)}, u32[]{:S(2)}) copy-start(f32[8,128,512]{2,1,0:T(8,128)} %copy-done.11) | copy-start | bytes 6291460

commit v3 on v2

--- a/solution.py
+++ b/solution.py
@@ -72,6 +72,15 @@
 def store(ref, tiles, *index):
     for c, tile in enumerate(tiles):
         ref[(*index, slice(c * LANES, (c + 1) * LANES))] = tile
+
+
+def load_field(ref, i, at):
+    return [ref[i, c, at, :] for c in range(ref.shape[1])]
+
+
+def store_field(ref, tiles, i, at):
+    for c, tile in enumerate(tiles):
+        ref[i, c, at, :] = tile
 
 
 def add(x, y):
@@ -115,7 +124,8 @@
 
 
 def bin_kernel(got_ref, p1_hbm, p2_hbm, b_ref, diag_ref, row0_ref, row7_ref, col0_ref, col7_ref, p1_ref, p2_ref, sems):
-    rows, cols, samples = b_ref.shape
+    rows, tiles, cols, _ = b_ref.shape
+    samples = tiles * LANES
     slots = got_ref.shape[0]
     copies = (
         pltpu.make_async_copy(p1_hbm.at[rows - 1], p1_ref, sems.at[0]),
@@ -136,7 +146,9 @@
     got = got_ref[:, :samples]
     for i in range(rows):
         place = (iota((cols, slots), 0) + i * cols == bin_of).astype(jnp.float32).astype(jnp.bfloat16)
-        b_ref[i] = jnp.dot(place, got, preferred_element_type=jnp.float32)
+        total = jnp.dot(place, got, preferred_element_type=jnp.float32)
+        for c in range(tiles):
+            b_ref[i, c] = total[:, c * LANES : (c + 1) * LANES]
         hits = jnp.dot(place, ones, preferred_element_type=jnp.float32)
         diag = 2.0 * hits + first_col
         diag_ref[i] = diag + not_first_row if i == 0 else diag
@@ -149,56 +161,54 @@
 
 
 def write_edges(v_ref, p1_last_row, p2_last_cols, row0_ref, row7_ref, col0_ref, col7_ref):
-    rows, cols, _ = v_ref.shape
+    rows, _, cols, _ = v_ref.shape
     for x in range(0, cols, SUBLANES):
         at = slice(x, x + SUBLANES)
-        store(row0_ref, load(v_ref, 0, at), at)
-        v = load(v_ref, rows - 1, at)
+        store(row0_ref, load_field(v_ref, 0, at), at)
+        v = load_field(v_ref, rows - 1, at)
         store(row7_ref, add(v, dip_part(p1_last_row(at), *stencil(v))), at)
     for i in range(rows):
-        store(col0_ref, load(v_ref, i, slice(0, 1)), slice(i, i + 1))
-        v = load(v_ref, i, slice(cols - SUBLANES, cols))
+        store(col0_ref, load_field(v_ref, i, slice(0, 1)), slice(i, i + 1))
+        v = load_field(v_ref, i, slice(cols - SUBLANES, cols))
         moved = add(v, dip_part(p2_last_cols(i), *stencil(v)))
         store(col7_ref, [t[SUBLANES - 1 :] for t in moved], slice(i, i + 1))
 
 
-def apply_kernel(v_ref, p1_ref, p2_ref, diag_ref, out_ref, sums_ref, first_ref):
-    rows, cols, samples = v_ref.shape
-    tiles = samples // LANES
+def apply_kernel(v_ref, p1_ref, p2_ref, diag_ref, out_ref, sums_ref, first_ref, second_ref):
+    rows, tiles, cols, _ = v_ref.shape
     sub_index = iota((SUBLANES, LANES), 0)
     zero = [jnp.zeros((SUBLANES, LANES), jnp.float32)] * tiles
     first_ref[...] = jnp.zeros_like(first_ref)
+    for c in range(tiles):
+        second_ref[c, :SUBLANES, :] = zero[0]
 
     def row(i, sums, last):
-        def fetch(x):
-            at = slice(x, x + SUBLANES)
-            v = load(v_ref, i, at)
-            below = zero if last else load(v_ref, i + 1, at)
-            lead = [pltpu.roll(t, SUBLANES - 1, 0) for t in v]
-            return v, lead, below, load(p1_ref, i, at), load(p2_ref, i, at), load(first_ref, at), diag_ref[i, at, :]
-
         vout, vv = zero[0], zero[0]
-        left_from = zero
-        ahead = fetch(0)
         for x in range(0, cols, SUBLANES):
             at = slice(x, x + SUBLANES)
-            v, lead, below, p1, p2, above, diag = ahead
-            ahead = fetch(x + SUBLANES) if x + SUBLANES < cols else (zero, zero)
-            right = [jnp.where(sub_index == SUBLANES - 1, b, a) for a, b in zip(lead, ahead[1])]
+            v = load_field(v_ref, i, at)
+            if x + SUBLANES < cols:
+                right = load_field(v_ref, i, slice(x + 1, x + 1 + SUBLANES))
+            else:
+                right = [jnp.where(sub_index == SUBLANES - 1, 0.0, pltpu.roll(t, SUBLANES - 1, 0)) for t in v]
+            below = zero if last else load_field(v_ref, i + 1, at)
+            p1, p2 = load(p1_ref, i, at), load(p2_ref, i, at)
             odd, even = stencil(v)
             first = sub(sub(below, v), dip_part(p1, odd, even))
             second = sub(sub(right, v), dip_part(p2, odd, even))
+            for c in range(tiles):
+                second_ref[c, x + SUBLANES : x + 2 * SUBLANES, :] = second[c]
             a1, b1 = adjoint_terms(p1, first)
             a2, b2 = adjoint_terms(p2, second)
             moved = adjoint_finish(add(first, second), add(a1, a2), add(b1, b2))
-            down = [pltpu.roll(t, 1, 0) for t in second]
-            left = [jnp.where(sub_index == 0, b, a) for a, b in zip(down, left_from)]
-            left_from = down
+            left = [second_ref[c, x + SUBLANES - 1 : x + 2 * SUBLANES - 1, :] for c in range(tiles)]
+            above = load(first_ref, at)
+            store(first_ref, first, at)
+            diag = diag_ref[i, at, :]
             out = [diag * c + ((f + s) - m) for c, f, s, m in zip(v, above, left, moved)]
+            store_field(out_ref, out, i, at)
             vout = vout + dot(v, out)
             vv = vv + dot(v, v)
-            store(first_ref, first, at)
-            store(out_ref, out, i, at)
         return sums[0] + vout, sums[1] + vv
 
     sums = lax.fori_loop(0, rows - 1, lambda i, sums: row(i, sums, False), (zero[0], zero[0]))
@@ -206,40 +216,40 @@
 
 
 def halo_corrections(out_ref, p1_ref, p2_ref, below_ref, above_ref, right_ref, left_ref):
-    rows, cols, _ = out_ref.shape
+    rows, _, cols, _ = out_ref.shape
     last = rows - 1
     sub_index = iota((SUBLANES, LANES), 0)
     for x in range(0, cols, SUBLANES):
         at = slice(x, x + SUBLANES)
-        store(out_ref, sub(load(out_ref, 0, at), load(above_ref, at)), 0, at)
+        store_field(out_ref, sub(load_field(out_ref, 0, at), load(above_ref, at)), 0, at)
         r = load(below_ref, at)
         moved = adjoint_finish(r, *adjoint_terms(load(p1_ref, last, at), r))
-        store(out_ref, sub(load(out_ref, last, at), moved), last, at)
+        store_field(out_ref, sub(load_field(out_ref, last, at), moved), last, at)
     for i in range(rows):
         at = slice(0, SUBLANES)
         r = [jnp.where(sub_index == 0, t, 0.0) for t in load(left_ref, slice(i, i + 1))]
-        store(out_ref, sub(load(out_ref, i, at), r), i, at)
+        store_field(out_ref, sub(load_field(out_ref, i, at), r), i, at)
         at = slice(cols - SUBLANES, cols)
         r = [jnp.where(sub_index == SUBLANES - 1, t, 0.0) for t in load(right_ref, slice(i, i + 1))]
         moved = adjoint_finish(r, *adjoint_terms(load(p2_ref, i, at), r))
-        store(out_ref, sub(load(out_ref, i, at), moved), i, at)
+        store_field(out_ref, sub(load_field(out_ref, i, at), moved), i, at)
 
 
 def correct_kernel(
     image_ref, p1_ref, p2_ref, below_ref, above_ref, right_ref, left_ref, out_ref, *edge_refs
 ):
     halo_corrections(out_ref, p1_ref, p2_ref, below_ref, above_ref, right_ref, left_ref)
-    if edge_refs:
-        rows, cols, _ = out_ref.shape
-        write_edges(
-            out_ref,
-            lambda at: load(p1_ref, rows - 1, at),
-            lambda i: load(p2_ref, i, slice(cols - SUBLANES, cols)),
-            *edge_refs,
-        )
-
-
-def moments_kernel(*refs):
+    rows, _, cols, _ = out_ref.shape
+    write_edges(
+        out_ref,
+        lambda at: load(p1_ref, rows - 1, at),
+        lambda i: load(p2_ref, i, slice(cols - SUBLANES, cols)),
+        *edge_refs,
+    )
+
+
+def moments_kernel(image_ref, p1_ref, p2_ref, below_ref, above_ref, right_ref, left_ref, *refs):
+    halo_corrections(refs[-2], p1_ref, p2_ref, below_ref, above_ref, right_ref, left_ref)
     out_ref = refs[-1]
     m = []
     for step in range(ITERS):
@@ -289,49 +299,62 @@
     return [2.0 * s for s in model] + residual
 
 
-def finish_kernel(parts_ref, b_ref, v1_ref, v2_ref, v3_ref, model_ref, residual_ref, weight_ref):
-    cols = b_ref.shape[1]
-    i = pl.program_id(0)
-
-    @pl.when(i == 0)
-    def _():
-        line = jnp.sum(parts_ref[...], axis=0)
-        sub_index, lane = iota((SUBLANES, LANES), 0), iota((SUBLANES, LANES), 1)
-        total = jnp.sum(jnp.where(sub_index == lane, line, 0.0), axis=1, keepdims=True)
-        total = jnp.broadcast_to(total, (SUBLANES, LANES))
-        m = [jnp.broadcast_to(total[k : k + 1], (SUBLANES, LANES)) for k in range(2 * ITERS)]
-        for k, weight in enumerate(coefficients(m)):
-            weight_ref[k] = weight
-
-    weights = [weight_ref[k] for k in range(2 * ITERS + 1)]
+def finish_kernel(parts_ref, b_ref, v1_ref, v2_ref, v3_ref, model_hbm, residual_hbm, model_ref, residual_ref, sems):
+    rows, _, cols, _ = b_ref.shape
+    line = jnp.sum(parts_ref[...], axis=0)
+    sub_index, lane = iota((SUBLANES, LANES), 0), iota((SUBLANES, LANES), 1)
+    total = jnp.sum(jnp.where(sub_index == lane, line, 0.0), axis=1, keepdims=True)
+    total = jnp.broadcast_to(total, (SUBLANES, LANES))
+    m = [jnp.broadcast_to(total[k : k + 1], (SUBLANES, LANES)) for k in range(2 * ITERS)]
+    weights = coefficients(m)
     model, residual = weights[:ITERS], weights[ITERS:]
-    for x in range(0, cols, SUBLANES):
-        at = slice(x, x + SUBLANES)
-        b, v1, v2, v3 = (load(ref, i, at) for ref in (b_ref, v1_ref, v2_ref, v3_ref))
-        store(model_ref, [model[0] * s + model[1] * t + model[2] * u for s, t, u in zip(b, v1, v2)], 0, at)
-        store(
-            residual_ref,
-            [(residual[0] * s + residual[1] * t) + (residual[2] * u + residual[3] * w) for s, t, u, w in zip(b, v1, v2, v3)],
-            0, at,
+
+    def copies(i):
+        return (
+            pltpu.make_async_copy(model_ref.at[i], model_hbm.at[i], sems.at[0, i]),
+            pltpu.make_async_copy(residual_ref.at[i], residual_hbm.at[i], sems.at[1, i]),
         )
+
+    def body(i, carry):
+        for x in range(0, cols, SUBLANES):
+            at = slice(x, x + SUBLANES)
+            b, v1, v2, v3 = (load_field(ref, i, at) for ref in (b_ref, v1_ref, v2_ref, v3_ref))
+            store(model_ref, [model[0] * s + model[1] * t + model[2] * u for s, t, u in zip(b, v1, v2)], i, at)
+            store(
+                residual_ref,
+                [(residual[0] * s + residual[1] * t) + (residual[2] * u + residual[3] * w) for s, t, u, w in zip(b, v1, v2, v3)],
+                i, at,
+            )
+        for copy in copies(i):
+            copy.start()
+        return carry
+
+    lax.fori_loop(0, rows, body, 0)
+    for i in range(rows):
+        for copy in copies(i):
+            copy.wait()
 
 
 def f32(*shape):
     return pltpu.VMEM(shape, jnp.float32)
 
 
-def call(kernel, outs, *args, name, scratch=(), aliases=None, cost=None, ins=None):
+def call(kernel, outs, *args, name, scratch=(), aliases=None, cost=None, ins=None, places=None):
     return pl.pallas_call(
         kernel,
         out_shape=outs,
         in_specs=ins or [IN_VMEM] * len(args),
-        out_specs=[IN_VMEM] * len(outs),
+        out_specs=places or [IN_VMEM] * len(outs),
         scratch_shapes=list(scratch),
         input_output_aliases=aliases or {},
         compiler_params=PARAMS,
         cost_estimate=cost,
         name=name,
     )(*args)
+
+
+def in_hbm(array):
+    return pltpu.with_memory_space_constraint(array, pltpu.HBM)
 
 
 def exchange(row0, row7, col0, col7):
@@ -352,15 +375,15 @@
     (sent,) = call(
         functools.partial(pack_kernel, capacity),
         [jax.ShapeDtypeStruct((slots, samples + LANES), jnp.bfloat16)],
-        trace_owner.reshape(1, held), trace_cell[None], acquired[None], traces,
+        *(in_hbm(x) for x in (trace_owner.reshape(1, held), trace_cell[None], acquired[None], traces)),
         name="pack", ins=[IN_HBM] * 4,
         scratch=[small, small, small, pltpu.VMEM((held, samples), jnp.bfloat16), pltpu.SemaphoreType.DMA((4,))],
     )
     got = lax.all_to_all(sent, ("inl", "xl"), split_axis=0, concat_axis=0, tiled=True)
     edge_shapes = [f32(cols, samples), f32(cols, samples), f32(rows, samples), f32(rows, samples)]
-    tile = f32(rows, cols, samples)
+    tile = f32(rows, samples // LANES, cols, LANES)
     b, diag, *edges = call(
-        bin_kernel, [tile, f32(rows, cols, LANES)] + edge_shapes, got, inline_dip, cross_dip,
+        bin_kernel, [tile, f32(rows, cols, LANES)] + edge_shapes, got, in_hbm(inline_dip), in_hbm(cross_dip),
         name="bin", ins=[IN_VMEM, IN_HBM, IN_HBM],
         scratch=[
             pltpu.VMEM((cols, samples), jnp.float32),
@@ -378,31 +401,37 @@
             apply_kernel,
             [tile, f32(2, SUBLANES, LANES)],
             fields[-1], inline_dip, cross_dip, diag,
-            name="apply", scratch=[pltpu.VMEM((cols, samples), jnp.float32)], cost=cost,
+            name="apply",
+            scratch=[
+                pltpu.VMEM((cols, samples), jnp.float32),
+                pltpu.VMEM((samples // LANES, SUBLANES + cols, LANES), jnp.float32),
+            ],
+            cost=cost,
         )
         products += [sums, edges[1], halo[0], edges[3], halo[2]]
-        image, *edges = call(
-            correct_kernel,
-            [tile] + (edge_shapes if step + 1 < ITERS else []),
-            image, inline_dip, cross_dip, *halo,
-            name="correct", aliases={0: 0},
-        )
+        if step + 1 < ITERS:
+            image, *edges = call(
+                correct_kernel, [tile] + edge_shapes, image, inline_dip, cross_dip, *halo,
+                name="correct", aliases={0: 0},
+            )
+        else:
+            image, parts = call(
+                moments_kernel, [tile, f32(devices, 1, LANES)], image, inline_dip, cross_dip, *halo, *products,
+                name="moments", aliases={0: 0},
+            )
         fields.append(image)
-    (parts,) = call(moments_kernel, [f32(devices, 1, LANES)], *products, name="moments")
     parts = lax.all_to_all(parts, ("inl", "xl"), split_axis=0, concat_axis=0, tiled=True)
     out = jax.ShapeDtypeStruct((rows, cols, samples), jnp.float32)
-    by_row = pl.BlockSpec((1, cols, samples), lambda i: (i, 0, 0))
     return tuple(
-        pl.pallas_call(
-            finish_kernel,
-            grid=(rows,),
-            out_shape=[out, out],
-            in_specs=[IN_VMEM] * (ITERS + 2),
-            out_specs=[by_row, by_row],
-            scratch_shapes=[pltpu.VMEM((2 * ITERS + 1, SUBLANES, LANES), jnp.float32)],
-            compiler_params=PARAMS,
-            name="finish",
-        )(parts, *fields)
+        call(
+            finish_kernel, [out, out], parts, *fields,
+            name="finish", places=[pl.BlockSpec(memory_space=pl.ANY)] * 2,
+            scratch=[
+                pltpu.VMEM((rows, cols, samples), jnp.float32),
+                pltpu.VMEM((rows, cols, samples), jnp.float32),
+                pltpu.SemaphoreType.DMA((2, rows)),
+            ],
+        )
     )
 
 

time: 113 us -> 100 us (0.88)
  local copies, waits for them, and re-layouts: 16.9 us -> 0.01 us
  blocking collectives: 24 us -> 36.5 us
  starting transfers between devices: 39.8 us -> 32.8 us
  waiting for transfers between devices: 1.46 us -> 0.03 us
    unnamed x34 -> x4, local copies, waits for them, and re-layouts: 16.9 us -> 0.01 us
    all_to_all x0 -> x1, blocking collectives: none -> 12.5 us  [per_device(): lax.all_to_all(parts, ('inl', 'xl'), split_axis=0, concat_axis=0, tiled=T...]
    all_to_all x1 -> x0, starting transfers between devices: 7.87 us -> none  [per_device(): lax.all_to_all(parts, ('inl', 'xl'), split_axis=0, concat_axis=0, tiled=T...]
    pallas_call x1 -> x0, Pallas kernels: 3.92 us -> none  [per_device(): pl.pallas_call(finish_kernel, grid=(rows,), out_shape=[out, out], in_spec...]
    pallas_call x9, Pallas kernels: 25.5 us -> 29.4 us  [call(): pl.pallas_call(kernel, out_shape=outs, in_specs=ins or [IN_VMEM] * len(ar...]
    ppermute x12, waiting for transfers between devices: 1.45 us -> 0.03 us  [shifted(): lax.ppermute(value, axis, [(source, source + steps) for source in range(i...]
  transfers between devices with their start and end apart: 13 -> 12, of which waited for: 1 -> 0; matrix products, arithmetic and copies ran while one was open for 0% -> 0% of each run, Pallas kernels for 20% -> 22%
where the time goes in v3:
time: 100 us; the launch traced here: 99.6 us
  blocking collectives  36.5 us (36%)
  starting transfers between devices  32.8 us (33%)
  Pallas kernels  29.4 us (29%)
    ppermute x12, starting transfers between devices, shifted(): lax.ppermute(value, axis, [(source, source + steps) for source in range(i...  32.8 us
    pallas_call x9, Pallas kernels, call(): pl.pallas_call(kernel, out_shape=outs, in_specs=ins or [IN_VMEM] * len(ar...  29.4 us
    all_to_all x1, blocking collectives, per_device(): lax.all_to_all(sent, ('inl', 'xl'), split_axis=0, concat_axis=0, tiled=True)  24 us
    all_to_all x1, blocking collectives, per_device(): lax.all_to_all(parts, ('inl', 'xl'), split_axis=0, concat_axis=0, tiled=T...  12.5 us
  transfers between devices with their start and end apart: 12, of which 0 were waited for; matrix products, arithmetic and copies ran while one was open for 0% of the time, Pallas kernels for 22%

profile of v3, /device:TPU:0, one launch (start us, length us, event | category | flops | bytes accessed | tf_op | source)
XLA Modules:
  0.0 99.6 jit_solution(37879638996739345)
XLA Ops:
  0.6 1.4 %pack.1 = bf16[512,640]{1,0:T(8,128)(2,1)S(1)} custom-call(s32[1,256]{1,0:T(1,128)} %bitcast.7, s32[1,256]{1,0:T(1,128)} %bitcast.8, s32[1,256]{1,0:T(1,128)} %bitcast.9, bf16[256,512]{1,0:T(8,128)(2,1)} %traces_hbm.1), custom_call_target="tpu_custom_call" | custom-call | tf_op jit(solution)/shard_map/pack/pallas_call | solution.py:343
  2.0 24.0 %all_to_all.16 = bf16[32,16,640]{2,1,0:T(8,128)(2,1)S(1)} all-to-all(bf16[32,16,640]{2,1,0:T(8,128)(2,1)S(1)} %bitcast.6), channel_id=1, replica_groups=mesh['inl'=8,'xl'=4] {'inl','xl'}, dimensions={0} | all-to-all | bytes 1310720 | tf_op jit(solution)/shard_map/all_to_all | solution.py:382
  26.0 0.0 copy-start
  26.0 0.0 copy-start.1
  26.0 2.6 %bin.1 = (f32[8,4,128,128]{3,2,1,0:T(8,128)S(1)}, f32[8,128,128]{2,1,0:T(8,128)S(1)}, f32[128,512]{1,0:T(8,128)S(1)}, f32[128,512]{1,0:T(8,128)S(1)}, f32[8,512]{1,0:T(8,128)S(1)}, /*index=5*/f32[8,512]{1,0:T(8,128)S(1)}) custom-call(bf16[512,640]{1,0:T(8,128)(2,1)S(1)} %bitcast.5, f32[8,128,512]{2,1,0:T(8,128)} %p1_ref.11, f32[8,128,512]{2,1,0:T(8,128)} %p2_ref.11), custom_call_target="tpu_custom_call" | custom-call | tf_op jit(solution)/shard_map/bin/pallas_call | solution.py:343
  28.6 1.3 %collective-permute-start = (f32[128,512]{1,0:T(8,128)S(1)}, f32[128,512]{1,0:T(8,128)S(1)}, u32[]{:S(2)}, u32[]{:S(2)}) collective-permute-start(f32[128,512]{1,0:T(8,128)S(1)} %get-tuple-element.29), channel_id=1, source_target_pairs={{4,0},{8,4},{12,8},{16,12},{20,16},{24,20},{28,24},{5,1},{9,5},{13... | collective-permute-start | bytes 786440 | tf_op jit(solution)/shard_map/ppermute | solution.py:23
  29.9 3.9 %collective-permute-start.1 = (f32[128,512]{1,0:T(8,128)S(1)}, f32[128,512]{1,0:T(8,128)S(1)}, u32[]{:S(2)}, u32[]{:S(2)}) collective-permute-start(f32[128,512]{1,0:T(8,128)S(1)} %get-tuple-element.30.refs_1_), channel_id=1, source_target_pairs={{0,4},{4,8},{8,12},{12,16},{16,20},{20,24},{24,28},{1,5},{5,9},{9,... | collective-permute-start | bytes 786440 | tf_op jit(solution)/shard_map/ppermute | solution.py:23
  33.9 1.3 %collective-permute-start.2 = (f32[8,512]{1,0:T(8,128)S(1)}, f32[8,512]{1,0:T(8,128)S(1)}, u32[]{:S(2)}, u32[]{:S(2)}) collective-permute-start(f32[8,512]{1,0:T(8,128)S(1)} %get-tuple-element.31), channel_id=1, source_target_pairs={{1,0},{2,1},{3,2},{5,4},{6,5},{7,6},{9,8},{10,9},{11,10},{13,12},{... | collective-permute-start | bytes 49160 | tf_op jit(solution)/shard_map/ppermute | solution.py:23
  35.2 4.5 %collective-permute-start.3 = (f32[8,512]{1,0:T(8,128)S(1)}, f32[8,512]{1,0:T(8,128)S(1)}, u32[]{:S(2)}, u32[]{:S(2)}) collective-permute-start(f32[8,512]{1,0:T(8,128)S(1)} %get-tuple-element.32.refs_3_), channel_id=1, source_target_pairs={{0,1},{1,2},{2,3},{4,5},{5,6},{6,7},{8,9},{9,10},{10,11},{12,13},{... | collective-permute-start | bytes 49160 | tf_op jit(solution)/shard_map/ppermute | solution.py:23
  39.7 0.0 copy-done
  39.8 0.0 copy-done.1
  39.8 7.2 %apply.3 = (f32[8,4,128,128]{3,2,1,0:T(8,128)S(1)}, f32[2,8,128]{2,1,0:T(8,128)S(1)}) custom-call(f32[8,4,128,128]{3,2,1,0:T(8,128)S(1)} %get-tuple-element.26.v_ref.b_ref, f32[8,128,512]{2,1,0:T(8,128)S(1)} %copy-done, f32[8,128,512]{2,1,0:T(8,128)S(1)} %copy-done.1, f32[8,128,128]{2,1,0:T(8,128)S(1)} %get-tuple-element.27.diag_ref), custom_call_target="tpu_custom_call" | custom-call | flops 31457280 | bytes 8388608 | tf_op jit(solution)/shard_map/apply/pallas_call | solution.py:343
  46.9 0.0 collective-permute-done.2.right_ref.refs_4_
  46.9 0.0 collective-permute-done.3.left_ref
  47.0 0.0 collective-permute-done.below_ref.refs_2_
  47.0 0.0 collective-permute-done.1.above_ref
  47.0 0.5 correct.2
  47.5 1.3 %collective-permute-start.4 = (f32[128,512]{1,0:T(8,128)S(1)}, f32[128,512]{1,0:T(8,128)S(1)}, u32[]{:S(2)}, u32[]{:S(2)}) collective-permute-start(f32[128,512]{1,0:T(8,128)S(1)} %get-tuple-element.35), channel_id=1, source_target_pairs={{4,0},{8,4},{12,8},{16,12},{20,16},{24,20},{28,24},{5,1},{9,5},{13... | collective-permute-start | bytes 786440 | tf_op jit(solution)/shard_map/ppermute | solution.py:23
  48.8 3.7 %collective-permute-start.5 = (f32[128,512]{1,0:T(8,128)S(1)}, f32[128,512]{1,0:T(8,128)S(1)}, u32[]{:S(2)}, u32[]{:S(2)}) collective-permute-start(f32[128,512]{1,0:T(8,128)S(1)} %get-tuple-element.36.refs_6_), channel_id=1, source_target_pairs={{0,4},{4,8},{8,12},{12,16},{16,20},{20,24},{24,28},{1,5},{5,9},{9,... | collective-permute-start | bytes 786440 | tf_op jit(solution)/shard_map/ppermute | solution.py:23
  52.5 1.3 %collective-permute-start.6 = (f32[8,512]{1,0:T(8,128)S(1)}, f32[8,512]{1,0:T(8,128)S(1)}, u32[]{:S(2)}, u32[]{:S(2)}) collective-permute-start(f32[8,512]{1,0:T(8,128)S(1)} %get-tuple-element.37), channel_id=1, source_target_pairs={{1,0},{2,1},{3,2},{5,4},{6,5},{7,6},{9,8},{10,9},{11,10},{13,12},{... | collective-permute-start | bytes 49160 | tf_op jit(solution)/shard_map/ppermute | solution.py:23
  53.8 4.5 %collective-permute-start.7 = (f32[8,512]{1,0:T(8,128)S(1)}, f32[8,512]{1,0:T(8,128)S(1)}, u32[]{:S(2)}, u32[]{:S(2)}) collective-permute-start(f32[8,512]{1,0:T(8,128)S(1)} %get-tuple-element.38.refs_8_), channel_id=1, source_target_pairs={{0,1},{1,2},{2,3},{4,5},{5,6},{6,7},{8,9},{9,10},{10,11},{12,13},{... | collective-permute-start | bytes 49160 | tf_op jit(solution)/shard_map/ppermute | solution.py:23
  58.4 7.2 %apply.4 = (f32[8,4,128,128]{3,2,1,0:T(8,128)S(1)}, f32[2,8,128]{2,1,0:T(8,128)S(1)}) custom-call(f32[8,4,128,128]{3,2,1,0:T(8,128)S(1)} %get-tuple-element.33.v_ref.v1_ref, f32[8,128,512]{2,1,0:T(8,128)S(1)} %copy-done, f32[8,128,512]{2,1,0:T(8,128)S(1)} %copy-done.1, f32[8,128,128]{2,1,0:T(8,128)S(1)} %get-tuple-element.27.diag_ref), custom_call_target="tpu_custom_call" | custom-call | flops 31457280 | bytes 8388608 | tf_op jit(solution)/shard_map/apply/pallas_call | solution.py:343
  65.6 0.0 collective-permute-done.6.right_ref.refs_9_
  65.6 0.0 collective-permute-done.7.left_ref
  65.6 0.0 collective-permute-done.4.below_ref.refs_7_
  65.6 0.0 collective-permute-done.5.above_ref
  65.6 0.5 correct.3
  66.1 1.3 %collective-permute-start.8 = (f32[128,512]{1,0:T(8,128)S(1)}, f32[128,512]{1,0:T(8,128)S(1)}, u32[]{:S(2)}, u32[]{:S(2)}) collective-permute-start(f32[128,512]{1,0:T(8,128)S(1)} %get-tuple-element.41), channel_id=1, source_target_pairs={{4,0},{8,4},{12,8},{16,12},{20,16},{24,20},{28,24},{5,1},{9,5},{13... | collective-permute-start | bytes 786440 | tf_op jit(solution)/shard_map/ppermute | solution.py:23
  67.4 3.7 %collective-permute-start.9 = (f32[128,512]{1,0:T(8,128)S(1)}, f32[128,512]{1,0:T(8,128)S(1)}, u32[]{:S(2)}, u32[]{:S(2)}) collective-permute-start(f32[128,512]{1,0:T(8,128)S(1)} %get-tuple-element.42.refs_11_), channel_id=1, source_target_pairs={{0,4},{4,8},{8,12},{12,16},{16,20},{20,24},{24,28},{1,5},{5,9},{9,... | collective-permute-start | bytes 786440 | tf_op jit(solution)/shard_map/ppermute | solution.py:23
  71.2 1.3 %collective-permute-start.10 = (f32[8,512]{1,0:T(8,128)S(1)}, f32[8,512]{1,0:T(8,128)S(1)}, u32[]{:S(2)}, u32[]{:S(2)}) collective-permute-start(f32[8,512]{1,0:T(8,128)S(1)} %get-tuple-element.43), channel_id=1, source_target_pairs={{1,0},{2,1},{3,2},{5,4},{6,5},{7,6},{9,8},{10,9},{11,10},{13,12},{... | collective-permute-start | bytes 49160 | tf_op jit(solution)/shard_map/ppermute | solution.py:23
  72.5 4.5 %collective-permute-start.11 = (f32[8,512]{1,0:T(8,128)S(1)}, f32[8,512]{1,0:T(8,128)S(1)}, u32[]{:S(2)}, u32[]{:S(2)}) collective-permute-start(f32[8,512]{1,0:T(8,128)S(1)} %get-tuple-element.44.refs_13_), channel_id=1, source_target_pairs={{0,1},{1,2},{2,3},{4,5},{5,6},{6,7},{8,9},{9,10},{10,11},{12,13},{... | collective-permute-start | bytes 49160 | tf_op jit(solution)/shard_map/ppermute | solution.py:23
  77.0 7.2 %apply.5 = (f32[8,4,128,128]{3,2,1,0:T(8,128)S(1)}, f32[2,8,128]{2,1,0:T(8,128)S(1)}) custom-call(f32[8,4,128,128]{3,2,1,0:T(8,128)S(1)} %get-tuple-element.39.v_ref.v2_ref, f32[8,128,512]{2,1,0:T(8,128)S(1)} %copy-done, f32[8,128,512]{2,1,0:T(8,128)S(1)} %copy-done.1, f32[8,128,128]{2,1,0:T(8,128)S(1)} %get-tuple-element.27.diag_ref), custom_call_target="tpu_custom_call" | custom-call | flops 31457280 | bytes 8388608 | tf_op jit(solution)/shard_map/apply/pallas_call | solution.py:343
  84.2 0.0 collective-permute-done.10.right_ref.refs_14_
  84.2 0.0 collective-permute-done.11.left_ref
  84.3 0.0 collective-permute-done.8.below_ref.refs_12_
  84.3 0.0 collective-permute-done.9.above_ref
  84.3 0.4 moments.1
  84.7 12.5 %all_to_all.17.parts_ref = f32[32,1,128]{2,1,0:T(1,128)S(1)} all-to-all(f32[32,1,128]{2,1,0:T(1,128)S(1)} %get-tuple-element.48), channel_id=1, replica_groups=mesh['inl'=8,'xl'=4] {'inl','xl'}, dimensions={0} | all-to-all | bytes 32768 | tf_op jit(solution)/shard_map/all_to_all | solution.py:423
  97.2 2.4 %finish.1 = (f32[8,128,512]{2,1,0:T(8,128)}, f32[8,128,512]{2,1,0:T(8,128)}) custom-call(f32[32,1,128]{2,1,0:T(1,128)S(1)} %all_to_all.17.parts_ref, f32[8,4,128,128]{3,2,1,0:T(8,128)S(1)} %get-tuple-element.26.v_ref.b_ref, f32[8,4,128,128]{3,2,1,0:T(8,128)S(1)} %get-tuple-element.33.v_ref.v1_ref, f32[8,4,128,128]{3,2,1,0:T(8,128)S(1)} %get-tuple-element.39.v_ref.v2_ref, ...), custom_call_target="tpu_custom_call" | custom-call | tf_op jit(solution)/shard_map/finish/pallas_call | solution.py:343
Async XLA Ops:
  26.0 13.7 %copy-start = (f32[8,128,512]{2,1,0:T(8,128)S(1)}, f32[8,128,512]{2,1,0:T(8,128)}, u32[]{:S(2)}) copy-start(f32[8,128,512]{2,1,0:T(8,128)} %p1_ref.11) | copy-start | bytes 6291460
  26.0 13.7 %copy-start.1 = (f32[8,128,512]{2,1,0:T(8,128)S(1)}, f32[8,128,512]{2,1,0:T(8,128)}, u32[]{:S(2)}) copy-start(f32[8,128,512]{2,1,0:T(8,128)} %p2_ref.11) | copy-start | bytes 6291460
  28.6 18.3 %collective-permute-start = (f32[128,512]{1,0:T(8,128)S(1)}, f32[128,512]{1,0:T(8,128)S(1)}, u32[]{:S(2)}, u32[]{:S(2)}) collective-permute-start(f32[128,512]{1,0:T(8,128)S(1)} %get-tuple-element.29), channel_id=1, source_target_pairs={{4,0},{8,4},{12,8},{16,12},{20,16},{24,20},{28,24},{5,1},{9,5},{13... | collective-permute-start | bytes 786440 | tf_op jit(solution)/shard_map/ppermute | solution.py:23
  29.9 17.0 %collective-permute-start.1 = (f32[128,512]{1,0:T(8,128)S(1)}, f32[128,512]{1,0:T(8,128)S(1)}, u32[]{:S(2)}, u32[]{:S(2)}) collective-permute-start(f32[128,512]{1,0:T(8,128)S(1)} %get-tuple-element.30.refs_1_), channel_id=1, source_target_pairs={{0,4},{4,8},{8,12},{12,16},{16,20},{20,24},{24,28},{1,5},{5,9},{9,... | collective-permute-start | bytes 786440 | tf_op jit(solution)/shard_map/ppermute | solution.py:23
  33.9 13.0 %collective-permute-start.2 = (f32[8,512]{1,0:T(8,128)S(1)}, f32[8,512]{1,0:T(8,128)S(1)}, u32[]{:S(2)}, u32[]{:S(2)}) collective-permute-start(f32[8,512]{1,0:T(8,128)S(1)} %get-tuple-element.31), channel_id=1, source_target_pairs={{1,0},{2,1},{3,2},{5,4},{6,5},{7,6},{9,8},{10,9},{11,10},{13,12},{... | collective-permute-start | bytes 49160 | tf_op jit(solution)/shard_map/ppermute | solution.py:23
  35.2 11.8 %collective-permute-start.3 = (f32[8,512]{1,0:T(8,128)S(1)}, f32[8,512]{1,0:T(8,128)S(1)}, u32[]{:S(2)}, u32[]{:S(2)}) collective-permute-start(f32[8,512]{1,0:T(8,128)S(1)} %get-tuple-element.32.refs_3_), channel_id=1, source_target_pairs={{0,1},{1,2},{2,3},{4,5},{5,6},{6,7},{8,9},{9,10},{10,11},{12,13},{... | collective-permute-start | bytes 49160 | tf_op jit(solution)/shard_map/ppermute | solution.py:23
  47.5 18.1 %collective-permute-start.4 = (f32[128,512]{1,0:T(8,128)S(1)}, f32[128,512]{1,0:T(8,128)S(1)}, u32[]{:S(2)}, u32[]{:S(2)}) collective-permute-start(f32[128,512]{1,0:T(8,128)S(1)} %get-tuple-element.35), channel_id=1, source_target_pairs={{4,0},{8,4},{12,8},{16,12},{20,16},{24,20},{28,24},{5,1},{9,5},{13... | collective-permute-start | bytes 786440 | tf_op jit(solution)/shard_map/ppermute | solution.py:23
  48.8 16.8 %collective-permute-start.5 = (f32[128,512]{1,0:T(8,128)S(1)}, f32[128,512]{1,0:T(8,128)S(1)}, u32[]{:S(2)}, u32[]{:S(2)}) collective-permute-start(f32[128,512]{1,0:T(8,128)S(1)} %get-tuple-element.36.refs_6_), channel_id=1, source_target_pairs={{0,4},{4,8},{8,12},{12,16},{16,20},{20,24},{24,28},{1,5},{5,9},{9,... | collective-permute-start | bytes 786440 | tf_op jit(solution)/shard_map/ppermute | solution.py:23
  52.5 13.0 %collective-permute-start.6 = (f32[8,512]{1,0:T(8,128)S(1)}, f32[8,512]{1,0:T(8,128)S(1)}, u32[]{:S(2)}, u32[]{:S(2)}) collective-permute-start(f32[8,512]{1,0:T(8,128)S(1)} %get-tuple-element.37), channel_id=1, source_target_pairs={{1,0},{2,1},{3,2},{5,4},{6,5},{7,6},{9,8},{10,9},{11,10},{13,12},{... | collective-permute-start | bytes 49160 | tf_op jit(solution)/shard_map/ppermute | solution.py:23
  53.8 11.7 %collective-permute-start.7 = (f32[8,512]{1,0:T(8,128)S(1)}, f32[8,512]{1,0:T(8,128)S(1)}, u32[]{:S(2)}, u32[]{:S(2)}) collective-permute-start(f32[8,512]{1,0:T(8,128)S(1)} %get-tuple-element.38.refs_8_), channel_id=1, source_target_pairs={{0,1},{1,2},{2,3},{4,5},{5,6},{6,7},{8,9},{9,10},{10,11},{12,13},{... | collective-permute-start | bytes 49160 | tf_op jit(solution)/shard_map/ppermute | solution.py:23
  66.1 18.1 %collective-permute-start.8 = (f32[128,512]{1,0:T(8,128)S(1)}, f32[128,512]{1,0:T(8,128)S(1)}, u32[]{:S(2)}, u32[]{:S(2)}) collective-permute-start(f32[128,512]{1,0:T(8,128)S(1)} %get-tuple-element.41), channel_id=1, source_target_pairs={{4,0},{8,4},{12,8},{16,12},{20,16},{24,20},{28,24},{5,1},{9,5},{13... | collective-permute-start | bytes 786440 | tf_op jit(solution)/shard_map/ppermute | solution.py:23
  67.4 16.8 %collective-permute-start.9 = (f32[128,512]{1,0:T(8,128)S(1)}, f32[128,512]{1,0:T(8,128)S(1)}, u32[]{:S(2)}, u32[]{:S(2)}) collective-permute-start(f32[128,512]{1,0:T(8,128)S(1)} %get-tuple-element.42.refs_11_), channel_id=1, source_target_pairs={{0,4},{4,8},{8,12},{12,16},{16,20},{20,24},{24,28},{1,5},{5,9},{9,... | collective-permute-start | bytes 786440 | tf_op jit(solution)/shard_map/ppermute | solution.py:23
  71.2 13.1 %collective-permute-start.10 = (f32[8,512]{1,0:T(8,128)S(1)}, f32[8,512]{1,0:T(8,128)S(1)}, u32[]{:S(2)}, u32[]{:S(2)}) collective-permute-start(f32[8,512]{1,0:T(8,128)S(1)} %get-tuple-element.43), channel_id=1, source_target_pairs={{1,0},{2,1},{3,2},{5,4},{6,5},{7,6},{9,8},{10,9},{11,10},{13,12},{... | collective-permute-start | bytes 49160 | tf_op jit(solution)/shard_map/ppermute | solution.py:23
  72.5 11.8 %collective-permute-start.11 = (f32[8,512]{1,0:T(8,128)S(1)}, f32[8,512]{1,0:T(8,128)S(1)}, u32[]{:S(2)}, u32[]{:S(2)}) collective-permute-start(f32[8,512]{1,0:T(8,128)S(1)} %get-tuple-element.44.refs_13_), channel_id=1, source_target_pairs={{0,1},{1,2},{2,3},{4,5},{5,6},{6,7},{8,9},{9,10},{10,11},{12,13},{... | collective-permute-start | bytes 49160 | tf_op jit(solution)/shard_map/ppermute | solution.py:23

commit v4 on v3

--- a/solution.py
+++ b/solution.py
@@ -74,6 +74,10 @@
         ref[(*index, slice(c * LANES, (c + 1) * LANES))] = tile
 
 
+def load_tiles(ref, at):
+    return [ref[c, at, :] for c in range(ref.shape[0])]
+
+
 def load_field(ref, i, at):
     return [ref[i, c, at, :] for c in range(ref.shape[1])]
 
@@ -95,10 +99,17 @@
     return functools.reduce(lambda s, t: s + t, [a * b for a, b in zip(x, y)])
 
 
-def pack_kernel(capacity, owner_hbm, cell_hbm, live_hbm, traces_hbm, out_ref, owner_ref, cell_ref, live_ref, traces_ref, sems):
+def pack_kernel(
+    capacity, owner_hbm, cell_hbm, live_hbm, traces_hbm, p1_hbm, p2_hbm, out_ref, p1_last_ref, p2_last_ref,
+    owner_ref, cell_ref, live_ref, traces_ref, sems,
+):
     held, samples = traces_ref.shape
     slots = out_ref.shape[0]
-    pairs = ((owner_hbm, owner_ref), (cell_hbm, cell_ref), (live_hbm, live_ref), (traces_hbm, traces_ref))
+    rows, cols, _ = p1_hbm.shape
+    pairs = (
+        (owner_hbm, owner_ref), (cell_hbm, cell_ref), (live_hbm, live_ref), (traces_hbm, traces_ref),
+        (p1_hbm.at[rows - 1], p1_last_ref), (p2_hbm.at[:, pl.ds(cols - SUBLANES, SUBLANES)], p2_last_ref),
+    )
     copies = [pltpu.make_async_copy(src, dst, sems.at[k]) for k, (src, dst) in enumerate(pairs)]
     for copy in copies:
         copy.start()
@@ -121,18 +132,14 @@
     copies[3].wait()
     rows = jnp.dot(chosen, traces_ref[...], preferred_element_type=jnp.float32)
     out_ref[:, :samples] = rows.astype(jnp.bfloat16)
-
-
-def bin_kernel(got_ref, p1_hbm, p2_hbm, b_ref, diag_ref, row0_ref, row7_ref, col0_ref, col7_ref, p1_ref, p2_ref, sems):
+    for copy in copies[4:]:
+        copy.wait()
+
+
+def bin_kernel(got_ref, p1_ref, p2_ref, b_ref, diag_ref, row0_ref, row7_ref, ends_ref):
     rows, tiles, cols, _ = b_ref.shape
     samples = tiles * LANES
     slots = got_ref.shape[0]
-    copies = (
-        pltpu.make_async_copy(p1_hbm.at[rows - 1], p1_ref, sems.at[0]),
-        pltpu.make_async_copy(p2_hbm.at[:, pl.ds(cols - SUBLANES, SUBLANES)], p2_ref, sems.at[1]),
-    )
-    for copy in copies:
-        copy.start()
     kind = iota((SUBLANES, LANES), 1)
     weight = jnp.where(kind == 0, 64.0, jnp.where(kind == 1, 1.0, 0.0)).astype(jnp.bfloat16)
     value = lax.dot_general(
@@ -152,15 +159,12 @@
         hits = jnp.dot(place, ones, preferred_element_type=jnp.float32)
         diag = 2.0 * hits + first_col
         diag_ref[i] = diag + not_first_row if i == 0 else diag
-    for copy in copies:
-        copy.wait()
     write_edges(
-        b_ref, lambda at: load(p1_ref, at), lambda i: load(p2_ref, i, slice(None)),
-        row0_ref, row7_ref, col0_ref, col7_ref,
-    )
-
-
-def write_edges(v_ref, p1_last_row, p2_last_cols, row0_ref, row7_ref, col0_ref, col7_ref):
+        b_ref, lambda at: load(p1_ref, at), lambda i: load(p2_ref, i, slice(None)), row0_ref, row7_ref, ends_ref
+    )
+
+
+def write_edges(v_ref, p1_last_row, p2_last_cols, row0_ref, row7_ref, ends_ref):
     rows, _, cols, _ = v_ref.shape
     for x in range(0, cols, SUBLANES):
         at = slice(x, x + SUBLANES)
@@ -168,10 +172,10 @@
         v = load_field(v_ref, rows - 1, at)
         store(row7_ref, add(v, dip_part(p1_last_row(at), *stencil(v))), at)
     for i in range(rows):
-        store(col0_ref, load_field(v_ref, i, slice(0, 1)), slice(i, i + 1))
+        store(ends_ref, load_field(v_ref, i, slice(0, 1)), 0, slice(i, i + 1))
         v = load_field(v_ref, i, slice(cols - SUBLANES, cols))
         moved = add(v, dip_part(p2_last_cols(i), *stencil(v)))
-        store(col7_ref, [t[SUBLANES - 1 :] for t in moved], slice(i, i + 1))
+        store(ends_ref, [t[SUBLANES - 1 :] for t in moved], 1, slice(i, i + 1))
 
 
 def apply_kernel(v_ref, p1_ref, p2_ref, diag_ref, out_ref, sums_ref, first_ref, second_ref):
@@ -183,16 +187,19 @@
         second_ref[c, :SUBLANES, :] = zero[0]
 
     def row(i, sums, last):
+        v_row, out_row, diag_row = v_ref.at[i], out_ref.at[i], diag_ref.at[i]
+        p1_row, p2_row = p1_ref.at[i], p2_ref.at[i]
+        below_row = None if last else v_ref.at[i + 1]
         vout, vv = zero[0], zero[0]
         for x in range(0, cols, SUBLANES):
             at = slice(x, x + SUBLANES)
-            v = load_field(v_ref, i, at)
+            v = load_tiles(v_row, at)
             if x + SUBLANES < cols:
-                right = load_field(v_ref, i, slice(x + 1, x + 1 + SUBLANES))
+                right = load_tiles(v_row, slice(x + 1, x + 1 + SUBLANES))
             else:
                 right = [jnp.where(sub_index == SUBLANES - 1, 0.0, pltpu.roll(t, SUBLANES - 1, 0)) for t in v]
-            below = zero if last else load_field(v_ref, i + 1, at)
-            p1, p2 = load(p1_ref, i, at), load(p2_ref, i, at)
+            below = zero if last else load_tiles(below_row, at)
+            p1, p2 = load(p1_row, at), load(p2_row, at)
             odd, even = stencil(v)
             first = sub(sub(below, v), dip_part(p1, odd, even))
             second = sub(sub(right, v), dip_part(p2, odd, even))
@@ -204,9 +211,10 @@
             left = [second_ref[c, x + SUBLANES - 1 : x + 2 * SUBLANES - 1, :] for c in range(tiles)]
             above = load(first_ref, at)
             store(first_ref, first, at)
-            diag = diag_ref[i, at, :]
+            diag = diag_row[at, :]
             out = [diag * c + ((f + s) - m) for c, f, s, m in zip(v, above, left, moved)]
-            store_field(out_ref, out, i, at)
+            for c in range(tiles):
+                out_row[c, at, :] = out[c]
             vout = vout + dot(v, out)
             vv = vv + dot(v, v)
         return sums[0] + vout, sums[1] + vv
@@ -235,30 +243,55 @@
         store_field(out_ref, sub(load_field(out_ref, i, at), moved), i, at)
 
 
+def settle(image_ref, p1_ref, p2_ref, below_ref, above_ref, gathered_hbm, row7_ref, ends_ref, out_ref, side_ref, sems):
+    here, count = lax.axis_index("xl"), lax.axis_size("xl")
+    copies = (
+        pltpu.make_async_copy(gathered_hbm.at[jnp.minimum(here + 1, count - 1), 0], side_ref.at[0], sems.at[0]),
+        pltpu.make_async_copy(gathered_hbm.at[jnp.maximum(here - 1, 0), 1], side_ref.at[1], sems.at[1]),
+    )
+    for copy in copies:
+        copy.start()
+    across = jnp.zeros((SUBLANES, LANES), jnp.float32)
+    for x in range(0, row7_ref.shape[0], SUBLANES):
+        at = slice(x, x + SUBLANES)
+        across = across + dot(load(row7_ref, at), load(below_ref, at))
+    for copy in copies:
+        copy.wait()
+    side_ref[0] = jnp.where(here + 1 < count, side_ref[0], 0.0)
+    side_ref[1] = jnp.where(here > 0, side_ref[1], 0.0)
+    for x in range(0, ends_ref.shape[1], SUBLANES):
+        at = slice(x, x + SUBLANES)
+        across = across + dot(load(ends_ref, 1, at), load(side_ref, 0, at))
+    halo_corrections(out_ref, p1_ref, p2_ref, below_ref, above_ref, side_ref.at[0], side_ref.at[1])
+    return across
+
+
 def correct_kernel(
-    image_ref, p1_ref, p2_ref, below_ref, above_ref, right_ref, left_ref, out_ref, *edge_refs
+    image_ref, p1_ref, p2_ref, below_ref, above_ref, gathered_hbm, row7_ref, ends_ref,
+    out_ref, across_ref, next_row0_ref, next_row7_ref, next_ends_ref, side_ref, sems,
 ):
-    halo_corrections(out_ref, p1_ref, p2_ref, below_ref, above_ref, right_ref, left_ref)
+    across_ref[...] = settle(
+        image_ref, p1_ref, p2_ref, below_ref, above_ref, gathered_hbm, row7_ref, ends_ref, out_ref, side_ref, sems
+    )
     rows, _, cols, _ = out_ref.shape
     write_edges(
         out_ref,
         lambda at: load(p1_ref, rows - 1, at),
         lambda i: load(p2_ref, i, slice(cols - SUBLANES, cols)),
-        *edge_refs,
-    )
-
-
-def moments_kernel(image_ref, p1_ref, p2_ref, below_ref, above_ref, right_ref, left_ref, *refs):
-    halo_corrections(refs[-2], p1_ref, p2_ref, below_ref, above_ref, right_ref, left_ref)
-    out_ref = refs[-1]
+        next_row0_ref, next_row7_ref, next_ends_ref,
+    )
+
+
+def moments_kernel(
+    image_ref, p1_ref, p2_ref, below_ref, above_ref, gathered_hbm, row7_ref, ends_ref, *refs
+):
+    sums_refs, across_refs = refs[:ITERS], refs[ITERS : 2 * ITERS - 1]
+    out_ref, message_ref, side_ref, sems = refs[2 * ITERS - 1 :]
+    final = settle(
+        image_ref, p1_ref, p2_ref, below_ref, above_ref, gathered_hbm, row7_ref, ends_ref, out_ref, side_ref, sems
+    )
     m = []
-    for step in range(ITERS):
-        sums_ref, row7, below, col7, right = refs[5 * step : 5 * step + 5]
-        across = jnp.zeros((SUBLANES, LANES), jnp.float32)
-        for mine, theirs in ((row7, below), (col7, right)):
-            for x in range(0, mine.shape[0], SUBLANES):
-                at = slice(x, x + SUBLANES)
-                across = across + dot(load(mine, at), load(theirs, at))
+    for sums_ref, across in zip(sums_refs, [ref[...] for ref in across_refs] + [final]):
         m.append(sums_ref[1])
         m.append(sums_ref[0] - 2.0 * across)
     sub_index, lane = iota((SUBLANES, LANES), 0), iota((SUBLANES, LANES), 1)
@@ -267,7 +300,7 @@
         block = jnp.where(sub_index == k, jnp.sum(part, axis=0, keepdims=True), block)
     total = jnp.sum(block, axis=1, keepdims=True)
     line = jnp.sum(jnp.where(sub_index == lane, total, 0.0), axis=0, keepdims=True)
-    out_ref[...] = jnp.broadcast_to(line[None], out_ref.shape)
+    message_ref[...] = jnp.broadcast_to(line, message_ref.shape)
 
 
 def coefficients(m):
@@ -301,7 +334,7 @@
 
 def finish_kernel(parts_ref, b_ref, v1_ref, v2_ref, v3_ref, model_hbm, residual_hbm, model_ref, residual_ref, sems):
     rows, _, cols, _ = b_ref.shape
-    line = jnp.sum(parts_ref[...], axis=0)
+    line = jnp.sum(parts_ref[...], axis=0)[:1]
     sub_index, lane = iota((SUBLANES, LANES), 0), iota((SUBLANES, LANES), 1)
     total = jnp.sum(jnp.where(sub_index == lane, line, 0.0), axis=1, keepdims=True)
     total = jnp.broadcast_to(total, (SUBLANES, LANES))
@@ -357,14 +390,6 @@
     return pltpu.with_memory_space_constraint(array, pltpu.HBM)
 
 
-def exchange(row0, row7, col0, col7):
-    below = shifted(row0, "inl", -1)
-    above = shifted(row7, "inl", 1)
-    right = shifted(col0, "xl", -1)
-    left = shifted(col7, "xl", 1)
-    return below, above, right, left
-
-
 def per_device(traces, trace_owner, trace_cell, acquired, inline_dip, cross_dip):
     rows, cols, samples = inline_dip.shape
     devices = lax.axis_size("inl") * lax.axis_size("xl")
@@ -372,32 +397,35 @@
     capacity = max(2, 2 * held // devices)
     slots = devices * capacity
     small = pltpu.VMEM((1, held), jnp.int32)
-    (sent,) = call(
+    inputs = (trace_owner.reshape(1, held), trace_cell[None], acquired[None], traces, inline_dip, cross_dip)
+    sent, p1_last, p2_last = call(
         functools.partial(pack_kernel, capacity),
-        [jax.ShapeDtypeStruct((slots, samples + LANES), jnp.bfloat16)],
-        *(in_hbm(x) for x in (trace_owner.reshape(1, held), trace_cell[None], acquired[None], traces)),
-        name="pack", ins=[IN_HBM] * 4,
-        scratch=[small, small, small, pltpu.VMEM((held, samples), jnp.bfloat16), pltpu.SemaphoreType.DMA((4,))],
+        [
+            jax.ShapeDtypeStruct((slots, samples + LANES), jnp.bfloat16),
+            f32(cols, samples),
+            f32(rows, SUBLANES, samples),
+        ],
+        *(in_hbm(x) for x in inputs),
+        name="pack", ins=[IN_HBM] * len(inputs),
+        scratch=[small, small, small, pltpu.VMEM((held, samples), jnp.bfloat16), pltpu.SemaphoreType.DMA((6,))],
     )
     got = lax.all_to_all(sent, ("inl", "xl"), split_axis=0, concat_axis=0, tiled=True)
-    edge_shapes = [f32(cols, samples), f32(cols, samples), f32(rows, samples), f32(rows, samples)]
+    edge_shapes = [f32(cols, samples), f32(cols, samples), jax.ShapeDtypeStruct((2, rows, samples), jnp.float32)]
     tile = f32(rows, samples // LANES, cols, LANES)
     b, diag, *edges = call(
-        bin_kernel, [tile, f32(rows, cols, LANES)] + edge_shapes, got, in_hbm(inline_dip), in_hbm(cross_dip),
-        name="bin", ins=[IN_VMEM, IN_HBM, IN_HBM],
-        scratch=[
-            pltpu.VMEM((cols, samples), jnp.float32),
-            pltpu.VMEM((rows, SUBLANES, samples), jnp.float32),
-            pltpu.SemaphoreType.DMA((2,)),
-        ],
-    )
-    fields, products = [b], []
+        bin_kernel, [tile, f32(rows, cols, LANES)] + edge_shapes, got, p1_last, p2_last, name="bin"
+    )
+    fields, sums, products = [b], [], []
     cost = pl.CostEstimate(
         flops=60 * rows * cols * samples, bytes_accessed=16 * rows * cols * samples, transcendentals=0
     )
+    side = [pltpu.VMEM((2, rows, samples), jnp.float32), pltpu.SemaphoreType.DMA((2,))]
     for step in range(ITERS):
-        halo = exchange(*edges)
-        image, sums = call(
+        row0, row7, ends = edges
+        gathered = lax.all_gather(ends, "xl")
+        below = shifted(row0, "inl", -1)
+        above = shifted(row7, "inl", 1)
+        image, partial = call(
             apply_kernel,
             [tile, f32(2, SUBLANES, LANES)],
             fields[-1], inline_dip, cross_dip, diag,
@@ -408,19 +436,22 @@
             ],
             cost=cost,
         )
-        products += [sums, edges[1], halo[0], edges[3], halo[2]]
+        sums.append(partial)
+        args = [image, inline_dip, cross_dip, below, above, in_hbm(gathered), row7, ends]
+        places = [IN_VMEM] * 5 + [IN_HBM] + [IN_VMEM] * 2
         if step + 1 < ITERS:
-            image, *edges = call(
-                correct_kernel, [tile] + edge_shapes, image, inline_dip, cross_dip, *halo,
-                name="correct", aliases={0: 0},
+            image, across, *edges = call(
+                correct_kernel, [tile, f32(SUBLANES, LANES)] + edge_shapes, *args,
+                name="correct", aliases={0: 0}, ins=places, scratch=side,
             )
+            products.append(across)
         else:
-            image, parts = call(
-                moments_kernel, [tile, f32(devices, 1, LANES)], image, inline_dip, cross_dip, *halo, *products,
-                name="moments", aliases={0: 0},
+            image, message = call(
+                moments_kernel, [tile, jax.ShapeDtypeStruct((SUBLANES, LANES), jnp.float32)], *args, *sums, *products,
+                name="moments", aliases={0: 0}, ins=places + [IN_VMEM] * (2 * ITERS - 1), scratch=side,
             )
         fields.append(image)
-    parts = lax.all_to_all(parts, ("inl", "xl"), split_axis=0, concat_axis=0, tiled=True)
+    parts = lax.all_gather(message, ("inl", "xl"))
     out = jax.ShapeDtypeStruct((rows, cols, samples), jnp.float32)
     return tuple(
         call(

time: 100 us -> 178 us (1.78)
  blocking collectives: 36.5 us -> 132 us
  starting transfers between devices: 32.8 us -> 13.9 us
    all_gather x0 -> x4, blocking collectives: none -> 108 us  [the longest x1 65.2 us: per_device(): parts = lax.all_gather(message, ('inl', 'xl'))]
    ppermute x12 -> x6, starting transfers between devices: 32.8 us -> 13.9 us  [shifted(): lax.ppermute(value, axis, [(source, source + steps) for source in range(i...]
    all_to_all x1 -> x0, blocking collectives: 12.5 us -> none  [per_device(): lax.all_to_all(parts, ('inl', 'xl'), split_axis=0, concat_axis=0, tiled=T...]
  transfers between devices with their start and end apart: 12 -> 6, of which waited for: 0 -> 0; matrix products, arithmetic and copies ran while one was open for 0% -> 0% of each run, Pallas kernels for 22% -> 12%
where the time goes in v4:
time: 178 us; the launch traced here: 177 us
  blocking collectives  132 us (74%)
  Pallas kernels  30.5 us (17%)
  starting transfers between devices  13.9 us (8%)
    all_gather x1, blocking collectives, per_device(): parts = lax.all_gather(message, ('inl', 'xl'))  65.2 us
    all_gather x3, blocking collectives, per_device(): gathered = lax.all_gather(ends, 'xl')  42.8 us
    pallas_call x9, Pallas kernels, call(): pl.pallas_call(kernel, out_shape=outs, in_specs=ins or [IN_VMEM] * len(ar...  30.5 us
    all_to_all x1, blocking collectives, per_device(): lax.all_to_all(sent, ('inl', 'xl'), split_axis=0, concat_axis=0, tiled=True)  24 us
    ppermute x6, starting transfers between devices, shifted(): lax.ppermute(value, axis, [(source, source + steps) for source in range(i...  13.9 us
  transfers between devices with their start and end apart: 6, of which 0 were waited for; matrix products, arithmetic and copies ran while one was open for 0% of the time, Pallas kernels for 12%

profile of v4, /device:TPU:0, one launch (start us, length us, event | category | flops | bytes accessed | tf_op | source)
XLA Modules:
  0.0 177.2 jit_solution(5987495111689176433)
XLA Ops:
  0.6 0.0 copy-start.1
  0.6 1.5 pack.1
  2.2 0.0 copy-start
  2.2 24.0 %all_to_all.11 = bf16[32,16,640]{2,1,0:T(8,128)(2,1)S(1)} all-to-all(bf16[32,16,640]{2,1,0:T(8,128)(2,1)S(1)} %bitcast.10), channel_id=1, replica_groups=mesh['inl'=8,'xl'=4] {'inl','xl'}, dimensions={0} | all-to-all | bytes 1310720 | tf_op jit(solution)/shard_map/all_to_all | solution.py:412
  26.2 1.3 bin.1
  27.5 1.3 collective-permute-start
  28.8 3.9 %collective-permute-start.1 = (f32[128,512]{1,0:T(8,128)S(1)}, f32[128,512]{1,0:T(8,128)S(1)}, u32[]{:S(2)}, u32[]{:S(2)}) collective-permute-start(f32[128,512]{1,0:T(8,128)S(1)} %get-tuple-element.35.row7_ref), channel_id=1, source_target_pairs={{0,4},{4,8},{8,12},{12,16},{16,20},{20,24},{24,28},{1,5},{5,9},{9,... | collective-permute-start | bytes 786440 | tf_op jit(solution)/shard_map/ppermute | solution.py:23
  32.8 0.0 copy-done.1
  32.8 0.0 copy-done
  32.8 7.2 %apply.3 = (f32[8,4,128,128]{3,2,1,0:T(8,128)S(1)}, f32[2,8,128]{2,1,0:T(8,128)S(1)}) custom-call(f32[8,4,128,128]{3,2,1,0:T(8,128)S(1)} %get-tuple-element.31.v_ref.b_ref, f32[8,128,512]{2,1,0:T(8,128)S(1)} %copy-done, f32[8,128,512]{2,1,0:T(8,128)S(1)} %copy-done.1, f32[8,128,128]{2,1,0:T(8,128)S(1)} %get-tuple-element.32.diag_ref), custom_call_target="tpu_custom_call" | custom-call | flops 31457280 | bytes 8388608 | tf_op jit(solution)/shard_map/apply/pallas_call | solution.py:376
  40.0 14.3 %all-gather = f32[8,8,512]{2,1,0:T(8,128)} all-gather(f32[2,8,512]{2,1,0:T(8,128)S(1)} %get-tuple-element.36.ends_ref), channel_id=2, replica_groups=mesh['inl'=8,'xl'=4] {'xl'}, dimensions={0}, use_global_device_ids=true | all-gather | bytes 163840 | tf_op jit(solution)/shard_map/all_gather | solution.py:425
  54.3 0.0 collective-permute-done.below_ref
  54.3 0.0 collective-permute-done.1.above_ref
  54.3 1.3 correct.2
  55.6 1.3 collective-permute-start.2
  56.9 3.0 %collective-permute-start.3 = (f32[128,512]{1,0:T(8,128)S(1)}, f32[128,512]{1,0:T(8,128)S(1)}, u32[]{:S(2)}, u32[]{:S(2)}) collective-permute-start(f32[128,512]{1,0:T(8,128)S(1)} %get-tuple-element.40.row7_ref), channel_id=1, source_target_pairs={{0,4},{4,8},{8,12},{12,16},{16,20},{20,24},{24,28},{1,5},{5,9},{9,... | collective-permute-start | bytes 786440 | tf_op jit(solution)/shard_map/ppermute | solution.py:23
  60.0 7.2 %apply.4 = (f32[8,4,128,128]{3,2,1,0:T(8,128)S(1)}, f32[2,8,128]{2,1,0:T(8,128)S(1)}) custom-call(f32[8,4,128,128]{3,2,1,0:T(8,128)S(1)} %get-tuple-element.37.v_ref.v1_ref, f32[8,128,512]{2,1,0:T(8,128)S(1)} %copy-done, f32[8,128,512]{2,1,0:T(8,128)S(1)} %copy-done.1, f32[8,128,128]{2,1,0:T(8,128)S(1)} %get-tuple-element.32.diag_ref), custom_call_target="tpu_custom_call" | custom-call | flops 31457280 | bytes 8388608 | tf_op jit(solution)/shard_map/apply/pallas_call | solution.py:376
  67.2 14.2 %all-gather.1 = f32[8,8,512]{2,1,0:T(8,128)} all-gather(f32[2,8,512]{2,1,0:T(8,128)S(1)} %get-tuple-element.41.ends_ref), channel_id=3, replica_groups=mesh['inl'=8,'xl'=4] {'xl'}, dimensions={0}, use_global_device_ids=true | all-gather | bytes 163840 | tf_op jit(solution)/shard_map/all_gather | solution.py:425
  81.4 0.0 collective-permute-done.2.below_ref
  81.4 0.0 collective-permute-done.3.above_ref
  81.4 1.3 correct.3
  82.7 1.3 collective-permute-start.4
  84.0 3.0 %collective-permute-start.5 = (f32[128,512]{1,0:T(8,128)S(1)}, f32[128,512]{1,0:T(8,128)S(1)}, u32[]{:S(2)}, u32[]{:S(2)}) collective-permute-start(f32[128,512]{1,0:T(8,128)S(1)} %get-tuple-element.45.row7_ref), channel_id=1, source_target_pairs={{0,4},{4,8},{8,12},{12,16},{16,20},{20,24},{24,28},{1,5},{5,9},{9,... | collective-permute-start | bytes 786440 | tf_op jit(solution)/shard_map/ppermute | solution.py:23
  87.1 7.2 %apply.5 = (f32[8,4,128,128]{3,2,1,0:T(8,128)S(1)}, f32[2,8,128]{2,1,0:T(8,128)S(1)}) custom-call(f32[8,4,128,128]{3,2,1,0:T(8,128)S(1)} %get-tuple-element.42.v_ref.v2_ref, f32[8,128,512]{2,1,0:T(8,128)S(1)} %copy-done, f32[8,128,512]{2,1,0:T(8,128)S(1)} %copy-done.1, f32[8,128,128]{2,1,0:T(8,128)S(1)} %get-tuple-element.32.diag_ref), custom_call_target="tpu_custom_call" | custom-call | flops 31457280 | bytes 8388608 | tf_op jit(solution)/shard_map/apply/pallas_call | solution.py:376
  94.3 14.2 %all-gather.2 = f32[8,8,512]{2,1,0:T(8,128)} all-gather(f32[2,8,512]{2,1,0:T(8,128)S(1)} %get-tuple-element.46.ends_ref), channel_id=4, replica_groups=mesh['inl'=8,'xl'=4] {'xl'}, dimensions={0}, use_global_device_ids=true | all-gather | bytes 163840 | tf_op jit(solution)/shard_map/all_gather | solution.py:425
  108.6 0.0 collective-permute-done.4.below_ref
  108.6 0.0 collective-permute-done.5.above_ref
  108.6 1.1 moments.1
  109.7 65.2 %all-gather.3 = f32[256,128]{1,0:T(8,128)S(1)} all-gather(f32[8,128]{1,0:T(8,128)S(1)} %get-tuple-element.52), channel_id=5, replica_groups=mesh['inl'=8,'xl'=4] {'inl','xl'}, dimensions={0}, use_global_device_ids=true | all-gather | bytes 135168 | tf_op jit(solution)/shard_map/all_gather | solution.py:454
  174.8 2.4 %finish.1 = (f32[8,128,512]{2,1,0:T(8,128)}, f32[8,128,512]{2,1,0:T(8,128)}) custom-call(f32[32,8,128]{2,1,0:T(8,128)S(1)} %bitcast.11, f32[8,4,128,128]{3,2,1,0:T(8,128)S(1)} %get-tuple-element.31.v_ref.b_ref, f32[8,4,128,128]{3,2,1,0:T(8,128)S(1)} %get-tuple-element.37.v_ref.v1_ref, f32[8,4,128,128]{3,2,1,0:T(8,128)S(1)} %get-tuple-element.42.v_ref.v2_ref, ...), custom_call_target="tpu_custom_call" | custom-call | tf_op jit(solution)/shard_map/finish/pallas_call | solution.py:376
Async XLA Ops:
  0.6 32.2 %copy-start.1 = (f32[8,128,512]{2,1,0:T(8,128)S(1)}, f32[8,128,512]{2,1,0:T(8,128)}, u32[]{:S(2)}) copy-start(f32[8,128,512]{2,1,0:T(8,128)} %p2_ref.11) | copy-start | bytes 6291460
  2.2 30.6 %copy-start = (f32[8,128,512]{2,1,0:T(8,128)S(1)}, f32[8,128,512]{2,1,0:T(8,128)}, u32[]{:S(2)}) copy-start(f32[8,128,512]{2,1,0:T(8,128)} %p1_ref.11) | copy-start | bytes 6291460
  27.5 26.8 %collective-permute-start = (f32[128,512]{1,0:T(8,128)S(1)}, f32[128,512]{1,0:T(8,128)S(1)}, u32[]{:S(2)}, u32[]{:S(2)}) collective-permute-start(f32[128,512]{1,0:T(8,128)S(1)} %get-tuple-element.34), channel_id=1, source_target_pairs={{4,0},{8,4},{12,8},{16,12},{20,16},{24,20},{28,24},{5,1},{9,5},{13... | collective-permute-start | bytes 786440 | tf_op jit(solution)/shard_map/ppermute | solution.py:23
  28.8 25.5 %collective-permute-start.1 = (f32[128,512]{1,0:T(8,128)S(1)}, f32[128,512]{1,0:T(8,128)S(1)}, u32[]{:S(2)}, u32[]{:S(2)}) collective-permute-start(f32[128,512]{1,0:T(8,128)S(1)} %get-tuple-element.35.row7_ref), channel_id=1, source_target_pairs={{0,4},{4,8},{8,12},{12,16},{16,20},{20,24},{24,28},{1,5},{5,9},{9,... | collective-permute-start | bytes 786440 | tf_op jit(solution)/shard_map/ppermute | solution.py:23
  55.6 25.8 %collective-permute-start.2 = (f32[128,512]{1,0:T(8,128)S(1)}, f32[128,512]{1,0:T(8,128)S(1)}, u32[]{:S(2)}, u32[]{:S(2)}) collective-permute-start(f32[128,512]{1,0:T(8,128)S(1)} %get-tuple-element.39), channel_id=1, source_target_pairs={{4,0},{8,4},{12,8},{16,12},{20,16},{24,20},{28,24},{5,1},{9,5},{13... | collective-permute-start | bytes 786440 | tf_op jit(solution)/shard_map/ppermute | solution.py:23
  56.9 24.5 %collective-permute-start.3 = (f32[128,512]{1,0:T(8,128)S(1)}, f32[128,512]{1,0:T(8,128)S(1)}, u32[]{:S(2)}, u32[]{:S(2)}) collective-permute-start(f32[128,512]{1,0:T(8,128)S(1)} %get-tuple-element.40.row7_ref), channel_id=1, source_target_pairs={{0,4},{4,8},{8,12},{12,16},{16,20},{20,24},{24,28},{1,5},{5,9},{9,... | collective-permute-start | bytes 786440 | tf_op jit(solution)/shard_map/ppermute | solution.py:23
  82.7 25.8 %collective-permute-start.4 = (f32[128,512]{1,0:T(8,128)S(1)}, f32[128,512]{1,0:T(8,128)S(1)}, u32[]{:S(2)}, u32[]{:S(2)}) collective-permute-start(f32[128,512]{1,0:T(8,128)S(1)} %get-tuple-element.44), channel_id=1, source_target_pairs={{4,0},{8,4},{12,8},{16,12},{20,16},{24,20},{28,24},{5,1},{9,5},{13... | collective-permute-start | bytes 786440 | tf_op jit(solution)/shard_map/ppermute | solution.py:23
  84.0 24.5 %collective-permute-start.5 = (f32[128,512]{1,0:T(8,128)S(1)}, f32[128,512]{1,0:T(8,128)S(1)}, u32[]{:S(2)}, u32[]{:S(2)}) collective-permute-start(f32[128,512]{1,0:T(8,128)S(1)} %get-tuple-element.45.row7_ref), channel_id=1, source_target_pairs={{0,4},{4,8},{8,12},{12,16},{16,20},{20,24},{24,28},{1,5},{5,9},{9,... | collective-permute-start | bytes 786440 | tf_op jit(solution)/shard_map/ppermute | solution.py:23

commit v5 on v4

--- a/solution.py
+++ b/solution.py
@@ -10,6 +10,7 @@
 ITERS = 3
 LANES = 128
 SUBLANES = 8
+GROUP = 32
 
 SHIFT = 6.0
 IN_VMEM = pl.BlockSpec(memory_space=pltpu.VMEM)
@@ -136,7 +137,7 @@
         copy.wait()
 
 
-def bin_kernel(got_ref, p1_ref, p2_ref, b_ref, diag_ref, row0_ref, row7_ref, ends_ref):
+def bin_kernel(got_ref, p1_ref, p2_ref, b_ref, diag_ref, *edge_refs):
     rows, tiles, cols, _ = b_ref.shape
     samples = tiles * LANES
     slots = got_ref.shape[0]
@@ -160,11 +161,11 @@
         diag = 2.0 * hits + first_col
         diag_ref[i] = diag + not_first_row if i == 0 else diag
     write_edges(
-        b_ref, lambda at: load(p1_ref, at), lambda i: load(p2_ref, i, slice(None)), row0_ref, row7_ref, ends_ref
-    )
-
-
-def write_edges(v_ref, p1_last_row, p2_last_cols, row0_ref, row7_ref, ends_ref):
+        b_ref, lambda at: load(p1_ref, at), lambda i: load(p2_ref, i, slice(None)), *edge_refs
+    )
+
+
+def write_edges(v_ref, p1_last_row, p2_last_cols, row0_ref, row7_ref, col0_ref, col7_ref):
     rows, _, cols, _ = v_ref.shape
     for x in range(0, cols, SUBLANES):
         at = slice(x, x + SUBLANES)
@@ -172,10 +173,10 @@
         v = load_field(v_ref, rows - 1, at)
         store(row7_ref, add(v, dip_part(p1_last_row(at), *stencil(v))), at)
     for i in range(rows):
-        store(ends_ref, load_field(v_ref, i, slice(0, 1)), 0, slice(i, i + 1))
+        store(col0_ref, load_field(v_ref, i, slice(0, 1)), slice(i, i + 1))
         v = load_field(v_ref, i, slice(cols - SUBLANES, cols))
         moved = add(v, dip_part(p2_last_cols(i), *stencil(v)))
-        store(ends_ref, [t[SUBLANES - 1 :] for t in moved], 1, slice(i, i + 1))
+        store(col7_ref, [t[SUBLANES - 1 :] for t in moved], slice(i, i + 1))
 
 
 def apply_kernel(v_ref, p1_ref, p2_ref, diag_ref, out_ref, sums_ref, first_ref, second_ref):
@@ -183,15 +184,16 @@
     sub_index = iota((SUBLANES, LANES), 0)
     zero = [jnp.zeros((SUBLANES, LANES), jnp.float32)] * tiles
     first_ref[...] = jnp.zeros_like(first_ref)
-    for c in range(tiles):
-        second_ref[c, :SUBLANES, :] = zero[0]
-
-    def row(i, sums, last):
-        v_row, out_row, diag_row = v_ref.at[i], out_ref.at[i], diag_ref.at[i]
+    for i in range(rows):
+        for c in range(tiles):
+            second_ref[i, c, :SUBLANES, :] = zero[0]
+
+    def body(i, sums, group, last):
+        v_row, out_row, diag_row, second_row = v_ref.at[i], out_ref.at[i], diag_ref.at[i], second_ref.at[i]
         p1_row, p2_row = p1_ref.at[i], p2_ref.at[i]
         below_row = None if last else v_ref.at[i + 1]
         vout, vv = zero[0], zero[0]
-        for x in range(0, cols, SUBLANES):
+        for x in range(group, group + GROUP, SUBLANES):
             at = slice(x, x + SUBLANES)
             v = load_tiles(v_row, at)
             if x + SUBLANES < cols:
@@ -204,11 +206,11 @@
             first = sub(sub(below, v), dip_part(p1, odd, even))
             second = sub(sub(right, v), dip_part(p2, odd, even))
             for c in range(tiles):
-                second_ref[c, x + SUBLANES : x + 2 * SUBLANES, :] = second[c]
+                second_row[c, x + SUBLANES : x + 2 * SUBLANES, :] = second[c]
             a1, b1 = adjoint_terms(p1, first)
             a2, b2 = adjoint_terms(p2, second)
             moved = adjoint_finish(add(first, second), add(a1, a2), add(b1, b2))
-            left = [second_ref[c, x + SUBLANES - 1 : x + 2 * SUBLANES - 1, :] for c in range(tiles)]
+            left = [second_row[c, x + SUBLANES - 1 : x + 2 * SUBLANES - 1, :] for c in range(tiles)]
             above = load(first_ref, at)
             store(first_ref, first, at)
             diag = diag_row[at, :]
@@ -219,8 +221,14 @@
             vv = vv + dot(v, v)
         return sums[0] + vout, sums[1] + vv
 
-    sums = lax.fori_loop(0, rows - 1, lambda i, sums: row(i, sums, False), (zero[0], zero[0]))
-    sums_ref[0], sums_ref[1] = row(rows - 1, sums, True)
+    total = (zero[0], zero[0])
+    for group in range(0, cols, GROUP):
+        sums = lax.fori_loop(
+            0, rows - 1, functools.partial(body, group=group, last=False), (zero[0], zero[0])
+        )
+        sums = body(rows - 1, sums, group, True)
+        total = (total[0] + sums[0], total[1] + sums[1])
+    sums_ref[0], sums_ref[1] = total
 
 
 def halo_corrections(out_ref, p1_ref, p2_ref, below_ref, above_ref, right_ref, left_ref):
@@ -243,52 +251,39 @@
         store_field(out_ref, sub(load_field(out_ref, i, at), moved), i, at)
 
 
-def settle(image_ref, p1_ref, p2_ref, below_ref, above_ref, gathered_hbm, row7_ref, ends_ref, out_ref, side_ref, sems):
-    here, count = lax.axis_index("xl"), lax.axis_size("xl")
-    copies = (
-        pltpu.make_async_copy(gathered_hbm.at[jnp.minimum(here + 1, count - 1), 0], side_ref.at[0], sems.at[0]),
-        pltpu.make_async_copy(gathered_hbm.at[jnp.maximum(here - 1, 0), 1], side_ref.at[1], sems.at[1]),
-    )
-    for copy in copies:
-        copy.start()
+def settle(image_ref, p1_ref, p2_ref, below_ref, above_ref, right_ref, left_ref, row7_ref, col7_ref, out_ref):
     across = jnp.zeros((SUBLANES, LANES), jnp.float32)
-    for x in range(0, row7_ref.shape[0], SUBLANES):
-        at = slice(x, x + SUBLANES)
-        across = across + dot(load(row7_ref, at), load(below_ref, at))
-    for copy in copies:
-        copy.wait()
-    side_ref[0] = jnp.where(here + 1 < count, side_ref[0], 0.0)
-    side_ref[1] = jnp.where(here > 0, side_ref[1], 0.0)
-    for x in range(0, ends_ref.shape[1], SUBLANES):
-        at = slice(x, x + SUBLANES)
-        across = across + dot(load(ends_ref, 1, at), load(side_ref, 0, at))
-    halo_corrections(out_ref, p1_ref, p2_ref, below_ref, above_ref, side_ref.at[0], side_ref.at[1])
+    for mine, theirs in ((row7_ref, below_ref), (col7_ref, right_ref)):
+        for x in range(0, mine.shape[0], SUBLANES):
+            at = slice(x, x + SUBLANES)
+            across = across + dot(load(mine, at), load(theirs, at))
+    halo_corrections(out_ref, p1_ref, p2_ref, below_ref, above_ref, right_ref, left_ref)
     return across
 
 
 def correct_kernel(
-    image_ref, p1_ref, p2_ref, below_ref, above_ref, gathered_hbm, row7_ref, ends_ref,
-    out_ref, across_ref, next_row0_ref, next_row7_ref, next_ends_ref, side_ref, sems,
+    image_ref, p1_ref, p2_ref, below_ref, above_ref, right_ref, left_ref, row7_ref, col7_ref,
+    out_ref, across_ref, *edge_refs,
 ):
     across_ref[...] = settle(
-        image_ref, p1_ref, p2_ref, below_ref, above_ref, gathered_hbm, row7_ref, ends_ref, out_ref, side_ref, sems
+        image_ref, p1_ref, p2_ref, below_ref, above_ref, right_ref, left_ref, row7_ref, col7_ref, out_ref
     )
     rows, _, cols, _ = out_ref.shape
     write_edges(
         out_ref,
         lambda at: load(p1_ref, rows - 1, at),
         lambda i: load(p2_ref, i, slice(cols - SUBLANES, cols)),
-        next_row0_ref, next_row7_ref, next_ends_ref,
+        *edge_refs,
     )
 
 
 def moments_kernel(
-    image_ref, p1_ref, p2_ref, below_ref, above_ref, gathered_hbm, row7_ref, ends_ref, *refs
+    image_ref, p1_ref, p2_ref, below_ref, above_ref, right_ref, left_ref, row7_ref, col7_ref, *refs
 ):
     sums_refs, across_refs = refs[:ITERS], refs[ITERS : 2 * ITERS - 1]
-    out_ref, message_ref, side_ref, sems = refs[2 * ITERS - 1 :]
+    out_ref, message_ref = refs[2 * ITERS - 1 :]
     final = settle(
-        image_ref, p1_ref, p2_ref, below_ref, above_ref, gathered_hbm, row7_ref, ends_ref, out_ref, side_ref, sems
+        image_ref, p1_ref, p2_ref, below_ref, above_ref, right_ref, left_ref, row7_ref, col7_ref, out_ref
     )
     m = []
     for sums_ref, across in zip(sums_refs, [ref[...] for ref in across_refs] + [final]):
@@ -300,7 +295,7 @@
         block = jnp.where(sub_index == k, jnp.sum(part, axis=0, keepdims=True), block)
     total = jnp.sum(block, axis=1, keepdims=True)
     line = jnp.sum(jnp.where(sub_index == lane, total, 0.0), axis=0, keepdims=True)
-    message_ref[...] = jnp.broadcast_to(line, message_ref.shape)
+    message_ref[...] = jnp.broadcast_to(line[None], message_ref.shape)
 
 
 def coefficients(m):
@@ -334,7 +329,7 @@
 
 def finish_kernel(parts_ref, b_ref, v1_ref, v2_ref, v3_ref, model_hbm, residual_hbm, model_ref, residual_ref, sems):
     rows, _, cols, _ = b_ref.shape
-    line = jnp.sum(parts_ref[...], axis=0)[:1]
+    line = jnp.sum(parts_ref[...], axis=0)
     sub_index, lane = iota((SUBLANES, LANES), 0), iota((SUBLANES, LANES), 1)
     total = jnp.sum(jnp.where(sub_index == lane, line, 0.0), axis=1, keepdims=True)
     total = jnp.broadcast_to(total, (SUBLANES, LANES))
@@ -410,7 +405,7 @@
         scratch=[small, small, small, pltpu.VMEM((held, samples), jnp.bfloat16), pltpu.SemaphoreType.DMA((6,))],
     )
     got = lax.all_to_all(sent, ("inl", "xl"), split_axis=0, concat_axis=0, tiled=True)
-    edge_shapes = [f32(cols, samples), f32(cols, samples), jax.ShapeDtypeStruct((2, rows, samples), jnp.float32)]
+    edge_shapes = [f32(cols, samples), f32(cols, samples), f32(rows, samples), f32(rows, samples)]
     tile = f32(rows, samples // LANES, cols, LANES)
     b, diag, *edges = call(
         bin_kernel, [tile, f32(rows, cols, LANES)] + edge_shapes, got, p1_last, p2_last, name="bin"
@@ -419,12 +414,12 @@
     cost = pl.CostEstimate(
         flops=60 * rows * cols * samples, bytes_accessed=16 * rows * cols * samples, transcendentals=0
     )
-    side = [pltpu.VMEM((2, rows, samples), jnp.float32), pltpu.SemaphoreType.DMA((2,))]
     for step in range(ITERS):
-        row0, row7, ends = edges
-        gathered = lax.all_gather(ends, "xl")
+        row0, row7, col0, col7 = edges
         below = shifted(row0, "inl", -1)
         above = shifted(row7, "inl", 1)
+        right = shifted(col0, "xl", -1)
+        left = shifted(col7, "xl", 1)
         image, partial = call(
             apply_kernel,
             [tile, f32(2, SUBLANES, LANES)],
@@ -432,26 +427,24 @@
             name="apply",
             scratch=[
                 pltpu.VMEM((cols, samples), jnp.float32),
-                pltpu.VMEM((samples // LANES, SUBLANES + cols, LANES), jnp.float32),
+                pltpu.VMEM((rows, samples // LANES, SUBLANES + cols, LANES), jnp.float32),
             ],
             cost=cost,
         )
         sums.append(partial)
-        args = [image, inline_dip, cross_dip, below, above, in_hbm(gathered), row7, ends]
-        places = [IN_VMEM] * 5 + [IN_HBM] + [IN_VMEM] * 2
+        args = [image, inline_dip, cross_dip, below, above, right, left, row7, col7]
         if step + 1 < ITERS:
             image, across, *edges = call(
-                correct_kernel, [tile, f32(SUBLANES, LANES)] + edge_shapes, *args,
-                name="correct", aliases={0: 0}, ins=places, scratch=side,
+                correct_kernel, [tile, f32(SUBLANES, LANES)] + edge_shapes, *args, name="correct", aliases={0: 0}
             )
             products.append(across)
         else:
             image, message = call(
-                moments_kernel, [tile, jax.ShapeDtypeStruct((SUBLANES, LANES), jnp.float32)], *args, *sums, *products,
-                name="moments", aliases={0: 0}, ins=places + [IN_VMEM] * (2 * ITERS - 1), scratch=side,
+                moments_kernel, [tile, f32(devices, 1, LANES)], *args, *sums, *products,
+                name="moments", aliases={0: 0},
             )
         fields.append(image)
-    parts = lax.all_gather(message, ("inl", "xl"))
+    parts = lax.all_to_all(message, ("inl", "xl"), split_axis=0, concat_axis=0, tiled=True)
     out = jax.ShapeDtypeStruct((rows, cols, samples), jnp.float32)
     return tuple(
         call(

time: 178 us -> 98.8 us (0.56)
  blocking collectives: 132 us -> 36.5 us
  starting transfers between devices: 13.9 us -> 32.8 us
  Pallas kernels: 30.5 us -> 28.2 us
    all_gather x4 -> x0, blocking collectives: 108 us -> none  [the longest x1 65.2 us: per_device(): parts = lax.all_gather(message, ('inl', 'xl'))]
    ppermute x6 -> x12, starting transfers between devices: 13.9 us -> 32.8 us  [shifted(): lax.ppermute(value, axis, [(source, source + steps) for source in range(i...]
    all_to_all x0 -> x1, blocking collectives: none -> 12.5 us  [per_device(): lax.all_to_all(message, ('inl', 'xl'), split_axis=0, concat_axis=0, tiled...]
    pallas_call x9, Pallas kernels: 30.5 us -> 28.2 us  [call(): pl.pallas_call(kernel, out_shape=outs, in_specs=ins or [IN_VMEM] * len(ar...]
  transfers between devices with their start and end apart: 6 -> 12, of which waited for: 0 -> 0; matrix products, arithmetic and copies ran while one was open for 0% -> 0% of each run, Pallas kernels for 12% -> 22%
where the time goes in v5:
time: 98.8 us; the launch traced here: 98.4 us
  blocking collectives  36.5 us (37%)
  starting transfers between devices  32.8 us (33%)
  Pallas kernels  28.2 us (29%)
    ppermute x12, starting transfers between devices, shifted(): lax.ppermute(value, axis, [(source, source + steps) for source in range(i...  32.8 us
    pallas_call x9, Pallas kernels, call(): pl.pallas_call(kernel, out_shape=outs, in_specs=ins or [IN_VMEM] * len(ar...  28.2 us
    all_to_all x1, blocking collectives, per_device(): lax.all_to_all(sent, ('inl', 'xl'), split_axis=0, concat_axis=0, tiled=True)  24 us
    all_to_all x1, blocking collectives, per_device(): lax.all_to_all(message, ('inl', 'xl'), split_axis=0, concat_axis=0, tiled...  12.5 us
  transfers between devices with their start and end apart: 12, of which 0 were waited for; matrix products, arithmetic and copies ran while one was open for 0% of the time, Pallas kernels for 22%

profile of v5, /device:TPU:0, one launch (start us, length us, event | category | flops | bytes accessed | tf_op | source)
XLA Modules:
  0.0 98.4 jit_solution(12160242333862813400)
XLA Ops:
  0.6 0.0 copy-start.1
  0.6 1.5 %pack.1 = (bf16[512,640]{1,0:T(8,128)(2,1)S(1)}, f32[128,512]{1,0:T(8,128)S(1)}, f32[8,8,512]{2,1,0:T(8,128)S(1)}) custom-call(s32[1,256]{1,0:T(1,128)} %bitcast.7, s32[1,256]{1,0:T(1,128)} %bitcast.8, s32[1,256]{1,0:T(1,128)} %bitcast.9, bf16[256,512]{1,0:T(8,128)(2,1)} %traces_hbm.1, f32[8,128,512]{2,1,0:T(8,128)} %p1_ref.11, f32[8,128,512]{2,1,0:T(8,128)} %p2_ref.11), custom_call_target="tpu_custom_call" | custom-call | tf_op jit(solution)/shard_map/pack/pallas_call | solution.py:371
  2.2 0.0 copy-start
  2.2 24.0 %all_to_all.16 = bf16[32,16,640]{2,1,0:T(8,128)(2,1)S(1)} all-to-all(bf16[32,16,640]{2,1,0:T(8,128)(2,1)S(1)} %bitcast.6), channel_id=1, replica_groups=mesh['inl'=8,'xl'=4] {'inl','xl'}, dimensions={0} | all-to-all | bytes 1310720 | tf_op jit(solution)/shard_map/all_to_all | solution.py:407
  26.2 1.3 %bin.1 = (f32[8,4,128,128]{3,2,1,0:T(8,128)S(1)}, f32[8,128,128]{2,1,0:T(8,128)S(1)}, f32[128,512]{1,0:T(8,128)S(1)}, f32[128,512]{1,0:T(8,128)S(1)}, f32[8,512]{1,0:T(8,128)S(1)}, /*index=5*/f32[8,512]{1,0:T(8,128)S(1)}) custom-call(bf16[512,640]{1,0:T(8,128)(2,1)S(1)} %bitcast.5, f32[128,512]{1,0:T(8,128)S(1)} %get-tuple-element.32.p1_ref, ...), custom_call_target="tpu_custom_call" | custom-call | tf_op jit(solution)/shard_map/bin/pallas_call | solution.py:371
  27.5 1.3 %collective-permute-start = (f32[128,512]{1,0:T(8,128)S(1)}, f32[128,512]{1,0:T(8,128)S(1)}, u32[]{:S(2)}, u32[]{:S(2)}) collective-permute-start(f32[128,512]{1,0:T(8,128)S(1)} %get-tuple-element.37), channel_id=1, source_target_pairs={{4,0},{8,4},{12,8},{16,12},{20,16},{24,20},{28,24},{5,1},{9,5},{13... | collective-permute-start | bytes 786440 | tf_op jit(solution)/shard_map/ppermute | solution.py:24
  28.8 3.9 %collective-permute-start.1 = (f32[128,512]{1,0:T(8,128)S(1)}, f32[128,512]{1,0:T(8,128)S(1)}, u32[]{:S(2)}, u32[]{:S(2)}) collective-permute-start(f32[128,512]{1,0:T(8,128)S(1)} %get-tuple-element.38.row7_ref), channel_id=1, source_target_pairs={{0,4},{4,8},{8,12},{12,16},{16,20},{20,24},{24,28},{1,5},{5,9},{9,... | collective-permute-start | bytes 786440 | tf_op jit(solution)/shard_map/ppermute | solution.py:24
  32.8 1.3 %collective-permute-start.2 = (f32[8,512]{1,0:T(8,128)S(1)}, f32[8,512]{1,0:T(8,128)S(1)}, u32[]{:S(2)}, u32[]{:S(2)}) collective-permute-start(f32[8,512]{1,0:T(8,128)S(1)} %get-tuple-element.39), channel_id=1, source_target_pairs={{1,0},{2,1},{3,2},{5,4},{6,5},{7,6},{9,8},{10,9},{11,10},{13,12},{... | collective-permute-start | bytes 49160 | tf_op jit(solution)/shard_map/ppermute | solution.py:24
  34.1 4.5 %collective-permute-start.3 = (f32[8,512]{1,0:T(8,128)S(1)}, f32[8,512]{1,0:T(8,128)S(1)}, u32[]{:S(2)}, u32[]{:S(2)}) collective-permute-start(f32[8,512]{1,0:T(8,128)S(1)} %get-tuple-element.40.col7_ref), channel_id=1, source_target_pairs={{0,1},{1,2},{2,3},{4,5},{5,6},{6,7},{8,9},{9,10},{10,11},{12,13},{... | collective-permute-start | bytes 49160 | tf_op jit(solution)/shard_map/ppermute | solution.py:24
  38.6 0.0 copy-done.1
  38.6 0.0 copy-done
  38.7 7.1 %apply.3 = (f32[8,4,128,128]{3,2,1,0:T(8,128)S(1)}, f32[2,8,128]{2,1,0:T(8,128)S(1)}) custom-call(f32[8,4,128,128]{3,2,1,0:T(8,128)S(1)} %get-tuple-element.34.v_ref.b_ref, f32[8,128,512]{2,1,0:T(8,128)S(1)} %copy-done, f32[8,128,512]{2,1,0:T(8,128)S(1)} %copy-done.1, f32[8,128,128]{2,1,0:T(8,128)S(1)} %get-tuple-element.35.diag_ref), custom_call_target="tpu_custom_call" | custom-call | flops 31457280 | bytes 8388608 | tf_op jit(solution)/shard_map/apply/pallas_call | solution.py:371
  45.8 0.0 collective-permute-done.2.right_ref
  45.8 0.0 collective-permute-done.3.left_ref
  45.8 0.0 collective-permute-done.below_ref
  45.8 0.0 collective-permute-done.1.above_ref
  45.8 0.6 correct.2
  46.4 1.3 %collective-permute-start.4 = (f32[128,512]{1,0:T(8,128)S(1)}, f32[128,512]{1,0:T(8,128)S(1)}, u32[]{:S(2)}, u32[]{:S(2)}) collective-permute-start(f32[128,512]{1,0:T(8,128)S(1)} %get-tuple-element.43), channel_id=1, source_target_pairs={{4,0},{8,4},{12,8},{16,12},{20,16},{24,20},{28,24},{5,1},{9,5},{13... | collective-permute-start | bytes 786440 | tf_op jit(solution)/shard_map/ppermute | solution.py:24
  47.7 3.7 %collective-permute-start.5 = (f32[128,512]{1,0:T(8,128)S(1)}, f32[128,512]{1,0:T(8,128)S(1)}, u32[]{:S(2)}, u32[]{:S(2)}) collective-permute-start(f32[128,512]{1,0:T(8,128)S(1)} %get-tuple-element.44.row7_ref), channel_id=1, source_target_pairs={{0,4},{4,8},{8,12},{12,16},{16,20},{20,24},{24,28},{1,5},{5,9},{9,... | collective-permute-start | bytes 786440 | tf_op jit(solution)/shard_map/ppermute | solution.py:24
  51.4 1.3 %collective-permute-start.6 = (f32[8,512]{1,0:T(8,128)S(1)}, f32[8,512]{1,0:T(8,128)S(1)}, u32[]{:S(2)}, u32[]{:S(2)}) collective-permute-start(f32[8,512]{1,0:T(8,128)S(1)} %get-tuple-element.45), channel_id=1, source_target_pairs={{1,0},{2,1},{3,2},{5,4},{6,5},{7,6},{9,8},{10,9},{11,10},{13,12},{... | collective-permute-start | bytes 49160 | tf_op jit(solution)/shard_map/ppermute | solution.py:24
  52.7 4.5 %collective-permute-start.7 = (f32[8,512]{1,0:T(8,128)S(1)}, f32[8,512]{1,0:T(8,128)S(1)}, u32[]{:S(2)}, u32[]{:S(2)}) collective-permute-start(f32[8,512]{1,0:T(8,128)S(1)} %get-tuple-element.46.col7_ref), channel_id=1, source_target_pairs={{0,1},{1,2},{2,3},{4,5},{5,6},{6,7},{8,9},{9,10},{10,11},{12,13},{... | collective-permute-start | bytes 49160 | tf_op jit(solution)/shard_map/ppermute | solution.py:24
  57.3 7.1 %apply.4 = (f32[8,4,128,128]{3,2,1,0:T(8,128)S(1)}, f32[2,8,128]{2,1,0:T(8,128)S(1)}) custom-call(f32[8,4,128,128]{3,2,1,0:T(8,128)S(1)} %get-tuple-element.41.v_ref.v1_ref, f32[8,128,512]{2,1,0:T(8,128)S(1)} %copy-done, f32[8,128,512]{2,1,0:T(8,128)S(1)} %copy-done.1, f32[8,128,128]{2,1,0:T(8,128)S(1)} %get-tuple-element.35.diag_ref), custom_call_target="tpu_custom_call" | custom-call | flops 31457280 | bytes 8388608 | tf_op jit(solution)/shard_map/apply/pallas_call | solution.py:371
  64.4 0.0 collective-permute-done.6.right_ref
  64.4 0.0 collective-permute-done.7.left_ref
  64.4 0.0 collective-permute-done.4.below_ref
  64.4 0.0 collective-permute-done.5.above_ref
  64.4 0.5 correct.3
  65.0 1.3 %collective-permute-start.8 = (f32[128,512]{1,0:T(8,128)S(1)}, f32[128,512]{1,0:T(8,128)S(1)}, u32[]{:S(2)}, u32[]{:S(2)}) collective-permute-start(f32[128,512]{1,0:T(8,128)S(1)} %get-tuple-element.49), channel_id=1, source_target_pairs={{4,0},{8,4},{12,8},{16,12},{20,16},{24,20},{28,24},{5,1},{9,5},{13... | collective-permute-start | bytes 786440 | tf_op jit(solution)/shard_map/ppermute | solution.py:24
  66.3 3.7 %collective-permute-start.9 = (f32[128,512]{1,0:T(8,128)S(1)}, f32[128,512]{1,0:T(8,128)S(1)}, u32[]{:S(2)}, u32[]{:S(2)}) collective-permute-start(f32[128,512]{1,0:T(8,128)S(1)} %get-tuple-element.50.row7_ref), channel_id=1, source_target_pairs={{0,4},{4,8},{8,12},{12,16},{16,20},{20,24},{24,28},{1,5},{5,9},{9,... | collective-permute-start | bytes 786440 | tf_op jit(solution)/shard_map/ppermute | solution.py:24
  70.0 1.3 %collective-permute-start.10 = (f32[8,512]{1,0:T(8,128)S(1)}, f32[8,512]{1,0:T(8,128)S(1)}, u32[]{:S(2)}, u32[]{:S(2)}) collective-permute-start(f32[8,512]{1,0:T(8,128)S(1)} %get-tuple-element.51), channel_id=1, source_target_pairs={{1,0},{2,1},{3,2},{5,4},{6,5},{7,6},{9,8},{10,9},{11,10},{13,12},{... | collective-permute-start | bytes 49160 | tf_op jit(solution)/shard_map/ppermute | solution.py:24
  71.3 4.5 %collective-permute-start.11 = (f32[8,512]{1,0:T(8,128)S(1)}, f32[8,512]{1,0:T(8,128)S(1)}, u32[]{:S(2)}, u32[]{:S(2)}) collective-permute-start(f32[8,512]{1,0:T(8,128)S(1)} %get-tuple-element.52.col7_ref), channel_id=1, source_target_pairs={{0,1},{1,2},{2,3},{4,5},{5,6},{6,7},{8,9},{9,10},{10,11},{12,13},{... | collective-permute-start | bytes 49160 | tf_op jit(solution)/shard_map/ppermute | solution.py:24
  75.8 7.2 %apply.5 = (f32[8,4,128,128]{3,2,1,0:T(8,128)S(1)}, f32[2,8,128]{2,1,0:T(8,128)S(1)}) custom-call(f32[8,4,128,128]{3,2,1,0:T(8,128)S(1)} %get-tuple-element.47.v_ref.v2_ref, f32[8,128,512]{2,1,0:T(8,128)S(1)} %copy-done, f32[8,128,512]{2,1,0:T(8,128)S(1)} %copy-done.1, f32[8,128,128]{2,1,0:T(8,128)S(1)} %get-tuple-element.35.diag_ref), custom_call_target="tpu_custom_call" | custom-call | flops 31457280 | bytes 8388608 | tf_op jit(solution)/shard_map/apply/pallas_call | solution.py:371
  83.1 0.0 collective-permute-done.10.right_ref
  83.1 0.0 collective-permute-done.11.left_ref
  83.1 0.0 collective-permute-done.8.below_ref
  83.1 0.0 collective-permute-done.9.above_ref
  83.1 0.4 moments.1
  83.5 12.5 %all_to_all.17.parts_ref = f32[32,1,128]{2,1,0:T(1,128)S(1)} all-to-all(f32[32,1,128]{2,1,0:T(1,128)S(1)} %get-tuple-element.58), channel_id=1, replica_groups=mesh['inl'=8,'xl'=4] {'inl','xl'}, dimensions={0} | all-to-all | bytes 32768 | tf_op jit(solution)/shard_map/all_to_all | solution.py:447
  96.0 2.4 %finish.1 = (f32[8,128,512]{2,1,0:T(8,128)}, f32[8,128,512]{2,1,0:T(8,128)}) custom-call(f32[32,1,128]{2,1,0:T(1,128)S(1)} %all_to_all.17.parts_ref, f32[8,4,128,128]{3,2,1,0:T(8,128)S(1)} %get-tuple-element.34.v_ref.b_ref, f32[8,4,128,128]{3,2,1,0:T(8,128)S(1)} %get-tuple-element.41.v_ref.v1_ref, f32[8,4,128,128]{3,2,1,0:T(8,128)S(1)} %get-tuple-element.47.v_ref.v2_ref, ...), custom_call_target="tpu_custom_call" | custom-call | tf_op jit(solution)/shard_map/finish/pallas_call | solution.py:371
Async XLA Ops:
  0.6 38.0 %copy-start.1 = (f32[8,128,512]{2,1,0:T(8,128)S(1)}, f32[8,128,512]{2,1,0:T(8,128)}, u32[]{:S(2)}) copy-start(f32[8,128,512]{2,1,0:T(8,128)} %p2_ref.11) | copy-start | bytes 6291460
  2.2 36.5 %copy-start = (f32[8,128,512]{2,1,0:T(8,128)S(1)}, f32[8,128,512]{2,1,0:T(8,128)}, u32[]{:S(2)}) copy-start(f32[8,128,512]{2,1,0:T(8,128)} %p1_ref.11) | copy-start | bytes 6291460
  27.5 18.3 %collective-permute-start = (f32[128,512]{1,0:T(8,128)S(1)}, f32[128,512]{1,0:T(8,128)S(1)}, u32[]{:S(2)}, u32[]{:S(2)}) collective-permute-start(f32[128,512]{1,0:T(8,128)S(1)} %get-tuple-element.37), channel_id=1, source_target_pairs={{4,0},{8,4},{12,8},{16,12},{20,16},{24,20},{28,24},{5,1},{9,5},{13... | collective-permute-start | bytes 786440 | tf_op jit(solution)/shard_map/ppermute | solution.py:24
  28.8 17.0 %collective-permute-start.1 = (f32[128,512]{1,0:T(8,128)S(1)}, f32[128,512]{1,0:T(8,128)S(1)}, u32[]{:S(2)}, u32[]{:S(2)}) collective-permute-start(f32[128,512]{1,0:T(8,128)S(1)} %get-tuple-element.38.row7_ref), channel_id=1, source_target_pairs={{0,4},{4,8},{8,12},{12,16},{16,20},{20,24},{24,28},{1,5},{5,9},{9,... | collective-permute-start | bytes 786440 | tf_op jit(solution)/shard_map/ppermute | solution.py:24
  32.8 13.0 %collective-permute-start.2 = (f32[8,512]{1,0:T(8,128)S(1)}, f32[8,512]{1,0:T(8,128)S(1)}, u32[]{:S(2)}, u32[]{:S(2)}) collective-permute-start(f32[8,512]{1,0:T(8,128)S(1)} %get-tuple-element.39), channel_id=1, source_target_pairs={{1,0},{2,1},{3,2},{5,4},{6,5},{7,6},{9,8},{10,9},{11,10},{13,12},{... | collective-permute-start | bytes 49160 | tf_op jit(solution)/shard_map/ppermute | solution.py:24
  34.1 11.7 %collective-permute-start.3 = (f32[8,512]{1,0:T(8,128)S(1)}, f32[8,512]{1,0:T(8,128)S(1)}, u32[]{:S(2)}, u32[]{:S(2)}) collective-permute-start(f32[8,512]{1,0:T(8,128)S(1)} %get-tuple-element.40.col7_ref), channel_id=1, source_target_pairs={{0,1},{1,2},{2,3},{4,5},{5,6},{6,7},{8,9},{9,10},{10,11},{12,13},{... | collective-permute-start | bytes 49160 | tf_op jit(solution)/shard_map/ppermute | solution.py:24
  46.4 18.0 %collective-permute-start.4 = (f32[128,512]{1,0:T(8,128)S(1)}, f32[128,512]{1,0:T(8,128)S(1)}, u32[]{:S(2)}, u32[]{:S(2)}) collective-permute-start(f32[128,512]{1,0:T(8,128)S(1)} %get-tuple-element.43), channel_id=1, source_target_pairs={{4,0},{8,4},{12,8},{16,12},{20,16},{24,20},{28,24},{5,1},{9,5},{13... | collective-permute-start | bytes 786440 | tf_op jit(solution)/shard_map/ppermute | solution.py:24
  47.7 16.7 %collective-permute-start.5 = (f32[128,512]{1,0:T(8,128)S(1)}, f32[128,512]{1,0:T(8,128)S(1)}, u32[]{:S(2)}, u32[]{:S(2)}) collective-permute-start(f32[128,512]{1,0:T(8,128)S(1)} %get-tuple-element.44.row7_ref), channel_id=1, source_target_pairs={{0,4},{4,8},{8,12},{12,16},{16,20},{20,24},{24,28},{1,5},{5,9},{9,... | collective-permute-start | bytes 786440 | tf_op jit(solution)/shard_map/ppermute | solution.py:24
  51.4 13.0 %collective-permute-start.6 = (f32[8,512]{1,0:T(8,128)S(1)}, f32[8,512]{1,0:T(8,128)S(1)}, u32[]{:S(2)}, u32[]{:S(2)}) collective-permute-start(f32[8,512]{1,0:T(8,128)S(1)} %get-tuple-element.45), channel_id=1, source_target_pairs={{1,0},{2,1},{3,2},{5,4},{6,5},{7,6},{9,8},{10,9},{11,10},{13,12},{... | collective-permute-start | bytes 49160 | tf_op jit(solution)/shard_map/ppermute | solution.py:24
  52.7 11.7 %collective-permute-start.7 = (f32[8,512]{1,0:T(8,128)S(1)}, f32[8,512]{1,0:T(8,128)S(1)}, u32[]{:S(2)}, u32[]{:S(2)}) collective-permute-start(f32[8,512]{1,0:T(8,128)S(1)} %get-tuple-element.46.col7_ref), channel_id=1, source_target_pairs={{0,1},{1,2},{2,3},{4,5},{5,6},{6,7},{8,9},{9,10},{10,11},{12,13},{... | collective-permute-start | bytes 49160 | tf_op jit(solution)/shard_map/ppermute | solution.py:24
  65.0 18.1 %collective-permute-start.8 = (f32[128,512]{1,0:T(8,128)S(1)}, f32[128,512]{1,0:T(8,128)S(1)}, u32[]{:S(2)}, u32[]{:S(2)}) collective-permute-start(f32[128,512]{1,0:T(8,128)S(1)} %get-tuple-element.49), channel_id=1, source_target_pairs={{4,0},{8,4},{12,8},{16,12},{20,16},{24,20},{28,24},{5,1},{9,5},{13... | collective-permute-start | bytes 786440 | tf_op jit(solution)/shard_map/ppermute | solution.py:24
  66.3 16.9 %collective-permute-start.9 = (f32[128,512]{1,0:T(8,128)S(1)}, f32[128,512]{1,0:T(8,128)S(1)}, u32[]{:S(2)}, u32[]{:S(2)}) collective-permute-start(f32[128,512]{1,0:T(8,128)S(1)} %get-tuple-element.50.row7_ref), channel_id=1, source_target_pairs={{0,4},{4,8},{8,12},{12,16},{16,20},{20,24},{24,28},{1,5},{5,9},{9,... | collective-permute-start | bytes 786440 | tf_op jit(solution)/shard_map/ppermute | solution.py:24
  70.0 13.1 %collective-permute-start.10 = (f32[8,512]{1,0:T(8,128)S(1)}, f32[8,512]{1,0:T(8,128)S(1)}, u32[]{:S(2)}, u32[]{:S(2)}) collective-permute-start(f32[8,512]{1,0:T(8,128)S(1)} %get-tuple-element.51), channel_id=1, source_target_pairs={{1,0},{2,1},{3,2},{5,4},{6,5},{7,6},{9,8},{10,9},{11,10},{13,12},{... | collective-permute-start | bytes 49160 | tf_op jit(solution)/shard_map/ppermute | solution.py:24
  71.3 11.8 %collective-permute-start.11 = (f32[8,512]{1,0:T(8,128)S(1)}, f32[8,512]{1,0:T(8,128)S(1)}, u32[]{:S(2)}, u32[]{:S(2)}) collective-permute-start(f32[8,512]{1,0:T(8,128)S(1)} %get-tuple-element.52.col7_ref), channel_id=1, source_target_pairs={{0,1},{1,2},{2,3},{4,5},{5,6},{6,7},{8,9},{9,10},{10,11},{12,13},{... | collective-permute-start | bytes 49160 | tf_op jit(solution)/shard_map/ppermute | solution.py:24

commit v6 on v5

--- a/solution.py
+++ b/solution.py
@@ -10,7 +10,6 @@
 ITERS = 3
 LANES = 128
 SUBLANES = 8
-GROUP = 32
 
 SHIFT = 6.0
 IN_VMEM = pl.BlockSpec(memory_space=pltpu.VMEM)
@@ -179,56 +178,69 @@
         store(col7_ref, [t[SUBLANES - 1 :] for t in moved], slice(i, i + 1))
 
 
-def apply_kernel(v_ref, p1_ref, p2_ref, diag_ref, out_ref, sums_ref, first_ref, second_ref):
+def apply_kernel(v_ref, p1_ref, p2_ref, diag_ref, out_ref, sums_ref, second_ref):
     rows, tiles, cols, _ = v_ref.shape
     sub_index = iota((SUBLANES, LANES), 0)
     zero = [jnp.zeros((SUBLANES, LANES), jnp.float32)] * tiles
-    first_ref[...] = jnp.zeros_like(first_ref)
     for i in range(rows):
         for c in range(tiles):
             second_ref[i, c, :SUBLANES, :] = zero[0]
 
-    def body(i, sums, group, last):
-        v_row, out_row, diag_row, second_row = v_ref.at[i], out_ref.at[i], diag_ref.at[i], second_ref.at[i]
-        p1_row, p2_row = p1_ref.at[i], p2_ref.at[i]
-        below_row = None if last else v_ref.at[i + 1]
-        vout, vv = zero[0], zero[0]
-        for x in range(group, group + GROUP, SUBLANES):
-            at = slice(x, x + SUBLANES)
-            v = load_tiles(v_row, at)
-            if x + SUBLANES < cols:
-                right = load_tiles(v_row, slice(x + 1, x + 1 + SUBLANES))
-            else:
-                right = [jnp.where(sub_index == SUBLANES - 1, 0.0, pltpu.roll(t, SUBLANES - 1, 0)) for t in v]
-            below = zero if last else load_tiles(below_row, at)
-            p1, p2 = load(p1_row, at), load(p2_row, at)
-            odd, even = stencil(v)
-            first = sub(sub(below, v), dip_part(p1, odd, even))
-            second = sub(sub(right, v), dip_part(p2, odd, even))
-            for c in range(tiles):
-                second_row[c, x + SUBLANES : x + 2 * SUBLANES, :] = second[c]
-            a1, b1 = adjoint_terms(p1, first)
-            a2, b2 = adjoint_terms(p2, second)
-            moved = adjoint_finish(add(first, second), add(a1, a2), add(b1, b2))
-            left = [second_row[c, x + SUBLANES - 1 : x + 2 * SUBLANES - 1, :] for c in range(tiles)]
-            above = load(first_ref, at)
-            store(first_ref, first, at)
-            diag = diag_row[at, :]
-            out = [diag * c + ((f + s) - m) for c, f, s, m in zip(v, above, left, moved)]
-            for c in range(tiles):
-                out_row[c, at, :] = out[c]
-            vout = vout + dot(v, out)
-            vv = vv + dot(v, v)
-        return sums[0] + vout, sums[1] + vv
-
-    total = (zero[0], zero[0])
-    for group in range(0, cols, GROUP):
-        sums = lax.fori_loop(
-            0, rows - 1, functools.partial(body, group=group, last=False), (zero[0], zero[0])
-        )
-        sums = body(rows - 1, sums, group, True)
-        total = (total[0] + sums[0], total[1] + sums[1])
-    sums_ref[0], sums_ref[1] = total
+    def filters(i, x, v, shifted_v, above, below):
+        at = slice(x, x + SUBLANES)
+        v_row, second_row = v_ref.at[i], second_ref.at[i]
+        odd, even = shifted_v
+        p1, p2 = load(p1_ref.at[i], at), load(p2_ref.at[i], at)
+        if x + SUBLANES < cols:
+            right = load_tiles(v_row, slice(x + 1, x + 1 + SUBLANES))
+        else:
+            right = [jnp.where(sub_index == SUBLANES - 1, 0.0, pltpu.roll(t, SUBLANES - 1, 0)) for t in v]
+        first = sub(sub(below, v), dip_part(p1, odd, even))
+        second = sub(sub(right, v), dip_part(p2, odd, even))
+        for c in range(tiles):
+            second_row[c, x + SUBLANES : x + 2 * SUBLANES, :] = second[c]
+        left = [second_row[c, x + SUBLANES - 1 : x + 2 * SUBLANES - 1, :] for c in range(tiles)]
+        a1, b1 = adjoint_terms(p1, first)
+        a2, b2 = adjoint_terms(p2, second)
+        a, b = add(a1, a2), add(b1, b2)
+        diag = diag_ref.at[i][at, :]
+        rest = [
+            (diag * c + (f + s)) - ((f1 + s1) - (y + y))
+            for c, f, s, f1, s1, y in zip(v, above, left, first, second, b)
+        ]
+        return first, (rest, add(a, b), sub(b, a))
+
+    def adjoint(i, x, pending):
+        at = slice(x, x + SUBLANES)
+        rest, up, down = pending
+        out = [r - (u + d) for r, u, d in zip(rest, later(up), earlier(down))]
+        out_row = out_ref.at[i]
+        for c in range(tiles):
+            out_row[c, at, :] = out[c]
+        return dot(load_tiles(v_ref.at[i], at), out)
+
+    vout, vv = zero[0], zero[0]
+    for x in range(0, cols, SUBLANES):
+        at = slice(x, x + SUBLANES)
+        v = load_tiles(v_ref.at[0], at)
+        below = load_tiles(v_ref.at[1], at)
+        below_shifted = stencil(below)
+        first, pending = filters(0, x, v, stencil(v), zero, below)
+
+        def body(i, carry):
+            v, shifted_v, first, pending, own, norm = carry
+            below = load_tiles(v_ref.at[i + 1], at)
+            below_shifted = stencil(below)
+            first, fresh = filters(i, x, v, shifted_v, first, below)
+            own = own + adjoint(i - 1, x, pending)
+            return below, below_shifted, first, fresh, own, norm + dot(v, v)
+
+        carry = (below, below_shifted, first, pending, zero[0], dot(v, v))
+        v, shifted_v, first, pending, own, norm = lax.fori_loop(1, rows - 1, body, carry)
+        first, fresh = filters(rows - 1, x, v, shifted_v, first, zero)
+        own = own + adjoint(rows - 2, x, pending) + adjoint(rows - 1, x, fresh)
+        vout, vv = vout + own, vv + (norm + dot(v, v))
+    sums_ref[0], sums_ref[1] = vout, vv
 
 
 def halo_corrections(out_ref, p1_ref, p2_ref, below_ref, above_ref, right_ref, left_ref):
@@ -425,10 +437,7 @@
             [tile, f32(2, SUBLANES, LANES)],
             fields[-1], inline_dip, cross_dip, diag,
             name="apply",
-            scratch=[
-                pltpu.VMEM((cols, samples), jnp.float32),
-                pltpu.VMEM((rows, samples // LANES, SUBLANES + cols, LANES), jnp.float32),
-            ],
+            scratch=[pltpu.VMEM((rows, samples // LANES, SUBLANES + cols, LANES), jnp.float32)],
             cost=cost,
         )
         sums.append(partial)

time: 98.8 us -> 109 us (1.10)
  Pallas kernels: 28.2 us -> 38 us
    pallas_call x9, Pallas kernels: 28.2 us -> 38 us  [call(): pl.pallas_call(kernel, out_shape=outs, in_specs=ins or [IN_VMEM] * len(ar...]
  transfers between devices with their start and end apart: 12 -> 12, of which waited for: 0 -> 0; matrix products, arithmetic and copies ran while one was open for 0% -> 0% of each run, Pallas kernels for 22% -> 29%
where the time goes in v6:
time: 109 us; the launch traced here: 108 us
  Pallas kernels  38 us (35%)
  blocking collectives  36.5 us (33%)
  starting transfers between devices  32.8 us (30%)
    pallas_call x9, Pallas kernels, call(): pl.pallas_call(kernel, out_shape=outs, in_specs=ins or [IN_VMEM] * len(ar...  38 us
    ppermute x12, starting transfers between devices, shifted(): lax.ppermute(value, axis, [(source, source + steps) for source in range(i...  32.8 us
    all_to_all x1, blocking collectives, per_device(): lax.all_to_all(sent, ('inl', 'xl'), split_axis=0, concat_axis=0, tiled=True)  24 us
    all_to_all x1, blocking collectives, per_device(): lax.all_to_all(message, ('inl', 'xl'), split_axis=0, concat_axis=0, tiled...  12.5 us
  transfers between devices with their start and end apart: 12, of which 0 were waited for; matrix products, arithmetic and copies ran while one was open for 0% of the time, Pallas kernels for 29%

profile of v6, /device:TPU:0, one launch (start us, length us, event | category | flops | bytes accessed | tf_op | source)
XLA Modules:
  0.0 108.2 jit_solution(942933333823984087)
XLA Ops:
  0.6 0.0 copy-start.1
  0.6 1.5 %pack.1 = (bf16[512,640]{1,0:T(8,128)(2,1)S(1)}, f32[128,512]{1,0:T(8,128)S(1)}, f32[8,8,512]{2,1,0:T(8,128)S(1)}) custom-call(s32[1,256]{1,0:T(1,128)} %bitcast.7, s32[1,256]{1,0:T(1,128)} %bitcast.8, s32[1,256]{1,0:T(1,128)} %bitcast.9, bf16[256,512]{1,0:T(8,128)(2,1)} %traces_hbm.1, f32[8,128,512]{2,1,0:T(8,128)} %p1_ref.11, f32[8,128,512]{2,1,0:T(8,128)} %p2_ref.11), custom_call_target="tpu_custom_call" | custom-call | tf_op jit(solution)/shard_map/pack/pallas_call | solution.py:383
  2.2 0.0 copy-start
  2.2 24.0 %all_to_all.16 = bf16[32,16,640]{2,1,0:T(8,128)(2,1)S(1)} all-to-all(bf16[32,16,640]{2,1,0:T(8,128)(2,1)S(1)} %bitcast.6), channel_id=1, replica_groups=mesh['inl'=8,'xl'=4] {'inl','xl'}, dimensions={0} | all-to-all | bytes 1310720 | tf_op jit(solution)/shard_map/all_to_all | solution.py:419
  26.2 1.3 %bin.1 = (f32[8,4,128,128]{3,2,1,0:T(8,128)S(1)}, f32[8,128,128]{2,1,0:T(8,128)S(1)}, f32[128,512]{1,0:T(8,128)S(1)}, f32[128,512]{1,0:T(8,128)S(1)}, f32[8,512]{1,0:T(8,128)S(1)}, /*index=5*/f32[8,512]{1,0:T(8,128)S(1)}) custom-call(bf16[512,640]{1,0:T(8,128)(2,1)S(1)} %bitcast.5, f32[128,512]{1,0:T(8,128)S(1)} %get-tuple-element.32.p1_ref, ...), custom_call_target="tpu_custom_call" | custom-call | tf_op jit(solution)/shard_map/bin/pallas_call | solution.py:383
  27.5 1.3 %collective-permute-start = (f32[128,512]{1,0:T(8,128)S(1)}, f32[128,512]{1,0:T(8,128)S(1)}, u32[]{:S(2)}, u32[]{:S(2)}) collective-permute-start(f32[128,512]{1,0:T(8,128)S(1)} %get-tuple-element.37), channel_id=1, source_target_pairs={{4,0},{8,4},{12,8},{16,12},{20,16},{24,20},{28,24},{5,1},{9,5},{13... | collective-permute-start | bytes 786440 | tf_op jit(solution)/shard_map/ppermute | solution.py:23
  28.8 3.9 %collective-permute-start.1 = (f32[128,512]{1,0:T(8,128)S(1)}, f32[128,512]{1,0:T(8,128)S(1)}, u32[]{:S(2)}, u32[]{:S(2)}) collective-permute-start(f32[128,512]{1,0:T(8,128)S(1)} %get-tuple-element.38.row7_ref), channel_id=1, source_target_pairs={{0,4},{4,8},{8,12},{12,16},{16,20},{20,24},{24,28},{1,5},{5,9},{9,... | collective-permute-start | bytes 786440 | tf_op jit(solution)/shard_map/ppermute | solution.py:23
  32.8 1.3 %collective-permute-start.2 = (f32[8,512]{1,0:T(8,128)S(1)}, f32[8,512]{1,0:T(8,128)S(1)}, u32[]{:S(2)}, u32[]{:S(2)}) collective-permute-start(f32[8,512]{1,0:T(8,128)S(1)} %get-tuple-element.39), channel_id=1, source_target_pairs={{1,0},{2,1},{3,2},{5,4},{6,5},{7,6},{9,8},{10,9},{11,10},{13,12},{... | collective-permute-start | bytes 49160 | tf_op jit(solution)/shard_map/ppermute | solution.py:23
  34.1 4.5 %collective-permute-start.3 = (f32[8,512]{1,0:T(8,128)S(1)}, f32[8,512]{1,0:T(8,128)S(1)}, u32[]{:S(2)}, u32[]{:S(2)}) collective-permute-start(f32[8,512]{1,0:T(8,128)S(1)} %get-tuple-element.40.col7_ref), channel_id=1, source_target_pairs={{0,1},{1,2},{2,3},{4,5},{5,6},{6,7},{8,9},{9,10},{10,11},{12,13},{... | collective-permute-start | bytes 49160 | tf_op jit(solution)/shard_map/ppermute | solution.py:23
  38.6 0.0 copy-done.1
  38.6 0.0 copy-done
  38.7 10.4 %apply.3 = (f32[8,4,128,128]{3,2,1,0:T(8,128)S(1)}, f32[2,8,128]{2,1,0:T(8,128)S(1)}) custom-call(f32[8,4,128,128]{3,2,1,0:T(8,128)S(1)} %get-tuple-element.34.v_ref.b_ref, f32[8,128,512]{2,1,0:T(8,128)S(1)} %copy-done, f32[8,128,512]{2,1,0:T(8,128)S(1)} %copy-done.1, f32[8,128,128]{2,1,0:T(8,128)S(1)} %get-tuple-element.35.diag_ref), custom_call_target="tpu_custom_call" | custom-call | flops 31457280 | bytes 8388608 | tf_op jit(solution)/shard_map/apply/pallas_call | solution.py:383
  49.1 0.0 collective-permute-done.2.right_ref
  49.1 0.0 collective-permute-done.3.left_ref
  49.1 0.0 collective-permute-done.below_ref
  49.1 0.0 collective-permute-done.1.above_ref
  49.1 0.6 correct.2
  49.7 1.3 %collective-permute-start.4 = (f32[128,512]{1,0:T(8,128)S(1)}, f32[128,512]{1,0:T(8,128)S(1)}, u32[]{:S(2)}, u32[]{:S(2)}) collective-permute-start(f32[128,512]{1,0:T(8,128)S(1)} %get-tuple-element.43), channel_id=1, source_target_pairs={{4,0},{8,4},{12,8},{16,12},{20,16},{24,20},{28,24},{5,1},{9,5},{13... | collective-permute-start | bytes 786440 | tf_op jit(solution)/shard_map/ppermute | solution.py:23
  51.0 3.7 %collective-permute-start.5 = (f32[128,512]{1,0:T(8,128)S(1)}, f32[128,512]{1,0:T(8,128)S(1)}, u32[]{:S(2)}, u32[]{:S(2)}) collective-permute-start(f32[128,512]{1,0:T(8,128)S(1)} %get-tuple-element.44.row7_ref), channel_id=1, source_target_pairs={{0,4},{4,8},{8,12},{12,16},{16,20},{20,24},{24,28},{1,5},{5,9},{9,... | collective-permute-start | bytes 786440 | tf_op jit(solution)/shard_map/ppermute | solution.py:23
  54.7 1.3 %collective-permute-start.6 = (f32[8,512]{1,0:T(8,128)S(1)}, f32[8,512]{1,0:T(8,128)S(1)}, u32[]{:S(2)}, u32[]{:S(2)}) collective-permute-start(f32[8,512]{1,0:T(8,128)S(1)} %get-tuple-element.45), channel_id=1, source_target_pairs={{1,0},{2,1},{3,2},{5,4},{6,5},{7,6},{9,8},{10,9},{11,10},{13,12},{... | collective-permute-start | bytes 49160 | tf_op jit(solution)/shard_map/ppermute | solution.py:23
  56.0 4.5 %collective-permute-start.7 = (f32[8,512]{1,0:T(8,128)S(1)}, f32[8,512]{1,0:T(8,128)S(1)}, u32[]{:S(2)}, u32[]{:S(2)}) collective-permute-start(f32[8,512]{1,0:T(8,128)S(1)} %get-tuple-element.46.col7_ref), channel_id=1, source_target_pairs={{0,1},{1,2},{2,3},{4,5},{5,6},{6,7},{8,9},{9,10},{10,11},{12,13},{... | collective-permute-start | bytes 49160 | tf_op jit(solution)/shard_map/ppermute | solution.py:23
  60.6 10.4 %apply.4 = (f32[8,4,128,128]{3,2,1,0:T(8,128)S(1)}, f32[2,8,128]{2,1,0:T(8,128)S(1)}) custom-call(f32[8,4,128,128]{3,2,1,0:T(8,128)S(1)} %get-tuple-element.41.v_ref.v1_ref, f32[8,128,512]{2,1,0:T(8,128)S(1)} %copy-done, f32[8,128,512]{2,1,0:T(8,128)S(1)} %copy-done.1, f32[8,128,128]{2,1,0:T(8,128)S(1)} %get-tuple-element.35.diag_ref), custom_call_target="tpu_custom_call" | custom-call | flops 31457280 | bytes 8388608 | tf_op jit(solution)/shard_map/apply/pallas_call | solution.py:383
  71.0 0.0 collective-permute-done.6.right_ref
  71.0 0.0 collective-permute-done.7.left_ref
  71.0 0.0 collective-permute-done.4.below_ref
  71.0 0.0 collective-permute-done.5.above_ref
  71.0 0.5 correct.3
  71.6 1.3 %collective-permute-start.8 = (f32[128,512]{1,0:T(8,128)S(1)}, f32[128,512]{1,0:T(8,128)S(1)}, u32[]{:S(2)}, u32[]{:S(2)}) collective-permute-start(f32[128,512]{1,0:T(8,128)S(1)} %get-tuple-element.49), channel_id=1, source_target_pairs={{4,0},{8,4},{12,8},{16,12},{20,16},{24,20},{28,24},{5,1},{9,5},{13... | collective-permute-start | bytes 786440 | tf_op jit(solution)/shard_map/ppermute | solution.py:23
  72.9 3.7 %collective-permute-start.9 = (f32[128,512]{1,0:T(8,128)S(1)}, f32[128,512]{1,0:T(8,128)S(1)}, u32[]{:S(2)}, u32[]{:S(2)}) collective-permute-start(f32[128,512]{1,0:T(8,128)S(1)} %get-tuple-element.50.row7_ref), channel_id=1, source_target_pairs={{0,4},{4,8},{8,12},{12,16},{16,20},{20,24},{24,28},{1,5},{5,9},{9,... | collective-permute-start | bytes 786440 | tf_op jit(solution)/shard_map/ppermute | solution.py:23
  76.6 1.3 %collective-permute-start.10 = (f32[8,512]{1,0:T(8,128)S(1)}, f32[8,512]{1,0:T(8,128)S(1)}, u32[]{:S(2)}, u32[]{:S(2)}) collective-permute-start(f32[8,512]{1,0:T(8,128)S(1)} %get-tuple-element.51), channel_id=1, source_target_pairs={{1,0},{2,1},{3,2},{5,4},{6,5},{7,6},{9,8},{10,9},{11,10},{13,12},{... | collective-permute-start | bytes 49160 | tf_op jit(solution)/shard_map/ppermute | solution.py:23
  77.9 4.5 %collective-permute-start.11 = (f32[8,512]{1,0:T(8,128)S(1)}, f32[8,512]{1,0:T(8,128)S(1)}, u32[]{:S(2)}, u32[]{:S(2)}) collective-permute-start(f32[8,512]{1,0:T(8,128)S(1)} %get-tuple-element.52.col7_ref), channel_id=1, source_target_pairs={{0,1},{1,2},{2,3},{4,5},{5,6},{6,7},{8,9},{9,10},{10,11},{12,13},{... | collective-permute-start | bytes 49160 | tf_op jit(solution)/shard_map/ppermute | solution.py:23
  82.5 10.5 %apply.5 = (f32[8,4,128,128]{3,2,1,0:T(8,128)S(1)}, f32[2,8,128]{2,1,0:T(8,128)S(1)}) custom-call(f32[8,4,128,128]{3,2,1,0:T(8,128)S(1)} %get-tuple-element.47.v_ref.v2_ref, f32[8,128,512]{2,1,0:T(8,128)S(1)} %copy-done, f32[8,128,512]{2,1,0:T(8,128)S(1)} %copy-done.1, f32[8,128,128]{2,1,0:T(8,128)S(1)} %get-tuple-element.35.diag_ref), custom_call_target="tpu_custom_call" | custom-call | flops 31457280 | bytes 8388608 | tf_op jit(solution)/shard_map/apply/pallas_call | solution.py:383
  93.0 0.0 collective-permute-done.10.right_ref
  93.0 0.0 collective-permute-done.11.left_ref
  93.0 0.0 collective-permute-done.8.below_ref
  93.0 0.0 collective-permute-done.9.above_ref
  93.0 0.4 moments.1
  93.4 12.5 %all_to_all.17.parts_ref = f32[32,1,128]{2,1,0:T(1,128)S(1)} all-to-all(f32[32,1,128]{2,1,0:T(1,128)S(1)} %get-tuple-element.58), channel_id=1, replica_groups=mesh['inl'=8,'xl'=4] {'inl','xl'}, dimensions={0} | all-to-all | bytes 32768 | tf_op jit(solution)/shard_map/all_to_all | solution.py:456
  105.8 2.4 %finish.1 = (f32[8,128,512]{2,1,0:T(8,128)}, f32[8,128,512]{2,1,0:T(8,128)}) custom-call(f32[32,1,128]{2,1,0:T(1,128)S(1)} %all_to_all.17.parts_ref, f32[8,4,128,128]{3,2,1,0:T(8,128)S(1)} %get-tuple-element.34.v_ref.b_ref, f32[8,4,128,128]{3,2,1,0:T(8,128)S(1)} %get-tuple-element.41.v_ref.v1_ref, f32[8,4,128,128]{3,2,1,0:T(8,128)S(1)} %get-tuple-element.47.v_ref.v2_ref, ...), custom_call_target="tpu_custom_call" | custom-call | tf_op jit(solution)/shard_map/finish/pallas_call | solution.py:383
Async XLA Ops:
  0.6 38.0 %copy-start.1 = (f32[8,128,512]{2,1,0:T(8,128)S(1)}, f32[8,128,512]{2,1,0:T(8,128)}, u32[]{:S(2)}) copy-start(f32[8,128,512]{2,1,0:T(8,128)} %p2_ref.11) | copy-start | bytes 6291460
  2.2 36.5 %copy-start = (f32[8,128,512]{2,1,0:T(8,128)S(1)}, f32[8,128,512]{2,1,0:T(8,128)}, u32[]{:S(2)}) copy-start(f32[8,128,512]{2,1,0:T(8,128)} %p1_ref.11) | copy-start | bytes 6291460
  27.5 21.6 %collective-permute-start = (f32[128,512]{1,0:T(8,128)S(1)}, f32[128,512]{1,0:T(8,128)S(1)}, u32[]{:S(2)}, u32[]{:S(2)}) collective-permute-start(f32[128,512]{1,0:T(8,128)S(1)} %get-tuple-element.37), channel_id=1, source_target_pairs={{4,0},{8,4},{12,8},{16,12},{20,16},{24,20},{28,24},{5,1},{9,5},{13... | collective-permute-start | bytes 786440 | tf_op jit(solution)/shard_map/ppermute | solution.py:23
  28.8 20.3 %collective-permute-start.1 = (f32[128,512]{1,0:T(8,128)S(1)}, f32[128,512]{1,0:T(8,128)S(1)}, u32[]{:S(2)}, u32[]{:S(2)}) collective-permute-start(f32[128,512]{1,0:T(8,128)S(1)} %get-tuple-element.38.row7_ref), channel_id=1, source_target_pairs={{0,4},{4,8},{8,12},{12,16},{16,20},{20,24},{24,28},{1,5},{5,9},{9,... | collective-permute-start | bytes 786440 | tf_op jit(solution)/shard_map/ppermute | solution.py:23
  32.8 16.3 %collective-permute-start.2 = (f32[8,512]{1,0:T(8,128)S(1)}, f32[8,512]{1,0:T(8,128)S(1)}, u32[]{:S(2)}, u32[]{:S(2)}) collective-permute-start(f32[8,512]{1,0:T(8,128)S(1)} %get-tuple-element.39), channel_id=1, source_target_pairs={{1,0},{2,1},{3,2},{5,4},{6,5},{7,6},{9,8},{10,9},{11,10},{13,12},{... | collective-permute-start | bytes 49160 | tf_op jit(solution)/shard_map/ppermute | solution.py:23
  34.1 15.0 %collective-permute-start.3 = (f32[8,512]{1,0:T(8,128)S(1)}, f32[8,512]{1,0:T(8,128)S(1)}, u32[]{:S(2)}, u32[]{:S(2)}) collective-permute-start(f32[8,512]{1,0:T(8,128)S(1)} %get-tuple-element.40.col7_ref), channel_id=1, source_target_pairs={{0,1},{1,2},{2,3},{4,5},{5,6},{6,7},{8,9},{9,10},{10,11},{12,13},{... | collective-permute-start | bytes 49160 | tf_op jit(solution)/shard_map/ppermute | solution.py:23
  49.7 21.3 %collective-permute-start.4 = (f32[128,512]{1,0:T(8,128)S(1)}, f32[128,512]{1,0:T(8,128)S(1)}, u32[]{:S(2)}, u32[]{:S(2)}) collective-permute-start(f32[128,512]{1,0:T(8,128)S(1)} %get-tuple-element.43), channel_id=1, source_target_pairs={{4,0},{8,4},{12,8},{16,12},{20,16},{24,20},{28,24},{5,1},{9,5},{13... | collective-permute-start | bytes 786440 | tf_op jit(solution)/shard_map/ppermute | solution.py:23
  51.0 20.0 %collective-permute-start.5 = (f32[128,512]{1,0:T(8,128)S(1)}, f32[128,512]{1,0:T(8,128)S(1)}, u32[]{:S(2)}, u32[]{:S(2)}) collective-permute-start(f32[128,512]{1,0:T(8,128)S(1)} %get-tuple-element.44.row7_ref), channel_id=1, source_target_pairs={{0,4},{4,8},{8,12},{12,16},{16,20},{20,24},{24,28},{1,5},{5,9},{9,... | collective-permute-start | bytes 786440 | tf_op jit(solution)/shard_map/ppermute | solution.py:23
  54.7 16.3 %collective-permute-start.6 = (f32[8,512]{1,0:T(8,128)S(1)}, f32[8,512]{1,0:T(8,128)S(1)}, u32[]{:S(2)}, u32[]{:S(2)}) collective-permute-start(f32[8,512]{1,0:T(8,128)S(1)} %get-tuple-element.45), channel_id=1, source_target_pairs={{1,0},{2,1},{3,2},{5,4},{6,5},{7,6},{9,8},{10,9},{11,10},{13,12},{... | collective-permute-start | bytes 49160 | tf_op jit(solution)/shard_map/ppermute | solution.py:23
  56.0 15.0 %collective-permute-start.7 = (f32[8,512]{1,0:T(8,128)S(1)}, f32[8,512]{1,0:T(8,128)S(1)}, u32[]{:S(2)}, u32[]{:S(2)}) collective-permute-start(f32[8,512]{1,0:T(8,128)S(1)} %get-tuple-element.46.col7_ref), channel_id=1, source_target_pairs={{0,1},{1,2},{2,3},{4,5},{5,6},{6,7},{8,9},{9,10},{10,11},{12,13},{... | collective-permute-start | bytes 49160 | tf_op jit(solution)/shard_map/ppermute | solution.py:23
  71.6 21.4 %collective-permute-start.8 = (f32[128,512]{1,0:T(8,128)S(1)}, f32[128,512]{1,0:T(8,128)S(1)}, u32[]{:S(2)}, u32[]{:S(2)}) collective-permute-start(f32[128,512]{1,0:T(8,128)S(1)} %get-tuple-element.49), channel_id=1, source_target_pairs={{4,0},{8,4},{12,8},{16,12},{20,16},{24,20},{28,24},{5,1},{9,5},{13... | collective-permute-start | bytes 786440 | tf_op jit(solution)/shard_map/ppermute | solution.py:23
  72.9 20.1 %collective-permute-start.9 = (f32[128,512]{1,0:T(8,128)S(1)}, f32[128,512]{1,0:T(8,128)S(1)}, u32[]{:S(2)}, u32[]{:S(2)}) collective-permute-start(f32[128,512]{1,0:T(8,128)S(1)} %get-tuple-element.50.row7_ref), channel_id=1, source_target_pairs={{0,4},{4,8},{8,12},{12,16},{16,20},{20,24},{24,28},{1,5},{5,9},{9,... | collective-permute-start | bytes 786440 | tf_op jit(solution)/shard_map/ppermute | solution.py:23
  76.6 16.4 %collective-permute-start.10 = (f32[8,512]{1,0:T(8,128)S(1)}, f32[8,512]{1,0:T(8,128)S(1)}, u32[]{:S(2)}, u32[]{:S(2)}) collective-permute-start(f32[8,512]{1,0:T(8,128)S(1)} %get-tuple-element.51), channel_id=1, source_target_pairs={{1,0},{2,1},{3,2},{5,4},{6,5},{7,6},{9,8},{10,9},{11,10},{13,12},{... | collective-permute-start | bytes 49160 | tf_op jit(solution)/shard_map/ppermute | solution.py:23
  77.9 15.1 %collective-permute-start.11 = (f32[8,512]{1,0:T(8,128)S(1)}, f32[8,512]{1,0:T(8,128)S(1)}, u32[]{:S(2)}, u32[]{:S(2)}) collective-permute-start(f32[8,512]{1,0:T(8,128)S(1)} %get-tuple-element.52.col7_ref), channel_id=1, source_target_pairs={{0,1},{1,2},{2,3},{4,5},{5,6},{6,7},{8,9},{9,10},{10,11},{12,13},{... | collective-permute-start | bytes 49160 | tf_op jit(solution)/shard_map/ppermute | solution.py:23

commit v7 on v6

--- a/solution.py
+++ b/solution.py
@@ -10,6 +10,7 @@
 ITERS = 3
 LANES = 128
 SUBLANES = 8
+GROUP = 16
 
 SHIFT = 6.0
 IN_VMEM = pl.BlockSpec(memory_space=pltpu.VMEM)
@@ -220,26 +221,44 @@
         return dot(load_tiles(v_ref.at[i], at), out)
 
     vout, vv = zero[0], zero[0]
-    for x in range(0, cols, SUBLANES):
-        at = slice(x, x + SUBLANES)
-        v = load_tiles(v_ref.at[0], at)
-        below = load_tiles(v_ref.at[1], at)
-        below_shifted = stencil(below)
-        first, pending = filters(0, x, v, stencil(v), zero, below)
+    for x in range(0, cols, GROUP):
+        chunks = range(x, x + GROUP, SUBLANES)
+
+        def fetch(i):
+            below = [load_tiles(v_ref.at[i], slice(k, k + SUBLANES)) for k in chunks]
+            return below, [stencil(tiles_of) for tiles_of in below]
+
+        def all_filters(i, v, shifted_v, first, below):
+            done = [filters(i, k, *rest) for k, *rest in zip(chunks, v, shifted_v, first, below)]
+            return [pair[0] for pair in done], [pair[1] for pair in done]
+
+        def all_adjoint(i, own, pending):
+            for k, waiting in zip(chunks, pending):
+                own = own + adjoint(i, k, waiting)
+            return own
+
+        def norms(norm, v):
+            for tiles_of in v:
+                norm = norm + dot(tiles_of, tiles_of)
+            return norm
+
+        nothing = [zero] * len(chunks)
+        v, shifted_v = fetch(0)
+        below, below_shifted = fetch(1)
+        first, pending = all_filters(0, v, shifted_v, nothing, below)
 
         def body(i, carry):
             v, shifted_v, first, pending, own, norm = carry
-            below = load_tiles(v_ref.at[i + 1], at)
-            below_shifted = stencil(below)
-            first, fresh = filters(i, x, v, shifted_v, first, below)
-            own = own + adjoint(i - 1, x, pending)
-            return below, below_shifted, first, fresh, own, norm + dot(v, v)
-
-        carry = (below, below_shifted, first, pending, zero[0], dot(v, v))
+            below, below_shifted = fetch(i + 1)
+            first, fresh = all_filters(i, v, shifted_v, first, below)
+            own = all_adjoint(i - 1, own, pending)
+            return below, below_shifted, first, fresh, own, norms(norm, v)
+
+        carry = (below, below_shifted, first, pending, zero[0], norms(zero[0], v))
         v, shifted_v, first, pending, own, norm = lax.fori_loop(1, rows - 1, body, carry)
-        first, fresh = filters(rows - 1, x, v, shifted_v, first, zero)
-        own = own + adjoint(rows - 2, x, pending) + adjoint(rows - 1, x, fresh)
-        vout, vv = vout + own, vv + (norm + dot(v, v))
+        first, fresh = all_filters(rows - 1, v, shifted_v, first, nothing)
+        own = all_adjoint(rows - 1, all_adjoint(rows - 2, own, pending), fresh)
+        vout, vv = vout + own, vv + norms(norm, v)
     sums_ref[0], sums_ref[1] = vout, vv
 
 

time: 109 us -> 97.7 us (0.90)
  Pallas kernels: 38 us -> 27.1 us
    pallas_call x9, Pallas kernels: 38 us -> 27.1 us  [call(): pl.pallas_call(kernel, out_shape=outs, in_specs=ins or [IN_VMEM] * len(ar...]
  transfers between devices with their start and end apart: 12 -> 12, of which waited for: 0 -> 0; matrix products, arithmetic and copies ran while one was open for 0% -> 0% of each run, Pallas kernels for 29% -> 21%
where the time goes in v7:
time: 97.7 us; the launch traced here: 97.3 us
  blocking collectives  36.5 us (37%)
  starting transfers between devices  32.8 us (34%)
  Pallas kernels  27.1 us (28%)
    ppermute x12, starting transfers between devices, shifted(): lax.ppermute(value, axis, [(source, source + steps) for source in range(i...  32.8 us
    pallas_call x9, Pallas kernels, call(): pl.pallas_call(kernel, out_shape=outs, in_specs=ins or [IN_VMEM] * len(ar...  27.1 us
    all_to_all x1, blocking collectives, per_device(): lax.all_to_all(sent, ('inl', 'xl'), split_axis=0, concat_axis=0, tiled=True)  24 us
    all_to_all x1, blocking collectives, per_device(): lax.all_to_all(message, ('inl', 'xl'), split_axis=0, concat_axis=0, tiled...  12.5 us
  transfers between devices with their start and end apart: 12, of which 0 were waited for; matrix products, arithmetic and copies ran while one was open for 0% of the time, Pallas kernels for 21%

profile of v7, /device:TPU:0, one launch (start us, length us, event | category | flops | bytes accessed | tf_op | source)
XLA Modules:
  0.0 97.3 jit_solution(11422508268506673670)
XLA Ops:
  0.6 0.0 copy-start.1
  0.6 1.5 %pack.1 = (bf16[512,640]{1,0:T(8,128)(2,1)S(1)}, f32[128,512]{1,0:T(8,128)S(1)}, f32[8,8,512]{2,1,0:T(8,128)S(1)}) custom-call(s32[1,256]{1,0:T(1,128)} %bitcast.7, s32[1,256]{1,0:T(1,128)} %bitcast.8, s32[1,256]{1,0:T(1,128)} %bitcast.9, bf16[256,512]{1,0:T(8,128)(2,1)} %traces_hbm.1, f32[8,128,512]{2,1,0:T(8,128)} %p1_ref.11, f32[8,128,512]{2,1,0:T(8,128)} %p2_ref.11), custom_call_target="tpu_custom_call" | custom-call | tf_op jit(solution)/shard_map/pack/pallas_call | solution.py:402
  2.2 0.0 copy-start
  2.2 24.0 %all_to_all.16 = bf16[32,16,640]{2,1,0:T(8,128)(2,1)S(1)} all-to-all(bf16[32,16,640]{2,1,0:T(8,128)(2,1)S(1)} %bitcast.6), channel_id=1, replica_groups=mesh['inl'=8,'xl'=4] {'inl','xl'}, dimensions={0} | all-to-all | bytes 1310720 | tf_op jit(solution)/shard_map/all_to_all | solution.py:438
  26.2 1.3 %bin.1 = (f32[8,4,128,128]{3,2,1,0:T(8,128)S(1)}, f32[8,128,128]{2,1,0:T(8,128)S(1)}, f32[128,512]{1,0:T(8,128)S(1)}, f32[128,512]{1,0:T(8,128)S(1)}, f32[8,512]{1,0:T(8,128)S(1)}, /*index=5*/f32[8,512]{1,0:T(8,128)S(1)}) custom-call(bf16[512,640]{1,0:T(8,128)(2,1)S(1)} %bitcast.5, f32[128,512]{1,0:T(8,128)S(1)} %get-tuple-element.32.p1_ref, ...), custom_call_target="tpu_custom_call" | custom-call | tf_op jit(solution)/shard_map/bin/pallas_call | solution.py:402
  27.5 1.3 %collective-permute-start = (f32[128,512]{1,0:T(8,128)S(1)}, f32[128,512]{1,0:T(8,128)S(1)}, u32[]{:S(2)}, u32[]{:S(2)}) collective-permute-start(f32[128,512]{1,0:T(8,128)S(1)} %get-tuple-element.37), channel_id=1, source_target_pairs={{4,0},{8,4},{12,8},{16,12},{20,16},{24,20},{28,24},{5,1},{9,5},{13... | collective-permute-start | bytes 786440 | tf_op jit(solution)/shard_map/ppermute | solution.py:24
  28.8 3.9 %collective-permute-start.1 = (f32[128,512]{1,0:T(8,128)S(1)}, f32[128,512]{1,0:T(8,128)S(1)}, u32[]{:S(2)}, u32[]{:S(2)}) collective-permute-start(f32[128,512]{1,0:T(8,128)S(1)} %get-tuple-element.38.row7_ref), channel_id=1, source_target_pairs={{0,4},{4,8},{8,12},{12,16},{16,20},{20,24},{24,28},{1,5},{5,9},{9,... | collective-permute-start | bytes 786440 | tf_op jit(solution)/shard_map/ppermute | solution.py:24
  32.8 1.3 %collective-permute-start.2 = (f32[8,512]{1,0:T(8,128)S(1)}, f32[8,512]{1,0:T(8,128)S(1)}, u32[]{:S(2)}, u32[]{:S(2)}) collective-permute-start(f32[8,512]{1,0:T(8,128)S(1)} %get-tuple-element.39), channel_id=1, source_target_pairs={{1,0},{2,1},{3,2},{5,4},{6,5},{7,6},{9,8},{10,9},{11,10},{13,12},{... | collective-permute-start | bytes 49160 | tf_op jit(solution)/shard_map/ppermute | solution.py:24
  34.1 4.5 %collective-permute-start.3 = (f32[8,512]{1,0:T(8,128)S(1)}, f32[8,512]{1,0:T(8,128)S(1)}, u32[]{:S(2)}, u32[]{:S(2)}) collective-permute-start(f32[8,512]{1,0:T(8,128)S(1)} %get-tuple-element.40.col7_ref), channel_id=1, source_target_pairs={{0,1},{1,2},{2,3},{4,5},{5,6},{6,7},{8,9},{9,10},{10,11},{12,13},{... | collective-permute-start | bytes 49160 | tf_op jit(solution)/shard_map/ppermute | solution.py:24
  38.6 0.0 copy-done.1
  38.6 0.0 copy-done
  38.7 6.8 %apply.3 = (f32[8,4,128,128]{3,2,1,0:T(8,128)S(1)}, f32[2,8,128]{2,1,0:T(8,128)S(1)}) custom-call(f32[8,4,128,128]{3,2,1,0:T(8,128)S(1)} %get-tuple-element.34.v_ref.b_ref, f32[8,128,512]{2,1,0:T(8,128)S(1)} %copy-done, f32[8,128,512]{2,1,0:T(8,128)S(1)} %copy-done.1, f32[8,128,128]{2,1,0:T(8,128)S(1)} %get-tuple-element.35.diag_ref), custom_call_target="tpu_custom_call" | custom-call | flops 31457280 | bytes 8388608 | tf_op jit(solution)/shard_map/apply/pallas_call | solution.py:402
  45.5 0.0 collective-permute-done.2.right_ref
  45.5 0.0 collective-permute-done.3.left_ref
  45.5 0.0 collective-permute-done.below_ref
  45.5 0.0 collective-permute-done.1.above_ref
  45.5 0.6 correct.2
  46.1 1.3 %collective-permute-start.4 = (f32[128,512]{1,0:T(8,128)S(1)}, f32[128,512]{1,0:T(8,128)S(1)}, u32[]{:S(2)}, u32[]{:S(2)}) collective-permute-start(f32[128,512]{1,0:T(8,128)S(1)} %get-tuple-element.43), channel_id=1, source_target_pairs={{4,0},{8,4},{12,8},{16,12},{20,16},{24,20},{28,24},{5,1},{9,5},{13... | collective-permute-start | bytes 786440 | tf_op jit(solution)/shard_map/ppermute | solution.py:24
  47.4 3.7 %collective-permute-start.5 = (f32[128,512]{1,0:T(8,128)S(1)}, f32[128,512]{1,0:T(8,128)S(1)}, u32[]{:S(2)}, u32[]{:S(2)}) collective-permute-start(f32[128,512]{1,0:T(8,128)S(1)} %get-tuple-element.44.row7_ref), channel_id=1, source_target_pairs={{0,4},{4,8},{8,12},{12,16},{16,20},{20,24},{24,28},{1,5},{5,9},{9,... | collective-permute-start | bytes 786440 | tf_op jit(solution)/shard_map/ppermute | solution.py:24
  51.1 1.3 %collective-permute-start.6 = (f32[8,512]{1,0:T(8,128)S(1)}, f32[8,512]{1,0:T(8,128)S(1)}, u32[]{:S(2)}, u32[]{:S(2)}) collective-permute-start(f32[8,512]{1,0:T(8,128)S(1)} %get-tuple-element.45), channel_id=1, source_target_pairs={{1,0},{2,1},{3,2},{5,4},{6,5},{7,6},{9,8},{10,9},{11,10},{13,12},{... | collective-permute-start | bytes 49160 | tf_op jit(solution)/shard_map/ppermute | solution.py:24
  52.4 4.5 %collective-permute-start.7 = (f32[8,512]{1,0:T(8,128)S(1)}, f32[8,512]{1,0:T(8,128)S(1)}, u32[]{:S(2)}, u32[]{:S(2)}) collective-permute-start(f32[8,512]{1,0:T(8,128)S(1)} %get-tuple-element.46.col7_ref), channel_id=1, source_target_pairs={{0,1},{1,2},{2,3},{4,5},{5,6},{6,7},{8,9},{9,10},{10,11},{12,13},{... | collective-permute-start | bytes 49160 | tf_op jit(solution)/shard_map/ppermute | solution.py:24
  56.9 6.8 %apply.4 = (f32[8,4,128,128]{3,2,1,0:T(8,128)S(1)}, f32[2,8,128]{2,1,0:T(8,128)S(1)}) custom-call(f32[8,4,128,128]{3,2,1,0:T(8,128)S(1)} %get-tuple-element.41.v_ref.v1_ref, f32[8,128,512]{2,1,0:T(8,128)S(1)} %copy-done, f32[8,128,512]{2,1,0:T(8,128)S(1)} %copy-done.1, f32[8,128,128]{2,1,0:T(8,128)S(1)} %get-tuple-element.35.diag_ref), custom_call_target="tpu_custom_call" | custom-call | flops 31457280 | bytes 8388608 | tf_op jit(solution)/shard_map/apply/pallas_call | solution.py:402
  63.8 0.0 collective-permute-done.6.right_ref
  63.8 0.0 collective-permute-done.7.left_ref
  63.8 0.0 collective-permute-done.4.below_ref
  63.8 0.0 collective-permute-done.5.above_ref
  63.8 0.5 correct.3
  64.4 1.3 %collective-permute-start.8 = (f32[128,512]{1,0:T(8,128)S(1)}, f32[128,512]{1,0:T(8,128)S(1)}, u32[]{:S(2)}, u32[]{:S(2)}) collective-permute-start(f32[128,512]{1,0:T(8,128)S(1)} %get-tuple-element.49), channel_id=1, source_target_pairs={{4,0},{8,4},{12,8},{16,12},{20,16},{24,20},{28,24},{5,1},{9,5},{13... | collective-permute-start | bytes 786440 | tf_op jit(solution)/shard_map/ppermute | solution.py:24
  65.7 3.7 %collective-permute-start.9 = (f32[128,512]{1,0:T(8,128)S(1)}, f32[128,512]{1,0:T(8,128)S(1)}, u32[]{:S(2)}, u32[]{:S(2)}) collective-permute-start(f32[128,512]{1,0:T(8,128)S(1)} %get-tuple-element.50.row7_ref), channel_id=1, source_target_pairs={{0,4},{4,8},{8,12},{12,16},{16,20},{20,24},{24,28},{1,5},{5,9},{9,... | collective-permute-start | bytes 786440 | tf_op jit(solution)/shard_map/ppermute | solution.py:24
  69.4 1.3 %collective-permute-start.10 = (f32[8,512]{1,0:T(8,128)S(1)}, f32[8,512]{1,0:T(8,128)S(1)}, u32[]{:S(2)}, u32[]{:S(2)}) collective-permute-start(f32[8,512]{1,0:T(8,128)S(1)} %get-tuple-element.51), channel_id=1, source_target_pairs={{1,0},{2,1},{3,2},{5,4},{6,5},{7,6},{9,8},{10,9},{11,10},{13,12},{... | collective-permute-start | bytes 49160 | tf_op jit(solution)/shard_map/ppermute | solution.py:24
  70.7 4.5 %collective-permute-start.11 = (f32[8,512]{1,0:T(8,128)S(1)}, f32[8,512]{1,0:T(8,128)S(1)}, u32[]{:S(2)}, u32[]{:S(2)}) collective-permute-start(f32[8,512]{1,0:T(8,128)S(1)} %get-tuple-element.52.col7_ref), channel_id=1, source_target_pairs={{0,1},{1,2},{2,3},{4,5},{5,6},{6,7},{8,9},{9,10},{10,11},{12,13},{... | collective-permute-start | bytes 49160 | tf_op jit(solution)/shard_map/ppermute | solution.py:24
  75.2 6.8 %apply.5 = (f32[8,4,128,128]{3,2,1,0:T(8,128)S(1)}, f32[2,8,128]{2,1,0:T(8,128)S(1)}) custom-call(f32[8,4,128,128]{3,2,1,0:T(8,128)S(1)} %get-tuple-element.47.v_ref.v2_ref, f32[8,128,512]{2,1,0:T(8,128)S(1)} %copy-done, f32[8,128,512]{2,1,0:T(8,128)S(1)} %copy-done.1, f32[8,128,128]{2,1,0:T(8,128)S(1)} %get-tuple-element.35.diag_ref), custom_call_target="tpu_custom_call" | custom-call | flops 31457280 | bytes 8388608 | tf_op jit(solution)/shard_map/apply/pallas_call | solution.py:402
  82.0 0.0 collective-permute-done.10.right_ref
  82.0 0.0 collective-permute-done.11.left_ref
  82.0 0.0 collective-permute-done.8.below_ref
  82.0 0.0 collective-permute-done.9.above_ref
  82.0 0.4 moments.1
  82.4 12.5 %all_to_all.17.parts_ref = f32[32,1,128]{2,1,0:T(1,128)S(1)} all-to-all(f32[32,1,128]{2,1,0:T(1,128)S(1)} %get-tuple-element.58), channel_id=1, replica_groups=mesh['inl'=8,'xl'=4] {'inl','xl'}, dimensions={0} | all-to-all | bytes 32768 | tf_op jit(solution)/shard_map/all_to_all | solution.py:475
  94.9 2.4 %finish.1 = (f32[8,128,512]{2,1,0:T(8,128)}, f32[8,128,512]{2,1,0:T(8,128)}) custom-call(f32[32,1,128]{2,1,0:T(1,128)S(1)} %all_to_all.17.parts_ref, f32[8,4,128,128]{3,2,1,0:T(8,128)S(1)} %get-tuple-element.34.v_ref.b_ref, f32[8,4,128,128]{3,2,1,0:T(8,128)S(1)} %get-tuple-element.41.v_ref.v1_ref, f32[8,4,128,128]{3,2,1,0:T(8,128)S(1)} %get-tuple-element.47.v_ref.v2_ref, ...), custom_call_target="tpu_custom_call" | custom-call | tf_op jit(solution)/shard_map/finish/pallas_call | solution.py:402
Async XLA Ops:
  0.6 38.0 %copy-start.1 = (f32[8,128,512]{2,1,0:T(8,128)S(1)}, f32[8,128,512]{2,1,0:T(8,128)}, u32[]{:S(2)}) copy-start(f32[8,128,512]{2,1,0:T(8,128)} %p2_ref.11) | copy-start | bytes 6291460
  2.2 36.5 %copy-start = (f32[8,128,512]{2,1,0:T(8,128)S(1)}, f32[8,128,512]{2,1,0:T(8,128)}, u32[]{:S(2)}) copy-start(f32[8,128,512]{2,1,0:T(8,128)} %p1_ref.11) | copy-start | bytes 6291460
  27.5 18.0 %collective-permute-start = (f32[128,512]{1,0:T(8,128)S(1)}, f32[128,512]{1,0:T(8,128)S(1)}, u32[]{:S(2)}, u32[]{:S(2)}) collective-permute-start(f32[128,512]{1,0:T(8,128)S(1)} %get-tuple-element.37), channel_id=1, source_target_pairs={{4,0},{8,4},{12,8},{16,12},{20,16},{24,20},{28,24},{5,1},{9,5},{13... | collective-permute-start | bytes 786440 | tf_op jit(solution)/shard_map/ppermute | solution.py:24
  28.8 16.7 %collective-permute-start.1 = (f32[128,512]{1,0:T(8,128)S(1)}, f32[128,512]{1,0:T(8,128)S(1)}, u32[]{:S(2)}, u32[]{:S(2)}) collective-permute-start(f32[128,512]{1,0:T(8,128)S(1)} %get-tuple-element.38.row7_ref), channel_id=1, source_target_pairs={{0,4},{4,8},{8,12},{12,16},{16,20},{20,24},{24,28},{1,5},{5,9},{9,... | collective-permute-start | bytes 786440 | tf_op jit(solution)/shard_map/ppermute | solution.py:24
  32.8 12.7 %collective-permute-start.2 = (f32[8,512]{1,0:T(8,128)S(1)}, f32[8,512]{1,0:T(8,128)S(1)}, u32[]{:S(2)}, u32[]{:S(2)}) collective-permute-start(f32[8,512]{1,0:T(8,128)S(1)} %get-tuple-element.39), channel_id=1, source_target_pairs={{1,0},{2,1},{3,2},{5,4},{6,5},{7,6},{9,8},{10,9},{11,10},{13,12},{... | collective-permute-start | bytes 49160 | tf_op jit(solution)/shard_map/ppermute | solution.py:24
  34.1 11.4 %collective-permute-start.3 = (f32[8,512]{1,0:T(8,128)S(1)}, f32[8,512]{1,0:T(8,128)S(1)}, u32[]{:S(2)}, u32[]{:S(2)}) collective-permute-start(f32[8,512]{1,0:T(8,128)S(1)} %get-tuple-element.40.col7_ref), channel_id=1, source_target_pairs={{0,1},{1,2},{2,3},{4,5},{5,6},{6,7},{8,9},{9,10},{10,11},{12,13},{... | collective-permute-start | bytes 49160 | tf_op jit(solution)/shard_map/ppermute | solution.py:24
  46.1 17.7 %collective-permute-start.4 = (f32[128,512]{1,0:T(8,128)S(1)}, f32[128,512]{1,0:T(8,128)S(1)}, u32[]{:S(2)}, u32[]{:S(2)}) collective-permute-start(f32[128,512]{1,0:T(8,128)S(1)} %get-tuple-element.43), channel_id=1, source_target_pairs={{4,0},{8,4},{12,8},{16,12},{20,16},{24,20},{28,24},{5,1},{9,5},{13... | collective-permute-start | bytes 786440 | tf_op jit(solution)/shard_map/ppermute | solution.py:24
  47.4 16.4 %collective-permute-start.5 = (f32[128,512]{1,0:T(8,128)S(1)}, f32[128,512]{1,0:T(8,128)S(1)}, u32[]{:S(2)}, u32[]{:S(2)}) collective-permute-start(f32[128,512]{1,0:T(8,128)S(1)} %get-tuple-element.44.row7_ref), channel_id=1, source_target_pairs={{0,4},{4,8},{8,12},{12,16},{16,20},{20,24},{24,28},{1,5},{5,9},{9,... | collective-permute-start | bytes 786440 | tf_op jit(solution)/shard_map/ppermute | solution.py:24
  51.1 12.7 %collective-permute-start.6 = (f32[8,512]{1,0:T(8,128)S(1)}, f32[8,512]{1,0:T(8,128)S(1)}, u32[]{:S(2)}, u32[]{:S(2)}) collective-permute-start(f32[8,512]{1,0:T(8,128)S(1)} %get-tuple-element.45), channel_id=1, source_target_pairs={{1,0},{2,1},{3,2},{5,4},{6,5},{7,6},{9,8},{10,9},{11,10},{13,12},{... | collective-permute-start | bytes 49160 | tf_op jit(solution)/shard_map/ppermute | solution.py:24
  52.4 11.4 %collective-permute-start.7 = (f32[8,512]{1,0:T(8,128)S(1)}, f32[8,512]{1,0:T(8,128)S(1)}, u32[]{:S(2)}, u32[]{:S(2)}) collective-permute-start(f32[8,512]{1,0:T(8,128)S(1)} %get-tuple-element.46.col7_ref), channel_id=1, source_target_pairs={{0,1},{1,2},{2,3},{4,5},{5,6},{6,7},{8,9},{9,10},{10,11},{12,13},{... | collective-permute-start | bytes 49160 | tf_op jit(solution)/shard_map/ppermute | solution.py:24
  64.4 17.7 %collective-permute-start.8 = (f32[128,512]{1,0:T(8,128)S(1)}, f32[128,512]{1,0:T(8,128)S(1)}, u32[]{:S(2)}, u32[]{:S(2)}) collective-permute-start(f32[128,512]{1,0:T(8,128)S(1)} %get-tuple-element.49), channel_id=1, source_target_pairs={{4,0},{8,4},{12,8},{16,12},{20,16},{24,20},{28,24},{5,1},{9,5},{13... | collective-permute-start | bytes 786440 | tf_op jit(solution)/shard_map/ppermute | solution.py:24
  65.7 16.4 %collective-permute-start.9 = (f32[128,512]{1,0:T(8,128)S(1)}, f32[128,512]{1,0:T(8,128)S(1)}, u32[]{:S(2)}, u32[]{:S(2)}) collective-permute-start(f32[128,512]{1,0:T(8,128)S(1)} %get-tuple-element.50.row7_ref), channel_id=1, source_target_pairs={{0,4},{4,8},{8,12},{12,16},{16,20},{20,24},{24,28},{1,5},{5,9},{9,... | collective-permute-start | bytes 786440 | tf_op jit(solution)/shard_map/ppermute | solution.py:24
  69.4 12.6 %collective-permute-start.10 = (f32[8,512]{1,0:T(8,128)S(1)}, f32[8,512]{1,0:T(8,128)S(1)}, u32[]{:S(2)}, u32[]{:S(2)}) collective-permute-start(f32[8,512]{1,0:T(8,128)S(1)} %get-tuple-element.51), channel_id=1, source_target_pairs={{1,0},{2,1},{3,2},{5,4},{6,5},{7,6},{9,8},{10,9},{11,10},{13,12},{... | collective-permute-start | bytes 49160 | tf_op jit(solution)/shard_map/ppermute | solution.py:24
  70.7 11.3 %collective-permute-start.11 = (f32[8,512]{1,0:T(8,128)S(1)}, f32[8,512]{1,0:T(8,128)S(1)}, u32[]{:S(2)}, u32[]{:S(2)}) collective-permute-start(f32[8,512]{1,0:T(8,128)S(1)} %get-tuple-element.52.col7_ref), channel_id=1, source_target_pairs={{0,1},{1,2},{2,3},{4,5},{5,6},{6,7},{8,9},{9,10},{10,11},{12,13},{... | collective-permute-start | bytes 49160 | tf_op jit(solution)/shard_map/ppermute | solution.py:24

commit v8 on v7

--- a/solution.py
+++ b/solution.py
@@ -10,7 +10,7 @@
 ITERS = 3
 LANES = 128
 SUBLANES = 8
-GROUP = 16
+GROUP = 32
 
 SHIFT = 6.0
 IN_VMEM = pl.BlockSpec(memory_space=pltpu.VMEM)
@@ -100,12 +100,16 @@
     return functools.reduce(lambda s, t: s + t, [a * b for a, b in zip(x, y)])
 
 
+def is_compact(capacity):
+    return capacity % 16 == 0 and LANES % capacity == 0
+
+
 def pack_kernel(
     capacity, owner_hbm, cell_hbm, live_hbm, traces_hbm, p1_hbm, p2_hbm, out_ref, p1_last_ref, p2_last_ref,
     owner_ref, cell_ref, live_ref, traces_ref, sems,
 ):
     held, samples = traces_ref.shape
-    slots = out_ref.shape[0]
+    slots = lax.axis_size("inl") * lax.axis_size("xl") * capacity
     rows, cols, _ = p1_hbm.shape
     pairs = (
         (owner_hbm, owner_ref), (cell_hbm, cell_ref), (live_hbm, live_ref), (traces_hbm, traces_ref),
@@ -128,30 +132,61 @@
     upper = (lax.shift_right_logical(cell, 6) + 1).astype(jnp.float32)
     lower = (cell & 63).astype(jnp.float32)
     codes = jnp.where(kind == 0, upper, jnp.where(kind == 1, lower, 0.0)).astype(jnp.bfloat16)
-    sent = lax.dot_general(chosen, codes, (((1,), (1,)), ((), ())), preferred_element_type=jnp.float32)
-    out_ref[:, samples:] = sent.astype(jnp.bfloat16)
-    copies[3].wait()
-    rows = jnp.dot(chosen, traces_ref[...], preferred_element_type=jnp.float32)
-    out_ref[:, :samples] = rows.astype(jnp.bfloat16)
+    if not is_compact(capacity):
+        sent = lax.dot_general(chosen, codes, (((1,), (1,)), ((), ())), preferred_element_type=jnp.float32)
+        out_ref[:, samples:] = sent.astype(jnp.bfloat16)
+        copies[3].wait()
+        packed = jnp.dot(chosen, traces_ref[...], preferred_element_type=jnp.float32)
+        out_ref[:, :samples] = packed.astype(jnp.bfloat16)
+    else:
+        sent = lax.dot_general(codes[:16], chosen, (((1,), (1,)), ((), ())), preferred_element_type=jnp.float32)
+        per = LANES // capacity
+        here = lax.rem(lax.axis_index("inl") * lax.axis_size("xl") + lax.axis_index("xl"), per)
+        mine = lax.div(iota((SUBLANES, LANES), 1), capacity) == here
+        moves = [lax.rem(here - j + per, per) * capacity for j in range(per)]
+        copies[3].wait()
+        packed = jnp.dot(chosen, traces_ref[...], preferred_element_type=jnp.float32)
+        for d in range(slots // capacity):
+            at = slice(d * capacity, (d + 1) * capacity)
+            tile = slice(d // per * LANES, (d // per + 1) * LANES)
+            code = jnp.where(mine, pltpu.roll(sent[:SUBLANES, tile], moves[d % per], 1), 0.0)
+            parts = [packed[at, c : c + LANES] for c in range(0, samples, LANES)]
+            out_ref[d] = jnp.concatenate(parts + [code], axis=0).astype(jnp.bfloat16)
     for copy in copies[4:]:
         copy.wait()
 
 
-def bin_kernel(got_ref, p1_ref, p2_ref, b_ref, diag_ref, *edge_refs):
+def unpack(capacity, samples, got_ref):
+    if not is_compact(capacity):
+        kind = iota((SUBLANES, LANES), 1)
+        weight = jnp.where(kind == 0, 64.0, jnp.where(kind == 1, 1.0, 0.0)).astype(jnp.bfloat16)
+        value = lax.dot_general(
+            weight, got_ref[:, samples:], (((1,), (1,)), ((), ())), preferred_element_type=jnp.float32
+        )
+        return got_ref[:, :samples], value[:1].astype(jnp.int32) - 64
+    sources, per = got_ref.shape[0], LANES // capacity
+    blocks = [got_ref[d].astype(jnp.float32) for d in range(sources)]
+    tiles = samples // LANES
+    values = []
+    for first in range(0, sources, per):
+        code = functools.reduce(lambda s, t: s + t, [blocks[d][tiles * capacity :] for d in range(first, first + per)])
+        values.append(64.0 * code[:1] + code[1:2] - 64.0)
+    columns = [
+        jnp.concatenate([blocks[d][c * capacity : (c + 1) * capacity] for d in range(sources)], axis=0)
+        for c in range(tiles)
+    ]
+    got = jnp.concatenate([column.astype(jnp.bfloat16) for column in columns], axis=1)
+    return got, jnp.concatenate(values, axis=1).astype(jnp.int32)
+
+
+def bin_kernel(capacity, got_ref, p1_ref, p2_ref, b_ref, diag_ref, *edge_refs):
     rows, tiles, cols, _ = b_ref.shape
-    samples = tiles * LANES
-    slots = got_ref.shape[0]
-    kind = iota((SUBLANES, LANES), 1)
-    weight = jnp.where(kind == 0, 64.0, jnp.where(kind == 1, 1.0, 0.0)).astype(jnp.bfloat16)
-    value = lax.dot_general(
-        weight, got_ref[:, samples:], (((1,), (1,)), ((), ())), preferred_element_type=jnp.float32
-    )
-    bin_of = value[:1].astype(jnp.int32) - 64
+    got, bin_of = unpack(capacity, tiles * LANES, got_ref)
+    slots = got.shape[0]
     not_first_row = (lax.axis_index("inl") > 0).astype(jnp.float32)
     not_first_col = (lax.axis_index("xl") > 0).astype(jnp.float32)
     ones = jnp.ones((slots, LANES), jnp.bfloat16)
     first_col = jnp.where(iota((cols, LANES), 0) == 0, not_first_col, 0.0) - SHIFT
-    got = got_ref[:, :samples]
     for i in range(rows):
         place = (iota((cols, slots), 0) + i * cols == bin_of).astype(jnp.float32).astype(jnp.bfloat16)
         total = jnp.dot(place, got, preferred_element_type=jnp.float32)
@@ -422,12 +457,15 @@
     held = traces.shape[0]
     capacity = max(2, 2 * held // devices)
     slots = devices * capacity
+    message = (slots, samples + LANES)
+    if is_compact(capacity):
+        message = (devices, samples // LANES * capacity + SUBLANES, LANES)
     small = pltpu.VMEM((1, held), jnp.int32)
     inputs = (trace_owner.reshape(1, held), trace_cell[None], acquired[None], traces, inline_dip, cross_dip)
     sent, p1_last, p2_last = call(
         functools.partial(pack_kernel, capacity),
         [
-            jax.ShapeDtypeStruct((slots, samples + LANES), jnp.bfloat16),
+            jax.ShapeDtypeStruct(message, jnp.bfloat16),
             f32(cols, samples),
             f32(rows, SUBLANES, samples),
         ],
@@ -439,7 +477,8 @@
     edge_shapes = [f32(cols, samples), f32(cols, samples), f32(rows, samples), f32(rows, samples)]
     tile = f32(rows, samples // LANES, cols, LANES)
     b, diag, *edges = call(
-        bin_kernel, [tile, f32(rows, cols, LANES)] + edge_shapes, got, p1_last, p2_last, name="bin"
+        functools.partial(bin_kernel, capacity), [tile, f32(rows, cols, LANES)] + edge_shapes, got, p1_last, p2_last,
+        name="bin",
     )
     fields, sums, products = [b], [], []
     cost = pl.CostEstimate(

time: 97.7 us -> 96 us (0.983)
  blocking collectives: 36.5 us -> 35.2 us
    all_to_all x1, blocking collectives: 24 us -> 22.7 us  [per_device(): lax.all_to_all(sent, ('inl', 'xl'), split_axis=0, concat_axis=0, tiled=True)]
where the time goes in v8:
time: 96 us; the launch traced here: 95.5 us
  blocking collectives  35.2 us (37%)
  starting transfers between devices  32.6 us (34%)
  Pallas kernels  26.8 us (28%)
    ppermute x12, starting transfers between devices, shifted(): lax.ppermute(value, axis, [(source, source + steps) for source in range(i...  32.6 us
    pallas_call x9, Pallas kernels, call(): pl.pallas_call(kernel, out_shape=outs, in_specs=ins or [IN_VMEM] * len(ar...  26.8 us
    all_to_all x1, blocking collectives, per_device(): lax.all_to_all(sent, ('inl', 'xl'), split_axis=0, concat_axis=0, tiled=True)  22.7 us
    all_to_all x1, blocking collectives, per_device(): lax.all_to_all(message, ('inl', 'xl'), split_axis=0, concat_axis=0, tiled...  12.5 us
  transfers between devices with their start and end apart: 12, of which 0 were waited for; matrix products, arithmetic and copies ran while one was open for 0% of the time, Pallas kernels for 21%

profile of v8, /device:TPU:0, one launch (start us, length us, event | category | flops | bytes accessed | tf_op | source)
XLA Modules:
  0.0 95.5 jit_solution(4753179594053051007)
XLA Ops:
  0.6 0.0 copy-start.1
  0.6 1.5 %pack.1 = (bf16[32,72,128]{2,1,0:T(8,128)(2,1)S(1)}, f32[128,512]{1,0:T(8,128)S(1)}, f32[8,8,512]{2,1,0:T(8,128)S(1)}) custom-call(s32[1,256]{1,0:T(1,128)} %bitcast.3, s32[1,256]{1,0:T(1,128)} %bitcast.4, s32[1,256]{1,0:T(1,128)} %bitcast.5, bf16[256,512]{1,0:T(8,128)(2,1)} %traces_hbm.1, f32[8,128,512]{2,1,0:T(8,128)} %p1_ref.11, f32[8,128,512]{2,1,0:T(8,128)} %p2_ref.11), custom_call_target="tpu_custom_call" | custom-call | tf_op jit(solution)/shard_map/pack/pallas_call | solution.py:437
  2.2 0.0 copy-start
  2.2 22.7 %all_to_all.10.got_ref = bf16[32,72,128]{2,1,0:T(8,128)(2,1)S(1)} all-to-all(bf16[32,72,128]{2,1,0:T(8,128)(2,1)S(1)} %get-tuple-element.31), channel_id=1, replica_groups=mesh['inl'=8,'xl'=4] {'inl','xl'}, dimensions={0} | all-to-all | bytes 1179648 | tf_op jit(solution)/shard_map/all_to_all | solution.py:476
  24.9 1.2 %bin.1 = (f32[8,4,128,128]{3,2,1,0:T(8,128)S(1)}, f32[8,128,128]{2,1,0:T(8,128)S(1)}, f32[128,512]{1,0:T(8,128)S(1)}, f32[128,512]{1,0:T(8,128)S(1)}, f32[8,512]{1,0:T(8,128)S(1)}, /*index=5*/f32[8,512]{1,0:T(8,128)S(1)}) custom-call(bf16[32,72,128]{2,1,0:T(8,128)(2,1)S(1)} %all_to_all.10.got_ref, f32[128,512]{1,0:T(8,128)S(1)} %get-tuple-element.32.p1_ref, ...), custom_call_target="tpu_custom_call" | custom-call | tf_op jit(solution)/shard_map/bin/pallas_call | solution.py:437
  26.1 1.3 %collective-permute-start = (f32[128,512]{1,0:T(8,128)S(1)}, f32[128,512]{1,0:T(8,128)S(1)}, u32[]{:S(2)}, u32[]{:S(2)}) collective-permute-start(f32[128,512]{1,0:T(8,128)S(1)} %get-tuple-element.37), channel_id=1, source_target_pairs={{4,0},{8,4},{12,8},{16,12},{20,16},{24,20},{28,24},{5,1},{9,5},{13... | collective-permute-start | bytes 786440 | tf_op jit(solution)/shard_map/ppermute | solution.py:24
  27.4 3.8 %collective-permute-start.1 = (f32[128,512]{1,0:T(8,128)S(1)}, f32[128,512]{1,0:T(8,128)S(1)}, u32[]{:S(2)}, u32[]{:S(2)}) collective-permute-start(f32[128,512]{1,0:T(8,128)S(1)} %get-tuple-element.38.row7_ref), channel_id=1, source_target_pairs={{0,4},{4,8},{8,12},{12,16},{16,20},{20,24},{24,28},{1,5},{5,9},{9,... | collective-permute-start | bytes 786440 | tf_op jit(solution)/shard_map/ppermute | solution.py:24
  31.3 1.3 %collective-permute-start.2 = (f32[8,512]{1,0:T(8,128)S(1)}, f32[8,512]{1,0:T(8,128)S(1)}, u32[]{:S(2)}, u32[]{:S(2)}) collective-permute-start(f32[8,512]{1,0:T(8,128)S(1)} %get-tuple-element.39), channel_id=1, source_target_pairs={{1,0},{2,1},{3,2},{5,4},{6,5},{7,6},{9,8},{10,9},{11,10},{13,12},{... | collective-permute-start | bytes 49160 | tf_op jit(solution)/shard_map/ppermute | solution.py:24
  32.6 4.5 %collective-permute-start.3 = (f32[8,512]{1,0:T(8,128)S(1)}, f32[8,512]{1,0:T(8,128)S(1)}, u32[]{:S(2)}, u32[]{:S(2)}) collective-permute-start(f32[8,512]{1,0:T(8,128)S(1)} %get-tuple-element.40.col7_ref), channel_id=1, source_target_pairs={{0,1},{1,2},{2,3},{4,5},{5,6},{6,7},{8,9},{9,10},{10,11},{12,13},{... | collective-permute-start | bytes 49160 | tf_op jit(solution)/shard_map/ppermute | solution.py:24
  37.1 0.0 copy-done.1
  37.1 0.0 copy-done
  37.1 6.8 %apply.3 = (f32[8,4,128,128]{3,2,1,0:T(8,128)S(1)}, f32[2,8,128]{2,1,0:T(8,128)S(1)}) custom-call(f32[8,4,128,128]{3,2,1,0:T(8,128)S(1)} %get-tuple-element.34.v_ref.b_ref, f32[8,128,512]{2,1,0:T(8,128)S(1)} %copy-done, f32[8,128,512]{2,1,0:T(8,128)S(1)} %copy-done.1, f32[8,128,128]{2,1,0:T(8,128)S(1)} %get-tuple-element.35.diag_ref), custom_call_target="tpu_custom_call" | custom-call | flops 31457280 | bytes 8388608 | tf_op jit(solution)/shard_map/apply/pallas_call | solution.py:437
  43.9 0.0 collective-permute-done.2.right_ref
  43.9 0.0 collective-permute-done.3.left_ref
  43.9 0.0 collective-permute-done.below_ref
  43.9 0.0 collective-permute-done.1.above_ref
  43.9 0.6 correct.2
  44.5 1.3 %collective-permute-start.4 = (f32[128,512]{1,0:T(8,128)S(1)}, f32[128,512]{1,0:T(8,128)S(1)}, u32[]{:S(2)}, u32[]{:S(2)}) collective-permute-start(f32[128,512]{1,0:T(8,128)S(1)} %get-tuple-element.43), channel_id=1, source_target_pairs={{4,0},{8,4},{12,8},{16,12},{20,16},{24,20},{28,24},{5,1},{9,5},{13... | collective-permute-start | bytes 786440 | tf_op jit(solution)/shard_map/ppermute | solution.py:24
  45.8 3.7 %collective-permute-start.5 = (f32[128,512]{1,0:T(8,128)S(1)}, f32[128,512]{1,0:T(8,128)S(1)}, u32[]{:S(2)}, u32[]{:S(2)}) collective-permute-start(f32[128,512]{1,0:T(8,128)S(1)} %get-tuple-element.44.row7_ref), channel_id=1, source_target_pairs={{0,4},{4,8},{8,12},{12,16},{16,20},{20,24},{24,28},{1,5},{5,9},{9,... | collective-permute-start | bytes 786440 | tf_op jit(solution)/shard_map/ppermute | solution.py:24
  49.5 1.3 %collective-permute-start.6 = (f32[8,512]{1,0:T(8,128)S(1)}, f32[8,512]{1,0:T(8,128)S(1)}, u32[]{:S(2)}, u32[]{:S(2)}) collective-permute-start(f32[8,512]{1,0:T(8,128)S(1)} %get-tuple-element.45), channel_id=1, source_target_pairs={{1,0},{2,1},{3,2},{5,4},{6,5},{7,6},{9,8},{10,9},{11,10},{13,12},{... | collective-permute-start | bytes 49160 | tf_op jit(solution)/shard_map/ppermute | solution.py:24
  50.8 4.5 %collective-permute-start.7 = (f32[8,512]{1,0:T(8,128)S(1)}, f32[8,512]{1,0:T(8,128)S(1)}, u32[]{:S(2)}, u32[]{:S(2)}) collective-permute-start(f32[8,512]{1,0:T(8,128)S(1)} %get-tuple-element.46.col7_ref), channel_id=1, source_target_pairs={{0,1},{1,2},{2,3},{4,5},{5,6},{6,7},{8,9},{9,10},{10,11},{12,13},{... | collective-permute-start | bytes 49160 | tf_op jit(solution)/shard_map/ppermute | solution.py:24
  55.4 6.8 %apply.4 = (f32[8,4,128,128]{3,2,1,0:T(8,128)S(1)}, f32[2,8,128]{2,1,0:T(8,128)S(1)}) custom-call(f32[8,4,128,128]{3,2,1,0:T(8,128)S(1)} %get-tuple-element.41.v_ref.v1_ref, f32[8,128,512]{2,1,0:T(8,128)S(1)} %copy-done, f32[8,128,512]{2,1,0:T(8,128)S(1)} %copy-done.1, f32[8,128,128]{2,1,0:T(8,128)S(1)} %get-tuple-element.35.diag_ref), custom_call_target="tpu_custom_call" | custom-call | flops 31457280 | bytes 8388608 | tf_op jit(solution)/shard_map/apply/pallas_call | solution.py:437
  62.1 0.0 collective-permute-done.6.right_ref
  62.2 0.0 collective-permute-done.7.left_ref
  62.2 0.0 collective-permute-done.4.below_ref
  62.2 0.0 collective-permute-done.5.above_ref
  62.2 0.5 correct.3
  62.7 1.3 %collective-permute-start.8 = (f32[128,512]{1,0:T(8,128)S(1)}, f32[128,512]{1,0:T(8,128)S(1)}, u32[]{:S(2)}, u32[]{:S(2)}) collective-permute-start(f32[128,512]{1,0:T(8,128)S(1)} %get-tuple-element.49), channel_id=1, source_target_pairs={{4,0},{8,4},{12,8},{16,12},{20,16},{24,20},{28,24},{5,1},{9,5},{13... | collective-permute-start | bytes 786440 | tf_op jit(solution)/shard_map/ppermute | solution.py:24
  64.0 3.7 %collective-permute-start.9 = (f32[128,512]{1,0:T(8,128)S(1)}, f32[128,512]{1,0:T(8,128)S(1)}, u32[]{:S(2)}, u32[]{:S(2)}) collective-permute-start(f32[128,512]{1,0:T(8,128)S(1)} %get-tuple-element.50.row7_ref), channel_id=1, source_target_pairs={{0,4},{4,8},{8,12},{12,16},{16,20},{20,24},{24,28},{1,5},{5,9},{9,... | collective-permute-start | bytes 786440 | tf_op jit(solution)/shard_map/ppermute | solution.py:24
  67.7 1.3 %collective-permute-start.10 = (f32[8,512]{1,0:T(8,128)S(1)}, f32[8,512]{1,0:T(8,128)S(1)}, u32[]{:S(2)}, u32[]{:S(2)}) collective-permute-start(f32[8,512]{1,0:T(8,128)S(1)} %get-tuple-element.51), channel_id=1, source_target_pairs={{1,0},{2,1},{3,2},{5,4},{6,5},{7,6},{9,8},{10,9},{11,10},{13,12},{... | collective-permute-start | bytes 49160 | tf_op jit(solution)/shard_map/ppermute | solution.py:24
  69.0 4.5 %collective-permute-start.11 = (f32[8,512]{1,0:T(8,128)S(1)}, f32[8,512]{1,0:T(8,128)S(1)}, u32[]{:S(2)}, u32[]{:S(2)}) collective-permute-start(f32[8,512]{1,0:T(8,128)S(1)} %get-tuple-element.52.col7_ref), channel_id=1, source_target_pairs={{0,1},{1,2},{2,3},{4,5},{5,6},{6,7},{8,9},{9,10},{10,11},{12,13},{... | collective-permute-start | bytes 49160 | tf_op jit(solution)/shard_map/ppermute | solution.py:24
  73.6 6.7 %apply.5 = (f32[8,4,128,128]{3,2,1,0:T(8,128)S(1)}, f32[2,8,128]{2,1,0:T(8,128)S(1)}) custom-call(f32[8,4,128,128]{3,2,1,0:T(8,128)S(1)} %get-tuple-element.47.v_ref.v2_ref, f32[8,128,512]{2,1,0:T(8,128)S(1)} %copy-done, f32[8,128,512]{2,1,0:T(8,128)S(1)} %copy-done.1, f32[8,128,128]{2,1,0:T(8,128)S(1)} %get-tuple-element.35.diag_ref), custom_call_target="tpu_custom_call" | custom-call | flops 31457280 | bytes 8388608 | tf_op jit(solution)/shard_map/apply/pallas_call | solution.py:437
  80.3 0.0 collective-permute-done.10.right_ref
  80.3 0.0 collective-permute-done.11.left_ref
  80.3 0.0 collective-permute-done.8.below_ref
  80.3 0.0 collective-permute-done.9.above_ref
  80.3 0.4 moments.1
  80.7 12.5 %all_to_all.11.parts_ref = f32[32,1,128]{2,1,0:T(1,128)S(1)} all-to-all(f32[32,1,128]{2,1,0:T(1,128)S(1)} %get-tuple-element.58), channel_id=1, replica_groups=mesh['inl'=8,'xl'=4] {'inl','xl'}, dimensions={0} | all-to-all | bytes 32768 | tf_op jit(solution)/shard_map/all_to_all | solution.py:514
  93.2 2.4 %finish.1 = (f32[8,128,512]{2,1,0:T(8,128)}, f32[8,128,512]{2,1,0:T(8,128)}) custom-call(f32[32,1,128]{2,1,0:T(1,128)S(1)} %all_to_all.11.parts_ref, f32[8,4,128,128]{3,2,1,0:T(8,128)S(1)} %get-tuple-element.34.v_ref.b_ref, f32[8,4,128,128]{3,2,1,0:T(8,128)S(1)} %get-tuple-element.41.v_ref.v1_ref, f32[8,4,128,128]{3,2,1,0:T(8,128)S(1)} %get-tuple-element.47.v_ref.v2_ref, ...), custom_call_target="tpu_custom_call" | custom-call | tf_op jit(solution)/shard_map/finish/pallas_call | solution.py:437
Async XLA Ops:
  0.6 36.5 %copy-start.1 = (f32[8,128,512]{2,1,0:T(8,128)S(1)}, f32[8,128,512]{2,1,0:T(8,128)}, u32[]{:S(2)}) copy-start(f32[8,128,512]{2,1,0:T(8,128)} %p2_ref.11) | copy-start | bytes 6291460
  2.2 34.9 %copy-start = (f32[8,128,512]{2,1,0:T(8,128)S(1)}, f32[8,128,512]{2,1,0:T(8,128)}, u32[]{:S(2)}) copy-start(f32[8,128,512]{2,1,0:T(8,128)} %p1_ref.11) | copy-start | bytes 6291460
  26.1 17.8 %collective-permute-start = (f32[128,512]{1,0:T(8,128)S(1)}, f32[128,512]{1,0:T(8,128)S(1)}, u32[]{:S(2)}, u32[]{:S(2)}) collective-permute-start(f32[128,512]{1,0:T(8,128)S(1)} %get-tuple-element.37), channel_id=1, source_target_pairs={{4,0},{8,4},{12,8},{16,12},{20,16},{24,20},{28,24},{5,1},{9,5},{13... | collective-permute-start | bytes 786440 | tf_op jit(solution)/shard_map/ppermute | solution.py:24
  27.4 16.5 %collective-permute-start.1 = (f32[128,512]{1,0:T(8,128)S(1)}, f32[128,512]{1,0:T(8,128)S(1)}, u32[]{:S(2)}, u32[]{:S(2)}) collective-permute-start(f32[128,512]{1,0:T(8,128)S(1)} %get-tuple-element.38.row7_ref), channel_id=1, source_target_pairs={{0,4},{4,8},{8,12},{12,16},{16,20},{20,24},{24,28},{1,5},{5,9},{9,... | collective-permute-start | bytes 786440 | tf_op jit(solution)/shard_map/ppermute | solution.py:24
  31.3 12.6 %collective-permute-start.2 = (f32[8,512]{1,0:T(8,128)S(1)}, f32[8,512]{1,0:T(8,128)S(1)}, u32[]{:S(2)}, u32[]{:S(2)}) collective-permute-start(f32[8,512]{1,0:T(8,128)S(1)} %get-tuple-element.39), channel_id=1, source_target_pairs={{1,0},{2,1},{3,2},{5,4},{6,5},{7,6},{9,8},{10,9},{11,10},{13,12},{... | collective-permute-start | bytes 49160 | tf_op jit(solution)/shard_map/ppermute | solution.py:24
  32.6 11.4 %collective-permute-start.3 = (f32[8,512]{1,0:T(8,128)S(1)}, f32[8,512]{1,0:T(8,128)S(1)}, u32[]{:S(2)}, u32[]{:S(2)}) collective-permute-start(f32[8,512]{1,0:T(8,128)S(1)} %get-tuple-element.40.col7_ref), channel_id=1, source_target_pairs={{0,1},{1,2},{2,3},{4,5},{5,6},{6,7},{8,9},{9,10},{10,11},{12,13},{... | collective-permute-start | bytes 49160 | tf_op jit(solution)/shard_map/ppermute | solution.py:24
  44.5 17.7 %collective-permute-start.4 = (f32[128,512]{1,0:T(8,128)S(1)}, f32[128,512]{1,0:T(8,128)S(1)}, u32[]{:S(2)}, u32[]{:S(2)}) collective-permute-start(f32[128,512]{1,0:T(8,128)S(1)} %get-tuple-element.43), channel_id=1, source_target_pairs={{4,0},{8,4},{12,8},{16,12},{20,16},{24,20},{28,24},{5,1},{9,5},{13... | collective-permute-start | bytes 786440 | tf_op jit(solution)/shard_map/ppermute | solution.py:24
  45.8 16.4 %collective-permute-start.5 = (f32[128,512]{1,0:T(8,128)S(1)}, f32[128,512]{1,0:T(8,128)S(1)}, u32[]{:S(2)}, u32[]{:S(2)}) collective-permute-start(f32[128,512]{1,0:T(8,128)S(1)} %get-tuple-element.44.row7_ref), channel_id=1, source_target_pairs={{0,4},{4,8},{8,12},{12,16},{16,20},{20,24},{24,28},{1,5},{5,9},{9,... | collective-permute-start | bytes 786440 | tf_op jit(solution)/shard_map/ppermute | solution.py:24
  49.5 12.6 %collective-permute-start.6 = (f32[8,512]{1,0:T(8,128)S(1)}, f32[8,512]{1,0:T(8,128)S(1)}, u32[]{:S(2)}, u32[]{:S(2)}) collective-permute-start(f32[8,512]{1,0:T(8,128)S(1)} %get-tuple-element.45), channel_id=1, source_target_pairs={{1,0},{2,1},{3,2},{5,4},{6,5},{7,6},{9,8},{10,9},{11,10},{13,12},{... | collective-permute-start | bytes 49160 | tf_op jit(solution)/shard_map/ppermute | solution.py:24
  50.8 11.3 %collective-permute-start.7 = (f32[8,512]{1,0:T(8,128)S(1)}, f32[8,512]{1,0:T(8,128)S(1)}, u32[]{:S(2)}, u32[]{:S(2)}) collective-permute-start(f32[8,512]{1,0:T(8,128)S(1)} %get-tuple-element.46.col7_ref), channel_id=1, source_target_pairs={{0,1},{1,2},{2,3},{4,5},{5,6},{6,7},{8,9},{9,10},{10,11},{12,13},{... | collective-permute-start | bytes 49160 | tf_op jit(solution)/shard_map/ppermute | solution.py:24
  62.7 17.6 %collective-permute-start.8 = (f32[128,512]{1,0:T(8,128)S(1)}, f32[128,512]{1,0:T(8,128)S(1)}, u32[]{:S(2)}, u32[]{:S(2)}) collective-permute-start(f32[128,512]{1,0:T(8,128)S(1)} %get-tuple-element.49), channel_id=1, source_target_pairs={{4,0},{8,4},{12,8},{16,12},{20,16},{24,20},{28,24},{5,1},{9,5},{13... | collective-permute-start | bytes 786440 | tf_op jit(solution)/shard_map/ppermute | solution.py:24
  64.0 16.3 %collective-permute-start.9 = (f32[128,512]{1,0:T(8,128)S(1)}, f32[128,512]{1,0:T(8,128)S(1)}, u32[]{:S(2)}, u32[]{:S(2)}) collective-permute-start(f32[128,512]{1,0:T(8,128)S(1)} %get-tuple-element.50.row7_ref), channel_id=1, source_target_pairs={{0,4},{4,8},{8,12},{12,16},{16,20},{20,24},{24,28},{1,5},{5,9},{9,... | collective-permute-start | bytes 786440 | tf_op jit(solution)/shard_map/ppermute | solution.py:24
  67.7 12.6 %collective-permute-start.10 = (f32[8,512]{1,0:T(8,128)S(1)}, f32[8,512]{1,0:T(8,128)S(1)}, u32[]{:S(2)}, u32[]{:S(2)}) collective-permute-start(f32[8,512]{1,0:T(8,128)S(1)} %get-tuple-element.51), channel_id=1, source_target_pairs={{1,0},{2,1},{3,2},{5,4},{6,5},{7,6},{9,8},{10,9},{11,10},{13,12},{... | collective-permute-start | bytes 49160 | tf_op jit(solution)/shard_map/ppermute | solution.py:24
  69.0 11.3 %collective-permute-start.11 = (f32[8,512]{1,0:T(8,128)S(1)}, f32[8,512]{1,0:T(8,128)S(1)}, u32[]{:S(2)}, u32[]{:S(2)}) collective-permute-start(f32[8,512]{1,0:T(8,128)S(1)} %get-tuple-element.52.col7_ref), channel_id=1, source_target_pairs={{0,1},{1,2},{2,3},{4,5},{5,6},{6,7},{8,9},{9,10},{10,11},{12,13},{... | collective-permute-start | bytes 49160 | tf_op jit(solution)/shard_map/ppermute | solution.py:24

commit v9 on v8

--- a/solution.py
+++ b/solution.py
@@ -10,7 +10,7 @@
 ITERS = 3
 LANES = 128
 SUBLANES = 8
-GROUP = 32
+GROUP = 16
 
 SHIFT = 6.0
 IN_VMEM = pl.BlockSpec(memory_space=pltpu.VMEM)
@@ -214,28 +214,23 @@
         store(col7_ref, [t[SUBLANES - 1 :] for t in moved], slice(i, i + 1))
 
 
-def apply_kernel(v_ref, p1_ref, p2_ref, diag_ref, out_ref, sums_ref, second_ref):
+def apply_kernel(v_ref, p1_ref, p2_ref, diag_ref, out_ref, sums_ref, edge_ref):
     rows, tiles, cols, _ = v_ref.shape
     sub_index = iota((SUBLANES, LANES), 0)
     zero = [jnp.zeros((SUBLANES, LANES), jnp.float32)] * tiles
-    for i in range(rows):
-        for c in range(tiles):
-            second_ref[i, c, :SUBLANES, :] = zero[0]
-
-    def filters(i, x, v, shifted_v, above, below):
+    edge_ref[...] = jnp.zeros_like(edge_ref)
+
+    def roll_tiles(values, steps):
+        return [pltpu.roll(t, steps, 0) for t in values]
+
+    def filters(i, x, v, right, shifted_v, above, below, down_before):
         at = slice(x, x + SUBLANES)
-        v_row, second_row = v_ref.at[i], second_ref.at[i]
         odd, even = shifted_v
         p1, p2 = load(p1_ref.at[i], at), load(p2_ref.at[i], at)
-        if x + SUBLANES < cols:
-            right = load_tiles(v_row, slice(x + 1, x + 1 + SUBLANES))
-        else:
-            right = [jnp.where(sub_index == SUBLANES - 1, 0.0, pltpu.roll(t, SUBLANES - 1, 0)) for t in v]
         first = sub(sub(below, v), dip_part(p1, odd, even))
         second = sub(sub(right, v), dip_part(p2, odd, even))
-        for c in range(tiles):
-            second_row[c, x + SUBLANES : x + 2 * SUBLANES, :] = second[c]
-        left = [second_row[c, x + SUBLANES - 1 : x + 2 * SUBLANES - 1, :] for c in range(tiles)]
+        down = roll_tiles(second, 1)
+        left = [jnp.where(sub_index == 0, e, t) for e, t in zip(down_before, down)]
         a1, b1 = adjoint_terms(p1, first)
         a2, b2 = adjoint_terms(p2, second)
         a, b = add(a1, a2), add(b1, b2)
@@ -244,7 +239,7 @@
             (diag * c + (f + s)) - ((f1 + s1) - (y + y))
             for c, f, s, f1, s1, y in zip(v, above, left, first, second, b)
         ]
-        return first, (rest, add(a, b), sub(b, a))
+        return first, (rest, add(a, b), sub(b, a)), down
 
     def adjoint(i, x, pending):
         at = slice(x, x + SUBLANES)
@@ -264,8 +259,23 @@
             return below, [stencil(tiles_of) for tiles_of in below]
 
         def all_filters(i, v, shifted_v, first, below):
-            done = [filters(i, k, *rest) for k, *rest in zip(chunks, v, shifted_v, first, below)]
-            return [pair[0] for pair in done], [pair[1] for pair in done]
+            leads = [roll_tiles(tiles_of, SUBLANES - 1) for tiles_of in v]
+            if x + GROUP < cols:
+                following = load_tiles(v_ref.at[i], slice(x + GROUP, x + GROUP + SUBLANES))
+                leads.append(roll_tiles(following, SUBLANES - 1))
+            else:
+                leads.append(zero)
+            edge_row = edge_ref.at[i]
+            down = load_tiles(edge_row, slice(None))
+            firsts, pending = [], []
+            for n, k in enumerate(chunks):
+                right = [jnp.where(sub_index == SUBLANES - 1, e, t) for e, t in zip(leads[n + 1], leads[n])]
+                made, waiting, down = filters(i, k, v[n], right, shifted_v[n], first[n], below[n], down)
+                firsts.append(made)
+                pending.append(waiting)
+            for c in range(tiles):
+                edge_row[c, :, :] = down[c]
+            return firsts, pending
 
         def all_adjoint(i, own, pending):
             for k, waiting in zip(chunks, pending):
@@ -495,7 +505,7 @@
             [tile, f32(2, SUBLANES, LANES)],
             fields[-1], inline_dip, cross_dip, diag,
             name="apply",
-            scratch=[pltpu.VMEM((rows, samples // LANES, SUBLANES + cols, LANES), jnp.float32)],
+            scratch=[pltpu.VMEM((rows, samples // LANES, SUBLANES, LANES), jnp.float32)],
             cost=cost,
         )
         sums.append(partial)

time: 96 us -> 95.4 us (level)
  no operation moved by 1% of the time
where the time goes in v9:
time: 95.4 us; the launch traced here: 95 us
  blocking collectives  35.2 us (37%)
  starting transfers between devices  32.6 us (34%)
  Pallas kernels  26.2 us (27%)
    ppermute x12, starting transfers between devices, shifted(): lax.ppermute(value, axis, [(source, source + steps) for source in range(i...  32.6 us
    pallas_call x9, Pallas kernels, call(): pl.pallas_call(kernel, out_shape=outs, in_specs=ins or [IN_VMEM] * len(ar...  26.2 us
    all_to_all x1, blocking collectives, per_device(): lax.all_to_all(sent, ('inl', 'xl'), split_axis=0, concat_axis=0, tiled=True)  22.7 us
    all_to_all x1, blocking collectives, per_device(): lax.all_to_all(message, ('inl', 'xl'), split_axis=0, concat_axis=0, tiled...  12.5 us
  transfers between devices with their start and end apart: 12, of which 0 were waited for; matrix products, arithmetic and copies ran while one was open for 0% of the time, Pallas kernels for 21%

profile of v9, /device:TPU:0, one launch (start us, length us, event | category | flops | bytes accessed | tf_op | source)
XLA Modules:
  0.0 95.0 jit_solution(15028740358786440892)
XLA Ops:
  0.6 0.0 copy-start.1
  0.6 1.5 %pack.1 = (bf16[32,72,128]{2,1,0:T(8,128)(2,1)S(1)}, f32[128,512]{1,0:T(8,128)S(1)}, f32[8,8,512]{2,1,0:T(8,128)S(1)}) custom-call(s32[1,256]{1,0:T(1,128)} %bitcast.3, s32[1,256]{1,0:T(1,128)} %bitcast.4, s32[1,256]{1,0:T(1,128)} %bitcast.5, bf16[256,512]{1,0:T(8,128)(2,1)} %traces_hbm.1, f32[8,128,512]{2,1,0:T(8,128)} %p1_ref.11, f32[8,128,512]{2,1,0:T(8,128)} %p2_ref.11), custom_call_target="tpu_custom_call" | custom-call | tf_op jit(solution)/shard_map/pack/pallas_call | solution.py:447
  2.2 0.0 copy-start
  2.2 22.7 %all_to_all.10.got_ref = bf16[32,72,128]{2,1,0:T(8,128)(2,1)S(1)} all-to-all(bf16[32,72,128]{2,1,0:T(8,128)(2,1)S(1)} %get-tuple-element.31), channel_id=1, replica_groups=mesh['inl'=8,'xl'=4] {'inl','xl'}, dimensions={0} | all-to-all | bytes 1179648 | tf_op jit(solution)/shard_map/all_to_all | solution.py:486
  24.9 1.2 %bin.1 = (f32[8,4,128,128]{3,2,1,0:T(8,128)S(1)}, f32[8,128,128]{2,1,0:T(8,128)S(1)}, f32[128,512]{1,0:T(8,128)S(1)}, f32[128,512]{1,0:T(8,128)S(1)}, f32[8,512]{1,0:T(8,128)S(1)}, /*index=5*/f32[8,512]{1,0:T(8,128)S(1)}) custom-call(bf16[32,72,128]{2,1,0:T(8,128)(2,1)S(1)} %all_to_all.10.got_ref, f32[128,512]{1,0:T(8,128)S(1)} %get-tuple-element.32.p1_ref, ...), custom_call_target="tpu_custom_call" | custom-call | tf_op jit(solution)/shard_map/bin/pallas_call | solution.py:447
  26.1 1.3 %collective-permute-start = (f32[128,512]{1,0:T(8,128)S(1)}, f32[128,512]{1,0:T(8,128)S(1)}, u32[]{:S(2)}, u32[]{:S(2)}) collective-permute-start(f32[128,512]{1,0:T(8,128)S(1)} %get-tuple-element.37), channel_id=1, source_target_pairs={{4,0},{8,4},{12,8},{16,12},{20,16},{24,20},{28,24},{5,1},{9,5},{13... | collective-permute-start | bytes 786440 | tf_op jit(solution)/shard_map/ppermute | solution.py:24
  27.4 3.8 %collective-permute-start.1 = (f32[128,512]{1,0:T(8,128)S(1)}, f32[128,512]{1,0:T(8,128)S(1)}, u32[]{:S(2)}, u32[]{:S(2)}) collective-permute-start(f32[128,512]{1,0:T(8,128)S(1)} %get-tuple-element.38.row7_ref), channel_id=1, source_target_pairs={{0,4},{4,8},{8,12},{12,16},{16,20},{20,24},{24,28},{1,5},{5,9},{9,... | collective-permute-start | bytes 786440 | tf_op jit(solution)/shard_map/ppermute | solution.py:24
  31.3 1.3 %collective-permute-start.2 = (f32[8,512]{1,0:T(8,128)S(1)}, f32[8,512]{1,0:T(8,128)S(1)}, u32[]{:S(2)}, u32[]{:S(2)}) collective-permute-start(f32[8,512]{1,0:T(8,128)S(1)} %get-tuple-element.39), channel_id=1, source_target_pairs={{1,0},{2,1},{3,2},{5,4},{6,5},{7,6},{9,8},{10,9},{11,10},{13,12},{... | collective-permute-start | bytes 49160 | tf_op jit(solution)/shard_map/ppermute | solution.py:24
  32.6 4.5 %collective-permute-start.3 = (f32[8,512]{1,0:T(8,128)S(1)}, f32[8,512]{1,0:T(8,128)S(1)}, u32[]{:S(2)}, u32[]{:S(2)}) collective-permute-start(f32[8,512]{1,0:T(8,128)S(1)} %get-tuple-element.40.col7_ref), channel_id=1, source_target_pairs={{0,1},{1,2},{2,3},{4,5},{5,6},{6,7},{8,9},{9,10},{10,11},{12,13},{... | collective-permute-start | bytes 49160 | tf_op jit(solution)/shard_map/ppermute | solution.py:24
  37.1 0.0 copy-done.1
  37.1 0.0 copy-done
  37.1 6.5 %apply.3 = (f32[8,4,128,128]{3,2,1,0:T(8,128)S(1)}, f32[2,8,128]{2,1,0:T(8,128)S(1)}) custom-call(f32[8,4,128,128]{3,2,1,0:T(8,128)S(1)} %get-tuple-element.34.v_ref.b_ref, f32[8,128,512]{2,1,0:T(8,128)S(1)} %copy-done, f32[8,128,512]{2,1,0:T(8,128)S(1)} %copy-done.1, f32[8,128,128]{2,1,0:T(8,128)S(1)} %get-tuple-element.35.diag_ref), custom_call_target="tpu_custom_call" | custom-call | flops 31457280 | bytes 8388608 | tf_op jit(solution)/shard_map/apply/pallas_call | solution.py:447
  43.7 0.0 collective-permute-done.2.right_ref
  43.7 0.0 collective-permute-done.3.left_ref
  43.7 0.0 collective-permute-done.below_ref
  43.7 0.0 collective-permute-done.1.above_ref
  43.7 0.6 correct.2
  44.3 1.3 %collective-permute-start.4 = (f32[128,512]{1,0:T(8,128)S(1)}, f32[128,512]{1,0:T(8,128)S(1)}, u32[]{:S(2)}, u32[]{:S(2)}) collective-permute-start(f32[128,512]{1,0:T(8,128)S(1)} %get-tuple-element.43), channel_id=1, source_target_pairs={{4,0},{8,4},{12,8},{16,12},{20,16},{24,20},{28,24},{5,1},{9,5},{13... | collective-permute-start | bytes 786440 | tf_op jit(solution)/shard_map/ppermute | solution.py:24
  45.6 3.7 %collective-permute-start.5 = (f32[128,512]{1,0:T(8,128)S(1)}, f32[128,512]{1,0:T(8,128)S(1)}, u32[]{:S(2)}, u32[]{:S(2)}) collective-permute-start(f32[128,512]{1,0:T(8,128)S(1)} %get-tuple-element.44.row7_ref), channel_id=1, source_target_pairs={{0,4},{4,8},{8,12},{12,16},{16,20},{20,24},{24,28},{1,5},{5,9},{9,... | collective-permute-start | bytes 786440 | tf_op jit(solution)/shard_map/ppermute | solution.py:24
  49.3 1.3 %collective-permute-start.6 = (f32[8,512]{1,0:T(8,128)S(1)}, f32[8,512]{1,0:T(8,128)S(1)}, u32[]{:S(2)}, u32[]{:S(2)}) collective-permute-start(f32[8,512]{1,0:T(8,128)S(1)} %get-tuple-element.45), channel_id=1, source_target_pairs={{1,0},{2,1},{3,2},{5,4},{6,5},{7,6},{9,8},{10,9},{11,10},{13,12},{... | collective-permute-start | bytes 49160 | tf_op jit(solution)/shard_map/ppermute | solution.py:24
  50.6 4.5 %collective-permute-start.7 = (f32[8,512]{1,0:T(8,128)S(1)}, f32[8,512]{1,0:T(8,128)S(1)}, u32[]{:S(2)}, u32[]{:S(2)}) collective-permute-start(f32[8,512]{1,0:T(8,128)S(1)} %get-tuple-element.46.col7_ref), channel_id=1, source_target_pairs={{0,1},{1,2},{2,3},{4,5},{5,6},{6,7},{8,9},{9,10},{10,11},{12,13},{... | collective-permute-start | bytes 49160 | tf_op jit(solution)/shard_map/ppermute | solution.py:24
  55.2 6.5 %apply.4 = (f32[8,4,128,128]{3,2,1,0:T(8,128)S(1)}, f32[2,8,128]{2,1,0:T(8,128)S(1)}) custom-call(f32[8,4,128,128]{3,2,1,0:T(8,128)S(1)} %get-tuple-element.41.v_ref.v1_ref, f32[8,128,512]{2,1,0:T(8,128)S(1)} %copy-done, f32[8,128,512]{2,1,0:T(8,128)S(1)} %copy-done.1, f32[8,128,128]{2,1,0:T(8,128)S(1)} %get-tuple-element.35.diag_ref), custom_call_target="tpu_custom_call" | custom-call | flops 31457280 | bytes 8388608 | tf_op jit(solution)/shard_map/apply/pallas_call | solution.py:447
  61.7 0.0 collective-permute-done.6.right_ref
  61.7 0.0 collective-permute-done.7.left_ref
  61.7 0.0 collective-permute-done.4.below_ref
  61.7 0.0 collective-permute-done.5.above_ref
  61.8 0.5 correct.3
  62.3 1.3 %collective-permute-start.8 = (f32[128,512]{1,0:T(8,128)S(1)}, f32[128,512]{1,0:T(8,128)S(1)}, u32[]{:S(2)}, u32[]{:S(2)}) collective-permute-start(f32[128,512]{1,0:T(8,128)S(1)} %get-tuple-element.49), channel_id=1, source_target_pairs={{4,0},{8,4},{12,8},{16,12},{20,16},{24,20},{28,24},{5,1},{9,5},{13... | collective-permute-start | bytes 786440 | tf_op jit(solution)/shard_map/ppermute | solution.py:24
  63.6 3.7 %collective-permute-start.9 = (f32[128,512]{1,0:T(8,128)S(1)}, f32[128,512]{1,0:T(8,128)S(1)}, u32[]{:S(2)}, u32[]{:S(2)}) collective-permute-start(f32[128,512]{1,0:T(8,128)S(1)} %get-tuple-element.50.row7_ref), channel_id=1, source_target_pairs={{0,4},{4,8},{8,12},{12,16},{16,20},{20,24},{24,28},{1,5},{5,9},{9,... | collective-permute-start | bytes 786440 | tf_op jit(solution)/shard_map/ppermute | solution.py:24
  67.3 1.3 %collective-permute-start.10 = (f32[8,512]{1,0:T(8,128)S(1)}, f32[8,512]{1,0:T(8,128)S(1)}, u32[]{:S(2)}, u32[]{:S(2)}) collective-permute-start(f32[8,512]{1,0:T(8,128)S(1)} %get-tuple-element.51), channel_id=1, source_target_pairs={{1,0},{2,1},{3,2},{5,4},{6,5},{7,6},{9,8},{10,9},{11,10},{13,12},{... | collective-permute-start | bytes 49160 | tf_op jit(solution)/shard_map/ppermute | solution.py:24
  68.6 4.5 %collective-permute-start.11 = (f32[8,512]{1,0:T(8,128)S(1)}, f32[8,512]{1,0:T(8,128)S(1)}, u32[]{:S(2)}, u32[]{:S(2)}) collective-permute-start(f32[8,512]{1,0:T(8,128)S(1)} %get-tuple-element.52.col7_ref), channel_id=1, source_target_pairs={{0,1},{1,2},{2,3},{4,5},{5,6},{6,7},{8,9},{9,10},{10,11},{12,13},{... | collective-permute-start | bytes 49160 | tf_op jit(solution)/shard_map/ppermute | solution.py:24
  73.2 6.6 %apply.5 = (f32[8,4,128,128]{3,2,1,0:T(8,128)S(1)}, f32[2,8,128]{2,1,0:T(8,128)S(1)}) custom-call(f32[8,4,128,128]{3,2,1,0:T(8,128)S(1)} %get-tuple-element.47.v_ref.v2_ref, f32[8,128,512]{2,1,0:T(8,128)S(1)} %copy-done, f32[8,128,512]{2,1,0:T(8,128)S(1)} %copy-done.1, f32[8,128,128]{2,1,0:T(8,128)S(1)} %get-tuple-element.35.diag_ref), custom_call_target="tpu_custom_call" | custom-call | flops 31457280 | bytes 8388608 | tf_op jit(solution)/shard_map/apply/pallas_call | solution.py:447
  79.7 0.0 collective-permute-done.10.right_ref
  79.7 0.0 collective-permute-done.11.left_ref
  79.8 0.0 collective-permute-done.8.below_ref
  79.8 0.0 collective-permute-done.9.above_ref
  79.8 0.4 moments.1
  80.1 12.5 %all_to_all.11.parts_ref = f32[32,1,128]{2,1,0:T(1,128)S(1)} all-to-all(f32[32,1,128]{2,1,0:T(1,128)S(1)} %get-tuple-element.58), channel_id=1, replica_groups=mesh['inl'=8,'xl'=4] {'inl','xl'}, dimensions={0} | all-to-all | bytes 32768 | tf_op jit(solution)/shard_map/all_to_all | solution.py:524
  92.6 2.4 %finish.1 = (f32[8,128,512]{2,1,0:T(8,128)}, f32[8,128,512]{2,1,0:T(8,128)}) custom-call(f32[32,1,128]{2,1,0:T(1,128)S(1)} %all_to_all.11.parts_ref, f32[8,4,128,128]{3,2,1,0:T(8,128)S(1)} %get-tuple-element.34.v_ref.b_ref, f32[8,4,128,128]{3,2,1,0:T(8,128)S(1)} %get-tuple-element.41.v_ref.v1_ref, f32[8,4,128,128]{3,2,1,0:T(8,128)S(1)} %get-tuple-element.47.v_ref.v2_ref, ...), custom_call_target="tpu_custom_call" | custom-call | tf_op jit(solution)/shard_map/finish/pallas_call | solution.py:447
Async XLA Ops:
  0.6 36.5 %copy-start.1 = (f32[8,128,512]{2,1,0:T(8,128)S(1)}, f32[8,128,512]{2,1,0:T(8,128)}, u32[]{:S(2)}) copy-start(f32[8,128,512]{2,1,0:T(8,128)} %p2_ref.11) | copy-start | bytes 6291460
  2.2 34.9 %copy-start = (f32[8,128,512]{2,1,0:T(8,128)S(1)}, f32[8,128,512]{2,1,0:T(8,128)}, u32[]{:S(2)}) copy-start(f32[8,128,512]{2,1,0:T(8,128)} %p1_ref.11) | copy-start | bytes 6291460
  26.1 17.6 %collective-permute-start = (f32[128,512]{1,0:T(8,128)S(1)}, f32[128,512]{1,0:T(8,128)S(1)}, u32[]{:S(2)}, u32[]{:S(2)}) collective-permute-start(f32[128,512]{1,0:T(8,128)S(1)} %get-tuple-element.37), channel_id=1, source_target_pairs={{4,0},{8,4},{12,8},{16,12},{20,16},{24,20},{28,24},{5,1},{9,5},{13... | collective-permute-start | bytes 786440 | tf_op jit(solution)/shard_map/ppermute | solution.py:24
  27.4 16.3 %collective-permute-start.1 = (f32[128,512]{1,0:T(8,128)S(1)}, f32[128,512]{1,0:T(8,128)S(1)}, u32[]{:S(2)}, u32[]{:S(2)}) collective-permute-start(f32[128,512]{1,0:T(8,128)S(1)} %get-tuple-element.38.row7_ref), channel_id=1, source_target_pairs={{0,4},{4,8},{8,12},{12,16},{16,20},{20,24},{24,28},{1,5},{5,9},{9,... | collective-permute-start | bytes 786440 | tf_op jit(solution)/shard_map/ppermute | solution.py:24
  31.3 12.4 %collective-permute-start.2 = (f32[8,512]{1,0:T(8,128)S(1)}, f32[8,512]{1,0:T(8,128)S(1)}, u32[]{:S(2)}, u32[]{:S(2)}) collective-permute-start(f32[8,512]{1,0:T(8,128)S(1)} %get-tuple-element.39), channel_id=1, source_target_pairs={{1,0},{2,1},{3,2},{5,4},{6,5},{7,6},{9,8},{10,9},{11,10},{13,12},{... | collective-permute-start | bytes 49160 | tf_op jit(solution)/shard_map/ppermute | solution.py:24
  32.6 11.1 %collective-permute-start.3 = (f32[8,512]{1,0:T(8,128)S(1)}, f32[8,512]{1,0:T(8,128)S(1)}, u32[]{:S(2)}, u32[]{:S(2)}) collective-permute-start(f32[8,512]{1,0:T(8,128)S(1)} %get-tuple-element.40.col7_ref), channel_id=1, source_target_pairs={{0,1},{1,2},{2,3},{4,5},{5,6},{6,7},{8,9},{9,10},{10,11},{12,13},{... | collective-permute-start | bytes 49160 | tf_op jit(solution)/shard_map/ppermute | solution.py:24
  44.3 17.4 %collective-permute-start.4 = (f32[128,512]{1,0:T(8,128)S(1)}, f32[128,512]{1,0:T(8,128)S(1)}, u32[]{:S(2)}, u32[]{:S(2)}) collective-permute-start(f32[128,512]{1,0:T(8,128)S(1)} %get-tuple-element.43), channel_id=1, source_target_pairs={{4,0},{8,4},{12,8},{16,12},{20,16},{24,20},{28,24},{5,1},{9,5},{13... | collective-permute-start | bytes 786440 | tf_op jit(solution)/shard_map/ppermute | solution.py:24
  45.6 16.2 %collective-permute-start.5 = (f32[128,512]{1,0:T(8,128)S(1)}, f32[128,512]{1,0:T(8,128)S(1)}, u32[]{:S(2)}, u32[]{:S(2)}) collective-permute-start(f32[128,512]{1,0:T(8,128)S(1)} %get-tuple-element.44.row7_ref), channel_id=1, source_target_pairs={{0,4},{4,8},{8,12},{12,16},{16,20},{20,24},{24,28},{1,5},{5,9},{9,... | collective-permute-start | bytes 786440 | tf_op jit(solution)/shard_map/ppermute | solution.py:24
  49.3 12.4 %collective-permute-start.6 = (f32[8,512]{1,0:T(8,128)S(1)}, f32[8,512]{1,0:T(8,128)S(1)}, u32[]{:S(2)}, u32[]{:S(2)}) collective-permute-start(f32[8,512]{1,0:T(8,128)S(1)} %get-tuple-element.45), channel_id=1, source_target_pairs={{1,0},{2,1},{3,2},{5,4},{6,5},{7,6},{9,8},{10,9},{11,10},{13,12},{... | collective-permute-start | bytes 49160 | tf_op jit(solution)/shard_map/ppermute | solution.py:24
  50.6 11.1 %collective-permute-start.7 = (f32[8,512]{1,0:T(8,128)S(1)}, f32[8,512]{1,0:T(8,128)S(1)}, u32[]{:S(2)}, u32[]{:S(2)}) collective-permute-start(f32[8,512]{1,0:T(8,128)S(1)} %get-tuple-element.46.col7_ref), channel_id=1, source_target_pairs={{0,1},{1,2},{2,3},{4,5},{5,6},{6,7},{8,9},{9,10},{10,11},{12,13},{... | collective-permute-start | bytes 49160 | tf_op jit(solution)/shard_map/ppermute | solution.py:24
  62.3 17.5 %collective-permute-start.8 = (f32[128,512]{1,0:T(8,128)S(1)}, f32[128,512]{1,0:T(8,128)S(1)}, u32[]{:S(2)}, u32[]{:S(2)}) collective-permute-start(f32[128,512]{1,0:T(8,128)S(1)} %get-tuple-element.49), channel_id=1, source_target_pairs={{4,0},{8,4},{12,8},{16,12},{20,16},{24,20},{28,24},{5,1},{9,5},{13... | collective-permute-start | bytes 786440 | tf_op jit(solution)/shard_map/ppermute | solution.py:24
  63.6 16.2 %collective-permute-start.9 = (f32[128,512]{1,0:T(8,128)S(1)}, f32[128,512]{1,0:T(8,128)S(1)}, u32[]{:S(2)}, u32[]{:S(2)}) collective-permute-start(f32[128,512]{1,0:T(8,128)S(1)} %get-tuple-element.50.row7_ref), channel_id=1, source_target_pairs={{0,4},{4,8},{8,12},{12,16},{16,20},{20,24},{24,28},{1,5},{5,9},{9,... | collective-permute-start | bytes 786440 | tf_op jit(solution)/shard_map/ppermute | solution.py:24
  67.3 12.4 %collective-permute-start.10 = (f32[8,512]{1,0:T(8,128)S(1)}, f32[8,512]{1,0:T(8,128)S(1)}, u32[]{:S(2)}, u32[]{:S(2)}) collective-permute-start(f32[8,512]{1,0:T(8,128)S(1)} %get-tuple-element.51), channel_id=1, source_target_pairs={{1,0},{2,1},{3,2},{5,4},{6,5},{7,6},{9,8},{10,9},{11,10},{13,12},{... | collective-permute-start | bytes 49160 | tf_op jit(solution)/shard_map/ppermute | solution.py:24
  68.6 11.1 %collective-permute-start.11 = (f32[8,512]{1,0:T(8,128)S(1)}, f32[8,512]{1,0:T(8,128)S(1)}, u32[]{:S(2)}, u32[]{:S(2)}) collective-permute-start(f32[8,512]{1,0:T(8,128)S(1)} %get-tuple-element.52.col7_ref), channel_id=1, source_target_pairs={{0,1},{1,2},{2,3},{4,5},{5,6},{6,7},{8,9},{9,10},{10,11},{12,13},{... | collective-permute-start | bytes 49160 | tf_op jit(solution)/shard_map/ppermute | solution.py:24

commit v10 on v9

--- a/solution.py
+++ b/solution.py
@@ -44,17 +44,17 @@
 
 def stencil(v):
     em, ep = earlier(v), later(v)
-    odd = [m - p for m, p in zip(em, ep)]
-    even = [(m + p) - (c + c) for m, p, c in zip(em, ep, v)]
+    odd = [0.5 * (m - p) for m, p in zip(em, ep)]
+    even = [0.5 * (m + p) - c for m, p, c in zip(em, ep, v)]
     return odd, even
 
 
 def dip_part(p, odd, even):
-    return [(0.5 * d) * (o + d * e) for d, o, e in zip(p, odd, even)]
+    return [d * (o + d * e) for d, o, e in zip(p, odd, even)]
 
 
 def adjoint_terms(p, r):
-    a = [(0.5 * d) * x for d, x in zip(p, r)]
+    a = [d * x for d, x in zip(p, r)]
     b = [d * x for d, x in zip(p, a)]
     return a, b
 
@@ -62,7 +62,7 @@
 def adjoint_finish(r, a, b):
     up = later([x + y for x, y in zip(a, b)])
     down = earlier([y - x for x, y in zip(a, b)])
-    return [(x + u) + (d - (y + y)) for x, u, d, y in zip(r, up, down, b)]
+    return [(x - y) + 0.5 * (u + d) for x, u, d, y in zip(r, up, down, b)]
 
 
 def load(ref, *index):
@@ -236,7 +236,7 @@
         a, b = add(a1, a2), add(b1, b2)
         diag = diag_ref.at[i][at, :]
         rest = [
-            (diag * c + (f + s)) - ((f1 + s1) - (y + y))
+            (diag * c + (f + s)) - ((f1 + s1) - y)
             for c, f, s, f1, s1, y in zip(v, above, left, first, second, b)
         ]
         return first, (rest, add(a, b), sub(b, a)), down
@@ -244,7 +244,7 @@
     def adjoint(i, x, pending):
         at = slice(x, x + SUBLANES)
         rest, up, down = pending
-        out = [r - (u + d) for r, u, d in zip(rest, later(up), earlier(down))]
+        out = [r - 0.5 * (u + d) for r, u, d in zip(rest, later(up), earlier(down))]
         out_row = out_ref.at[i]
         for c in range(tiles):
             out_row[c, at, :] = out[c]

time: 95.4 us -> 95.7 us (level)
  no operation moved by 1% of the time
where the time goes in v10:
time: 95.7 us; the launch traced here: 95.2 us
  blocking collectives  35.2 us (37%)
  starting transfers between devices  32.6 us (34%)
  Pallas kernels  26.5 us (28%)
    ppermute x12, starting transfers between devices, shifted(): lax.ppermute(value, axis, [(source, source + steps) for source in range(i...  32.6 us
    pallas_call x9, Pallas kernels, call(): pl.pallas_call(kernel, out_shape=outs, in_specs=ins or [IN_VMEM] * len(ar...  26.5 us
    all_to_all x1, blocking collectives, per_device(): lax.all_to_all(sent, ('inl', 'xl'), split_axis=0, concat_axis=0, tiled=True)  22.7 us
    all_to_all x1, blocking collectives, per_device(): lax.all_to_all(message, ('inl', 'xl'), split_axis=0, concat_axis=0, tiled...  12.5 us
  transfers between devices with their start and end apart: 12, of which 0 were waited for; matrix products, arithmetic and copies ran while one was open for 0% of the time, Pallas kernels for 21%

profile of v10, /device:TPU:0, one launch (start us, length us, event | category | flops | bytes accessed | tf_op | source)
XLA Modules:
  0.0 95.2 jit_solution(5895593357547508176)
XLA Ops:
  0.6 0.0 copy-start.1
  0.6 1.5 %pack.1 = (bf16[32,72,128]{2,1,0:T(8,128)(2,1)S(1)}, f32[128,512]{1,0:T(8,128)S(1)}, f32[8,8,512]{2,1,0:T(8,128)S(1)}) custom-call(s32[1,256]{1,0:T(1,128)} %bitcast.3, s32[1,256]{1,0:T(1,128)} %bitcast.4, s32[1,256]{1,0:T(1,128)} %bitcast.5, bf16[256,512]{1,0:T(8,128)(2,1)} %traces_hbm.1, f32[8,128,512]{2,1,0:T(8,128)} %p1_ref.11, f32[8,128,512]{2,1,0:T(8,128)} %p2_ref.11), custom_call_target="tpu_custom_call" | custom-call | tf_op jit(solution)/shard_map/pack/pallas_call | solution.py:447
  2.2 0.0 copy-start
  2.2 22.7 %all_to_all.10.got_ref = bf16[32,72,128]{2,1,0:T(8,128)(2,1)S(1)} all-to-all(bf16[32,72,128]{2,1,0:T(8,128)(2,1)S(1)} %get-tuple-element.31), channel_id=1, replica_groups=mesh['inl'=8,'xl'=4] {'inl','xl'}, dimensions={0} | all-to-all | bytes 1179648 | tf_op jit(solution)/shard_map/all_to_all | solution.py:486
  24.9 1.2 %bin.1 = (f32[8,4,128,128]{3,2,1,0:T(8,128)S(1)}, f32[8,128,128]{2,1,0:T(8,128)S(1)}, f32[128,512]{1,0:T(8,128)S(1)}, f32[128,512]{1,0:T(8,128)S(1)}, f32[8,512]{1,0:T(8,128)S(1)}, /*index=5*/f32[8,512]{1,0:T(8,128)S(1)}) custom-call(bf16[32,72,128]{2,1,0:T(8,128)(2,1)S(1)} %all_to_all.10.got_ref, f32[128,512]{1,0:T(8,128)S(1)} %get-tuple-element.32.p1_ref, ...), custom_call_target="tpu_custom_call" | custom-call | tf_op jit(solution)/shard_map/bin/pallas_call | solution.py:447
  26.1 1.3 %collective-permute-start = (f32[128,512]{1,0:T(8,128)S(1)}, f32[128,512]{1,0:T(8,128)S(1)}, u32[]{:S(2)}, u32[]{:S(2)}) collective-permute-start(f32[128,512]{1,0:T(8,128)S(1)} %get-tuple-element.37), channel_id=1, source_target_pairs={{4,0},{8,4},{12,8},{16,12},{20,16},{24,20},{28,24},{5,1},{9,5},{13... | collective-permute-start | bytes 786440 | tf_op jit(solution)/shard_map/ppermute | solution.py:24
  27.4 3.8 %collective-permute-start.1 = (f32[128,512]{1,0:T(8,128)S(1)}, f32[128,512]{1,0:T(8,128)S(1)}, u32[]{:S(2)}, u32[]{:S(2)}) collective-permute-start(f32[128,512]{1,0:T(8,128)S(1)} %get-tuple-element.38.row7_ref), channel_id=1, source_target_pairs={{0,4},{4,8},{8,12},{12,16},{16,20},{20,24},{24,28},{1,5},{5,9},{9,... | collective-permute-start | bytes 786440 | tf_op jit(solution)/shard_map/ppermute | solution.py:24
  31.3 1.3 %collective-permute-start.2 = (f32[8,512]{1,0:T(8,128)S(1)}, f32[8,512]{1,0:T(8,128)S(1)}, u32[]{:S(2)}, u32[]{:S(2)}) collective-permute-start(f32[8,512]{1,0:T(8,128)S(1)} %get-tuple-element.39), channel_id=1, source_target_pairs={{1,0},{2,1},{3,2},{5,4},{6,5},{7,6},{9,8},{10,9},{11,10},{13,12},{... | collective-permute-start | bytes 49160 | tf_op jit(solution)/shard_map/ppermute | solution.py:24
  32.6 4.5 %collective-permute-start.3 = (f32[8,512]{1,0:T(8,128)S(1)}, f32[8,512]{1,0:T(8,128)S(1)}, u32[]{:S(2)}, u32[]{:S(2)}) collective-permute-start(f32[8,512]{1,0:T(8,128)S(1)} %get-tuple-element.40.col7_ref), channel_id=1, source_target_pairs={{0,1},{1,2},{2,3},{4,5},{5,6},{6,7},{8,9},{9,10},{10,11},{12,13},{... | collective-permute-start | bytes 49160 | tf_op jit(solution)/shard_map/ppermute | solution.py:24
  37.1 0.0 copy-done.1
  37.1 0.0 copy-done
  37.1 6.6 %apply.3 = (f32[8,4,128,128]{3,2,1,0:T(8,128)S(1)}, f32[2,8,128]{2,1,0:T(8,128)S(1)}) custom-call(f32[8,4,128,128]{3,2,1,0:T(8,128)S(1)} %get-tuple-element.34.v_ref.b_ref, f32[8,128,512]{2,1,0:T(8,128)S(1)} %copy-done, f32[8,128,512]{2,1,0:T(8,128)S(1)} %copy-done.1, f32[8,128,128]{2,1,0:T(8,128)S(1)} %get-tuple-element.35.diag_ref), custom_call_target="tpu_custom_call" | custom-call | flops 31457280 | bytes 8388608 | tf_op jit(solution)/shard_map/apply/pallas_call | solution.py:447
  43.8 0.0 collective-permute-done.2.right_ref
  43.8 0.0 collective-permute-done.3.left_ref
  43.8 0.0 collective-permute-done.below_ref
  43.8 0.0 collective-permute-done.1.above_ref
  43.8 0.6 correct.2
  44.4 1.3 %collective-permute-start.4 = (f32[128,512]{1,0:T(8,128)S(1)}, f32[128,512]{1,0:T(8,128)S(1)}, u32[]{:S(2)}, u32[]{:S(2)}) collective-permute-start(f32[128,512]{1,0:T(8,128)S(1)} %get-tuple-element.43), channel_id=1, source_target_pairs={{4,0},{8,4},{12,8},{16,12},{20,16},{24,20},{28,24},{5,1},{9,5},{13... | collective-permute-start | bytes 786440 | tf_op jit(solution)/shard_map/ppermute | solution.py:24
  45.7 3.7 %collective-permute-start.5 = (f32[128,512]{1,0:T(8,128)S(1)}, f32[128,512]{1,0:T(8,128)S(1)}, u32[]{:S(2)}, u32[]{:S(2)}) collective-permute-start(f32[128,512]{1,0:T(8,128)S(1)} %get-tuple-element.44.row7_ref), channel_id=1, source_target_pairs={{0,4},{4,8},{8,12},{12,16},{16,20},{20,24},{24,28},{1,5},{5,9},{9,... | collective-permute-start | bytes 786440 | tf_op jit(solution)/shard_map/ppermute | solution.py:24
  49.4 1.3 %collective-permute-start.6 = (f32[8,512]{1,0:T(8,128)S(1)}, f32[8,512]{1,0:T(8,128)S(1)}, u32[]{:S(2)}, u32[]{:S(2)}) collective-permute-start(f32[8,512]{1,0:T(8,128)S(1)} %get-tuple-element.45), channel_id=1, source_target_pairs={{1,0},{2,1},{3,2},{5,4},{6,5},{7,6},{9,8},{10,9},{11,10},{13,12},{... | collective-permute-start | bytes 49160 | tf_op jit(solution)/shard_map/ppermute | solution.py:24
  50.7 4.5 %collective-permute-start.7 = (f32[8,512]{1,0:T(8,128)S(1)}, f32[8,512]{1,0:T(8,128)S(1)}, u32[]{:S(2)}, u32[]{:S(2)}) collective-permute-start(f32[8,512]{1,0:T(8,128)S(1)} %get-tuple-element.46.col7_ref), channel_id=1, source_target_pairs={{0,1},{1,2},{2,3},{4,5},{5,6},{6,7},{8,9},{9,10},{10,11},{12,13},{... | collective-permute-start | bytes 49160 | tf_op jit(solution)/shard_map/ppermute | solution.py:24
  55.2 6.6 %apply.4 = (f32[8,4,128,128]{3,2,1,0:T(8,128)S(1)}, f32[2,8,128]{2,1,0:T(8,128)S(1)}) custom-call(f32[8,4,128,128]{3,2,1,0:T(8,128)S(1)} %get-tuple-element.41.v_ref.v1_ref, f32[8,128,512]{2,1,0:T(8,128)S(1)} %copy-done, f32[8,128,512]{2,1,0:T(8,128)S(1)} %copy-done.1, f32[8,128,128]{2,1,0:T(8,128)S(1)} %get-tuple-element.35.diag_ref), custom_call_target="tpu_custom_call" | custom-call | flops 31457280 | bytes 8388608 | tf_op jit(solution)/shard_map/apply/pallas_call | solution.py:447
  61.9 0.0 collective-permute-done.6.right_ref
  61.9 0.0 collective-permute-done.7.left_ref
  61.9 0.0 collective-permute-done.4.below_ref
  61.9 0.0 collective-permute-done.5.above_ref
  61.9 0.5 correct.3
  62.5 1.3 %collective-permute-start.8 = (f32[128,512]{1,0:T(8,128)S(1)}, f32[128,512]{1,0:T(8,128)S(1)}, u32[]{:S(2)}, u32[]{:S(2)}) collective-permute-start(f32[128,512]{1,0:T(8,128)S(1)} %get-tuple-element.49), channel_id=1, source_target_pairs={{4,0},{8,4},{12,8},{16,12},{20,16},{24,20},{28,24},{5,1},{9,5},{13... | collective-permute-start | bytes 786440 | tf_op jit(solution)/shard_map/ppermute | solution.py:24
  63.8 3.7 %collective-permute-start.9 = (f32[128,512]{1,0:T(8,128)S(1)}, f32[128,512]{1,0:T(8,128)S(1)}, u32[]{:S(2)}, u32[]{:S(2)}) collective-permute-start(f32[128,512]{1,0:T(8,128)S(1)} %get-tuple-element.50.row7_ref), channel_id=1, source_target_pairs={{0,4},{4,8},{8,12},{12,16},{16,20},{20,24},{24,28},{1,5},{5,9},{9,... | collective-permute-start | bytes 786440 | tf_op jit(solution)/shard_map/ppermute | solution.py:24
  67.5 1.3 %collective-permute-start.10 = (f32[8,512]{1,0:T(8,128)S(1)}, f32[8,512]{1,0:T(8,128)S(1)}, u32[]{:S(2)}, u32[]{:S(2)}) collective-permute-start(f32[8,512]{1,0:T(8,128)S(1)} %get-tuple-element.51), channel_id=1, source_target_pairs={{1,0},{2,1},{3,2},{5,4},{6,5},{7,6},{9,8},{10,9},{11,10},{13,12},{... | collective-permute-start | bytes 49160 | tf_op jit(solution)/shard_map/ppermute | solution.py:24
  68.8 4.5 %collective-permute-start.11 = (f32[8,512]{1,0:T(8,128)S(1)}, f32[8,512]{1,0:T(8,128)S(1)}, u32[]{:S(2)}, u32[]{:S(2)}) collective-permute-start(f32[8,512]{1,0:T(8,128)S(1)} %get-tuple-element.52.col7_ref), channel_id=1, source_target_pairs={{0,1},{1,2},{2,3},{4,5},{5,6},{6,7},{8,9},{9,10},{10,11},{12,13},{... | collective-permute-start | bytes 49160 | tf_op jit(solution)/shard_map/ppermute | solution.py:24
  73.3 6.7 %apply.5 = (f32[8,4,128,128]{3,2,1,0:T(8,128)S(1)}, f32[2,8,128]{2,1,0:T(8,128)S(1)}) custom-call(f32[8,4,128,128]{3,2,1,0:T(8,128)S(1)} %get-tuple-element.47.v_ref.v2_ref, f32[8,128,512]{2,1,0:T(8,128)S(1)} %copy-done, f32[8,128,512]{2,1,0:T(8,128)S(1)} %copy-done.1, f32[8,128,128]{2,1,0:T(8,128)S(1)} %get-tuple-element.35.diag_ref), custom_call_target="tpu_custom_call" | custom-call | flops 31457280 | bytes 8388608 | tf_op jit(solution)/shard_map/apply/pallas_call | solution.py:447
  80.0 0.0 collective-permute-done.10.right_ref
  80.0 0.0 collective-permute-done.11.left_ref
  80.0 0.0 collective-permute-done.8.below_ref
  80.0 0.0 collective-permute-done.9.above_ref
  80.0 0.4 moments.1
  80.4 12.5 %all_to_all.11.parts_ref = f32[32,1,128]{2,1,0:T(1,128)S(1)} all-to-all(f32[32,1,128]{2,1,0:T(1,128)S(1)} %get-tuple-element.58), channel_id=1, replica_groups=mesh['inl'=8,'xl'=4] {'inl','xl'}, dimensions={0} | all-to-all | bytes 32768 | tf_op jit(solution)/shard_map/all_to_all | solution.py:524
  92.9 2.4 %finish.1 = (f32[8,128,512]{2,1,0:T(8,128)}, f32[8,128,512]{2,1,0:T(8,128)}) custom-call(f32[32,1,128]{2,1,0:T(1,128)S(1)} %all_to_all.11.parts_ref, f32[8,4,128,128]{3,2,1,0:T(8,128)S(1)} %get-tuple-element.34.v_ref.b_ref, f32[8,4,128,128]{3,2,1,0:T(8,128)S(1)} %get-tuple-element.41.v_ref.v1_ref, f32[8,4,128,128]{3,2,1,0:T(8,128)S(1)} %get-tuple-element.47.v_ref.v2_ref, ...), custom_call_target="tpu_custom_call" | custom-call | tf_op jit(solution)/shard_map/finish/pallas_call | solution.py:447
Async XLA Ops:
  0.6 36.5 %copy-start.1 = (f32[8,128,512]{2,1,0:T(8,128)S(1)}, f32[8,128,512]{2,1,0:T(8,128)}, u32[]{:S(2)}) copy-start(f32[8,128,512]{2,1,0:T(8,128)} %p2_ref.11) | copy-start | bytes 6291460
  2.2 34.9 %copy-start = (f32[8,128,512]{2,1,0:T(8,128)S(1)}, f32[8,128,512]{2,1,0:T(8,128)}, u32[]{:S(2)}) copy-start(f32[8,128,512]{2,1,0:T(8,128)} %p1_ref.11) | copy-start | bytes 6291460
  26.1 17.7 %collective-permute-start = (f32[128,512]{1,0:T(8,128)S(1)}, f32[128,512]{1,0:T(8,128)S(1)}, u32[]{:S(2)}, u32[]{:S(2)}) collective-permute-start(f32[128,512]{1,0:T(8,128)S(1)} %get-tuple-element.37), channel_id=1, source_target_pairs={{4,0},{8,4},{12,8},{16,12},{20,16},{24,20},{28,24},{5,1},{9,5},{13... | collective-permute-start | bytes 786440 | tf_op jit(solution)/shard_map/ppermute | solution.py:24
  27.4 16.4 %collective-permute-start.1 = (f32[128,512]{1,0:T(8,128)S(1)}, f32[128,512]{1,0:T(8,128)S(1)}, u32[]{:S(2)}, u32[]{:S(2)}) collective-permute-start(f32[128,512]{1,0:T(8,128)S(1)} %get-tuple-element.38.row7_ref), channel_id=1, source_target_pairs={{0,4},{4,8},{8,12},{12,16},{16,20},{20,24},{24,28},{1,5},{5,9},{9,... | collective-permute-start | bytes 786440 | tf_op jit(solution)/shard_map/ppermute | solution.py:24
  31.3 12.5 %collective-permute-start.2 = (f32[8,512]{1,0:T(8,128)S(1)}, f32[8,512]{1,0:T(8,128)S(1)}, u32[]{:S(2)}, u32[]{:S(2)}) collective-permute-start(f32[8,512]{1,0:T(8,128)S(1)} %get-tuple-element.39), channel_id=1, source_target_pairs={{1,0},{2,1},{3,2},{5,4},{6,5},{7,6},{9,8},{10,9},{11,10},{13,12},{... | collective-permute-start | bytes 49160 | tf_op jit(solution)/shard_map/ppermute | solution.py:24
  32.6 11.2 %collective-permute-start.3 = (f32[8,512]{1,0:T(8,128)S(1)}, f32[8,512]{1,0:T(8,128)S(1)}, u32[]{:S(2)}, u32[]{:S(2)}) collective-permute-start(f32[8,512]{1,0:T(8,128)S(1)} %get-tuple-element.40.col7_ref), channel_id=1, source_target_pairs={{0,1},{1,2},{2,3},{4,5},{5,6},{6,7},{8,9},{9,10},{10,11},{12,13},{... | collective-permute-start | bytes 49160 | tf_op jit(solution)/shard_map/ppermute | solution.py:24
  44.4 17.5 %collective-permute-start.4 = (f32[128,512]{1,0:T(8,128)S(1)}, f32[128,512]{1,0:T(8,128)S(1)}, u32[]{:S(2)}, u32[]{:S(2)}) collective-permute-start(f32[128,512]{1,0:T(8,128)S(1)} %get-tuple-element.43), channel_id=1, source_target_pairs={{4,0},{8,4},{12,8},{16,12},{20,16},{24,20},{28,24},{5,1},{9,5},{13... | collective-permute-start | bytes 786440 | tf_op jit(solution)/shard_map/ppermute | solution.py:24
  45.7 16.2 %collective-permute-start.5 = (f32[128,512]{1,0:T(8,128)S(1)}, f32[128,512]{1,0:T(8,128)S(1)}, u32[]{:S(2)}, u32[]{:S(2)}) collective-permute-start(f32[128,512]{1,0:T(8,128)S(1)} %get-tuple-element.44.row7_ref), channel_id=1, source_target_pairs={{0,4},{4,8},{8,12},{12,16},{16,20},{20,24},{24,28},{1,5},{5,9},{9,... | collective-permute-start | bytes 786440 | tf_op jit(solution)/shard_map/ppermute | solution.py:24
  49.4 12.5 %collective-permute-start.6 = (f32[8,512]{1,0:T(8,128)S(1)}, f32[8,512]{1,0:T(8,128)S(1)}, u32[]{:S(2)}, u32[]{:S(2)}) collective-permute-start(f32[8,512]{1,0:T(8,128)S(1)} %get-tuple-element.45), channel_id=1, source_target_pairs={{1,0},{2,1},{3,2},{5,4},{6,5},{7,6},{9,8},{10,9},{11,10},{13,12},{... | collective-permute-start | bytes 49160 | tf_op jit(solution)/shard_map/ppermute | solution.py:24
  50.7 11.2 %collective-permute-start.7 = (f32[8,512]{1,0:T(8,128)S(1)}, f32[8,512]{1,0:T(8,128)S(1)}, u32[]{:S(2)}, u32[]{:S(2)}) collective-permute-start(f32[8,512]{1,0:T(8,128)S(1)} %get-tuple-element.46.col7_ref), channel_id=1, source_target_pairs={{0,1},{1,2},{2,3},{4,5},{5,6},{6,7},{8,9},{9,10},{10,11},{12,13},{... | collective-permute-start | bytes 49160 | tf_op jit(solution)/shard_map/ppermute | solution.py:24
  62.5 17.6 %collective-permute-start.8 = (f32[128,512]{1,0:T(8,128)S(1)}, f32[128,512]{1,0:T(8,128)S(1)}, u32[]{:S(2)}, u32[]{:S(2)}) collective-permute-start(f32[128,512]{1,0:T(8,128)S(1)} %get-tuple-element.49), channel_id=1, source_target_pairs={{4,0},{8,4},{12,8},{16,12},{20,16},{24,20},{28,24},{5,1},{9,5},{13... | collective-permute-start | bytes 786440 | tf_op jit(solution)/shard_map/ppermute | solution.py:24
  63.8 16.3 %collective-permute-start.9 = (f32[128,512]{1,0:T(8,128)S(1)}, f32[128,512]{1,0:T(8,128)S(1)}, u32[]{:S(2)}, u32[]{:S(2)}) collective-permute-start(f32[128,512]{1,0:T(8,128)S(1)} %get-tuple-element.50.row7_ref), channel_id=1, source_target_pairs={{0,4},{4,8},{8,12},{12,16},{16,20},{20,24},{24,28},{1,5},{5,9},{9,... | collective-permute-start | bytes 786440 | tf_op jit(solution)/shard_map/ppermute | solution.py:24
  67.5 12.5 %collective-permute-start.10 = (f32[8,512]{1,0:T(8,128)S(1)}, f32[8,512]{1,0:T(8,128)S(1)}, u32[]{:S(2)}, u32[]{:S(2)}) collective-permute-start(f32[8,512]{1,0:T(8,128)S(1)} %get-tuple-element.51), channel_id=1, source_target_pairs={{1,0},{2,1},{3,2},{5,4},{6,5},{7,6},{9,8},{10,9},{11,10},{13,12},{... | collective-permute-start | bytes 49160 | tf_op jit(solution)/shard_map/ppermute | solution.py:24
  68.8 11.2 %collective-permute-start.11 = (f32[8,512]{1,0:T(8,128)S(1)}, f32[8,512]{1,0:T(8,128)S(1)}, u32[]{:S(2)}, u32[]{:S(2)}) collective-permute-start(f32[8,512]{1,0:T(8,128)S(1)} %get-tuple-element.52.col7_ref), channel_id=1, source_target_pairs={{0,1},{1,2},{2,3},{4,5},{5,6},{6,7},{8,9},{9,10},{10,11},{12,13},{... | collective-permute-start | bytes 49160 | tf_op jit(solution)/shard_map/ppermute | solution.py:24

commit v11 on v9

--- a/solution.py
+++ b/solution.py
@@ -10,7 +10,7 @@
 ITERS = 3
 LANES = 128
 SUBLANES = 8
-GROUP = 16
+GROUP = 32
 
 SHIFT = 6.0
 IN_VMEM = pl.BlockSpec(memory_space=pltpu.VMEM)

time: 95.4 us -> 94.5 us (level)
  transfers between devices with their start and end apart: 12 -> 12, of which waited for: 0 -> 0; matrix products, arithmetic and copies ran while one was open for 0% -> 0% of each run, Pallas kernels for 21% -> 20%
where the time goes in v11:
time: 94.5 us; the launch traced here: 94 us
  blocking collectives  35.2 us (37%)
  starting transfers between devices  32.6 us (34%)
  Pallas kernels  25.3 us (27%)
    ppermute x12, starting transfers between devices, shifted(): lax.ppermute(value, axis, [(source, source + steps) for source in range(i...  32.6 us
    pallas_call x9, Pallas kernels, call(): pl.pallas_call(kernel, out_shape=outs, in_specs=ins or [IN_VMEM] * len(ar...  25.3 us
    all_to_all x1, blocking collectives, per_device(): lax.all_to_all(sent, ('inl', 'xl'), split_axis=0, concat_axis=0, tiled=True)  22.7 us
    all_to_all x1, blocking collectives, per_device(): lax.all_to_all(message, ('inl', 'xl'), split_axis=0, concat_axis=0, tiled...  12.5 us
  transfers between devices with their start and end apart: 12, of which 0 were waited for; matrix products, arithmetic and copies ran while one was open for 0% of the time, Pallas kernels for 20%

profile of v11, /device:TPU:0, one launch (start us, length us, event | category | flops | bytes accessed | tf_op | source)
XLA Modules:
  0.0 94.0 jit_solution(17583848976718717716)
XLA Ops:
  0.6 0.0 copy-start.1
  0.6 1.5 %pack.1 = (bf16[32,72,128]{2,1,0:T(8,128)(2,1)S(1)}, f32[128,512]{1,0:T(8,128)S(1)}, f32[8,8,512]{2,1,0:T(8,128)S(1)}) custom-call(s32[1,256]{1,0:T(1,128)} %bitcast.3, s32[1,256]{1,0:T(1,128)} %bitcast.4, s32[1,256]{1,0:T(1,128)} %bitcast.5, bf16[256,512]{1,0:T(8,128)(2,1)} %traces_hbm.1, f32[8,128,512]{2,1,0:T(8,128)} %p1_ref.11, f32[8,128,512]{2,1,0:T(8,128)} %p2_ref.11), custom_call_target="tpu_custom_call" | custom-call | tf_op jit(solution)/shard_map/pack/pallas_call | solution.py:447
  2.2 0.0 copy-start
  2.2 22.7 %all_to_all.10.got_ref = bf16[32,72,128]{2,1,0:T(8,128)(2,1)S(1)} all-to-all(bf16[32,72,128]{2,1,0:T(8,128)(2,1)S(1)} %get-tuple-element.31), channel_id=1, replica_groups=mesh['inl'=8,'xl'=4] {'inl','xl'}, dimensions={0} | all-to-all | bytes 1179648 | tf_op jit(solution)/shard_map/all_to_all | solution.py:486
  24.9 1.2 %bin.1 = (f32[8,4,128,128]{3,2,1,0:T(8,128)S(1)}, f32[8,128,128]{2,1,0:T(8,128)S(1)}, f32[128,512]{1,0:T(8,128)S(1)}, f32[128,512]{1,0:T(8,128)S(1)}, f32[8,512]{1,0:T(8,128)S(1)}, /*index=5*/f32[8,512]{1,0:T(8,128)S(1)}) custom-call(bf16[32,72,128]{2,1,0:T(8,128)(2,1)S(1)} %all_to_all.10.got_ref, f32[128,512]{1,0:T(8,128)S(1)} %get-tuple-element.32.p1_ref, ...), custom_call_target="tpu_custom_call" | custom-call | tf_op jit(solution)/shard_map/bin/pallas_call | solution.py:447
  26.1 1.3 %collective-permute-start = (f32[128,512]{1,0:T(8,128)S(1)}, f32[128,512]{1,0:T(8,128)S(1)}, u32[]{:S(2)}, u32[]{:S(2)}) collective-permute-start(f32[128,512]{1,0:T(8,128)S(1)} %get-tuple-element.37), channel_id=1, source_target_pairs={{4,0},{8,4},{12,8},{16,12},{20,16},{24,20},{28,24},{5,1},{9,5},{13... | collective-permute-start | bytes 786440 | tf_op jit(solution)/shard_map/ppermute | solution.py:24
  27.4 3.8 %collective-permute-start.1 = (f32[128,512]{1,0:T(8,128)S(1)}, f32[128,512]{1,0:T(8,128)S(1)}, u32[]{:S(2)}, u32[]{:S(2)}) collective-permute-start(f32[128,512]{1,0:T(8,128)S(1)} %get-tuple-element.38.row7_ref), channel_id=1, source_target_pairs={{0,4},{4,8},{8,12},{12,16},{16,20},{20,24},{24,28},{1,5},{5,9},{9,... | collective-permute-start | bytes 786440 | tf_op jit(solution)/shard_map/ppermute | solution.py:24
  31.3 1.3 %collective-permute-start.2 = (f32[8,512]{1,0:T(8,128)S(1)}, f32[8,512]{1,0:T(8,128)S(1)}, u32[]{:S(2)}, u32[]{:S(2)}) collective-permute-start(f32[8,512]{1,0:T(8,128)S(1)} %get-tuple-element.39), channel_id=1, source_target_pairs={{1,0},{2,1},{3,2},{5,4},{6,5},{7,6},{9,8},{10,9},{11,10},{13,12},{... | collective-permute-start | bytes 49160 | tf_op jit(solution)/shard_map/ppermute | solution.py:24
  32.6 4.5 %collective-permute-start.3 = (f32[8,512]{1,0:T(8,128)S(1)}, f32[8,512]{1,0:T(8,128)S(1)}, u32[]{:S(2)}, u32[]{:S(2)}) collective-permute-start(f32[8,512]{1,0:T(8,128)S(1)} %get-tuple-element.40.col7_ref), channel_id=1, source_target_pairs={{0,1},{1,2},{2,3},{4,5},{5,6},{6,7},{8,9},{9,10},{10,11},{12,13},{... | collective-permute-start | bytes 49160 | tf_op jit(solution)/shard_map/ppermute | solution.py:24
  37.1 0.0 copy-done.1
  37.1 0.0 copy-done
  37.1 6.3 %apply.3 = (f32[8,4,128,128]{3,2,1,0:T(8,128)S(1)}, f32[2,8,128]{2,1,0:T(8,128)S(1)}) custom-call(f32[8,4,128,128]{3,2,1,0:T(8,128)S(1)} %get-tuple-element.34.v_ref.b_ref, f32[8,128,512]{2,1,0:T(8,128)S(1)} %copy-done, f32[8,128,512]{2,1,0:T(8,128)S(1)} %copy-done.1, f32[8,128,128]{2,1,0:T(8,128)S(1)} %get-tuple-element.35.diag_ref), custom_call_target="tpu_custom_call" | custom-call | flops 31457280 | bytes 8388608 | tf_op jit(solution)/shard_map/apply/pallas_call | solution.py:447
  43.4 0.0 collective-permute-done.2.right_ref
  43.4 0.0 collective-permute-done.3.left_ref
  43.4 0.0 collective-permute-done.below_ref
  43.4 0.0 collective-permute-done.1.above_ref
  43.4 0.6 correct.2
  44.0 1.3 %collective-permute-start.4 = (f32[128,512]{1,0:T(8,128)S(1)}, f32[128,512]{1,0:T(8,128)S(1)}, u32[]{:S(2)}, u32[]{:S(2)}) collective-permute-start(f32[128,512]{1,0:T(8,128)S(1)} %get-tuple-element.43), channel_id=1, source_target_pairs={{4,0},{8,4},{12,8},{16,12},{20,16},{24,20},{28,24},{5,1},{9,5},{13... | collective-permute-start | bytes 786440 | tf_op jit(solution)/shard_map/ppermute | solution.py:24
  45.3 3.7 %collective-permute-start.5 = (f32[128,512]{1,0:T(8,128)S(1)}, f32[128,512]{1,0:T(8,128)S(1)}, u32[]{:S(2)}, u32[]{:S(2)}) collective-permute-start(f32[128,512]{1,0:T(8,128)S(1)} %get-tuple-element.44.row7_ref), channel_id=1, source_target_pairs={{0,4},{4,8},{8,12},{12,16},{16,20},{20,24},{24,28},{1,5},{5,9},{9,... | collective-permute-start | bytes 786440 | tf_op jit(solution)/shard_map/ppermute | solution.py:24
  49.0 1.3 %collective-permute-start.6 = (f32[8,512]{1,0:T(8,128)S(1)}, f32[8,512]{1,0:T(8,128)S(1)}, u32[]{:S(2)}, u32[]{:S(2)}) collective-permute-start(f32[8,512]{1,0:T(8,128)S(1)} %get-tuple-element.45), channel_id=1, source_target_pairs={{1,0},{2,1},{3,2},{5,4},{6,5},{7,6},{9,8},{10,9},{11,10},{13,12},{... | collective-permute-start | bytes 49160 | tf_op jit(solution)/shard_map/ppermute | solution.py:24
  50.3 4.5 %collective-permute-start.7 = (f32[8,512]{1,0:T(8,128)S(1)}, f32[8,512]{1,0:T(8,128)S(1)}, u32[]{:S(2)}, u32[]{:S(2)}) collective-permute-start(f32[8,512]{1,0:T(8,128)S(1)} %get-tuple-element.46.col7_ref), channel_id=1, source_target_pairs={{0,1},{1,2},{2,3},{4,5},{5,6},{6,7},{8,9},{9,10},{10,11},{12,13},{... | collective-permute-start | bytes 49160 | tf_op jit(solution)/shard_map/ppermute | solution.py:24
  54.9 6.3 %apply.4 = (f32[8,4,128,128]{3,2,1,0:T(8,128)S(1)}, f32[2,8,128]{2,1,0:T(8,128)S(1)}) custom-call(f32[8,4,128,128]{3,2,1,0:T(8,128)S(1)} %get-tuple-element.41.v_ref.v1_ref, f32[8,128,512]{2,1,0:T(8,128)S(1)} %copy-done, f32[8,128,512]{2,1,0:T(8,128)S(1)} %copy-done.1, f32[8,128,128]{2,1,0:T(8,128)S(1)} %get-tuple-element.35.diag_ref), custom_call_target="tpu_custom_call" | custom-call | flops 31457280 | bytes 8388608 | tf_op jit(solution)/shard_map/apply/pallas_call | solution.py:447
  61.1 0.0 collective-permute-done.6.right_ref
  61.1 0.0 collective-permute-done.7.left_ref
  61.1 0.0 collective-permute-done.4.below_ref
  61.1 0.0 collective-permute-done.5.above_ref
  61.2 0.5 correct.3
  61.7 1.3 %collective-permute-start.8 = (f32[128,512]{1,0:T(8,128)S(1)}, f32[128,512]{1,0:T(8,128)S(1)}, u32[]{:S(2)}, u32[]{:S(2)}) collective-permute-start(f32[128,512]{1,0:T(8,128)S(1)} %get-tuple-element.49), channel_id=1, source_target_pairs={{4,0},{8,4},{12,8},{16,12},{20,16},{24,20},{28,24},{5,1},{9,5},{13... | collective-permute-start | bytes 786440 | tf_op jit(solution)/shard_map/ppermute | solution.py:24
  63.0 3.7 %collective-permute-start.9 = (f32[128,512]{1,0:T(8,128)S(1)}, f32[128,512]{1,0:T(8,128)S(1)}, u32[]{:S(2)}, u32[]{:S(2)}) collective-permute-start(f32[128,512]{1,0:T(8,128)S(1)} %get-tuple-element.50.row7_ref), channel_id=1, source_target_pairs={{0,4},{4,8},{8,12},{12,16},{16,20},{20,24},{24,28},{1,5},{5,9},{9,... | collective-permute-start | bytes 786440 | tf_op jit(solution)/shard_map/ppermute | solution.py:24
  66.7 1.3 %collective-permute-start.10 = (f32[8,512]{1,0:T(8,128)S(1)}, f32[8,512]{1,0:T(8,128)S(1)}, u32[]{:S(2)}, u32[]{:S(2)}) collective-permute-start(f32[8,512]{1,0:T(8,128)S(1)} %get-tuple-element.51), channel_id=1, source_target_pairs={{1,0},{2,1},{3,2},{5,4},{6,5},{7,6},{9,8},{10,9},{11,10},{13,12},{... | collective-permute-start | bytes 49160 | tf_op jit(solution)/shard_map/ppermute | solution.py:24
  68.0 4.5 %collective-permute-start.11 = (f32[8,512]{1,0:T(8,128)S(1)}, f32[8,512]{1,0:T(8,128)S(1)}, u32[]{:S(2)}, u32[]{:S(2)}) collective-permute-start(f32[8,512]{1,0:T(8,128)S(1)} %get-tuple-element.52.col7_ref), channel_id=1, source_target_pairs={{0,1},{1,2},{2,3},{4,5},{5,6},{6,7},{8,9},{9,10},{10,11},{12,13},{... | collective-permute-start | bytes 49160 | tf_op jit(solution)/shard_map/ppermute | solution.py:24
  72.6 6.2 %apply.5 = (f32[8,4,128,128]{3,2,1,0:T(8,128)S(1)}, f32[2,8,128]{2,1,0:T(8,128)S(1)}) custom-call(f32[8,4,128,128]{3,2,1,0:T(8,128)S(1)} %get-tuple-element.47.v_ref.v2_ref, f32[8,128,512]{2,1,0:T(8,128)S(1)} %copy-done, f32[8,128,512]{2,1,0:T(8,128)S(1)} %copy-done.1, f32[8,128,128]{2,1,0:T(8,128)S(1)} %get-tuple-element.35.diag_ref), custom_call_target="tpu_custom_call" | custom-call | flops 31457280 | bytes 8388608 | tf_op jit(solution)/shard_map/apply/pallas_call | solution.py:447
  78.8 0.0 collective-permute-done.10.right_ref
  78.8 0.0 collective-permute-done.11.left_ref
  78.8 0.0 collective-permute-done.8.below_ref
  78.8 0.0 collective-permute-done.9.above_ref
  78.8 0.4 moments.1
  79.2 12.5 %all_to_all.11.parts_ref = f32[32,1,128]{2,1,0:T(1,128)S(1)} all-to-all(f32[32,1,128]{2,1,0:T(1,128)S(1)} %get-tuple-element.58), channel_id=1, replica_groups=mesh['inl'=8,'xl'=4] {'inl','xl'}, dimensions={0} | all-to-all | bytes 32768 | tf_op jit(solution)/shard_map/all_to_all | solution.py:524
  91.7 2.4 %finish.1 = (f32[8,128,512]{2,1,0:T(8,128)}, f32[8,128,512]{2,1,0:T(8,128)}) custom-call(f32[32,1,128]{2,1,0:T(1,128)S(1)} %all_to_all.11.parts_ref, f32[8,4,128,128]{3,2,1,0:T(8,128)S(1)} %get-tuple-element.34.v_ref.b_ref, f32[8,4,128,128]{3,2,1,0:T(8,128)S(1)} %get-tuple-element.41.v_ref.v1_ref, f32[8,4,128,128]{3,2,1,0:T(8,128)S(1)} %get-tuple-element.47.v_ref.v2_ref, ...), custom_call_target="tpu_custom_call" | custom-call | tf_op jit(solution)/shard_map/finish/pallas_call | solution.py:447
Async XLA Ops:
  0.6 36.5 %copy-start.1 = (f32[8,128,512]{2,1,0:T(8,128)S(1)}, f32[8,128,512]{2,1,0:T(8,128)}, u32[]{:S(2)}) copy-start(f32[8,128,512]{2,1,0:T(8,128)} %p2_ref.11) | copy-start | bytes 6291460
  2.2 34.9 %copy-start = (f32[8,128,512]{2,1,0:T(8,128)S(1)}, f32[8,128,512]{2,1,0:T(8,128)}, u32[]{:S(2)}) copy-start(f32[8,128,512]{2,1,0:T(8,128)} %p1_ref.11) | copy-start | bytes 6291460
  26.1 17.3 %collective-permute-start = (f32[128,512]{1,0:T(8,128)S(1)}, f32[128,512]{1,0:T(8,128)S(1)}, u32[]{:S(2)}, u32[]{:S(2)}) collective-permute-start(f32[128,512]{1,0:T(8,128)S(1)} %get-tuple-element.37), channel_id=1, source_target_pairs={{4,0},{8,4},{12,8},{16,12},{20,16},{24,20},{28,24},{5,1},{9,5},{13... | collective-permute-start | bytes 786440 | tf_op jit(solution)/shard_map/ppermute | solution.py:24
  27.4 16.0 %collective-permute-start.1 = (f32[128,512]{1,0:T(8,128)S(1)}, f32[128,512]{1,0:T(8,128)S(1)}, u32[]{:S(2)}, u32[]{:S(2)}) collective-permute-start(f32[128,512]{1,0:T(8,128)S(1)} %get-tuple-element.38.row7_ref), channel_id=1, source_target_pairs={{0,4},{4,8},{8,12},{12,16},{16,20},{20,24},{24,28},{1,5},{5,9},{9,... | collective-permute-start | bytes 786440 | tf_op jit(solution)/shard_map/ppermute | solution.py:24
  31.3 12.1 %collective-permute-start.2 = (f32[8,512]{1,0:T(8,128)S(1)}, f32[8,512]{1,0:T(8,128)S(1)}, u32[]{:S(2)}, u32[]{:S(2)}) collective-permute-start(f32[8,512]{1,0:T(8,128)S(1)} %get-tuple-element.39), channel_id=1, source_target_pairs={{1,0},{2,1},{3,2},{5,4},{6,5},{7,6},{9,8},{10,9},{11,10},{13,12},{... | collective-permute-start | bytes 49160 | tf_op jit(solution)/shard_map/ppermute | solution.py:24
  32.6 10.8 %collective-permute-start.3 = (f32[8,512]{1,0:T(8,128)S(1)}, f32[8,512]{1,0:T(8,128)S(1)}, u32[]{:S(2)}, u32[]{:S(2)}) collective-permute-start(f32[8,512]{1,0:T(8,128)S(1)} %get-tuple-element.40.col7_ref), channel_id=1, source_target_pairs={{0,1},{1,2},{2,3},{4,5},{5,6},{6,7},{8,9},{9,10},{10,11},{12,13},{... | collective-permute-start | bytes 49160 | tf_op jit(solution)/shard_map/ppermute | solution.py:24
  44.0 17.2 %collective-permute-start.4 = (f32[128,512]{1,0:T(8,128)S(1)}, f32[128,512]{1,0:T(8,128)S(1)}, u32[]{:S(2)}, u32[]{:S(2)}) collective-permute-start(f32[128,512]{1,0:T(8,128)S(1)} %get-tuple-element.43), channel_id=1, source_target_pairs={{4,0},{8,4},{12,8},{16,12},{20,16},{24,20},{28,24},{5,1},{9,5},{13... | collective-permute-start | bytes 786440 | tf_op jit(solution)/shard_map/ppermute | solution.py:24
  45.3 15.9 %collective-permute-start.5 = (f32[128,512]{1,0:T(8,128)S(1)}, f32[128,512]{1,0:T(8,128)S(1)}, u32[]{:S(2)}, u32[]{:S(2)}) collective-permute-start(f32[128,512]{1,0:T(8,128)S(1)} %get-tuple-element.44.row7_ref), channel_id=1, source_target_pairs={{0,4},{4,8},{8,12},{12,16},{16,20},{20,24},{24,28},{1,5},{5,9},{9,... | collective-permute-start | bytes 786440 | tf_op jit(solution)/shard_map/ppermute | solution.py:24
  49.0 12.1 %collective-permute-start.6 = (f32[8,512]{1,0:T(8,128)S(1)}, f32[8,512]{1,0:T(8,128)S(1)}, u32[]{:S(2)}, u32[]{:S(2)}) collective-permute-start(f32[8,512]{1,0:T(8,128)S(1)} %get-tuple-element.45), channel_id=1, source_target_pairs={{1,0},{2,1},{3,2},{5,4},{6,5},{7,6},{9,8},{10,9},{11,10},{13,12},{... | collective-permute-start | bytes 49160 | tf_op jit(solution)/shard_map/ppermute | solution.py:24
  50.3 10.8 %collective-permute-start.7 = (f32[8,512]{1,0:T(8,128)S(1)}, f32[8,512]{1,0:T(8,128)S(1)}, u32[]{:S(2)}, u32[]{:S(2)}) collective-permute-start(f32[8,512]{1,0:T(8,128)S(1)} %get-tuple-element.46.col7_ref), channel_id=1, source_target_pairs={{0,1},{1,2},{2,3},{4,5},{5,6},{6,7},{8,9},{9,10},{10,11},{12,13},{... | collective-permute-start | bytes 49160 | tf_op jit(solution)/shard_map/ppermute | solution.py:24
  61.7 17.1 %collective-permute-start.8 = (f32[128,512]{1,0:T(8,128)S(1)}, f32[128,512]{1,0:T(8,128)S(1)}, u32[]{:S(2)}, u32[]{:S(2)}) collective-permute-start(f32[128,512]{1,0:T(8,128)S(1)} %get-tuple-element.49), channel_id=1, source_target_pairs={{4,0},{8,4},{12,8},{16,12},{20,16},{24,20},{28,24},{5,1},{9,5},{13... | collective-permute-start | bytes 786440 | tf_op jit(solution)/shard_map/ppermute | solution.py:24
  63.0 15.8 %collective-permute-start.9 = (f32[128,512]{1,0:T(8,128)S(1)}, f32[128,512]{1,0:T(8,128)S(1)}, u32[]{:S(2)}, u32[]{:S(2)}) collective-permute-start(f32[128,512]{1,0:T(8,128)S(1)} %get-tuple-element.50.row7_ref), channel_id=1, source_target_pairs={{0,4},{4,8},{8,12},{12,16},{16,20},{20,24},{24,28},{1,5},{5,9},{9,... | collective-permute-start | bytes 786440 | tf_op jit(solution)/shard_map/ppermute | solution.py:24
  66.7 12.1 %collective-permute-start.10 = (f32[8,512]{1,0:T(8,128)S(1)}, f32[8,512]{1,0:T(8,128)S(1)}, u32[]{:S(2)}, u32[]{:S(2)}) collective-permute-start(f32[8,512]{1,0:T(8,128)S(1)} %get-tuple-element.51), channel_id=1, source_target_pairs={{1,0},{2,1},{3,2},{5,4},{6,5},{7,6},{9,8},{10,9},{11,10},{13,12},{... | collective-permute-start | bytes 49160 | tf_op jit(solution)/shard_map/ppermute | solution.py:24
  68.0 10.8 %collective-permute-start.11 = (f32[8,512]{1,0:T(8,128)S(1)}, f32[8,512]{1,0:T(8,128)S(1)}, u32[]{:S(2)}, u32[]{:S(2)}) collective-permute-start(f32[8,512]{1,0:T(8,128)S(1)} %get-tuple-element.52.col7_ref), channel_id=1, source_target_pairs={{0,1},{1,2},{2,3},{4,5},{5,6},{6,7},{8,9},{9,10},{10,11},{12,13},{... | collective-permute-start | bytes 49160 | tf_op jit(solution)/shard_map/ppermute | solution.py:24
